TPU v7x, 32 devices: a whole 2x2x4 slice. The times are simulated.
32 devices in a mesh: ctx: 8 (over y, x, core), exp: 4 (over z).
Axes of the slice: x: 2, y: 2, z: 4, core: 2. Of those that a mesh axis runs over, the one named last changes fastest.
Arguments:
- queries: bfloat16 [2048, 4096], P('ctx', 'exp'), may hold values from -6 to 6
- key_rows: bfloat16 [2048, 4096], P('ctx', 'exp'), may hold values from -6 to 6
- value_rows: bfloat16 [2048, 4096], P('ctx', 'exp'), may hold values from -6 to 6
- decay_rate: float32 [32], P('exp'), may hold values from 1.953125e-05 to 0.06
- out_weight: bfloat16 [4096, 3072], P('exp', 'ctx'), may hold values from -0.09375 to 0.09375
- residual: bfloat16 [2048, 3072], P(('ctx', 'exp')), may hold values from -6 to 6
- moe_gain: float32 [3072], replicated, may hold values from 0.1 to 1.9
- expert_ids: int32 [2048, 2], P(('ctx', 'exp')), may hold values from 0 to 3, all different within a row; in each aligned block of 64 rows (0 to 63, 64 to 127, ...) at most 48 rows name the same one
- gate_weight: bfloat16 [4, 4608, 3072], P('exp', 'ctx'), may hold values from -0.109375 to 0.109375
- up_weight: bfloat16 [4, 4608, 3072], P('exp', 'ctx'), may hold values from -0.109375 to 0.109375
Outputs:
- mixed: bfloat16 [2048, 3072], P(('ctx', 'exp'))
- expert_hidden: bfloat16 [4, 4608, 1536], P('exp', 'ctx')
Inputs may be any that keep to these rules, and one draw needn't show every extreme that they name: `expert_ids`: in each aligned block of 64 tokens (the rows of one device) no expert is named by more than 48 of the block's routes; some block names some expert exactly 48 times; a token's two ids differ.
All inputs are finite; a program needn't handle non-finite values.
Results may differ from a plain program's by a relative error of at most 0.0079.
Values may be sent and summed in bfloat16 or wider, within the bound.
No kernel may reach another device: no remote copies, remote signals or barrier semaphores. Data moves between devices by JAX's collectives and lax.ppermute only.
A program may use at most 64 MiB of HBM per device.

v0:
```python
import jax
import jax.numpy as jnp
from jax import lax
from jax.sharding import PartitionSpec as P


def entering(value, axis, combine, identity):
    devices, position = (lax.axis_size(axis), lax.axis_index(axis))
    everything = jax.tree.map(lambda part: lax.all_gather(part, axis), value)
    start = jax.tree.map(
        lambda part, zero: jnp.broadcast_to(jnp.asarray(zero, part.dtype), part.shape),
        value,
        identity,
    )

    def hop(k, before):
        reached = k < position
        new = combine(before, jax.tree.map(lambda part: part[k], everything))
        return jax.tree.map(lambda a, b: jnp.where(reached, a, b), new, before)

    return lax.fori_loop(0, devices, hop, start)


def route_slots(id_rows):
    count = id_rows.shape[1]
    same = id_rows[:, :, None] == id_rows[:, None, :]
    before = lax.broadcasted_iota(jnp.int32, (count, count), 1) < lax.broadcasted_iota(
        jnp.int32, (count, count), 0
    )
    return jnp.sum((same & before[None]).astype(jnp.int32), axis=2)


def select_matrix(id_rows, slot_rows, owners, capacity):
    routes = id_rows.shape[1]
    places = jnp.arange(capacity, dtype=jnp.int32)
    hits = (id_rows[:, None, None, :] == owners[None, :, None, None]) & (
        slot_rows[:, None, None, :] == places[None, None, :, None]
    )
    to_token = (
        jnp.arange(routes, dtype=jnp.int32)[:, None] // 2
        == jnp.arange(routes // 2, dtype=jnp.int32)[None, :]
    ).astype(jnp.float32)
    return jnp.einsum("bepr,rt->bept", hits.astype(jnp.float32), to_token)


def per_device(
    queries,
    key_rows,
    value_rows,
    decay_rate,
    out_weight,
    residual,
    moe_gain,
    expert_ids,
    gate_weight,
    up_weight,
):
    highest = lax.Precision.HIGHEST
    block_len = queries.shape[0]
    heads_here = decay_rate.shape[0]
    width_here = queries.shape[1]
    head_size = width_here // heads_here
    exp_count = lax.axis_size("exp")
    tok_count = block_len // exp_count
    capacity = max(2, 3 * tok_count // exp_count)
    query_here = queries.reshape(block_len, heads_here, head_size)
    key_here = key_rows.reshape(block_len, heads_here, head_size)
    value_here = value_rows.reshape(block_len, heads_here, head_size)
    position = jnp.arange(block_len, dtype=jnp.float32)
    offset = position[:, None] - position[None, :]
    masked = jnp.where(
        (offset >= 0)[None],
        jnp.exp(-decay_rate[:, None, None] * jnp.maximum(offset, 0.0)[None]),
        0.0,
    )
    inner = jnp.exp(-decay_rate[None, :] * position[:, None])
    tail = jnp.exp(-decay_rate[None, :] * (block_len - position[:, None]))
    whole = jnp.exp(-decay_rate * block_len)
    scores = jnp.einsum("ihd,jhd->hij", query_here, key_here, preferred_element_type=jnp.float32)
    weighted = (scores * masked).astype(jnp.bfloat16)
    local_part = jnp.einsum(
        "hij,jhd->ihd", weighted, value_here, preferred_element_type=jnp.float32
    )
    fresh = jnp.einsum(
        "jhd,jhe->hde",
        key_here.astype(jnp.float32) * tail[:, :, None],
        value_here.astype(jnp.float32),
        precision=highest,
    )

    def combine(earlier, later):
        return (earlier[0] * later[0], later[0][:, None, None] * earlier[1] + later[1])

    unused, state_in = entering(
        (whole, fresh), "ctx", combine, (jnp.ones_like(whole), jnp.zeros_like(fresh))
    )
    carried = (
        jnp.einsum("ihd,hde->ihe", query_here.astype(jnp.float32), state_in, precision=highest)
        * inner[:, :, None]
    )
    attended = local_part + carried
    scale_rows = lax.rsqrt(jnp.mean(attended * attended, axis=-1, keepdims=True) + 1e-05)
    head_out = (attended * scale_rows).astype(jnp.bfloat16).reshape(block_len, width_here)
    partial_rows = jnp.dot(
        head_out,
        lax.all_gather(out_weight, "ctx", axis=1, tiled=True),
        preferred_element_type=jnp.float32,
    )
    attn = lax.psum_scatter(partial_rows, "exp", scatter_dimension=0, tiled=True)
    mixed = (residual.astype(jnp.float32) + attn).astype(jnp.bfloat16)
    mixed_f = mixed.astype(jnp.float32)
    normed = (
        mixed_f * lax.rsqrt(jnp.mean(mixed_f * mixed_f, axis=-1, keepdims=True) + 1e-05) * moe_gain
    ).astype(jnp.bfloat16)
    id_rows = expert_ids.reshape(1, 2 * tok_count)
    slot_rows = route_slots(id_rows)
    picks = select_matrix(id_rows, slot_rows, jnp.arange(exp_count, dtype=jnp.int32), capacity)[0]
    picks = picks.reshape(exp_count * capacity, tok_count).astype(jnp.bfloat16)
    buffer = jnp.dot(picks, normed, preferred_element_type=jnp.float32).astype(jnp.bfloat16)
    received = lax.all_to_all(buffer, "exp", split_axis=0, concat_axis=0, tiled=True)
    gate_here = gate_weight[0]
    up_here = up_weight[0]
    contract = (((1,), (1,)), ((), ()))
    piece = lax.all_gather(received, "ctx", axis=0, tiled=True)
    gated = lax.dot_general(gate_here, piece, contract, preferred_element_type=jnp.float32)
    lifted = lax.dot_general(up_here, piece, contract, preferred_element_type=jnp.float32)
    hidden = (jax.nn.silu(gated) * lifted).astype(jnp.bfloat16)
    return (mixed, hidden[None])


def solution(mesh):
    in_specs = (
        P("ctx", "exp"),
        P("ctx", "exp"),
        P("ctx", "exp"),
        P("exp"),
        P("exp", "ctx"),
        P(("ctx", "exp"), None),
        P(),
        P(("ctx", "exp"), None),
        P("exp", "ctx", None),
        P("exp", "ctx", None),
    )
    out_specs = (P(("ctx", "exp"), None), P("exp", "ctx", None))
    return jax.shard_map(
        per_device, mesh=mesh, in_specs=in_specs, out_specs=out_specs, check_vma=False
    )
```

profile of v0, /device:TPU:0, one launch (start us, length us, event | category | flops | bytes accessed | tf_op | source)
XLA Modules:
  0.0 290.0 jit_solution(2006252163031624732)
XLA Ops:
  7.2 0.0 copy-start
  7.2 0.0 all-gather.10.cloned.1.call-start
  7.2 2.2 copy.41
  9.5 1.2 dynamic-slice
  11.4 0.7 fusion.48
  12.1 0.0 copy-start.5
  12.1 0.1 multiply_exponential_fusion
  12.2 0.4 copy-done.5
  12.6 2.7 fusion.18
  15.3 0.0 all-gather.10.cloned.1.call-update
  15.3 0.0 all-gather.6.cloned.1.call-start
  15.4 0.7 all-gather.6.cloned.1.call-update
  16.1 0.0 reduce-scatter.2.cloned.1.call-start
  16.2 16.0 %all-reduce = f32[64]{0:T(128)} all-reduce(f32[64]{0:T(128)} %copy-done.5), channel_id=2, replica_groups=mesh['ctx'=8,'exp'=4] {'ctx'}, use_global_device_ids=true, to_apply=%add | all-reduce | flops 64 | bytes 512
  32.1 0.7 reshape.299
  32.9 0.7 fusion.43
  33.6 0.8 fusion.42
  34.3 20.6 %all-gather.10.cloned.1.call-done = f32[64,128,128]{2,1,0:T(8,128)} async-done(((f32[8,128,128]{2,1,0:T(8,128)}), f32[64,128,128]{2,1,0:T(8,128)}) %all-gather.10.cloned.1.call-update) | async-done | bytes 4194320 | tf_op jit(solution)/shard_map/all_gather | solution.py:9
  54.9 16.9 %while.14 = (s32[]{:T(128)}, f32[8,128,128]{2,1,0:T(8,128)}, s32[]{:T(128)}, f32[8,8]{1,0:T(8,128)S(1)}, f32[8,8,128,128]{3,2,1,0:T(8,128)}, /*index=5*/s32[]{:T(128)}, s32[]{:T(128)}) while((s32[]{:T(128)}, f32[8,128,128]{2,1,0:T(8,128)}, s32[]{:T(128)}, f32[8,8]{1,0:T(8,128)S(1)}, f32[8,8,128,128]{3,2,1,0:T(8,128)}, ...), condition=%wide.region_1.2_spmd.clone, body=%wide.region_0.1_spmd.clone.sunk | while | flops 524292 | bytes 1573073 | solution.py:21
  54.9 2.0 fusion.64
  56.9 2.1 fusion.64
  59.0 2.1 fusion.64
  61.1 2.1 fusion.64
  63.3 2.2 fusion.64
  65.5 2.2 fusion.64
  67.7 2.1 fusion.64
  69.8 2.1 fusion.64
  71.9 2.8 fusion.17
  74.7 3.7 %multiply_reduce_fusion = (f32[256,8]{0,1:T(8,128)S(1)}, f32[256,8,128]{0,2,1:T(8,128)}) fusion(f32[256,8,128]{0,2,1:T(8,128)} %fusion.17, bf16[256,8,128]{0,2,1:T(8,128)(2,1)} %bitcast.99, f32[256,256]{1,0:T(8,128)} %fusion.42, f32[8]{0:T(128)S(1)} %get-tuple-element.129, pred[256,256]{1,0:T(8,128)(4,1)} %fusion.43, bf16[256,1024]{1,0:T(8,128)(2,1)} %param.14, ...), kind=kOutput, calls=%fused_computation.24 | convolution fusion | flops 271316992 | bytes 4005920 | tf_op jit(solution)/shard_map/hij,jhd->ihd/dot_general | solution.py:81
  78.4 2.1 multiply_convert_fusion.1
  80.5 23.0 %all-gather.6.cloned.1.call-done = bf16[1024,3072]{1,0:T(8,128)(2,1)} async-done(((bf16[1024,384]{1,0:T(8,128)(2,1)}), bf16[1024,3072]{1,0:T(8,128)(2,1)}) %all-gather.6.cloned.1.call-update) | async-done | bytes 6291472 | tf_op jit(solution)/shard_map/all_gather | solution.py:106
  103.5 0.0 copy-start.2
  103.5 6.5 %fusion.51 = f32[256,3072]{1,0:T(8,128)} fusion(bf16[256,1024]{0,1:T(8,128)(2,1)} %bitcast.97, bf16[1024,3072]{1,0:T(8,128)(2,1)} %all-gather.6.cloned.1.call-done), kind=kOutput, calls=%fused_computation.72 | convolution fusion | flops 1610612736 | bytes 9961472 | tf_op jit(solution)/shard_map/dot_general | solution.py:104
  110.0 0.0 copy-start.1
  110.0 0.0 reduce-scatter.2.cloned.1.call-update
  110.1 0.0 all-gather.8.cloned.1.call-start
  110.1 0.0 copy-done.2
  110.1 0.7 copy.39
  110.8 1.4 eq.72
  112.2 0.9 convert_reduce_fusion
  113.1 0.7 iota_compare_fusion.5
  113.8 0.6 broadcast_and_fusion
  114.4 56.0 %reduce-scatter.2.cloned.1.call-done = f32[64,3072]{1,0:T(8,128)} async-done(((f32[256,3072]{1,0:T(8,128)}), f32[64,3072]{1,0:T(8,128)}) %reduce-scatter.2.cloned.1.call-update) | async-done | bytes 786448 | tf_op jit(solution)/shard_map/reduce_scatter | solution.py:109
  170.5 2.2 fusion.25
  172.7 0.6 add_rsqrt_fusion.1
  173.3 0.0 copy-done.1
  173.3 2.8 convolution_convert_fusion
  176.1 33.0 %all_to_all.12 = bf16[4,48,3072]{2,1,0:T(8,128)(2,1)} all-to-all(bf16[4,48,3072]{2,1,0:T(8,128)(2,1)} %bitcast.96), channel_id=1, replica_groups=mesh['ctx'=8,'exp'=4] {'exp'}, dimensions={0} | all-to-all | bytes 2359296 | tf_op jit(solution)/shard_map/all_to_all | solution.py:120
  209.1 0.0 all-gather.8.cloned.1.call-update
  209.1 58.0 %all-gather.8.cloned.1.call-done = bf16[1536,3072]{1,0:T(8,128)(2,1)} async-done(((bf16[192,3072]{1,0:T(8,128)(2,1)}), bf16[1536,3072]{1,0:T(8,128)(2,1)}) %all-gather.8.cloned.1.call-update) | async-done | bytes 9437200 | tf_op jit(solution)/shard_map/all_gather | solution.py:124
  267.1 0.0 copy-done
  267.1 0.0 copy-start.3
  267.1 0.0 copy-start.4
  267.1 9.2 %fusion.7 = f32[1536,576]{0,1:T(8,128)S(1)} fusion(bf16[1536,3072]{1,0:T(8,128)(2,1)} %all-gather.8.cloned.1.call-done, bf16[1,576,3072]{2,1,0:T(8,128)(2,1)S(1)} %copy-done), kind=kOutput, calls=%fused_computation.13 | convolution fusion | flops 5435817984 | bytes 16515072 | tf_op jit(solution)/shard_map/dot_general | solution.py:125
  276.3 0.0 copy-done.3
  276.3 0.0 copy-done.4
  276.3 7.1 %fusion.11 = bf16[1,576,1536]{2,1,0:T(8,128)(2,1)} fusion(bf16[1536,3072]{1,0:T(8,128)(2,1)S(1)} %copy-done.3, bf16[1,576,3072]{2,1,0:T(8,128)(2,1)S(1)} %copy-done.4, f32[1536,576]{0,1:T(8,128)S(1)} %fusion.7), kind=kOutput, calls=%fused_computation.15 | convolution fusion | flops 5441126400 | bytes 18284544 | tf_op jit(solution)/shard_map/dot_general | solution.py:126
  (14 shorter events, 0.1 us)
Async XLA Ops:
  7.2 259.9 %copy-start = (bf16[1,576,3072]{2,1,0:T(8,128)(2,1)S(1)}, bf16[1,576,3072]{2,1,0:T(8,128)(2,1)}, u32[]{:S(2)}) copy-start(bf16[1,576,3072]{2,1,0:T(8,128)(2,1)} %param.20) | copy-start | bytes 10616836
  7.2 47.8 %all-gather.10.cloned.1.call-start = ((), (), s32[]{:S(2)}) async-start(), calls=%async_computation.5 | async-start | bytes 4718592 | tf_op jit(solution)/shard_map/all_gather | solution.py:9
  12.1 0.5 copy-start.5
  15.3 88.2 %all-gather.6.cloned.1.call-start = ((), (), s32[]{:S(2)}) async-start(), calls=%async_computation.2 | async-start | bytes 7077888 | tf_op jit(solution)/shard_map/all_gather | solution.py:106
  16.1 154.4 %reduce-scatter.2.cloned.1.call-start = ((), (), s32[]{:S(2)}) async-start(), calls=%async_computation.3 | async-start | bytes 3932160 | tf_op jit(solution)/shard_map/reduce_scatter | solution.py:109
  103.5 6.6 %copy-start.2 = (s32[64,2]{0,1:T(2,128)S(1)}, s32[64,2]{0,1:T(2,128)}, u32[]{:S(2)}) copy-start(s32[64,2]{0,1:T(2,128)} %param.19) | copy-start | bytes 1540
  110.0 63.2 %copy-start.1 = (f32[3072]{0:T(1024)S(1)}, f32[3072]{0:T(1024)}, u32[]{:S(2)}) copy-start(f32[3072]{0:T(1024)} %param.18) | copy-start | bytes 36868
  110.1 157.0 %all-gather.8.cloned.1.call-start = ((), (), s32[]{:S(2)}) async-start(), calls=%async_computation.4 | async-start | bytes 10616832 | tf_op jit(solution)/shard_map/all_gather | solution.py:124
  267.1 9.2 %copy-start.3 = (bf16[1536,3072]{1,0:T(8,128)(2,1)S(1)}, bf16[1536,3072]{1,0:T(8,128)(2,1)}, u32[]{:S(2)}) copy-start(bf16[1536,3072]{1,0:T(8,128)(2,1)} %all-gather.8.cloned.1.call-done) | copy-start | bytes 28311556
  267.1 9.2 %copy-start.4 = (bf16[1,576,3072]{2,1,0:T(8,128)(2,1)S(1)}, bf16[1,576,3072]{2,1,0:T(8,128)(2,1)}, u32[]{:S(2)}) copy-start(bf16[1,576,3072]{2,1,0:T(8,128)(2,1)} %param.21) | copy-start | bytes 10616836
Sparse Core Ops, SparseCore 0:
  15.5 39.4 all-gather.9
  56.8 46.6 all-gather.5
  110.2 60.2 reduce-scatter.1
  209.2 57.8 all-gather.7
where the time goes:
time: 291 us; the launch traced here: 290 us
  waiting for transfers between devices  158 us (54%)
  blocking collectives  49 us (17%)
  matrix products  34.8 us (12%)
  other arithmetic  26.3 us (9%)
  between operations  14.5 us (5%)
  local copies, waits for them, and re-layouts  6.81 us (2%)
    all_gather x1, waiting for transfers between devices, per_device(): piece = lax.all_gather(received, 'ctx', axis=0, tiled=True)  58 us
    reduce_scatter x1, waiting for transfers between devices, per_device(): lax.psum_scatter(partial_rows, 'exp', scatter_dimension=0, tiled=True)  56 us
    all_to_all x1, blocking collectives, per_device(): lax.all_to_all(buffer, 'exp', split_axis=0, concat_axis=0, tiled=True)  33 us
    all_gather x1, waiting for transfers between devices, per_device(): lax.all_gather(out_weight, 'ctx', axis=1, tiled=True)  23 us
    all_gather x1, waiting for transfers between devices, entering(): everything = jax.tree.map(lambda part: lax.all_gather(part, axis), value)  20.6 us
    select_n x8, other arithmetic, hop(): return jax.tree.map(lambda a, b: jnp.where(reached, a, b), new, before)  16.9 us
    unnamed x1, blocking collectives  16 us
    dot_general x1, matrix products, per_device(): lax.dot_general(gate_here, piece, contract, preferred_element_type=jnp.fl...  9.19 us
  transfers between devices with their start and end apart: 4, of which 4 were waited for; matrix products, arithmetic and copies ran while one was open for 11% of the time, Pallas kernels for 0%

commit v1 on v0

v1 whole, which is shorter than its diff:
```python
import functools

import jax
import jax.numpy as jnp
from jax import lax
from jax.experimental import pallas as pl
from jax.experimental.pallas import tpu as pltpu
from jax.sharding import PartitionSpec as P

GROUPS = 4
VMEM_LIMIT = 48 * 1024 * 1024
BF16 = jnp.bfloat16
F32 = jnp.float32
NT = (((1,), (1,)), ((), ()))
TN = (((0,), (0,)), ((), ()))
NN = (((1,), (0,)), ((), ()))


def dot(a, b, dims):
    return lax.dot_general(a, b, dims, preferred_element_type=F32)


def halves(x):
    high = x.astype(BF16)
    return high, (x - high.astype(F32)).astype(BF16)


def call(kernel, out_shape, flops, nbytes, exps=0, **kwargs):
    return pl.pallas_call(
        kernel,
        out_shape=out_shape,
        compiler_params=pltpu.CompilerParams(vmem_limit_bytes=VMEM_LIMIT),
        cost_estimate=pl.CostEstimate(
            flops=int(flops), bytes_accessed=int(nbytes), transcendentals=int(exps)
        ),
        **kwargs,
    )


VM = pl.BlockSpec(memory_space=pltpu.VMEM)
SM = pl.BlockSpec(memory_space=pltpu.SMEM)


def fresh_kernel(rate_ref, k_ref, v_ref, out_ref):
    heads, size = out_ref.shape[0], out_ref.shape[1]
    length = k_ref.shape[0]
    left = length - lax.broadcasted_iota(jnp.int32, (length, size), 0).astype(F32)
    for h in range(heads):
        cols = slice(h * size, (h + 1) * size)
        tail = jnp.exp(-rate_ref[h] * left)
        high, low = halves(k_ref[:, cols].astype(F32) * tail)
        v = v_ref[:, cols]
        out_ref[h] = dot(high, v, TN) + dot(low, v, TN)


def local_kernel(rate_ref, q_ref, k_ref, v_ref, out_ref):
    heads = rate_ref.shape[0]
    length = k_ref.shape[0]
    size = k_ref.shape[1] // heads
    rows = lax.broadcasted_iota(jnp.int32, (length, length), 0)
    cols = lax.broadcasted_iota(jnp.int32, (length, length), 1)
    offset = (rows - cols).astype(F32)
    keep = offset >= 0
    offset = jnp.maximum(offset, 0.0)
    for h in range(heads):
        at = slice(h * size, (h + 1) * size)
        masked = jnp.where(keep, jnp.exp(-rate_ref[h] * offset), 0.0)
        weighted = (dot(q_ref[:, at], k_ref[:, at], NT) * masked).astype(BF16)
        out_ref[:, at] = dot(weighted, v_ref[:, at], NN)


def head_kernel(rate_ref, coef_ref, q_ref, local_ref, state_ref, got_ref, out_ref):
    heads, size = state_ref.shape[0], state_ref.shape[1]
    length = q_ref.shape[0]
    pos = lax.broadcasted_iota(jnp.int32, (length, size), 0).astype(F32)
    for h in range(heads):
        at = slice(h * size, (h + 1) * size)
        state = state_ref[h] + coef_ref[h] * got_ref[h].astype(F32)
        high, low = halves(state)
        q = q_ref[:, at]
        carried = (dot(q, high, NN) + dot(q, low, NN)) * jnp.exp(-rate_ref[h] * pos)
        attended = local_ref[:, at] + carried
        scale = lax.rsqrt(jnp.mean(attended * attended, axis=-1, keepdims=True) + 1e-05)
        out_ref[:, at] = (attended * scale).astype(BF16)


def xor_permute(x, step):
    n = lax.axis_size("ctx")
    return lax.ppermute(x, "ctx", [(d, d ^ step) for d in range(n)])


def across_groups(x):
    low = lax.axis_size("ctx") // GROUPS
    cut = x.shape[0] // 2
    one = xor_permute(x, low)
    two = xor_permute(x, 2 * low)
    top = xor_permute(one[:cut], 2 * low)
    bottom = xor_permute(two[cut:], low)
    return [x, one, two, jnp.concatenate([top, bottom], axis=0)]


def within_group(x):
    n = lax.axis_size("ctx")
    low = n // GROUPS
    got = [x]
    for step in range(1, low):
        got.append(
            lax.ppermute(
                x, "ctx", [(d, d // low * low + (d % low - step) % low) for d in range(n)]
            )
        )
    return got


def in_order(pieces, member, axis):
    low, width = len(pieces), pieces[0].shape[axis]
    ring = jnp.concatenate(pieces + pieces[:-1], axis=axis)
    return lax.dynamic_slice_in_dim(ring, lax.rem(low - member, low) * width, low * width, axis)


def line_sum(part, place):
    n = lax.axis_size("exp")
    half = n // 2
    for hop in range(half - 1):
        got = lax.ppermute(part.astype(BF16), "exp", [(hop, hop + 1), (n - 1 - hop, n - 2 - hop)])
        part = part + got.astype(F32)
    mine = part.astype(BF16)
    other = lax.ppermute(mine, "exp", [(half - 1, half), (half, half - 1)])
    total = (mine.astype(F32) + other.astype(F32)).astype(BF16)
    for hop in range(half - 1):
        here, there = half - 1 - hop, half + hop
        got = lax.ppermute(total, "exp", [(here, here - 1), (there, there + 1)])
        total = jnp.where((place == here - 1) | (place == there + 1), got, total)
    return total


def expert_kernel(chunks, low, final, has_acc, place_ref, *refs):
    refs = list(refs)
    pieces = [[refs.pop(0) for _ in range(low)] for _ in range(chunks)]
    gates = [refs.pop(0) for _ in range(chunks)]
    ups = [refs.pop(0) for _ in range(chunks)]
    sums = [refs.pop(0), refs.pop(0)] if has_acc else None
    if final and final != "first":
        refs.pop(0)
    outs = [refs.pop(0)] if final else [refs.pop(0), refs.pop(0)]
    held = refs
    rows = pieces[0][0].shape[0]

    @pl.when(pl.program_id(0) == 0)
    def _():
        for t in range(chunks):
            for a in range(low):
                member = lax.rem(place_ref[1] + a, low)
                held[t][pl.ds(pl.multiple_of(member * rows, rows), rows), :] = pieces[t][a][...]

    width = gates[0].shape[1]
    gated, lifted = (sums[0][...], sums[1][...]) if has_acc else (0.0, 0.0)
    for t in range(chunks):
        x = held[t][:, :width]
        gated = gated + dot(gates[t][...], x, NT)
        lifted = lifted + dot(ups[t][...], x, NT)
    if final:
        extra = held[chunks - 1][:, width:]
        pick = (lax.broadcasted_iota(jnp.int32, (8, extra.shape[1]), 1) < 3).astype(BF16)
        scale = dot(pick, extra, NT)[0:1, :]
        gated, lifted = gated * scale, lifted * scale
        outs[0][...] = (gated / (1.0 + jnp.exp(-gated)) * lifted).astype(BF16)
    else:
        outs[0][...] = gated
        outs[1][...] = lifted


def expert_step(place, s, chunk_ids, pieces, gate, up, sums, hidden, final, width):
    hid = gate.shape[0]
    low, rows = len(pieces[0]), pieces[0][0].shape[0]
    slots = low * rows
    block = max(b for b in range(16, min(hid, 192) + 1, 16) if hid % b == 0)
    chunks = len(chunk_ids)
    has_acc = sums is not None

    def whole(x):
        return pl.BlockSpec(x.shape, lambda r, p: (0, 0))

    def weight(t):
        return pl.BlockSpec((block, width), lambda r, p: (r, p[0] ^ (s ^ t)))

    acc_spec = pl.BlockSpec((block, slots), lambda r, p: (r, 0))
    operands = [x for per in pieces for x in per]
    specs = [whole(x) for x in operands]
    operands += [gate] * chunks + [up] * chunks
    specs += [weight(t) for t in chunk_ids] * 2
    if has_acc:
        operands += list(sums)
        specs += [acc_spec] * 2
    aliases = {}
    if final:
        out_shape = jax.ShapeDtypeStruct((hid, slots * GROUPS), BF16)
        out_specs = pl.BlockSpec((block, slots), lambda r, p: (r, p[0] ^ s))
        if hidden is not None:
            operands.append(hidden)
            specs.append(pl.BlockSpec(memory_space=pl.ANY))
            aliases = {len(operands): 0}
        mode = "first" if hidden is None else "next"
    else:
        out_shape = [jax.ShapeDtypeStruct((hid, slots), F32)] * 2
        out_specs = [acc_spec] * 2
        mode = None
    return call(
        functools.partial(expert_kernel, chunks, low, mode, has_acc),
        out_shape,
        4 * hid * slots * width * chunks,
        4 * hid * width * chunks + 8 * hid * slots * (1 + has_acc) + 2 * slots * width * chunks,
        hid * slots if final else 0,
        grid_spec=pltpu.PrefetchScalarGridSpec(
            num_scalar_prefetch=1,
            grid=(hid // block,),
            in_specs=specs,
            out_specs=out_specs,
            scratch_shapes=[pltpu.VMEM((slots, per[0].shape[1]), BF16) for per in pieces],
        ),
        input_output_aliases=aliases,
    )(place, *operands)


def per_device(
    queries,
    key_rows,
    value_rows,
    decay_rate,
    out_weight,
    residual,
    moe_gain,
    expert_ids,
    gate_weight,
    up_weight,
):
    n_ctx, n_exp = lax.axis_size("ctx"), lax.axis_size("exp")
    low = n_ctx // GROUPS
    ctx, exp = lax.axis_index("ctx"), lax.axis_index("exp")
    group, member = ctx // low, lax.rem(ctx, low)
    place = jnp.stack([group, member]).astype(jnp.int32)
    length, here = queries.shape
    heads = decay_rate.shape[0]
    size = here // heads
    model = residual.shape[1]
    width = model // GROUPS
    tokens = length // n_exp
    capacity = max(2, 3 * tokens // n_exp)

    state_type = jax.ShapeDtypeStruct((heads, size, size), F32)
    total = call(
        fresh_kernel,
        state_type,
        4 * heads * length * size * size,
        4 * length * here + 4 * heads * size * size,
        heads * length * size,
        in_specs=[SM, VM, VM],
        out_specs=VM,
    )(decay_rate, key_rows, value_rows)
    local = call(
        local_kernel,
        jax.ShapeDtypeStruct((length, here), F32),
        4 * heads * length * length * size,
        10 * length * here,
        heads * length * length,
        in_specs=[SM, VM, VM, VM],
        out_specs=VM,
    )(decay_rate, queries, key_rows, value_rows)

    def fade(blocks):
        return jnp.exp(-decay_rate * (length * blocks))

    state = jnp.zeros_like(total)
    got, coef = jnp.zeros(total.shape, BF16), jnp.zeros_like(decay_rate)
    step = 1
    while step < n_ctx:
        upper = (ctx & step) != 0
        coef = jnp.where(upper, fade((ctx & (step - 1)).astype(F32)), 0.0)
        if 2 * step < n_ctx:
            got = xor_permute(total.astype(BF16), step)
            gotten = got.astype(F32)
            state = state + coef[:, None, None] * gotten
            span = fade(float(step))[:, None, None]
            total = jnp.where(upper, span * gotten + total, span * total + gotten)
        else:
            got = lax.ppermute(total.astype(BF16), "ctx", [(d, d + step) for d in range(step)])
        step *= 2
    head_out = call(
        head_kernel,
        jax.ShapeDtypeStruct((length, here), BF16),
        4 * heads * length * size * size,
        8 * length * here + 6 * heads * size * size,
        heads * length * size,
        in_specs=[SM, SM, VM, VM, VM, VM],
        out_specs=VM,
    )(decay_rate, coef, queries, local, state, got)

    columns = [in_order(within_group(w), member, 1) for w in across_groups(out_weight)]

    ids = expert_ids.T
    id_parts = [ids]
    for shift in range(1, n_exp):
        id_parts.append(
            lax.ppermute(ids, "exp", [(d, (d - shift) % n_exp) for d in range(n_exp)])
        )
    all_ids = in_order_ring(id_parts, exp)
    named = (all_ids[0] == exp) | (all_ids[1] == exp)
    token = jnp.arange(length, dtype=jnp.int32)
    earlier = (token[:, None] < token[None, :]) & (
        token[:, None] // tokens == token[None, :] // tokens
    )
    rank = jnp.sum((earlier & named[:, None]).astype(jnp.int32), axis=0)
    row = jnp.where(named & (rank < capacity), token // tokens * capacity + rank, -1)
    slots = jnp.arange(n_exp * capacity, dtype=jnp.int32)
    picks = slots[:, None] == row[None, :]

    own_rows = (exp * tokens).astype(jnp.int32)
    mixed_out = jnp.zeros((tokens, model), BF16)
    squares = jnp.zeros((length,), F32)
    received = []
    for t in range(GROUPS):
        start = ((group ^ t) * width).astype(jnp.int32)
        part = dot(head_out, columns[t], NN)
        own = lax.dynamic_slice(residual, (jnp.int32(0), start), (tokens, width)).astype(F32)
        tiled = jnp.tile(own, (n_exp, 1))
        part = part + jnp.where((token // tokens == exp)[:, None], tiled, 0.0)
        mixed = line_sum(part, exp)
        mixed_out = lax.dynamic_update_slice(
            mixed_out,
            lax.dynamic_slice(mixed, (own_rows, jnp.int32(0)), (tokens, width)),
            (jnp.int32(0), start),
        )
        mixed_f = mixed.astype(F32)
        squares = squares + jnp.sum(mixed_f * mixed_f, axis=1)
        gain = lax.dynamic_slice(moe_gain, (start,), (width,))
        rows = dot(picks.astype(BF16), (mixed_f * gain).astype(BF16), NN).astype(BF16)
        if t == GROUPS - 1:
            scale = lax.rsqrt(squares / model + 1e-05)
            scale = jnp.sum(jnp.where(picks, scale[None, :], 0.0), axis=1)
            high, rest = scale.astype(BF16), scale
            parts = []
            for _ in range(3):
                high = rest.astype(BF16)
                rest = rest - high.astype(F32)
                parts.append(high)
            extra = jnp.stack(parts, axis=1)
            rows = jnp.concatenate(
                [rows, jnp.pad(extra, ((0, 0), (0, 128 - extra.shape[1])))], axis=1
            )
        received.append([within_group(x) for x in across_groups(rows)])

    gate, up = gate_weight[0], up_weight[0]
    sums = [None] * GROUPS
    early = list(range(GROUPS - 1))
    for s in range(GROUPS):
        sums[s] = expert_step(
            place, s, early, [received[t][s] for t in early], gate, up, None, None, False, width
        )
    hidden = None
    for s in range(GROUPS):
        last = GROUPS - 1
        hidden = expert_step(
            place, s, [last], [received[last][s]], gate, up, sums[s], hidden, True, width
        )
    return (mixed_out, hidden[None])


def in_order_ring(parts, first):
    n, width = len(parts), parts[0].shape[1]
    ring = jnp.concatenate(parts + parts[:-1], axis=1)
    return lax.dynamic_slice_in_dim(ring, lax.rem(n - first, n) * width, n * width, 1)


def solution(mesh):
    in_specs = (
        P("ctx", "exp"),
        P("ctx", "exp"),
        P("ctx", "exp"),
        P("exp"),
        P("exp", "ctx"),
        P(("ctx", "exp"), None),
        P(),
        P(("ctx", "exp"), None),
        P("exp", "ctx", None),
        P("exp", "ctx", None),
    )
    out_specs = (P(("ctx", "exp"), None), P("exp", "ctx", None))
    return jax.shard_map(
        per_device, mesh=mesh, in_specs=in_specs, out_specs=out_specs, check_vma=False
    )
```

time: 291 us -> 213 us (0.73)
  waiting for transfers between devices: 158 us -> 65.2 us
  starting transfers between devices: 0.16 us -> 66.5 us
  blocking collectives: 49 us -> 0 us
  Pallas kernels: 0 us -> 48.2 us
  matrix products: 34.8 us -> 10.7 us
  other arithmetic: 26.3 us -> 5.39 us
  between operations: 14.5 us -> 1.43 us
  local copies, waits for them, and re-layouts: 6.81 us -> 14 us
    all_gather x3 -> x0, waiting for transfers between devices: 102 us -> none  [the longest x1 58 us: per_device(): piece = lax.all_gather(received, 'ctx', axis=0, tiled=True)]
    ppermute x0 -> x58, starting transfers between devices: none -> 66.5 us  [the longest x22 27.2 us: xor_permute(): return lax.ppermute(x, 'ctx', [(d, d ^ step) for d in range(n)])]
    ppermute x0 -> x58, waiting for transfers between devices: none -> 65.2 us  [the longest x22 17.9 us: xor_permute(): return lax.ppermute(x, 'ctx', [(d, d ^ step) for d in range(n)])]
    reduce_scatter x1 -> x0, waiting for transfers between devices: 56 us -> none  [per_device(): lax.psum_scatter(partial_rows, 'exp', scatter_dimension=0, tiled=True)]
    pallas_call x0 -> x11, Pallas kernels: none -> 48.2 us  [the longest x8 44.4 us: expert_step(): call(functools.partial(expert_kernel, chunks, low, mode, has_acc), out_sh...]
    all_to_all x1 -> x0, blocking collectives: 33 us -> none  [per_device(): lax.all_to_all(buffer, 'exp', split_axis=0, concat_axis=0, tiled=True)]
    dot_general x7 -> x8, matrix products: 34.8 us -> 10.7 us  [dot(): return lax.dot_general(a, b, dims, preferred_element_type=F32)]
    unnamed x1 -> x0, blocking collectives: 16 us -> none
  transfers between devices with their start and end apart: 4 -> 58, of which waited for: 4 -> 17; matrix products, arithmetic and copies ran while one was open for 11% -> 12% of each run, Pallas kernels for 0% -> 20%
where the time goes in v1:
time: 213 us; the launch traced here: 211 us
  starting transfers between devices  66.5 us (31%)
  waiting for transfers between devices  65.2 us (31%)
  Pallas kernels  48.2 us (23%)
  local copies, waits for them, and re-layouts  14 us (7%)
  matrix products  10.7 us (5%)
  other arithmetic  5.39 us (3%)
    pallas_call x8, Pallas kernels, expert_step(): call(functools.partial(expert_kernel, chunks, low, mode, has_acc), out_sh...  44.4 us
    ppermute x22, starting transfers between devices, xor_permute(): return lax.ppermute(x, 'ctx', [(d, d ^ step) for d in range(n)])  27.2 us
    ppermute x4, starting transfers between devices, line_sum(): lax.ppermute(part.astype(BF16), 'exp', [(hop, hop + 1), (n - 1 - hop, n -...  19.1 us
    ppermute x22, waiting for transfers between devices, xor_permute(): return lax.ppermute(x, 'ctx', [(d, d ^ step) for d in range(n)])  17.9 us
    ppermute x4, waiting for transfers between devices, line_sum(): got = lax.ppermute(total, 'exp', [(here, here - 1), (there, there + 1)])  13.3 us
    ppermute x4, waiting for transfers between devices, line_sum(): lax.ppermute(part.astype(BF16), 'exp', [(hop, hop + 1), (n - 1 - hop, n -...  11.9 us
    ppermute x1, waiting for transfers between devices, per_device(): lax.ppermute(total.astype(BF16), 'ctx', [(d, d + step) for d in range(ste...  11.2 us
    ppermute x3, waiting for transfers between devices, per_device(): lax.ppermute(ids, 'exp', [(d, (d - shift) % n_exp) for d in range(n_exp)])  10.9 us
  transfers between devices with their start and end apart: 58, of which 17 were waited for; matrix products, arithmetic and copies ran while one was open for 12% of the time, Pallas kernels for 20%

profile of v1, /device:TPU:0, one launch (start us, length us, event | category | flops | bytes accessed | tf_op | source)
XLA Modules:
  0.0 211.5 jit_solution(12747744691107165908)
XLA Ops:
  0.6 1.0 copy-done.2
  1.7 1.0 copy-done.4
  3.4 1.1 shard_map.114
  5.1 1.1 collective-permute-done
  6.4 2.9 %collective-permute-start.1 = (bf16[8,128,128]{2,1,0:T(8,128)(2,1)S(1)}, bf16[8,128,128]{2,1,0:T(8,128)(2,1)S(1)}, u32[]{:S(2)}, u32[]{:S(2)}) collective-permute-start(bf16[8,128,128]{2,1,0:T(8,128)(2,1)S(1)} %fusion.54), channel_id=1, source_target_pairs={{0,8},{4,12},{8,0},{12,4},{16,24},{20,28},{24,16},{28,20},{1,9},{5... | collective-permute-start | bytes 786440 | tf_op jit(solution)/shard_map/ppermute | solution.py:89
  9.3 1.5 collective-permute-start.12
  10.9 3.6 %collective-permute-start.23 = (s32[2,64]{1,0:T(2,128)S(1)}, s32[2,64]{1,0:T(2,128)S(1)}, u32[]{:S(2)}, u32[]{:S(2)}) collective-permute-start(s32[2,64]{1,0:T(2,128)S(1)} %bitcast.62), channel_id=1, source_target_pairs={{0,3},{1,0},{2,1},{3,2},{4,7},{5,4},{6,5},{7,6},{8,11},{9,8},{10,9... | collective-permute-start | bytes 1544 | tf_op jit(solution)/shard_map/ppermute | solution.py:304
  14.5 1.5 collective-permute-done.1
  16.3 3.8 %collective-permute-start.2 = (bf16[8,128,128]{2,1,0:T(8,128)(2,1)S(1)}, bf16[8,128,128]{2,1,0:T(8,128)(2,1)S(1)}, u32[]{:S(2)}, u32[]{:S(2)}) collective-permute-start(bf16[8,128,128]{2,1,0:T(8,128)(2,1)S(1)} %get-tuple-element.28), channel_id=1, source_target_pairs={{0,16},{4,20},{8,24},{12,28},{1,17},{5,21},{9,25},{13,29},{2,18},{... | collective-permute-start | bytes 786440 | tf_op jit(solution)/shard_map/ppermute | solution.py:286
  20.2 1.2 bitcast_select_fusion
  21.4 1.5 shard_map.113.local_ref
  23.0 11.2 %collective-permute-done.2.got_ref = bf16[8,128,128]{2,1,0:T(8,128)(2,1)S(1)} collective-permute-done((bf16[8,128,128]{2,1,0:T(8,128)(2,1)S(1)}, bf16[8,128,128]{2,1,0:T(8,128)(2,1)S(1)}, u32[]{:S(2)}, u32[]{:S(2)}) %collective-permute-start.2) | collective-permute-done | bytes 262176 | tf_op jit(solution)/shard_map/ppermute | solution.py:286
  34.7 1.2 shard_map.115
  35.9 0.9 copy-done.16
  36.8 3.2 %fusion.72 = (bf16[256,768]{1,0:T(8,128)(2,1)}, f32[256,768]{1,0:T(8,128)S(1)}) fusion(f32[256,768]{1,0:T(8,128)S(1)} %get-tuple-element.43, bf16[256,1024]{1,0:T(8,128)(2,1)S(1)} %shard_map.115, s32[]{:T(128)S(6)} %select_n.165, bf16[1024,384]{1,0:T(8,128)(2,1)} %param.14, bf16[1024,384]{1,0:T(8,128)(2,1)} %copy-done.16), kind=kOutput, calls=%fused_computation.147 | convolution fusion | flops 407764992 | bytes 4063236 | tf_op jit(solution)/shard_map/dot_general | solution.py:20
  40.0 3.5 %collective-permute-start.4 = (bf16[256,768]{1,0:T(8,128)(2,1)}, bf16[256,768]{1,0:T(8,128)(2,1)S(1)}, u32[]{:S(2)}, u32[]{:S(2)}) collective-permute-start(bf16[256,768]{1,0:T(8,128)(2,1)} %get-tuple-element.49), channel_id=1, source_target_pairs={{0,1},{3,2},{4,5},{7,6},{8,9},{11,10},{12,13},{15,14},{16,17},{19,... | collective-permute-start | bytes 1179656 | tf_op jit(solution)/shard_map/ppermute | solution.py:125
  43.7 10.9 %collective-permute-done.25 = s32[2,64]{1,0:T(2,128)S(1)} collective-permute-done((s32[2,64]{1,0:T(2,128)S(1)}, s32[2,64]{1,0:T(2,128)S(1)}, u32[]{:S(2)}, u32[]{:S(2)}) %collective-permute-start.25) | collective-permute-done | bytes 544 | tf_op jit(solution)/shard_map/ppermute | solution.py:304
  55.0 1.0 slice.48
  56.0 2.6 %collective-permute-start.17 = (bf16[512,384]{1,0:T(8,128)(2,1)S(1)}, bf16[512,384]{1,0:T(8,128)(2,1)S(1)}, u32[]{:S(2)}, u32[]{:S(2)}) collective-permute-start(bf16[512,384]{1,0:T(8,128)(2,1)S(1)} %slice.48), channel_id=1, source_target_pairs={{0,16},{4,20},{8,24},{12,28},{16,0},{20,4},{24,8},{28,12},{1,17},{... | collective-permute-start | bytes 1179656 | tf_op jit(solution)/shard_map/ppermute | solution.py:89
  58.6 1.0 slice.49
  59.6 1.6 collective-permute-start.18
  62.6 3.5 %collective-permute-done.17 = bf16[512,384]{1,0:T(8,128)(2,1)S(1)} collective-permute-done((bf16[512,384]{1,0:T(8,128)(2,1)S(1)}, bf16[512,384]{1,0:T(8,128)(2,1)S(1)}, u32[]{:S(2)}, u32[]{:S(2)}) %collective-permute-start.17) | collective-permute-done | bytes 393248 | tf_op jit(solution)/shard_map/ppermute | solution.py:89
  66.1 2.5 %collective-permute-done.18 = bf16[512,384]{1,0:T(8,128)(2,1)S(1)} collective-permute-done((bf16[512,384]{1,0:T(8,128)(2,1)S(1)}, bf16[512,384]{1,0:T(8,128)(2,1)S(1)}, u32[]{:S(2)}, u32[]{:S(2)}) %collective-permute-start.18) | collective-permute-done | bytes 393248 | tf_op jit(solution)/shard_map/ppermute | solution.py:89
  68.9 1.3 collective-permute-start.6
  70.2 2.2 %fusion.74 = (bf16[256,768]{1,0:T(8,128)(2,1)S(1)}, f32[256,768]{1,0:T(8,128)S(1)}) fusion(f32[256,768]{1,0:T(8,128)S(1)} %copy-done.11, bf16[256,1024]{1,0:T(8,128)(2,1)S(1)} %shard_map.115, s32[]{:T(128)S(6)} %select_n.165, bf16[1024,384]{1,0:T(8,128)(2,1)} %collective-permute-done.12, bf16[1024,384]{1,0:T(8,128)(2,1)S(1)} %collective-permute-done.13), kind=kOutput, calls=%fused_computation.149 | convolution fusion | flops 407764992 | bytes 4063236 | tf_op jit(solution)/shard_map/dot_general | solution.py:20
  72.5 7.4 %collective-permute-start.14 = (bf16[256,768]{1,0:T(8,128)(2,1)S(1)}, bf16[256,768]{1,0:T(8,128)(2,1)S(1)}, u32[]{:S(2)}, u32[]{:S(2)}) collective-permute-start(bf16[256,768]{1,0:T(8,128)(2,1)S(1)} %get-tuple-element.53), channel_id=1, source_target_pairs={{0,1},{3,2},{4,5},{7,6},{8,9},{11,10},{12,13},{15,14},{16,17},{19,... | collective-permute-start | bytes 1179656 | tf_op jit(solution)/shard_map/ppermute | solution.py:125
  79.9 2.2 %fusion.73 = (bf16[256,768]{1,0:T(8,128)(2,1)S(1)}, f32[256,768]{1,0:T(8,128)S(1)}) fusion(f32[256,768]{1,0:T(8,128)S(1)} %get-tuple-element.41, bf16[256,1024]{1,0:T(8,128)(2,1)S(1)} %shard_map.115, s32[]{:T(128)S(6)} %select_n.165, bf16[1024,384]{1,0:T(8,128)(2,1)} %collective-permute-done.7, bf16[1024,384]{1,0:T(8,128)(2,1)S(1)} %collective-permute-done.8), kind=kOutput, calls=%fused_computation.148 | convolution fusion | flops 407764992 | bytes 4063236 | tf_op jit(solution)/shard_map/dot_general | solution.py:20
  82.1 1.3 collective-permute-start.9
  83.4 1.2 collective-permute-done.6
  85.1 1.3 collective-permute-start.31
  86.4 2.9 %collective-permute-done.14 = bf16[256,768]{1,0:T(8,128)(2,1)S(1)} collective-permute-done((bf16[256,768]{1,0:T(8,128)(2,1)S(1)}, bf16[256,768]{1,0:T(8,128)(2,1)S(1)}, u32[]{:S(2)}, u32[]{:S(2)}) %collective-permute-start.14) | collective-permute-done | bytes 393248 | tf_op jit(solution)/shard_map/ppermute | solution.py:125
  90.1 6.4 %collective-permute-done.9 = bf16[256,768]{1,0:T(8,128)(2,1)S(1)} collective-permute-done((bf16[256,768]{1,0:T(8,128)(2,1)S(1)}, bf16[256,768]{1,0:T(8,128)(2,1)S(1)}, u32[]{:S(2)}, u32[]{:S(2)}) %collective-permute-start.9) | collective-permute-done | bytes 393248 | tf_op jit(solution)/shard_map/ppermute | solution.py:125
  97.3 1.1 fusion.75
  98.4 6.9 %collective-permute-start.20 = (bf16[256,768]{1,0:T(8,128)(2,1)S(1)}, bf16[256,768]{1,0:T(8,128)(2,1)S(1)}, u32[]{:S(2)}, u32[]{:S(2)}) collective-permute-start(bf16[256,768]{1,0:T(8,128)(2,1)S(1)} %get-tuple-element.55), channel_id=1, source_target_pairs={{0,1},{3,2},{4,5},{7,6},{8,9},{11,10},{12,13},{15,14},{16,17},{19,... | collective-permute-start | bytes 1179656 | tf_op jit(solution)/shard_map/ppermute | solution.py:125
  105.4 1.6 collective-permute-start.34
  107.1 1.3 collective-permute-start.16
  108.5 1.3 collective-permute-start.11
  109.8 2.5 %collective-permute-done.20 = bf16[256,768]{1,0:T(8,128)(2,1)S(1)} collective-permute-done((bf16[256,768]{1,0:T(8,128)(2,1)S(1)}, bf16[256,768]{1,0:T(8,128)(2,1)S(1)}, u32[]{:S(2)}, u32[]{:S(2)}) %collective-permute-start.20) | collective-permute-done | bytes 393248 | tf_op jit(solution)/shard_map/ppermute | solution.py:125
  113.3 7.7 %collective-permute-done.16 = bf16[256,768]{1,0:T(8,128)(2,1)S(1)} collective-permute-done((bf16[256,768]{1,0:T(8,128)(2,1)S(1)}, bf16[256,768]{1,0:T(8,128)(2,1)S(1)}, u32[]{:S(2)}, u32[]{:S(2)}) %collective-permute-start.16) | collective-permute-done | bytes 393248 | tf_op jit(solution)/shard_map/ppermute | solution.py:132
  122.1 4.3 %collective-permute-done.11 = bf16[256,768]{1,0:T(8,128)(2,1)S(1)} collective-permute-done((bf16[256,768]{1,0:T(8,128)(2,1)S(1)}, bf16[256,768]{1,0:T(8,128)(2,1)S(1)}, u32[]{:S(2)}, u32[]{:S(2)}) %collective-permute-start.11) | collective-permute-done | bytes 393248 | tf_op jit(solution)/shard_map/ppermute | solution.py:132
  127.7 1.8 collective-permute-start.43
  130.1 4.5 %collective-permute-done.36.refs_2_ = bf16[192,768]{1,0:T(8,128)(2,1)S(1)} collective-permute-done((bf16[192,768]{1,0:T(8,128)(2,1)S(1)}, bf16[192,768]{1,0:T(8,128)(2,1)S(1)}, u32[]{:S(2)}, u32[]{:S(2)}) %collective-permute-start.36) | collective-permute-done | bytes 294944 | tf_op jit(solution)/shard_map/ppermute | solution.py:89
  134.6 2.0 collective-permute-start.38
  137.6 1.3 collective-permute-start.22
  141.0 2.5 %collective-permute-done.38.refs_2_ = bf16[192,768]{1,0:T(8,128)(2,1)S(1)} collective-permute-done((bf16[192,768]{1,0:T(8,128)(2,1)S(1)}, bf16[192,768]{1,0:T(8,128)(2,1)S(1)}, u32[]{:S(2)}, u32[]{:S(2)}) %collective-permute-start.38) | collective-permute-done | bytes 294944 | tf_op jit(solution)/shard_map/ppermute | solution.py:89
  144.2 1.7 collective-permute-start.42
  145.9 1.5 collective-permute-start.44
  147.7 6.1 %shard_map.119 = (f32[576,384]{1,0:T(8,128)S(1)}, f32[576,384]{1,0:T(8,128)S(1)}) custom-call(s32[2]{0:T(128)S(1)} %pad_add_fusion.place_ref, bf16[192,768]{1,0:T(8,128)(2,1)S(1)} %convolution_convert_fusion.2.refs_0_, bf16[192,768]{1,0:T(8,128)(2,1)S(1)} %collective-permute-done.55.refs_1_, bf16[192,768]{1,0:T(8,128)(2,1)S(1)} %convolution_convert_fusion.1.refs_2_, ...), custom_call_target="tpu_custom_call" | custom-call | flops 2038431744 | bytes 8847360 | tf_op jit(solution)/shard_map/pallas_call | solution.py:208
  155.8 1.3 convolution_convert_fusion.3
  157.8 1.5 dynamic-slice_dynamic-update-slice_fusion
  159.9 0.9 constant_dynamic-update-slice_fusion.9
  161.4 0.9 constant_dynamic-update-slice_fusion.7
  162.4 1.6 collective-permute-start.26
  163.9 1.7 collective-permute-start.28
  165.6 0.9 constant_dynamic-update-slice_fusion.8.refs_4_
  166.6 1.2 collective-permute-done.39
  168.4 6.6 %shard_map.118 = (f32[576,384]{1,0:T(8,128)S(1)}, f32[576,384]{1,0:T(8,128)S(1)}) custom-call(s32[2]{0:T(128)S(1)} %pad_add_fusion.place_ref, bf16[192,768]{1,0:T(8,128)(2,1)S(1)} %collective-permute-done.31.refs_0_, bf16[192,768]{1,0:T(8,128)(2,1)} %collective-permute-done.51.refs_1_, bf16[192,768]{1,0:T(8,128)(2,1)S(1)} %collective-permute-done.36.refs_2_, ...), custom_call_target="tpu_custom_call" | custom-call | flops 2038431744 | bytes 8847360 | tf_op jit(solution)/shard_map/pallas_call | solution.py:208
  176.2 1.7 collective-permute-start.27
  178.5 6.4 %shard_map.117 = (f32[576,384]{1,0:T(8,128)S(1)}, f32[576,384]{1,0:T(8,128)S(1)}) custom-call(s32[2]{0:T(128)S(1)} %pad_add_fusion.place_ref, bf16[192,768]{1,0:T(8,128)(2,1)S(1)} %collective-permute-done.33.refs_0_, bf16[192,768]{1,0:T(8,128)(2,1)S(1)} %collective-permute-done.47.refs_1_, bf16[192,768]{1,0:T(8,128)(2,1)S(1)} %collective-permute-done.38.refs_2_, ...), custom_call_target="tpu_custom_call" | custom-call | flops 2038431744 | bytes 8847360 | tf_op jit(solution)/shard_map/pallas_call | solution.py:208
  186.2 4.7 %shard_map.120.refs_6_ = bf16[576,1536]{1,0:T(8,128)(2,1)} custom-call(s32[2]{0:T(128)S(1)} %pad_add_fusion.place_ref, bf16[192,896]{1,0:T(8,128)(2,1)S(1)} %fusion.51.refs_0_, bf16[192,896]{1,0:T(8,128)(2,1)S(1)} %collective-permute-done.54.refs_1_, bf16[576,3072]{1,0:T(8,128)(2,1)S(1)} %bitcast.33, bf16[576,3072]{1,0:T(8,128)(2,1)} %bitcast.46, ...), custom_call_target="tpu_custom_call" | custom-call | flops 679477248 | bytes 5898240 | tf_op jit(solution)/shard_map/pallas_call | solution.py:208
  190.9 6.4 %shard_map.116 = (f32[576,384]{1,0:T(8,128)S(1)}, f32[576,384]{1,0:T(8,128)S(1)}) custom-call(s32[2]{0:T(128)S(1)} %pad_add_fusion.place_ref, bf16[192,768]{1,0:T(8,128)(2,1)S(1)} %copy-done.8, bf16[192,768]{1,0:T(8,128)(2,1)S(1)} %collective-permute-done.35.refs_1_, bf16[192,768]{1,0:T(8,128)(2,1)S(1)} %constant_dynamic-update-slice_fusion.6.refs_2_, ...), custom_call_target="tpu_custom_call" | custom-call | flops 2038431744 | bytes 8847360 | tf_op jit(solution)/shard_map/pallas_call | solution.py:208
  197.4 4.7 %shard_map.121.refs_6_ = bf16[576,1536]{1,0:T(8,128)(2,1)} custom-call(s32[2]{0:T(128)S(1)} %pad_add_fusion.place_ref, bf16[192,896]{1,0:T(8,128)(2,1)S(1)} %collective-permute-done.26.refs_0_, bf16[192,896]{1,0:T(8,128)(2,1)S(1)} %collective-permute-done.50.refs_1_, bf16[576,3072]{1,0:T(8,128)(2,1)S(1)} %bitcast.34, ...), custom_call_target="tpu_custom_call", output_to_operand_aliasing={{}: (7, {})} | custom-call | flops 679477248 | bytes 5898240 | tf_op jit(solution)/shard_map/pallas_call | solution.py:208
  202.1 4.7 %shard_map.122.refs_6_ = bf16[576,1536]{1,0:T(8,128)(2,1)} custom-call(s32[2]{0:T(128)S(1)} %pad_add_fusion.place_ref, bf16[192,896]{1,0:T(8,128)(2,1)S(1)} %collective-permute-done.28.refs_0_, bf16[192,896]{1,0:T(8,128)(2,1)S(1)} %collective-permute-done.46.refs_1_, bf16[576,3072]{1,0:T(8,128)(2,1)S(1)} %bitcast.35, ...), custom_call_target="tpu_custom_call", output_to_operand_aliasing={{}: (7, {})} | custom-call | flops 679477248 | bytes 5898240 | tf_op jit(solution)/shard_map/pallas_call | solution.py:208
  206.8 4.7 %shard_map.123 = bf16[576,1536]{1,0:T(8,128)(2,1)} custom-call(s32[2]{0:T(128)S(1)} %pad_add_fusion.place_ref, bf16[192,896]{1,0:T(8,128)(2,1)S(1)} %constant_dynamic-update-slice_fusion.2.refs_0_, bf16[192,896]{1,0:T(8,128)(2,1)S(1)} %collective-permute-done.30.refs_1_, bf16[576,3072]{1,0:T(8,128)(2,1)S(1)} %bitcast.36, ...), custom_call_target="tpu_custom_call", output_to_operand_aliasing={{}: (7, {})} | custom-call | flops 679477248 | bytes 5898240 | tf_op jit(solution)/shard_map/pallas_call | solution.py:208
  (163 shorter events, 22.1 us)
Async XLA Ops:
  3.4 7.5 %copy-start.15 = (s32[64,2]{0,1:T(2,128)S(1)}, s32[64,2]{0,1:T(2,128)}, u32[]{:S(2)}) copy-start(s32[64,2]{0,1:T(2,128)} %param.17) | copy-start | bytes 1540
  3.4 16.8 %copy-start.13 = (bf16[64,3072]{1,0:T(8,128)(2,1)S(1)}, bf16[64,3072]{1,0:T(8,128)(2,1)}, u32[]{:S(2)}) copy-start(bf16[64,3072]{1,0:T(8,128)(2,1)} %param.15) | copy-start | bytes 1179652
  4.5 1.7 collective-permute-start
  6.4 9.5 %collective-permute-start.1 = (bf16[8,128,128]{2,1,0:T(8,128)(2,1)S(1)}, bf16[8,128,128]{2,1,0:T(8,128)(2,1)S(1)}, u32[]{:S(2)}, u32[]{:S(2)}) collective-permute-start(bf16[8,128,128]{2,1,0:T(8,128)(2,1)S(1)} %fusion.54), channel_id=1, source_target_pairs={{0,8},{4,12},{8,0},{12,4},{16,24},{20,28},{24,16},{28,20},{1,9},{5... | collective-permute-start | bytes 786440 | tf_op jit(solution)/shard_map/ppermute | solution.py:89
  9.3 26.6 %collective-permute-start.3 = (bf16[1024,384]{1,0:T(8,128)(2,1)}, bf16[1024,384]{1,0:T(8,128)(2,1)S(1)}, u32[]{:S(2)}, u32[]{:S(2)}) collective-permute-start(bf16[1024,384]{1,0:T(8,128)(2,1)} %param.14), channel_id=1, source_target_pairs={{0,4},{4,0},{8,12},{12,8},{16,20},{20,16},{24,28},{28,24},{1,5},{5... | collective-permute-start | bytes 2359304 | tf_op jit(solution)/shard_map/ppermute | solution.py:108
  9.3 49.2 %collective-permute-start.12 = (bf16[1024,384]{1,0:T(8,128)(2,1)}, bf16[1024,384]{1,0:T(8,128)(2,1)}, u32[]{:S(2)}, u32[]{:S(2)}) collective-permute-start(bf16[1024,384]{1,0:T(8,128)(2,1)} %param.14), channel_id=1, source_target_pairs={{0,16},{4,20},{8,24},{12,28},{16,0},{20,4},{24,8},{28,12},{1,17},{... | collective-permute-start | bytes 2359304 | tf_op jit(solution)/shard_map/ppermute | solution.py:89
  10.9 32.8 %collective-permute-start.23 = (s32[2,64]{1,0:T(2,128)S(1)}, s32[2,64]{1,0:T(2,128)S(1)}, u32[]{:S(2)}, u32[]{:S(2)}) collective-permute-start(s32[2,64]{1,0:T(2,128)S(1)} %bitcast.62), channel_id=1, source_target_pairs={{0,3},{1,0},{2,1},{3,2},{4,7},{5,4},{6,5},{7,6},{8,11},{9,8},{10,9... | collective-permute-start | bytes 1544 | tf_op jit(solution)/shard_map/ppermute | solution.py:304
  14.5 29.2 %collective-permute-start.24 = (s32[2,64]{1,0:T(2,128)S(1)}, s32[2,64]{1,0:T(2,128)S(1)}, u32[]{:S(2)}, u32[]{:S(2)}) collective-permute-start(s32[2,64]{1,0:T(2,128)S(1)} %bitcast.63), channel_id=1, source_target_pairs={{0,2},{1,3},{2,0},{3,1},{4,6},{5,7},{6,4},{7,5},{8,10},{9,11},{10,... | collective-permute-start | bytes 1544 | tf_op jit(solution)/shard_map/ppermute | solution.py:304
  16.3 17.8 %collective-permute-start.2 = (bf16[8,128,128]{2,1,0:T(8,128)(2,1)S(1)}, bf16[8,128,128]{2,1,0:T(8,128)(2,1)S(1)}, u32[]{:S(2)}, u32[]{:S(2)}) collective-permute-start(bf16[8,128,128]{2,1,0:T(8,128)(2,1)S(1)} %get-tuple-element.28), channel_id=1, source_target_pairs={{0,16},{4,20},{8,24},{12,28},{1,17},{5,21},{9,25},{13,29},{2,18},{... | collective-permute-start | bytes 786440 | tf_op jit(solution)/shard_map/ppermute | solution.py:286
  34.2 20.8 %collective-permute-start.7 = (bf16[1024,384]{1,0:T(8,128)(2,1)}, bf16[1024,384]{1,0:T(8,128)(2,1)}, u32[]{:S(2)}, u32[]{:S(2)}) collective-permute-start(bf16[1024,384]{1,0:T(8,128)(2,1)} %param.14), channel_id=1, source_target_pairs={{0,8},{4,12},{8,0},{12,4},{16,24},{20,28},{24,16},{28,20},{1,9},{5... | collective-permute-start | bytes 2359304 | tf_op jit(solution)/shard_map/ppermute | solution.py:89
  40.0 21.2 %collective-permute-start.4 = (bf16[256,768]{1,0:T(8,128)(2,1)}, bf16[256,768]{1,0:T(8,128)(2,1)S(1)}, u32[]{:S(2)}, u32[]{:S(2)}) collective-permute-start(bf16[256,768]{1,0:T(8,128)(2,1)} %get-tuple-element.49), channel_id=1, source_target_pairs={{0,1},{3,2},{4,5},{7,6},{8,9},{11,10},{12,13},{15,14},{16,17},{19,... | collective-permute-start | bytes 1179656 | tf_op jit(solution)/shard_map/ppermute | solution.py:125
  43.7 10.9 %collective-permute-start.25 = (s32[2,64]{1,0:T(2,128)S(1)}, s32[2,64]{1,0:T(2,128)S(1)}, u32[]{:S(2)}, u32[]{:S(2)}) collective-permute-start(s32[2,64]{1,0:T(2,128)S(1)} %bitcast.64), channel_id=1, source_target_pairs={{0,1},{1,2},{2,3},{3,0},{4,5},{5,6},{6,7},{7,4},{8,9},{9,10},{10,1... | collective-permute-start | bytes 1544 | tf_op jit(solution)/shard_map/ppermute | solution.py:304
  56.0 10.1 %collective-permute-start.17 = (bf16[512,384]{1,0:T(8,128)(2,1)S(1)}, bf16[512,384]{1,0:T(8,128)(2,1)S(1)}, u32[]{:S(2)}, u32[]{:S(2)}) collective-permute-start(bf16[512,384]{1,0:T(8,128)(2,1)S(1)} %slice.48), channel_id=1, source_target_pairs={{0,16},{4,20},{8,24},{12,28},{16,0},{20,4},{24,8},{28,12},{1,17},{... | collective-permute-start | bytes 1179656 | tf_op jit(solution)/shard_map/ppermute | solution.py:89
  59.6 10.6 %copy-start.11 = (f32[256,768]{1,0:T(8,128)S(1)}, f32[256,768]{1,0:T(8,128)}, u32[]{:S(2)}) copy-start(f32[256,768]{1,0:T(8,128)} %get-tuple-element.42) | copy-start | bytes 2359300
  59.6 9.0 %collective-permute-start.18 = (bf16[512,384]{1,0:T(8,128)(2,1)S(1)}, bf16[512,384]{1,0:T(8,128)(2,1)S(1)}, u32[]{:S(2)}, u32[]{:S(2)}) collective-permute-start(bf16[512,384]{1,0:T(8,128)(2,1)S(1)} %slice.49), channel_id=1, source_target_pairs={{0,8},{4,12},{8,0},{12,4},{16,24},{20,28},{24,16},{28,20},{1,9},{5... | collective-permute-start | bytes 1179656 | tf_op jit(solution)/shard_map/ppermute | solution.py:89
  61.2 9.0 %collective-permute-start.13 = (bf16[1024,384]{1,0:T(8,128)(2,1)}, bf16[1024,384]{1,0:T(8,128)(2,1)S(1)}, u32[]{:S(2)}, u32[]{:S(2)}) collective-permute-start(bf16[1024,384]{1,0:T(8,128)(2,1)} %collective-permute-done.12), channel_id=1, source_target_pairs={{0,4},{4,0},{8,12},{12,8},{16,20},{20,16},{24,28},{28,24},{1,5},{5... | collective-permute-start | bytes 2359304 | tf_op jit(solution)/shard_map/ppermute | solution.py:108
  61.3 7.5 %collective-permute-start.5 = (bf16[256,768]{1,0:T(8,128)(2,1)S(1)}, bf16[256,768]{1,0:T(8,128)(2,1)S(1)}, u32[]{:S(2)}, u32[]{:S(2)}) collective-permute-start(bf16[256,768]{1,0:T(8,128)(2,1)S(1)} %add_convert_fusion.7), channel_id=1, source_target_pairs={{1,2},{2,1},{5,6},{6,5},{9,10},{10,9},{13,14},{14,13},{17,18},{18,... | collective-permute-start | bytes 1179656 | tf_op jit(solution)/shard_map/ppermute | solution.py:128
  62.0 17.9 %collective-permute-start.8 = (bf16[1024,384]{1,0:T(8,128)(2,1)}, bf16[1024,384]{1,0:T(8,128)(2,1)S(1)}, u32[]{:S(2)}, u32[]{:S(2)}) collective-permute-start(bf16[1024,384]{1,0:T(8,128)(2,1)} %collective-permute-done.7), channel_id=1, source_target_pairs={{0,4},{4,0},{8,12},{12,8},{16,20},{20,16},{24,28},{28,24},{1,5},{5... | collective-permute-start | bytes 2359304 | tf_op jit(solution)/shard_map/ppermute | solution.py:108
  68.7 28.6 %collective-permute-start.19 = (bf16[1024,384]{1,0:T(8,128)(2,1)S(1)}, bf16[1024,384]{1,0:T(8,128)(2,1)S(1)}, u32[]{:S(2)}, u32[]{:S(2)}) collective-permute-start(bf16[1024,384]{1,0:T(8,128)(2,1)S(1)} %constant_dynamic-update-slice_fusion), channel_id=1, source_target_pairs={{0,4},{4,0},{8,12},{12,8},{16,20},{20,16},{24,28},{28,24},{1,5},{5... | collective-permute-start | bytes 2359304 | tf_op jit(solution)/shard_map/ppermute | solution.py:108
  68.9 15.7 %collective-permute-start.6 = (bf16[256,768]{1,0:T(8,128)(2,1)S(1)}, bf16[256,768]{1,0:T(8,128)(2,1)S(1)}, u32[]{:S(2)}, u32[]{:S(2)}) collective-permute-start(bf16[256,768]{1,0:T(8,128)(2,1)S(1)} %add_convert_fusion.6), channel_id=1, source_target_pairs={{1,0},{2,3},{5,4},{6,7},{9,8},{10,11},{13,12},{14,15},{17,16},{18,... | collective-permute-start | bytes 1179656 | tf_op jit(solution)/shard_map/ppermute | solution.py:132
  72.5 16.9 %collective-permute-start.14 = (bf16[256,768]{1,0:T(8,128)(2,1)S(1)}, bf16[256,768]{1,0:T(8,128)(2,1)S(1)}, u32[]{:S(2)}, u32[]{:S(2)}) collective-permute-start(bf16[256,768]{1,0:T(8,128)(2,1)S(1)} %get-tuple-element.53), channel_id=1, source_target_pairs={{0,1},{3,2},{4,5},{7,6},{8,9},{11,10},{12,13},{15,14},{16,17},{19,... | collective-permute-start | bytes 1179656 | tf_op jit(solution)/shard_map/ppermute | solution.py:125
  82.1 14.4 %collective-permute-start.9 = (bf16[256,768]{1,0:T(8,128)(2,1)S(1)}, bf16[256,768]{1,0:T(8,128)(2,1)S(1)}, u32[]{:S(2)}, u32[]{:S(2)}) collective-permute-start(bf16[256,768]{1,0:T(8,128)(2,1)S(1)} %get-tuple-element.51), channel_id=1, source_target_pairs={{0,1},{3,2},{4,5},{7,6},{8,9},{11,10},{12,13},{15,14},{16,17},{19,... | collective-permute-start | bytes 1179656 | tf_op jit(solution)/shard_map/ppermute | solution.py:125
  85.1 20.2 %collective-permute-start.31 = (bf16[192,768]{1,0:T(8,128)(2,1)S(1)}, bf16[192,768]{1,0:T(8,128)(2,1)S(1)}, u32[]{:S(2)}, u32[]{:S(2)}) collective-permute-start(bf16[192,768]{1,0:T(8,128)(2,1)S(1)} %convolution_convert_fusion.2.refs_0_), channel_id=1, source_target_pairs={{0,8},{4,12},{8,0},{12,4},{16,24},{20,28},{24,16},{28,20},{1,9},{5... | collective-permute-start | bytes 884744 | tf_op jit(solution)/shard_map/ppermute | solution.py:89
  86.4 19.0 %collective-permute-start.33 = (bf16[192,768]{1,0:T(8,128)(2,1)S(1)}, bf16[192,768]{1,0:T(8,128)(2,1)S(1)}, u32[]{:S(2)}, u32[]{:S(2)}) collective-permute-start(bf16[192,768]{1,0:T(8,128)(2,1)S(1)} %convolution_convert_fusion.2.refs_0_), channel_id=1, source_target_pairs={{0,16},{4,20},{8,24},{12,28},{16,0},{20,4},{24,8},{28,12},{1,17},{... | collective-permute-start | bytes 884744 | tf_op jit(solution)/shard_map/ppermute | solution.py:89
  89.4 17.5 %collective-permute-start.15 = (bf16[256,768]{1,0:T(8,128)(2,1)S(1)}, bf16[256,768]{1,0:T(8,128)(2,1)S(1)}, u32[]{:S(2)}, u32[]{:S(2)}) collective-permute-start(bf16[256,768]{1,0:T(8,128)(2,1)S(1)} %add_convert_fusion.3), channel_id=1, source_target_pairs={{1,2},{2,1},{5,6},{6,5},{9,10},{10,9},{13,14},{14,13},{17,18},{18,... | collective-permute-start | bytes 1179656 | tf_op jit(solution)/shard_map/ppermute | solution.py:128
  96.6 11.8 %collective-permute-start.10 = (bf16[256,768]{1,0:T(8,128)(2,1)S(1)}, bf16[256,768]{1,0:T(8,128)(2,1)S(1)}, u32[]{:S(2)}, u32[]{:S(2)}) collective-permute-start(bf16[256,768]{1,0:T(8,128)(2,1)S(1)} %add_convert_fusion.5), channel_id=1, source_target_pairs={{1,2},{2,1},{5,6},{6,5},{9,10},{10,9},{13,14},{14,13},{17,18},{18,... | collective-permute-start | bytes 1179656 | tf_op jit(solution)/shard_map/ppermute | solution.py:128
  98.4 14.0 %collective-permute-start.20 = (bf16[256,768]{1,0:T(8,128)(2,1)S(1)}, bf16[256,768]{1,0:T(8,128)(2,1)S(1)}, u32[]{:S(2)}, u32[]{:S(2)}) collective-permute-start(bf16[256,768]{1,0:T(8,128)(2,1)S(1)} %get-tuple-element.55), channel_id=1, source_target_pairs={{0,1},{3,2},{4,5},{7,6},{8,9},{11,10},{12,13},{15,14},{16,17},{19,... | collective-permute-start | bytes 1179656 | tf_op jit(solution)/shard_map/ppermute | solution.py:125
  105.3 22.2 %collective-permute-start.32 = (bf16[96,768]{1,0:T(8,128)(2,1)S(1)}, bf16[96,768]{1,0:T(8,128)(2,1)S(1)}, u32[]{:S(2)}, u32[]{:S(2)}) collective-permute-start(bf16[96,768]{1,0:T(8,128)(2,1)S(1)} %slice.52), channel_id=1, source_target_pairs={{0,16},{4,20},{8,24},{12,28},{16,0},{20,4},{24,8},{28,12},{1,17},{... | collective-permute-start | bytes 442376 | tf_op jit(solution)/shard_map/ppermute | solution.py:89
  105.4 22.2 %collective-permute-start.34 = (bf16[96,768]{1,0:T(8,128)(2,1)S(1)}, bf16[96,768]{1,0:T(8,128)(2,1)S(1)}, u32[]{:S(2)}, u32[]{:S(2)}) collective-permute-start(bf16[96,768]{1,0:T(8,128)(2,1)S(1)} %slice.53), channel_id=1, source_target_pairs={{0,8},{4,12},{8,0},{12,4},{16,24},{20,28},{24,16},{28,20},{1,9},{5... | collective-permute-start | bytes 442376 | tf_op jit(solution)/shard_map/ppermute | solution.py:89
  107.1 13.9 %collective-permute-start.16 = (bf16[256,768]{1,0:T(8,128)(2,1)S(1)}, bf16[256,768]{1,0:T(8,128)(2,1)S(1)}, u32[]{:S(2)}, u32[]{:S(2)}) collective-permute-start(bf16[256,768]{1,0:T(8,128)(2,1)S(1)} %add_convert_fusion.2), channel_id=1, source_target_pairs={{1,0},{2,3},{5,4},{6,7},{9,8},{10,11},{13,12},{14,15},{17,16},{18,... | collective-permute-start | bytes 1179656 | tf_op jit(solution)/shard_map/ppermute | solution.py:132
  108.5 17.9 %collective-permute-start.11 = (bf16[256,768]{1,0:T(8,128)(2,1)S(1)}, bf16[256,768]{1,0:T(8,128)(2,1)S(1)}, u32[]{:S(2)}, u32[]{:S(2)}) collective-permute-start(bf16[256,768]{1,0:T(8,128)(2,1)S(1)} %add_convert_fusion.4), channel_id=1, source_target_pairs={{1,0},{2,3},{5,4},{6,7},{9,8},{10,11},{13,12},{14,15},{17,16},{18,... | collective-permute-start | bytes 1179656 | tf_op jit(solution)/shard_map/ppermute | solution.py:132
  112.4 17.1 %collective-permute-start.21 = (bf16[256,768]{1,0:T(8,128)(2,1)S(1)}, bf16[256,768]{1,0:T(8,128)(2,1)S(1)}, u32[]{:S(2)}, u32[]{:S(2)}) collective-permute-start(bf16[256,768]{1,0:T(8,128)(2,1)S(1)} %add_convert_fusion.1), channel_id=1, source_target_pairs={{1,2},{2,1},{5,6},{6,5},{9,10},{10,9},{13,14},{14,13},{17,18},{18,... | collective-permute-start | bytes 1179656 | tf_op jit(solution)/shard_map/ppermute | solution.py:128
  121.5 8.4 %collective-permute-start.41 = (bf16[192,768]{1,0:T(8,128)(2,1)S(1)}, bf16[192,768]{1,0:T(8,128)(2,1)S(1)}, u32[]{:S(2)}, u32[]{:S(2)}) collective-permute-start(bf16[192,768]{1,0:T(8,128)(2,1)S(1)} %convolution_convert_fusion.refs_4_), channel_id=1, source_target_pairs={{0,8},{4,12},{8,0},{12,4},{16,24},{20,28},{24,16},{28,20},{1,9},{5... | collective-permute-start | bytes 884744 | tf_op jit(solution)/shard_map/ppermute | solution.py:89
  126.9 7.7 %collective-permute-start.36 = (bf16[192,768]{1,0:T(8,128)(2,1)S(1)}, bf16[192,768]{1,0:T(8,128)(2,1)S(1)}, u32[]{:S(2)}, u32[]{:S(2)}) collective-permute-start(bf16[192,768]{1,0:T(8,128)(2,1)S(1)} %convolution_convert_fusion.1.refs_2_), channel_id=1, source_target_pairs={{0,8},{4,12},{8,0},{12,4},{16,24},{20,28},{24,16},{28,20},{1,9},{5... | collective-permute-start | bytes 884744 | tf_op jit(solution)/shard_map/ppermute | solution.py:89
  127.6 16.6 %collective-permute-start.55 = (bf16[192,768]{1,0:T(8,128)(2,1)S(1)}, bf16[192,768]{1,0:T(8,128)(2,1)S(1)}, u32[]{:S(2)}, u32[]{:S(2)}) collective-permute-start(bf16[192,768]{1,0:T(8,128)(2,1)S(1)} %convolution_convert_fusion.2.refs_0_), channel_id=1, source_target_pairs={{0,4},{4,0},{8,12},{12,8},{16,20},{20,16},{24,28},{28,24},{1,5},{5... | collective-permute-start | bytes 884744 | tf_op jit(solution)/shard_map/ppermute | solution.py:108
  127.7 9.9 %collective-permute-start.43 = (bf16[192,768]{1,0:T(8,128)(2,1)S(1)}, bf16[192,768]{1,0:T(8,128)(2,1)S(1)}, u32[]{:S(2)}, u32[]{:S(2)}) collective-permute-start(bf16[192,768]{1,0:T(8,128)(2,1)S(1)} %convolution_convert_fusion.refs_4_), channel_id=1, source_target_pairs={{0,16},{4,20},{8,24},{12,28},{16,0},{20,4},{24,8},{28,12},{1,17},{... | collective-permute-start | bytes 884744 | tf_op jit(solution)/shard_map/ppermute | solution.py:89
  129.5 18.2 %copy-start.7 = (bf16[192,768]{1,0:T(8,128)(2,1)}, bf16[192,768]{1,0:T(8,128)(2,1)S(1)}, u32[]{:S(2)}) copy-start(bf16[192,768]{1,0:T(8,128)(2,1)S(1)} %constant_dynamic-update-slice_fusion.4.refs_0_) | copy-start | bytes 884740
  129.5 16.4 %collective-permute-start.57 = (bf16[192,768]{1,0:T(8,128)(2,1)S(1)}, bf16[192,768]{1,0:T(8,128)(2,1)S(1)}, u32[]{:S(2)}, u32[]{:S(2)}) collective-permute-start(bf16[192,768]{1,0:T(8,128)(2,1)S(1)} %convolution_convert_fusion.refs_4_), channel_id=1, source_target_pairs={{0,4},{4,0},{8,12},{12,8},{16,20},{20,16},{24,28},{28,24},{1,5},{5... | collective-permute-start | bytes 884744 | tf_op jit(solution)/shard_map/ppermute | solution.py:108
  129.9 17.5 %collective-permute-start.56 = (bf16[192,768]{1,0:T(8,128)(2,1)S(1)}, bf16[192,768]{1,0:T(8,128)(2,1)S(1)}, u32[]{:S(2)}, u32[]{:S(2)}) collective-permute-start(bf16[192,768]{1,0:T(8,128)(2,1)S(1)} %convolution_convert_fusion.1.refs_2_), channel_id=1, source_target_pairs={{0,4},{4,0},{8,12},{12,8},{16,20},{20,16},{24,28},{28,24},{1,5},{5... | collective-permute-start | bytes 884744 | tf_op jit(solution)/shard_map/ppermute | solution.py:108
  134.6 8.8 %collective-permute-start.38 = (bf16[192,768]{1,0:T(8,128)(2,1)S(1)}, bf16[192,768]{1,0:T(8,128)(2,1)S(1)}, u32[]{:S(2)}, u32[]{:S(2)}) collective-permute-start(bf16[192,768]{1,0:T(8,128)(2,1)S(1)} %convolution_convert_fusion.1.refs_2_), channel_id=1, source_target_pairs={{0,16},{4,20},{8,24},{12,28},{16,0},{20,4},{24,8},{28,12},{1,17},{... | collective-permute-start | bytes 884744 | tf_op jit(solution)/shard_map/ppermute | solution.py:89
  137.6 16.3 %collective-permute-start.22 = (bf16[256,768]{1,0:T(8,128)(2,1)S(1)}, bf16[256,768]{1,0:T(8,128)(2,1)S(1)}, u32[]{:S(2)}, u32[]{:S(2)}) collective-permute-start(bf16[256,768]{1,0:T(8,128)(2,1)S(1)} %add_convert_fusion), channel_id=1, source_target_pairs={{1,0},{2,3},{5,4},{6,7},{9,8},{10,11},{13,12},{14,15},{17,16},{18,... | collective-permute-start | bytes 1179656 | tf_op jit(solution)/shard_map/ppermute | solution.py:132
  138.9 15.0 %copy-start.12 = (bf16[64,3072]{1,0:T(8,128)(2,1)}, bf16[64,3072]{1,0:T(8,128)(2,1)S(1)}, u32[]{:S(2)}) copy-start(bf16[64,3072]{1,0:T(8,128)(2,1)S(1)} %dynamic-slice_dynamic-update-slice_fusion.1) | copy-start | bytes 1179652
  143.5 18.9 %collective-permute-start.51 = (bf16[192,768]{1,0:T(8,128)(2,1)S(1)}, bf16[192,768]{1,0:T(8,128)(2,1)}, u32[]{:S(2)}, u32[]{:S(2)}) collective-permute-start(bf16[192,768]{1,0:T(8,128)(2,1)S(1)} %collective-permute-done.31.refs_0_), channel_id=1, source_target_pairs={{0,4},{4,0},{8,12},{12,8},{16,20},{20,16},{24,28},{28,24},{1,5},{5... | collective-permute-start | bytes 884744 | tf_op jit(solution)/shard_map/ppermute | solution.py:108
  144.2 15.2 %collective-permute-start.42 = (bf16[96,768]{1,0:T(8,128)(2,1)}, bf16[96,768]{1,0:T(8,128)(2,1)}, u32[]{:S(2)}, u32[]{:S(2)}) collective-permute-start(bf16[96,768]{1,0:T(8,128)(2,1)} %slice.56), channel_id=1, source_target_pairs={{0,16},{4,20},{8,24},{12,28},{16,0},{20,4},{24,8},{28,12},{1,17},{... | collective-permute-start | bytes 442376 | tf_op jit(solution)/shard_map/ppermute | solution.py:89
  145.9 18.0 %collective-permute-start.44 = (bf16[96,768]{1,0:T(8,128)(2,1)}, bf16[96,768]{1,0:T(8,128)(2,1)}, u32[]{:S(2)}, u32[]{:S(2)}) collective-permute-start(bf16[96,768]{1,0:T(8,128)(2,1)} %slice.57), channel_id=1, source_target_pairs={{0,8},{4,12},{8,0},{12,4},{16,24},{20,28},{24,16},{28,20},{1,9},{5... | collective-permute-start | bytes 442376 | tf_op jit(solution)/shard_map/ppermute | solution.py:89
  147.4 13.4 %collective-permute-start.37 = (bf16[96,768]{1,0:T(8,128)(2,1)}, bf16[96,768]{1,0:T(8,128)(2,1)}, u32[]{:S(2)}, u32[]{:S(2)}) collective-permute-start(bf16[96,768]{1,0:T(8,128)(2,1)} %slice.54), channel_id=1, source_target_pairs={{0,16},{4,20},{8,24},{12,28},{16,0},{20,4},{24,8},{28,12},{1,17},{... | collective-permute-start | bytes 442376 | tf_op jit(solution)/shard_map/ppermute | solution.py:89
  153.9 14.0 %collective-permute-start.53 = (bf16[192,768]{1,0:T(8,128)(2,1)S(1)}, bf16[192,768]{1,0:T(8,128)(2,1)}, u32[]{:S(2)}, u32[]{:S(2)}) collective-permute-start(bf16[192,768]{1,0:T(8,128)(2,1)S(1)} %collective-permute-done.41.refs_4_), channel_id=1, source_target_pairs={{0,4},{4,0},{8,12},{12,8},{16,20},{20,16},{24,28},{28,24},{1,5},{5... | collective-permute-start | bytes 884744 | tf_op jit(solution)/shard_map/ppermute | solution.py:108
  159.4 8.9 %collective-permute-start.52 = (bf16[192,768]{1,0:T(8,128)(2,1)S(1)}, bf16[192,768]{1,0:T(8,128)(2,1)S(1)}, u32[]{:S(2)}, u32[]{:S(2)}) collective-permute-start(bf16[192,768]{1,0:T(8,128)(2,1)S(1)} %collective-permute-done.36.refs_2_), channel_id=1, source_target_pairs={{0,4},{4,0},{8,12},{12,8},{16,20},{20,16},{24,28},{28,24},{1,5},{5... | collective-permute-start | bytes 884744 | tf_op jit(solution)/shard_map/ppermute | solution.py:108
  160.8 7.0 %collective-permute-start.39 = (bf16[96,768]{1,0:T(8,128)(2,1)}, bf16[96,768]{1,0:T(8,128)(2,1)S(1)}, u32[]{:S(2)}, u32[]{:S(2)}) collective-permute-start(bf16[96,768]{1,0:T(8,128)(2,1)} %slice.55), channel_id=1, source_target_pairs={{0,8},{4,12},{8,0},{12,4},{16,24},{20,28},{24,16},{28,20},{1,9},{5... | collective-permute-start | bytes 442376 | tf_op jit(solution)/shard_map/ppermute | solution.py:89
  162.4 12.6 %collective-permute-start.26 = (bf16[192,896]{1,0:T(8,128)(2,1)S(1)}, bf16[192,896]{1,0:T(8,128)(2,1)S(1)}, u32[]{:S(2)}, u32[]{:S(2)}) collective-permute-start(bf16[192,896]{1,0:T(8,128)(2,1)S(1)} %fusion.51.refs_0_), channel_id=1, source_target_pairs={{0,8},{4,12},{8,0},{12,4},{16,24},{20,28},{24,16},{28,20},{1,9},{5... | collective-permute-start | bytes 1032200 | tf_op jit(solution)/shard_map/ppermute | solution.py:89
  163.9 11.6 %collective-permute-start.28 = (bf16[192,896]{1,0:T(8,128)(2,1)S(1)}, bf16[192,896]{1,0:T(8,128)(2,1)S(1)}, u32[]{:S(2)}, u32[]{:S(2)}) collective-permute-start(bf16[192,896]{1,0:T(8,128)(2,1)S(1)} %fusion.51.refs_0_), channel_id=1, source_target_pairs={{0,16},{4,20},{8,24},{12,28},{16,0},{20,4},{24,8},{28,12},{1,17},{... | collective-permute-start | bytes 1032200 | tf_op jit(solution)/shard_map/ppermute | solution.py:89
  167.8 7.9 %collective-permute-start.47 = (bf16[192,768]{1,0:T(8,128)(2,1)S(1)}, bf16[192,768]{1,0:T(8,128)(2,1)S(1)}, u32[]{:S(2)}, u32[]{:S(2)}) collective-permute-start(bf16[192,768]{1,0:T(8,128)(2,1)S(1)} %collective-permute-done.33.refs_0_), channel_id=1, source_target_pairs={{0,4},{4,0},{8,12},{12,8},{16,20},{20,16},{24,28},{28,24},{1,5},{5... | collective-permute-start | bytes 884744 | tf_op jit(solution)/shard_map/ppermute | solution.py:108
  167.8 8.4 %collective-permute-start.49 = (bf16[192,768]{1,0:T(8,128)(2,1)S(1)}, bf16[192,768]{1,0:T(8,128)(2,1)S(1)}, u32[]{:S(2)}, u32[]{:S(2)}) collective-permute-start(bf16[192,768]{1,0:T(8,128)(2,1)S(1)} %collective-permute-done.43.refs_4_), channel_id=1, source_target_pairs={{0,4},{4,0},{8,12},{12,8},{16,20},{20,16},{24,28},{28,24},{1,5},{5... | collective-permute-start | bytes 884744 | tf_op jit(solution)/shard_map/ppermute | solution.py:108
  168.3 9.6 %collective-permute-start.48 = (bf16[192,768]{1,0:T(8,128)(2,1)S(1)}, bf16[192,768]{1,0:T(8,128)(2,1)S(1)}, u32[]{:S(2)}, u32[]{:S(2)}) collective-permute-start(bf16[192,768]{1,0:T(8,128)(2,1)S(1)} %collective-permute-done.38.refs_2_), channel_id=1, source_target_pairs={{0,4},{4,0},{8,12},{12,8},{16,20},{20,16},{24,28},{28,24},{1,5},{5... | collective-permute-start | bytes 884744 | tf_op jit(solution)/shard_map/ppermute | solution.py:108
  175.0 10.0 %collective-permute-start.35 = (bf16[192,768]{1,0:T(8,128)(2,1)S(1)}, bf16[192,768]{1,0:T(8,128)(2,1)S(1)}, u32[]{:S(2)}, u32[]{:S(2)}) collective-permute-start(bf16[192,768]{1,0:T(8,128)(2,1)S(1)} %copy-done.8), channel_id=1, source_target_pairs={{0,4},{4,0},{8,12},{12,8},{16,20},{20,16},{24,28},{28,24},{1,5},{5... | collective-permute-start | bytes 884744 | tf_op jit(solution)/shard_map/ppermute | solution.py:108
  175.5 10.1 %collective-permute-start.54 = (bf16[192,896]{1,0:T(8,128)(2,1)S(1)}, bf16[192,896]{1,0:T(8,128)(2,1)S(1)}, u32[]{:S(2)}, u32[]{:S(2)}) collective-permute-start(bf16[192,896]{1,0:T(8,128)(2,1)S(1)} %fusion.51.refs_0_), channel_id=1, source_target_pairs={{0,4},{4,0},{8,12},{12,8},{16,20},{20,16},{24,28},{28,24},{1,5},{5... | collective-permute-start | bytes 1032200 | tf_op jit(solution)/shard_map/ppermute | solution.py:108
  175.7 15.2 %collective-permute-start.45 = (bf16[192,768]{1,0:T(8,128)(2,1)S(1)}, bf16[192,768]{1,0:T(8,128)(2,1)S(1)}, u32[]{:S(2)}, u32[]{:S(2)}) collective-permute-start(bf16[192,768]{1,0:T(8,128)(2,1)S(1)} %constant_dynamic-update-slice_fusion.8.refs_4_), channel_id=1, source_target_pairs={{0,4},{4,0},{8,12},{12,8},{16,20},{20,16},{24,28},{28,24},{1,5},{5... | collective-permute-start | bytes 884744 | tf_op jit(solution)/shard_map/ppermute | solution.py:108
  176.2 8.7 %collective-permute-start.27 = (bf16[96,896]{1,0:T(8,128)(2,1)S(1)}, bf16[96,896]{1,0:T(8,128)(2,1)S(1)}, u32[]{:S(2)}, u32[]{:S(2)}) collective-permute-start(bf16[96,896]{1,0:T(8,128)(2,1)S(1)} %slice.50), channel_id=1, source_target_pairs={{0,16},{4,20},{8,24},{12,28},{16,0},{20,4},{24,8},{28,12},{1,17},{... | collective-permute-start | bytes 516104 | tf_op jit(solution)/shard_map/ppermute | solution.py:89
  177.9 7.6 %collective-permute-start.29 = (bf16[96,896]{1,0:T(8,128)(2,1)S(1)}, bf16[96,896]{1,0:T(8,128)(2,1)S(1)}, u32[]{:S(2)}, u32[]{:S(2)}) collective-permute-start(bf16[96,896]{1,0:T(8,128)(2,1)S(1)} %slice.51), channel_id=1, source_target_pairs={{0,8},{4,12},{8,0},{12,4},{16,24},{20,28},{24,16},{28,20},{1,9},{5... | collective-permute-start | bytes 516104 | tf_op jit(solution)/shard_map/ppermute | solution.py:89
  178.5 7.7 %copy-start = (bf16[1,576,3072]{2,1,0:T(8,128)(2,1)S(1)}, bf16[1,576,3072]{2,1,0:T(8,128)(2,1)}, u32[]{:S(2)}) copy-start(bf16[1,576,3072]{2,1,0:T(8,128)(2,1)} %param.18) | copy-start | bytes 10616836
  184.9 6.0 %collective-permute-start.40 = (bf16[192,768]{1,0:T(8,128)(2,1)S(1)}, bf16[192,768]{1,0:T(8,128)(2,1)S(1)}, u32[]{:S(2)}, u32[]{:S(2)}) collective-permute-start(bf16[192,768]{1,0:T(8,128)(2,1)S(1)} %constant_dynamic-update-slice_fusion.6.refs_2_), channel_id=1, source_target_pairs={{0,4},{4,0},{8,12},{12,8},{16,20},{20,16},{24,28},{28,24},{1,5},{5... | collective-permute-start | bytes 884744 | tf_op jit(solution)/shard_map/ppermute | solution.py:108
  185.0 12.3 %collective-permute-start.50 = (bf16[192,896]{1,0:T(8,128)(2,1)S(1)}, bf16[192,896]{1,0:T(8,128)(2,1)S(1)}, u32[]{:S(2)}, u32[]{:S(2)}) collective-permute-start(bf16[192,896]{1,0:T(8,128)(2,1)S(1)} %collective-permute-done.26.refs_0_), channel_id=1, source_target_pairs={{0,4},{4,0},{8,12},{12,8},{16,20},{20,16},{24,28},{28,24},{1,5},{5... | collective-permute-start | bytes 1032200 | tf_op jit(solution)/shard_map/ppermute | solution.py:108
  185.6 16.5 %collective-permute-start.46 = (bf16[192,896]{1,0:T(8,128)(2,1)S(1)}, bf16[192,896]{1,0:T(8,128)(2,1)S(1)}, u32[]{:S(2)}, u32[]{:S(2)}) collective-permute-start(bf16[192,896]{1,0:T(8,128)(2,1)S(1)} %collective-permute-done.28.refs_0_), channel_id=1, source_target_pairs={{0,4},{4,0},{8,12},{12,8},{16,20},{20,16},{24,28},{28,24},{1,5},{5... | collective-permute-start | bytes 1032200 | tf_op jit(solution)/shard_map/ppermute | solution.py:108
  185.7 21.1 %collective-permute-start.30 = (bf16[192,896]{1,0:T(8,128)(2,1)S(1)}, bf16[192,896]{1,0:T(8,128)(2,1)S(1)}, u32[]{:S(2)}, u32[]{:S(2)}) collective-permute-start(bf16[192,896]{1,0:T(8,128)(2,1)S(1)} %constant_dynamic-update-slice_fusion.2.refs_0_), channel_id=1, source_target_pairs={{0,4},{4,0},{8,12},{12,8},{16,20},{20,16},{24,28},{28,24},{1,5},{5... | collective-permute-start | bytes 1032200 | tf_op jit(solution)/shard_map/ppermute | solution.py:108
  (11 other events, 40.5 us)

commit v2 on v1

v2 whole, which is shorter than its diff:
```python
import functools

import jax
import jax.numpy as jnp
from jax import lax
from jax.experimental import pallas as pl
from jax.experimental.pallas import tpu as pltpu
from jax.sharding import PartitionSpec as P

GROUPS = 4
VMEM_LIMIT = 48 * 1024 * 1024
BF16 = jnp.bfloat16
F32 = jnp.float32
NT = (((1,), (1,)), ((), ()))
TN = (((0,), (0,)), ((), ()))
NN = (((1,), (0,)), ((), ()))


def dot(a, b, dims):
    return lax.dot_general(a, b, dims, preferred_element_type=F32)


def halves(x):
    high = x.astype(BF16)
    return high, (x - high.astype(F32)).astype(BF16)


def call(kernel, out_shape, flops, nbytes, exps=0, **kwargs):
    return pl.pallas_call(
        kernel,
        out_shape=out_shape,
        compiler_params=pltpu.CompilerParams(vmem_limit_bytes=VMEM_LIMIT),
        cost_estimate=pl.CostEstimate(
            flops=int(flops), bytes_accessed=int(nbytes), transcendentals=int(exps)
        ),
        **kwargs,
    )


VM = pl.BlockSpec(memory_space=pltpu.VMEM)
SM = pl.BlockSpec(memory_space=pltpu.SMEM)


def fresh_kernel(place_ref, rate_ref, k_ref, v_ref, *outs):
    part, size = outs[0].shape[0], outs[0].shape[1]
    length = k_ref.shape[0]
    left = length - lax.broadcasted_iota(jnp.int32, (length, size), 0).astype(F32)
    for a, out_ref in enumerate(outs):
        first = lax.rem(place_ref[1] + a, len(outs)) * part
        for j in range(part):
            cols = pl.ds(pl.multiple_of((first + j) * size, size), size)
            tail = jnp.exp(-rate_ref[first + j] * left)
            high, low = halves(k_ref[:, cols].astype(F32) * tail)
            v = v_ref[:, cols]
            out_ref[j] = dot(high, v, TN) + dot(low, v, TN)


def local_kernel(rate_ref, q_ref, k_ref, v_ref, out_ref):
    heads = rate_ref.shape[0]
    length = k_ref.shape[0]
    size = k_ref.shape[1] // heads
    rows = lax.broadcasted_iota(jnp.int32, (length, length), 0)
    cols = lax.broadcasted_iota(jnp.int32, (length, length), 1)
    offset = (rows - cols).astype(F32)
    keep = offset >= 0
    offset = jnp.maximum(offset, 0.0)
    for h in range(heads):
        at = slice(h * size, (h + 1) * size)
        masked = jnp.where(keep, jnp.exp(-rate_ref[h] * offset), 0.0)
        weighted = (dot(q_ref[:, at], k_ref[:, at], NT) * masked).astype(BF16)
        out_ref[:, at] = dot(weighted, v_ref[:, at], NN)


def head_kernel(place_ref, rate_ref, q_ref, local_ref, *refs):
    states, out_ref = refs[:-1], refs[-1]
    part, size = states[0].shape[0], states[0].shape[1]
    length = q_ref.shape[0]
    pos = lax.broadcasted_iota(jnp.int32, (length, size), 0).astype(F32)
    for a, state_ref in enumerate(states):
        first = lax.rem(place_ref[1] + a, len(states)) * part
        for j in range(part):
            at = pl.ds(pl.multiple_of((first + j) * size, size), size)
            high, low = halves(state_ref[j])
            q = q_ref[:, at]
            carried = dot(q, high, NN) + dot(q, low, NN)
            carried = carried * jnp.exp(-rate_ref[first + j] * pos)
            attended = local_ref[:, at] + carried
            scale = lax.rsqrt(jnp.mean(attended * attended, axis=-1, keepdims=True) + 1e-05)
            out_ref[:, at] = (attended * scale).astype(BF16)


def xor_permute(x, step):
    n = lax.axis_size("ctx")
    return lax.ppermute(x, "ctx", [(d, d ^ step) for d in range(n)])


def after(x, *others):
    return lax.optimization_barrier((x,) + others)[0]


def within_group(x):
    n = lax.axis_size("ctx")
    low = n // GROUPS
    got = [x]
    for step in range(1, low):
        got.append(
            lax.ppermute(
                x, "ctx", [(d, d // low * low + (d % low - step) % low) for d in range(n)]
            )
        )
    return got


def in_order(pieces, first, axis):
    n, width = len(pieces), pieces[0].shape[axis]
    ring = jnp.concatenate(pieces + pieces[:-1], axis=axis)
    return lax.dynamic_slice_in_dim(ring, lax.rem(n - first, n) * width, n * width, axis)


def gather_doubling(x, axis, count, place):
    n = lax.axis_size(axis)
    step = 1
    while step < count:
        got = lax.ppermute(x, axis, [(d, d ^ step) for d in range(n)])
        upper = (place & step) != 0
        x = jnp.where(
            upper, jnp.concatenate([got, x], axis=1), jnp.concatenate([x, got], axis=1)
        )
        step *= 2
    return x


def line_sum(part, sent, place):
    n = lax.axis_size("exp")
    half = n // 2
    for hop in range(half - 1):
        got = lax.ppermute(sent, "exp", [(hop, hop + 1), (n - 1 - hop, n - 2 - hop)])
        part = part + got.astype(F32)
        sent = part.astype(BF16)
    other = lax.ppermute(sent, "exp", [(half - 1, half), (half, half - 1)])
    total = (part + other.astype(F32)).astype(BF16)
    for hop in range(half - 1):
        here, there = half - 1 - hop, half + hop
        got = lax.ppermute(total, "exp", [(here, here - 1), (there, there + 1)])
        total = jnp.where((place == here - 1) | (place == there + 1), got, total)
    return total


def project_kernel(low, place_ref, *refs):
    heads, (w_ref,), rests = refs[:low], refs[low : low + 1], refs[low + 1 : 2 * low + 1]
    sum_ref, sent_ref = refs[2 * low + 1 :]
    length, tokens = heads[0].shape[0], rests[0].shape[0]
    for a in range(low):
        first = lax.rem(place_ref[1] + a, low) * length
        at = pl.ds(pl.multiple_of(first, length), length)
        sum_ref[at, :] = dot(heads[a][...], w_ref[...], NN)
        own = pl.ds(pl.multiple_of(first + place_ref[2] * tokens, tokens), tokens)
        sum_ref[own, :] += rests[a][...].astype(F32)
        sent_ref[at, :] = sum_ref[at, :].astype(BF16)


def dispatch_kernel(count, *refs):
    mixed, gain_ref, picks_ref, out_ref = refs[:count], refs[count], refs[count + 1], refs[count + 2]
    cols = gain_ref.shape[1]
    value = mixed[-1][...].astype(F32)
    rows = (value * gain_ref[...]).astype(BF16)
    out_ref[:, :cols] = dot(picks_ref[...], rows, NN).astype(BF16)
    if count > 1:
        squares = jnp.sum(value * value, axis=1, keepdims=True)
        for ref in mixed[:-1]:
            value = ref[...].astype(F32)
            squares = squares + jnp.sum(value * value, axis=1, keepdims=True)
        lane = lax.broadcasted_iota(jnp.int32, (squares.shape[0], 128), 1)
        rest, extra = squares, jnp.zeros((squares.shape[0], 128), F32)
        for place in range(3):
            high = rest.astype(BF16).astype(F32)
            extra = jnp.where(lane == place, high, extra)
            rest = rest - high
        extra = dot(picks_ref[...], extra.astype(BF16), NN).astype(BF16)
        out_ref[:, out_ref.shape[1] - 128 :] = extra


def mixed_kernel(low, place_ref, *refs):
    out_ref = refs[-1]
    cols = refs[0].shape[1]
    tokens = out_ref.shape[0]
    length = refs[0].shape[0] // low
    for t in range(GROUPS):
        block = (place_ref[0] ^ t) * low
        own = pl.ds(pl.multiple_of(place_ref[1] * length + place_ref[2] * tokens, tokens), tokens)
        at = pl.multiple_of((block + place_ref[1]) * cols, cols)
        out_ref[:, pl.ds(at, cols)] = refs[t][own, :]
        for a in range(1, low):
            at = pl.multiple_of((block + lax.rem(place_ref[1] + a, low)) * cols, cols)
            got = refs[GROUPS + a - 1]
            out_ref[:, pl.ds(at, cols)] = got[:, t * cols : (t + 1) * cols]


def expert_kernel(count, mode, has_acc, model, place_ref, *refs):
    refs = list(refs)
    pieces, gates, ups = refs[:count], refs[count : 2 * count], refs[2 * count : 3 * count]
    refs = refs[3 * count :]
    gated, lifted = (refs.pop(0)[...], refs.pop(0)[...]) if has_acc else (0.0, 0.0)
    outs = refs[1:] if mode == "next" else refs
    squares = 0.0
    for piece, gate, up in zip(pieces, gates, ups):
        width = gate.shape[1]
        x = piece[:, :width]
        gated = gated + dot(gate[...], x, NT)
        lifted = lifted + dot(up[...], x, NT)
        if piece.shape[1] > width:
            extra = piece[:, width:]
            lane = lax.broadcasted_iota(jnp.int32, (8, extra.shape[1]), 1)
            squares = squares + dot((lax.rem(lane, 128) < 3).astype(BF16), extra, NT)[0:1, :]
    if mode is None:
        outs[0][...] = gated
        outs[1][...] = lifted
    else:
        scale = lax.rsqrt(squares / model + 1e-05)
        gated, lifted = gated * scale, lifted * scale
        outs[0][...] = (gated / (1.0 + jnp.exp(-gated)) * lifted).astype(BF16)


def expert_step(place, s, chunk_ids, pieces, gate, up, sums, hidden, final):
    hid, model = gate.shape
    low = len(pieces[0])
    slots = pieces[0][0].shape[0]
    width = model // GROUPS // low
    has_acc = sums is not None
    count = low * len(chunk_ids)

    def whole(x):
        return pl.BlockSpec(x.shape, lambda r, p: (0, 0))

    def weight(t, a):
        return pl.BlockSpec(
            (hid, width), lambda r, p: (0, (p[0] ^ (s ^ t)) * low + lax.rem(p[1] + a, low))
        )

    acc_spec = pl.BlockSpec((hid, slots), lambda r, p: (0, 0))
    operands = [x for per in pieces for x in per]
    specs = [whole(x) for x in operands]
    operands += [gate] * count + [up] * count
    specs += [weight(t, a) for t in chunk_ids for a in range(low)] * 2
    if has_acc:
        operands += list(sums)
        specs += [acc_spec] * 2
    aliases = {}
    if final:
        out_shape = jax.ShapeDtypeStruct((hid, slots * GROUPS), BF16)
        out_specs = pl.BlockSpec((hid, slots), lambda r, p: (0, p[0] ^ s))
        if hidden is not None:
            operands.append(hidden)
            specs.append(pl.BlockSpec(memory_space=pl.ANY))
            aliases = {len(operands): 0}
        mode = "first" if hidden is None else "next"
    else:
        out_shape = [jax.ShapeDtypeStruct((hid, slots), F32)] * 2
        out_specs = [acc_spec] * 2
        mode = None
    return call(
        functools.partial(expert_kernel, count, mode, has_acc, model),
        out_shape,
        4 * hid * slots * width * count,
        4 * hid * width * count + 8 * hid * slots * (1 + has_acc) + 2 * slots * width * count,
        hid * slots if final else 0,
        grid_spec=pltpu.PrefetchScalarGridSpec(
            num_scalar_prefetch=1, grid=(1,), in_specs=specs, out_specs=out_specs
        ),
        input_output_aliases=aliases,
    )(place, *operands)


def states_by_pairs(place, decay_rate, key_rows, value_rows, length, size):
    heads = decay_rate.shape[0]
    half = heads // 2
    mine, theirs = call(
        fresh_kernel,
        [jax.ShapeDtypeStruct((half, size, size), F32)] * 2,
        4 * heads * length * size * size,
        4 * length * heads * size + 4 * heads * size * size,
        heads * length * size,
        in_specs=[SM, SM, VM, VM],
        out_specs=[VM, VM],
    )(place, decay_rate, key_rows, value_rows)
    group, first = place[0], place[1] == 0
    rates = lax.dynamic_slice(decay_rate, (place[1] * half,), (half,))

    def fade(blocks):
        return jnp.exp(-rates * (length * blocks))[:, None, None]

    got = xor_permute(theirs, 1)
    early = jnp.where(first, mine, got)
    total = fade(1.0) * early + jnp.where(first, got, mine)
    state, marks = jnp.zeros_like(total), [got]
    step = 1
    while step < GROUPS:
        upper = (group & step) != 0
        coef = jnp.where(upper, fade(2.0 * (group & (step - 1)).astype(F32)), 0.0)
        if 2 * step < GROUPS:
            got = xor_permute(total, 2 * step)
            state = state + coef * got
            span = fade(2.0 * step)
            total = jnp.where(upper, span * got + total, span * total + got)
        else:
            got = lax.ppermute(total, "ctx", [(d, d + 2 * step) for d in range(2 * step)])
            state = state + coef * got
        marks.append(got)
        step *= 2
    late = fade(1.0) * state + early
    return [
        jnp.where(first, state, late),
        xor_permute(jnp.where(first, late, state), 1),
    ], marks


def states_by_steps(place, ctx, decay_rate, key_rows, value_rows, length, size):
    n_ctx, heads = lax.axis_size("ctx"), decay_rate.shape[0]
    (total,) = call(
        fresh_kernel,
        [jax.ShapeDtypeStruct((heads, size, size), F32)],
        4 * heads * length * size * size,
        4 * length * heads * size + 4 * heads * size * size,
        heads * length * size,
        in_specs=[SM, SM, VM, VM],
        out_specs=[VM],
    )(place, decay_rate, key_rows, value_rows)

    def fade(blocks):
        return jnp.exp(-decay_rate * (length * blocks))[:, None, None]

    state, step, got = jnp.zeros_like(total), 1, total
    while step < n_ctx:
        upper = (ctx & step) != 0
        got = xor_permute(total, step)
        state = state + jnp.where(upper, fade((ctx & (step - 1)).astype(F32)), 0.0) * got
        span = fade(float(step))
        total = jnp.where(upper, span * got + total, span * total + got)
        step *= 2
    return [state], [got] * 3


def per_device(
    queries,
    key_rows,
    value_rows,
    decay_rate,
    out_weight,
    residual,
    moe_gain,
    expert_ids,
    gate_weight,
    up_weight,
):
    n_ctx, n_exp = lax.axis_size("ctx"), lax.axis_size("exp")
    low = n_ctx // GROUPS
    ctx, exp = lax.axis_index("ctx"), lax.axis_index("exp")
    group, member = ctx // low, lax.rem(ctx, low)
    place = jnp.stack([group, member, exp]).astype(jnp.int32)
    length, here = queries.shape
    heads = decay_rate.shape[0]
    size = here // heads
    model = residual.shape[1]
    cols = model // n_ctx
    tokens = length // n_exp
    capacity = max(2, 3 * tokens // n_exp)
    aligned = cols % 128 == 0

    local = call(
        local_kernel,
        jax.ShapeDtypeStruct((length, here), F32),
        4 * heads * length * length * size,
        10 * length * here,
        heads * length * length,
        in_specs=[SM, VM, VM, VM],
        out_specs=VM,
    )(decay_rate, queries, key_rows, value_rows)
    if low == 2 and heads % 2 == 0:
        states, marks = states_by_pairs(place, decay_rate, key_rows, value_rows, length, size)
    else:
        states, marks = states_by_steps(
            place, ctx, decay_rate, key_rows, value_rows, length, size
        )

    rest_rows = within_group(after(residual, marks[0]))
    ids = gather_doubling(after(expert_ids.T, marks[0]), "exp", n_exp, exp)
    ids = gather_doubling(ids, "ctx", low, member)
    cut = out_weight.shape[0] // 2
    w_one = xor_permute(after(out_weight, marks[1]), low)
    w_two = xor_permute(after(out_weight, marks[2]), 2 * low)
    w_top = xor_permute(w_one[:cut], 2 * low)
    w_bottom = xor_permute(w_two[cut:], low)
    columns = [out_weight, w_one, w_two, jnp.concatenate([w_top, w_bottom], axis=0)]

    named = (ids[0] == exp) | (ids[1] == exp)
    every = low * length
    token = jnp.arange(every, dtype=jnp.int32)
    earlier = (token[:, None] < token[None, :]) & (
        token[:, None] // tokens == token[None, :] // tokens
    )
    rank = jnp.sum((earlier & named[:, None]).astype(jnp.int32), axis=0)
    row = jnp.where(named & (rank < capacity), token // tokens * capacity + rank, -1)
    slots = low * n_exp * capacity
    picks = (jnp.arange(slots, dtype=jnp.int32)[:, None] == row[None, :]).astype(BF16)

    head_out = call(
        head_kernel,
        jax.ShapeDtypeStruct((length, here), BF16),
        4 * heads * length * size * size,
        8 * length * here + 4 * heads * size * size,
        heads * length * size,
        in_specs=[SM, SM, VM, VM] + [VM] * len(states),
        out_specs=VM,
    )(place, decay_rate, queries, local, *states)
    group_heads = within_group(head_out)

    gains, rests = [], []
    for t in range(GROUPS):
        start = (((group ^ t) * low + member) * cols).astype(jnp.int32)
        gains.append(lax.dynamic_slice(moe_gain, (start,), (cols,))[None])
        rests.append(
            [lax.dynamic_slice(r, (jnp.int32(0), start), (tokens, cols)) for r in rest_rows]
        )

    mixed, received = [], []
    for t in range(GROUPS):
        part, sent = call(
            functools.partial(project_kernel, low),
            [jax.ShapeDtypeStruct((every, cols), F32), jax.ShapeDtypeStruct((every, cols), BF16)],
            2 * every * here * cols,
            2 * every * here + 2 * here * cols + 6 * every * cols,
            in_specs=[SM] + [VM] * (2 * low + 1),
            out_specs=[VM, VM],
        )(place, *group_heads, columns[t], *rests[t])
        mixed.append(line_sum(part, sent, exp))
        last = t == GROUPS - 1
        wide = (cols + 127) // 128 * 128 + 128 if last else cols
        x = call(
            functools.partial(dispatch_kernel, GROUPS if last else 1),
            jax.ShapeDtypeStruct((slots, wide), BF16),
            2 * slots * every * wide,
            2 * every * (slots + cols) + 2 * slots * wide,
            in_specs=[VM] * ((GROUPS if last else 1) + 2),
            out_specs=VM,
        )(*(mixed if last else mixed[-1:]), gains[t], picks)
        one, two = xor_permute(x, low), xor_permute(x, 2 * low)
        three = xor_permute(one, 2 * low) if t % 2 == 0 else xor_permute(two, low)
        got = [within_group(y) for y in (x, one, two, three)]
        if not aligned:
            joined = []
            for per in got:
                whole = in_order([y[:, :cols] for y in per], member, 1)
                if last:
                    whole = jnp.concatenate([whole] + [y[:, wide - 128 :] for y in per], axis=1)
                joined.append([whole])
            got = joined
        received.append(got)

    own = exp * tokens
    gotten = []
    for a in range(1, low):
        first = lax.rem(member + a, low) * length + own
        rows = [lax.dynamic_slice_in_dim(m, first, tokens, 0) for m in mixed]
        gotten.append(
            lax.ppermute(
                jnp.concatenate(rows, axis=1),
                "ctx",
                [(d, d // low * low + (d % low + a) % low) for d in range(n_ctx)],
            )
        )
    gotten = gotten[::-1]
    if aligned:
        mixed_out = call(
            functools.partial(mixed_kernel, low),
            jax.ShapeDtypeStruct((tokens, model), BF16),
            0,
            6 * tokens * model,
            in_specs=[SM] + [VM] * (GROUPS + low - 1),
            out_specs=VM,
        )(place, *mixed, *gotten)
    else:
        rows = [lax.dynamic_slice_in_dim(m, member * length + own, tokens, 0) for m in mixed]
        parts = [jnp.concatenate(rows, axis=1)] + gotten
        mixed_out = jnp.zeros((tokens, model), BF16)
        for a, part in enumerate(parts):
            for t in range(GROUPS):
                start = ((group ^ t) * low + lax.rem(member + a, low)) * cols
                mixed_out = lax.dynamic_update_slice_in_dim(
                    mixed_out, part[:, t * cols : (t + 1) * cols], start, 1
                )

    gate, up = gate_weight[0], up_weight[0]
    sums = [None] * GROUPS
    for chunk_ids in ([0, 1], [2]):
        for s in range(GROUPS):
            sums[s] = expert_step(
                place, s, chunk_ids, [received[t][s] for t in chunk_ids], gate, up, sums[s], None, False
            )
    hidden = None
    for s in range(GROUPS):
        last = GROUPS - 1
        hidden = expert_step(
            place, s, [last], [received[last][s]], gate, up, sums[s], hidden, True
        )
    return (mixed_out, hidden[None])


def solution(mesh):
    in_specs = (
        P("ctx", "exp"),
        P("ctx", "exp"),
        P("ctx", "exp"),
        P("exp"),
        P("exp", "ctx"),
        P(("ctx", "exp"), None),
        P(),
        P(("ctx", "exp"), None),
        P("exp", "ctx", None),
        P("exp", "ctx", None),
    )
    out_specs = (P(("ctx", "exp"), None), P("exp", "ctx", None))
    return jax.shard_map(
        per_device, mesh=mesh, in_specs=in_specs, out_specs=out_specs, check_vma=False
    )
```

time: 213 us -> 218 us (1.023)
  waiting for transfers between devices: 65.2 us -> 81.3 us
  Pallas kernels: 48.2 us -> 63.1 us
  matrix products: 10.7 us -> 0 us
  local copies, waits for them, and re-layouts: 14 us -> 5.71 us
  starting transfers between devices: 66.5 us -> 61.9 us
    ppermute x22 -> x19, waiting for transfers between devices: 17.9 us -> 44 us  [xor_permute(): return lax.ppermute(x, 'ctx', [(d, d ^ step) for d in range(n)])]
    ppermute x12 -> x13, waiting for transfers between devices: 34 us -> 17.9 us  [the longest x4 15.7 us: line_sum(): lax.ppermute(sent, 'exp', [(hop, hop + 1), (n - 1 - hop, n - 2 - hop)])]
    pallas_call x9 -> x22, Pallas kernels: 45.5 us -> 60.4 us  [the longest x12 51.1 us: expert_step(): call(functools.partial(expert_kernel, count, mode, has_acc, model), out_s...]
    dot_general x8 -> x0, matrix products: 10.7 us -> none  [dot(): return lax.dot_general(a, b, dims, preferred_element_type=F32)]
    ppermute x12 -> x13, starting transfers between devices: 29.5 us -> 22.4 us  [the longest x4 11.8 us: line_sum(): lax.ppermute(sent, 'exp', [(hop, hop + 1), (n - 1 - hop, n - 2 - hop)])]
    ppermute x4, waiting for transfers between devices: 13.3 us -> 19.3 us  [line_sum(): got = lax.ppermute(total, 'exp', [(here, here - 1), (there, there + 1)])]
    slice x10 -> x2, local copies, waits for them, and re-layouts: 4.85 us -> 0.08 us  [the longest x1 0.04 us: per_device(): w_top = xor_permute(w_one[:cut], 2 * low)]
    ppermute x22 -> x19, starting transfers between devices: 27.2 us -> 30.3 us  [xor_permute(): return lax.ppermute(x, 'ctx', [(d, d ^ step) for d in range(n)])]
  transfers between devices with their start and end apart: 58 -> 54, of which waited for: 17 -> 19; matrix products, arithmetic and copies ran while one was open for 12% -> 2% of each run, Pallas kernels for 20% -> 26%
where the time goes in v2:
time: 218 us; the launch traced here: 217 us
  waiting for transfers between devices  81.3 us (37%)
  Pallas kernels  63.1 us (29%)
  starting transfers between devices  61.9 us (28%)
  local copies, waits for them, and re-layouts  5.71 us (3%)
  other arithmetic  3.93 us (2%)
    pallas_call x12, Pallas kernels, expert_step(): call(functools.partial(expert_kernel, count, mode, has_acc, model), out_s...  51.1 us
    ppermute x19, waiting for transfers between devices, xor_permute(): return lax.ppermute(x, 'ctx', [(d, d ^ step) for d in range(n)])  44 us
    ppermute x19, starting transfers between devices, xor_permute(): return lax.ppermute(x, 'ctx', [(d, d ^ step) for d in range(n)])  30.3 us
    ppermute x4, waiting for transfers between devices, line_sum(): got = lax.ppermute(total, 'exp', [(here, here - 1), (there, there + 1)])  19.3 us
    ppermute x4, waiting for transfers between devices, line_sum(): lax.ppermute(sent, 'exp', [(hop, hop + 1), (n - 1 - hop, n - 2 - hop)])  15.7 us
    ppermute x4, starting transfers between devices, line_sum(): lax.ppermute(sent, 'exp', [(hop, hop + 1), (n - 1 - hop, n - 2 - hop)])  11.8 us
    unnamed x60, local copies, waits for them, and re-layouts  5.44 us
    ppermute x4, starting transfers between devices, line_sum(): got = lax.ppermute(total, 'exp', [(here, here - 1), (there, there + 1)])  5.34 us
  transfers between devices with their start and end apart: 54, of which 19 were waited for; matrix products, arithmetic and copies ran while one was open for 2% of the time, Pallas kernels for 26%

profile of v2, /device:TPU:0, one launch (start us, length us, event | category | flops | bytes accessed | tf_op | source)
XLA Modules:
  0.0 217.4 jit_solution(14252602006372485260)
XLA Ops:
  0.7 1.0 copy-done.2
  1.8 1.0 copy-done.4
  3.5 1.1 shard_map.114
  5.2 1.1 collective-permute-done
  6.4 2.9 %collective-permute-start.1 = (f32[4,128,128]{2,1,0:T(8,128)S(1)}, f32[4,128,128]{2,1,0:T(8,128)S(1)}, u32[]{:S(2)}, u32[]{:S(2)}) collective-permute-start(f32[4,128,128]{2,1,0:T(8,128)S(1)} %select_add_fusion), channel_id=1, source_target_pairs={{0,8},{4,12},{8,0},{12,4},{16,24},{20,28},{24,16},{28,20},{1,9},{5... | collective-permute-start | bytes 786440 | tf_op jit(solution)/shard_map/ppermute | solution.py:94
  9.3 6.6 %collective-permute-done.1 = f32[4,128,128]{2,1,0:T(8,128)S(1)} collective-permute-done((f32[4,128,128]{2,1,0:T(8,128)S(1)}, f32[4,128,128]{2,1,0:T(8,128)S(1)}, u32[]{:S(2)}, u32[]{:S(2)}) %collective-permute-start.1) | collective-permute-done | bytes 262176 | tf_op jit(solution)/shard_map/ppermute | solution.py:94
  16.0 3.7 %collective-permute-start.2 = (f32[4,128,128]{2,1,0:T(8,128)S(1)}, f32[4,128,128]{2,1,0:T(8,128)S(1)}, u32[]{:S(2)}, u32[]{:S(2)}) collective-permute-start(f32[4,128,128]{2,1,0:T(8,128)S(1)} %add_select_fusion), channel_id=1, source_target_pairs={{0,16},{4,20},{8,24},{12,28},{1,17},{5,21},{9,25},{13,29},{2,18},{... | collective-permute-start | bytes 786440 | tf_op jit(solution)/shard_map/ppermute | solution.py:306
  19.9 1.5 shard_map.113.local_ref
  21.5 1.6 collective-permute-start.23
  23.2 1.6 collective-permute-done.2
  25.2 2.6 %collective-permute-start.24 = (s32[2,128]{1,0:T(2,128)S(1)}, s32[2,128]{1,0:T(2,128)S(1)}, u32[]{:S(2)}, u32[]{:S(2)}) collective-permute-start(s32[2,128]{1,0:T(2,128)S(1)} %add_select_fusion.4), channel_id=1, source_target_pairs={{0,2},{1,3},{2,0},{3,1},{4,6},{5,7},{6,4},{7,5},{8,10},{9,11},{10,... | collective-permute-start | bytes 3080 | tf_op jit(solution)/shard_map/ppermute | solution.py:124
  27.8 1.5 collective-permute-start.9
  29.7 1.2 shard_map.115.refs_0_
  31.6 2.3 %collective-permute-start.13 = (bf16[1024,384]{1,0:T(8,128)(2,1)S(1)}, bf16[1024,384]{1,0:T(8,128)(2,1)S(1)}, u32[]{:S(2)}, u32[]{:S(2)}) collective-permute-start(bf16[1024,384]{1,0:T(8,128)(2,1)S(1)} %copy-done.11), channel_id=1, source_target_pairs={{0,16},{4,20},{8,24},{12,28},{16,0},{20,4},{24,8},{28,12},{1,17},{... | collective-permute-start | bytes 2359304 | tf_op jit(solution)/shard_map/ppermute | solution.py:94
  34.2 13.1 %collective-permute-done.9.refs_2_ = bf16[1024,384]{1,0:T(8,128)(2,1)S(1)} collective-permute-done((bf16[1024,384]{1,0:T(8,128)(2,1)S(1)}, bf16[1024,384]{1,0:T(8,128)(2,1)S(1)}, u32[]{:S(2)}, u32[]{:S(2)}) %collective-permute-start.9) | collective-permute-done | bytes 786464 | tf_op jit(solution)/shard_map/ppermute | solution.py:94
  47.3 1.3 shard_map.117
  48.6 3.5 %collective-permute-start.10 = (bf16[512,384]{1,0:T(8,128)(2,1)S(1)}, bf16[512,384]{1,0:T(8,128)(2,1)S(1)}, u32[]{:S(2)}, u32[]{:S(2)}) collective-permute-start(bf16[512,384]{1,0:T(8,128)(2,1)S(1)} %get-tuple-element.39), channel_id=1, source_target_pairs={{0,1},{3,2},{4,5},{7,6},{8,9},{11,10},{12,13},{15,14},{16,17},{19,... | collective-permute-start | bytes 1179656 | tf_op jit(solution)/shard_map/ppermute | solution.py:137
  52.1 1.3 shard_map.116
  53.4 1.3 collective-permute-start.6
  54.9 2.5 %collective-permute-start.17 = (bf16[512,384]{1,0:T(8,128)(2,1)S(1)}, bf16[512,384]{1,0:T(8,128)(2,1)S(1)}, u32[]{:S(2)}, u32[]{:S(2)}) collective-permute-start(bf16[512,384]{1,0:T(8,128)(2,1)S(1)} %slice.16), channel_id=1, source_target_pairs={{0,16},{4,20},{8,24},{12,28},{16,0},{20,4},{24,8},{28,12},{1,17},{... | collective-permute-start | bytes 1179656 | tf_op jit(solution)/shard_map/ppermute | solution.py:94
  57.4 1.3 shard_map.118
  58.7 1.3 collective-permute-start.14
  60.1 1.6 collective-permute-start.18
  62.4 7.6 %collective-permute-done.6 = bf16[512,384]{1,0:T(8,128)(2,1)S(1)} collective-permute-done((bf16[512,384]{1,0:T(8,128)(2,1)S(1)}, bf16[512,384]{1,0:T(8,128)(2,1)S(1)}, u32[]{:S(2)}, u32[]{:S(2)}) %collective-permute-start.6) | collective-permute-done | bytes 393248 | tf_op jit(solution)/shard_map/ppermute | solution.py:137
  70.9 5.8 %collective-permute-done.14 = bf16[512,384]{1,0:T(8,128)(2,1)S(1)} collective-permute-done((bf16[512,384]{1,0:T(8,128)(2,1)S(1)}, bf16[512,384]{1,0:T(8,128)(2,1)S(1)}, u32[]{:S(2)}, u32[]{:S(2)}) %collective-permute-start.14) | collective-permute-done | bytes 393248 | tf_op jit(solution)/shard_map/ppermute | solution.py:137
  77.5 1.3 shard_map.119
  78.8 5.6 %collective-permute-start.19 = (bf16[512,384]{1,0:T(8,128)(2,1)S(1)}, bf16[512,384]{1,0:T(8,128)(2,1)S(1)}, u32[]{:S(2)}, u32[]{:S(2)}) collective-permute-start(bf16[512,384]{1,0:T(8,128)(2,1)S(1)} %get-tuple-element.44), channel_id=1, source_target_pairs={{0,1},{3,2},{4,5},{7,6},{8,9},{11,10},{12,13},{15,14},{16,17},{19,... | collective-permute-start | bytes 1179656 | tf_op jit(solution)/shard_map/ppermute | solution.py:137
  84.6 1.3 collective-permute-start.12
  86.1 1.3 collective-permute-start.8
  87.5 1.3 collective-permute-start.16
  88.8 2.4 %collective-permute-done.19 = bf16[512,384]{1,0:T(8,128)(2,1)S(1)} collective-permute-done((bf16[512,384]{1,0:T(8,128)(2,1)S(1)}, bf16[512,384]{1,0:T(8,128)(2,1)S(1)}, u32[]{:S(2)}, u32[]{:S(2)}) %collective-permute-start.19) | collective-permute-done | bytes 393248 | tf_op jit(solution)/shard_map/ppermute | solution.py:137
  91.9 6.6 %collective-permute-done.12 = bf16[512,384]{1,0:T(8,128)(2,1)S(1)} collective-permute-done((bf16[512,384]{1,0:T(8,128)(2,1)S(1)}, bf16[512,384]{1,0:T(8,128)(2,1)S(1)}, u32[]{:S(2)}, u32[]{:S(2)}) %collective-permute-start.12) | collective-permute-done | bytes 393248 | tf_op jit(solution)/shard_map/ppermute | solution.py:144
  99.1 7.9 %collective-permute-done.8 = bf16[512,384]{1,0:T(8,128)(2,1)S(1)} collective-permute-done((bf16[512,384]{1,0:T(8,128)(2,1)S(1)}, bf16[512,384]{1,0:T(8,128)(2,1)S(1)}, u32[]{:S(2)}, u32[]{:S(2)}) %collective-permute-start.8) | collective-permute-done | bytes 393248 | tf_op jit(solution)/shard_map/ppermute | solution.py:144
  107.5 4.8 %collective-permute-done.16 = bf16[512,384]{1,0:T(8,128)(2,1)S(1)} collective-permute-done((bf16[512,384]{1,0:T(8,128)(2,1)S(1)}, bf16[512,384]{1,0:T(8,128)(2,1)S(1)}, u32[]{:S(2)}, u32[]{:S(2)}) %collective-permute-start.16) | collective-permute-done | bytes 393248 | tf_op jit(solution)/shard_map/ppermute | solution.py:144
  112.9 1.6 collective-permute-start.48
  115.7 1.5 collective-permute-start.29
  117.2 2.9 %collective-permute-start.35 = (bf16[384,384]{1,0:T(8,128)(2,1)S(1)}, bf16[384,384]{1,0:T(8,128)(2,1)}, u32[]{:S(2)}, u32[]{:S(2)}) collective-permute-start(bf16[384,384]{1,0:T(8,128)(2,1)S(1)} %shard_map.124.refs_2_), channel_id=1, source_target_pairs={{0,16},{4,20},{8,24},{12,28},{16,0},{20,4},{24,8},{28,12},{1,17},{... | collective-permute-start | bytes 884744 | tf_op jit(solution)/shard_map/ppermute | solution.py:94
  120.9 1.5 collective-permute-start.21
  122.8 2.9 %collective-permute-start.41 = (bf16[384,384]{1,0:T(8,128)(2,1)S(1)}, bf16[384,384]{1,0:T(8,128)(2,1)}, u32[]{:S(2)}, u32[]{:S(2)}) collective-permute-start(bf16[384,384]{1,0:T(8,128)(2,1)S(1)} %shard_map.123.refs_0_), channel_id=1, source_target_pairs={{0,16},{4,20},{8,24},{12,28},{16,0},{20,4},{24,8},{28,12},{1,17},{... | collective-permute-start | bytes 884744 | tf_op jit(solution)/shard_map/ppermute | solution.py:94
  125.7 3.3 %collective-permute-done.32.refs_0_ = bf16[384,384]{1,0:T(8,128)(2,1)S(1)} collective-permute-done((bf16[384,384]{1,0:T(8,128)(2,1)S(1)}, bf16[384,384]{1,0:T(8,128)(2,1)S(1)}, u32[]{:S(2)}, u32[]{:S(2)}) %collective-permute-start.32) | collective-permute-done | bytes 294944 | tf_op jit(solution)/shard_map/ppermute | solution.py:94
  129.0 2.9 %collective-permute-start.39 = (bf16[384,384]{1,0:T(8,128)(2,1)S(1)}, bf16[384,384]{1,0:T(8,128)(2,1)S(1)}, u32[]{:S(2)}, u32[]{:S(2)}) collective-permute-start(bf16[384,384]{1,0:T(8,128)(2,1)S(1)} %shard_map.122.refs_0_), channel_id=1, source_target_pairs={{0,16},{4,20},{8,24},{12,28},{16,0},{20,4},{24,8},{28,12},{1,17},{... | collective-permute-start | bytes 884744 | tf_op jit(solution)/shard_map/ppermute | solution.py:94
  132.0 3.0 %collective-permute-done.29.refs_0_ = bf16[384,384]{1,0:T(8,128)(2,1)S(1)} collective-permute-done((bf16[384,384]{1,0:T(8,128)(2,1)S(1)}, bf16[384,384]{1,0:T(8,128)(2,1)S(1)}, u32[]{:S(2)}, u32[]{:S(2)}) %collective-permute-start.29) | collective-permute-done | bytes 294944 | tf_op jit(solution)/shard_map/ppermute | solution.py:94
  135.6 3.8 %collective-permute-done.39.refs_0_ = bf16[384,384]{1,0:T(8,128)(2,1)S(1)} collective-permute-done((bf16[384,384]{1,0:T(8,128)(2,1)S(1)}, bf16[384,384]{1,0:T(8,128)(2,1)S(1)}, u32[]{:S(2)}, u32[]{:S(2)}) %collective-permute-start.39) | collective-permute-done | bytes 294944 | tf_op jit(solution)/shard_map/ppermute | solution.py:94
  140.1 1.0 broadcast_select_fusion.refs_3_
  141.9 1.8 collective-permute-start.26
  144.6 1.8 collective-permute-start.30
  146.4 1.5 collective-permute-start.44
  147.9 5.9 %collective-permute-done.36.refs_2_ = bf16[384,384]{1,0:T(8,128)(2,1)S(1)} collective-permute-done((bf16[384,384]{1,0:T(8,128)(2,1)}, bf16[384,384]{1,0:T(8,128)(2,1)S(1)}, u32[]{:S(2)}, u32[]{:S(2)}) %collective-permute-start.36) | collective-permute-done | bytes 294944 | tf_op jit(solution)/shard_map/ppermute | solution.py:94
  153.8 6.3 %collective-permute-done.33.refs_0_ = bf16[384,384]{1,0:T(8,128)(2,1)S(1)} collective-permute-done((bf16[384,384]{1,0:T(8,128)(2,1)S(1)}, bf16[384,384]{1,0:T(8,128)(2,1)S(1)}, u32[]{:S(2)}, u32[]{:S(2)}) %collective-permute-start.33) | collective-permute-done | bytes 294944 | tf_op jit(solution)/shard_map/ppermute | solution.py:94
  160.7 4.8 %shard_map.131 = (f32[576,384]{1,0:T(8,128)S(1)}, f32[576,384]{1,0:T(8,128)S(1)}) custom-call(s32[3]{0:T(128)S(1)} %pad_add_fusion.place_ref, bf16[384,384]{1,0:T(8,128)(2,1)S(1)} %shard_map.123.refs_0_, bf16[384,384]{1,0:T(8,128)(2,1)S(1)} %copy-done.23, bf16[384,384]{1,0:T(8,128)(2,1)S(1)} %shard_map.124.refs_2_, bf16[384,384]{1,0:T(8,128)(2,1)S(1)} %copy-done.21, ...), custom_call_target="tpu_custom_call" | custom-call | flops 1358954496 | bytes 6488064 | tf_op jit(solution)/shard_map/pallas_call | solution.py:261
  166.0 3.2 %shard_map.132 = (f32[576,384]{1,0:T(8,128)S(1)}, f32[576,384]{1,0:T(8,128)S(1)}) custom-call(s32[3]{0:T(128)S(1)} %pad_add_fusion.place_ref, bf16[384,384]{1,0:T(8,128)(2,1)S(1)} %shard_map.122.refs_0_, bf16[384,384]{1,0:T(8,128)(2,1)S(1)} %collective-permute-done.51.refs_1_, bf16[576,3072]{1,0:T(8,128)(2,1)} %bitcast.13, bf16[576,3072]{1,0:T(8,128)(2,1)} %bitcast.14, ...), custom_call_target="tpu_custom_call" | custom-call | flops 679477248 | bytes 5898240 | tf_op jit(solution)/shard_map/pallas_call | solution.py:261
  169.3 0.9 copy-done.7
  170.2 0.9 copy-done.9
  171.1 5.0 %shard_map.129 = (f32[576,384]{1,0:T(8,128)S(1)}, f32[576,384]{1,0:T(8,128)S(1)}) custom-call(s32[3]{0:T(128)S(1)} %pad_add_fusion.place_ref, bf16[384,384]{1,0:T(8,128)(2,1)S(1)} %copy-done.25, bf16[384,384]{1,0:T(8,128)(2,1)S(1)} %collective-permute-done.47.refs_1_, bf16[384,384]{1,0:T(8,128)(2,1)} %collective-permute-done.48.refs_2_, ...), custom_call_target="tpu_custom_call" | custom-call | flops 1358954496 | bytes 6488064 | tf_op jit(solution)/shard_map/pallas_call | solution.py:261
  176.8 5.0 %shard_map.127 = (f32[576,384]{1,0:T(8,128)S(1)}, f32[576,384]{1,0:T(8,128)S(1)}) custom-call(s32[3]{0:T(128)S(1)} %pad_add_fusion.place_ref, bf16[384,384]{1,0:T(8,128)(2,1)} %collective-permute-done.41.refs_0_, bf16[384,384]{1,0:T(8,128)(2,1)S(1)} %collective-permute-done.42.refs_1_, bf16[384,384]{1,0:T(8,128)(2,1)} %collective-permute-done.35.refs_2_, ...), custom_call_target="tpu_custom_call" | custom-call | flops 1358954496 | bytes 6488064 | tf_op jit(solution)/shard_map/pallas_call | solution.py:261
  182.4 3.2 %shard_map.130 = (f32[576,384]{1,0:T(8,128)S(1)}, f32[576,384]{1,0:T(8,128)S(1)}) custom-call(s32[3]{0:T(128)S(1)} %pad_add_fusion.place_ref, bf16[384,384]{1,0:T(8,128)(2,1)S(1)} %copy-done.13, bf16[384,384]{1,0:T(8,128)(2,1)S(1)} %collective-permute-done.46.refs_1_, bf16[576,3072]{1,0:T(8,128)(2,1)} %bitcast.24, bf16[576,3072]{1,0:T(8,128)(2,1)} %bitcast.23, ...), custom_call_target="tpu_custom_call" | custom-call | flops 679477248 | bytes 5898240 | tf_op jit(solution)/shard_map/pallas_call | solution.py:261
  186.2 3.7 %shard_map.128 = (f32[576,384]{1,0:T(8,128)S(1)}, f32[576,384]{1,0:T(8,128)S(1)}) custom-call(s32[3]{0:T(128)S(1)} %pad_add_fusion.place_ref, bf16[384,384]{1,0:T(8,128)(2,1)S(1)} %copy-done.15, bf16[384,384]{1,0:T(8,128)(2,1)S(1)} %copy-done.17, bf16[576,3072]{1,0:T(8,128)(2,1)} %bitcast.25, bf16[576,3072]{1,0:T(8,128)(2,1)} %bitcast.26, ...), custom_call_target="tpu_custom_call" | custom-call | flops 679477248 | bytes 5898240 | tf_op jit(solution)/shard_map/pallas_call | solution.py:261
  189.9 1.3 shard_map.120
  191.3 4.3 %shard_map.133.refs_8_ = bf16[576,1536]{1,0:T(8,128)(2,1)} custom-call(s32[3]{0:T(128)S(1)} %pad_add_fusion.place_ref, bf16[384,512]{1,0:T(8,128)(2,1)S(1)} %shard_map.121.refs_0_, bf16[384,512]{1,0:T(8,128)(2,1)S(1)} %collective-permute-done.50.refs_1_, bf16[576,3072]{1,0:T(8,128)(2,1)S(1)} %bitcast.33, bf16[576,3072]{1,0:T(8,128)(2,1)S(1)} %bitcast.34, ...), custom_call_target="tpu_custom_call" | custom-call | flops 679477248 | bytes 5898240 | tf_op jit(solution)/shard_map/pallas_call | solution.py:261
  195.7 4.9 %shard_map.125 = (f32[576,384]{1,0:T(8,128)S(1)}, f32[576,384]{1,0:T(8,128)S(1)}) custom-call(s32[3]{0:T(128)S(1)} %pad_add_fusion.place_ref, bf16[384,384]{1,0:T(8,128)(2,1)S(1)} %collective-permute-done.33.refs_0_, bf16[384,384]{1,0:T(8,128)(2,1)S(1)} %collective-permute-done.34.refs_1_, bf16[384,384]{1,0:T(8,128)(2,1)S(1)} %collective-permute-done.36.refs_2_, ...), custom_call_target="tpu_custom_call" | custom-call | flops 1358954496 | bytes 6488064 | tf_op jit(solution)/shard_map/pallas_call | solution.py:261
  200.6 3.5 %shard_map.126 = (f32[576,384]{1,0:T(8,128)S(1)}, f32[576,384]{1,0:T(8,128)S(1)}) custom-call(s32[3]{0:T(128)S(1)} %pad_add_fusion.place_ref, bf16[384,384]{1,0:T(8,128)(2,1)S(1)} %copy-done.19, bf16[384,384]{1,0:T(8,128)(2,1)S(1)} %collective-permute-done.31.refs_1_, bf16[576,3072]{1,0:T(8,128)(2,1)} %bitcast.31, bf16[576,3072]{1,0:T(8,128)(2,1)} %bitcast.32, ...), custom_call_target="tpu_custom_call" | custom-call | flops 679477248 | bytes 5898240 | tf_op jit(solution)/shard_map/pallas_call | solution.py:261
  204.1 4.4 %shard_map.134.refs_8_ = bf16[576,1536]{1,0:T(8,128)(2,1)} custom-call(s32[3]{0:T(128)S(1)} %pad_add_fusion.place_ref, bf16[384,512]{1,0:T(8,128)(2,1)} %collective-permute-done.44.refs_0_, bf16[384,512]{1,0:T(8,128)(2,1)S(1)} %collective-permute-done.45.refs_1_, bf16[576,3072]{1,0:T(8,128)(2,1)S(1)} %bitcast.35, ...), custom_call_target="tpu_custom_call", output_to_operand_aliasing={{}: (9, {})} | custom-call | flops 679477248 | bytes 5898240 | tf_op jit(solution)/shard_map/pallas_call | solution.py:261
  208.5 4.4 %shard_map.135.refs_8_ = bf16[576,1536]{1,0:T(8,128)(2,1)} custom-call(s32[3]{0:T(128)S(1)} %pad_add_fusion.place_ref, bf16[384,512]{1,0:T(8,128)(2,1)} %collective-permute-done.26.refs_0_, bf16[384,512]{1,0:T(8,128)(2,1)S(1)} %collective-permute-done.38.refs_1_, bf16[576,3072]{1,0:T(8,128)(2,1)S(1)} %bitcast.37, ...), custom_call_target="tpu_custom_call", output_to_operand_aliasing={{}: (9, {})} | custom-call | flops 679477248 | bytes 5898240 | tf_op jit(solution)/shard_map/pallas_call | solution.py:261
  212.9 4.5 %shard_map.136 = bf16[576,1536]{1,0:T(8,128)(2,1)} custom-call(s32[3]{0:T(128)S(1)} %pad_add_fusion.place_ref, bf16[384,512]{1,0:T(8,128)(2,1)} %collective-permute-done.27.refs_0_, bf16[384,512]{1,0:T(8,128)(2,1)} %collective-permute-done.28.refs_1_, bf16[576,3072]{1,0:T(8,128)(2,1)S(1)} %bitcast.39, ...), custom_call_target="tpu_custom_call", output_to_operand_aliasing={{}: (9, {})} | custom-call | flops 679477248 | bytes 5898240 | tf_op jit(solution)/shard_map/pallas_call | solution.py:261
  (169 shorter events, 17.2 us)
Async XLA Ops:
  0.6 19.2 %copy-start.28 = (f32[3072]{0:T(1024)S(1)}, f32[3072]{0:T(1024)}, u32[]{:S(2)}) copy-start(f32[3072]{0:T(1024)} %param.16) | copy-start | bytes 36868
  3.5 16.4 %copy-start.3 = (bf16[256,1024]{1,0:T(8,128)(2,1)S(1)}, bf16[256,1024]{1,0:T(8,128)(2,1)}, u32[]{:S(2)}) copy-start(bf16[256,1024]{1,0:T(8,128)(2,1)} %k_ref.3) | copy-start | bytes 1572868
  3.5 16.4 %copy-start.5 = (bf16[256,1024]{1,0:T(8,128)(2,1)S(1)}, bf16[256,1024]{1,0:T(8,128)(2,1)}, u32[]{:S(2)}) copy-start(bf16[256,1024]{1,0:T(8,128)(2,1)} %v_ref.3) | copy-start | bytes 1572868
  3.5 16.4 %copy-start.6 = (bf16[256,1024]{1,0:T(8,128)(2,1)S(1)}, bf16[256,1024]{1,0:T(8,128)(2,1)}, u32[]{:S(2)}) copy-start(bf16[256,1024]{1,0:T(8,128)(2,1)} %q_ref.3) | copy-start | bytes 1572868
  4.6 1.7 collective-permute-start
  6.4 15.2 %copy-start.29 = (s32[64,2]{0,1:T(2,128)S(1)}, s32[64,2]{0,1:T(2,128)}, u32[]{:S(2)}) copy-start(s32[64,2]{0,1:T(2,128)} %param.17) | copy-start | bytes 1540
  6.4 9.5 %collective-permute-start.1 = (f32[4,128,128]{2,1,0:T(8,128)S(1)}, f32[4,128,128]{2,1,0:T(8,128)S(1)}, u32[]{:S(2)}, u32[]{:S(2)}) collective-permute-start(f32[4,128,128]{2,1,0:T(8,128)S(1)} %select_add_fusion), channel_id=1, source_target_pairs={{0,8},{4,12},{8,0},{12,4},{16,24},{20,28},{24,16},{28,20},{1,9},{5... | collective-permute-start | bytes 786440 | tf_op jit(solution)/shard_map/ppermute | solution.py:94
  16.0 8.7 %collective-permute-start.2 = (f32[4,128,128]{2,1,0:T(8,128)S(1)}, f32[4,128,128]{2,1,0:T(8,128)S(1)}, u32[]{:S(2)}, u32[]{:S(2)}) collective-permute-start(f32[4,128,128]{2,1,0:T(8,128)S(1)} %add_select_fusion), channel_id=1, source_target_pairs={{0,16},{4,20},{8,24},{12,28},{1,17},{5,21},{9,25},{13,29},{2,18},{... | collective-permute-start | bytes 786440 | tf_op jit(solution)/shard_map/ppermute | solution.py:306
  21.4 12.7 %collective-permute-start.5 = (bf16[64,3072]{1,0:T(8,128)(2,1)}, bf16[64,3072]{1,0:T(8,128)(2,1)S(1)}, u32[]{:S(2)}, u32[]{:S(2)}) collective-permute-start(bf16[64,3072]{1,0:T(8,128)(2,1)} %param.15), channel_id=1, source_target_pairs={{0,4},{4,0},{8,12},{12,8},{16,20},{20,16},{24,28},{28,24},{1,5},{5... | collective-permute-start | bytes 1179656 | tf_op jit(solution)/shard_map/ppermute | solution.py:107
  21.5 3.6 %collective-permute-start.23 = (s32[2,64]{1,0:T(2,128)S(1)}, s32[2,64]{1,0:T(2,128)S(1)}, u32[]{:S(2)}, u32[]{:S(2)}) collective-permute-start(s32[2,64]{1,0:T(2,128)S(1)} %bitcast.76), channel_id=1, source_target_pairs={{0,1},{1,0},{2,3},{3,2},{4,5},{5,4},{6,7},{7,6},{8,9},{9,8},{10,11... | collective-permute-start | bytes 1544 | tf_op jit(solution)/shard_map/ppermute | solution.py:124
  24.9 4.8 %collective-permute-start.3 = (f32[4,128,128]{2,1,0:T(8,128)S(1)}, f32[4,128,128]{2,1,0:T(8,128)S(1)}, u32[]{:S(2)}, u32[]{:S(2)}) collective-permute-start(f32[4,128,128]{2,1,0:T(8,128)S(1)} %get-tuple-element.66), channel_id=1, source_target_pairs={{0,4},{4,0},{8,12},{12,8},{16,20},{20,16},{24,28},{28,24},{1,5},{5... | collective-permute-start | bytes 786440 | tf_op jit(solution)/shard_map/ppermute | solution.py:94
  25.2 4.5 %collective-permute-start.24 = (s32[2,128]{1,0:T(2,128)S(1)}, s32[2,128]{1,0:T(2,128)S(1)}, u32[]{:S(2)}, u32[]{:S(2)}) collective-permute-start(s32[2,128]{1,0:T(2,128)S(1)} %add_select_fusion.4), channel_id=1, source_target_pairs={{0,2},{1,3},{2,0},{3,1},{4,6},{5,7},{6,4},{7,5},{8,10},{9,11},{10,... | collective-permute-start | bytes 3080 | tf_op jit(solution)/shard_map/ppermute | solution.py:124
  27.8 19.5 %collective-permute-start.9 = (bf16[1024,384]{1,0:T(8,128)(2,1)S(1)}, bf16[1024,384]{1,0:T(8,128)(2,1)S(1)}, u32[]{:S(2)}, u32[]{:S(2)}) collective-permute-start(bf16[1024,384]{1,0:T(8,128)(2,1)S(1)} %copy-done.11), channel_id=1, source_target_pairs={{0,8},{4,12},{8,0},{12,4},{16,24},{20,28},{24,16},{28,20},{1,9},{5... | collective-permute-start | bytes 2359304 | tf_op jit(solution)/shard_map/ppermute | solution.py:94
  29.7 1.8 collective-permute-start.25
  31.0 16.3 %collective-permute-start.4 = (bf16[256,1024]{1,0:T(8,128)(2,1)S(1)}, bf16[256,1024]{1,0:T(8,128)(2,1)S(1)}, u32[]{:S(2)}, u32[]{:S(2)}) collective-permute-start(bf16[256,1024]{1,0:T(8,128)(2,1)S(1)} %shard_map.115.refs_0_), channel_id=1, source_target_pairs={{0,4},{4,0},{8,12},{12,8},{16,20},{20,16},{24,28},{28,24},{1,5},{5... | collective-permute-start | bytes 1572872 | tf_op jit(solution)/shard_map/ppermute | solution.py:107
  31.6 25.9 %collective-permute-start.13 = (bf16[1024,384]{1,0:T(8,128)(2,1)S(1)}, bf16[1024,384]{1,0:T(8,128)(2,1)S(1)}, u32[]{:S(2)}, u32[]{:S(2)}) collective-permute-start(bf16[1024,384]{1,0:T(8,128)(2,1)S(1)} %copy-done.11), channel_id=1, source_target_pairs={{0,16},{4,20},{8,24},{12,28},{16,0},{20,4},{24,8},{28,12},{1,17},{... | collective-permute-start | bytes 2359304 | tf_op jit(solution)/shard_map/ppermute | solution.py:94
  48.6 13.0 %collective-permute-start.10 = (bf16[512,384]{1,0:T(8,128)(2,1)S(1)}, bf16[512,384]{1,0:T(8,128)(2,1)S(1)}, u32[]{:S(2)}, u32[]{:S(2)}) collective-permute-start(bf16[512,384]{1,0:T(8,128)(2,1)S(1)} %get-tuple-element.39), channel_id=1, source_target_pairs={{0,1},{3,2},{4,5},{7,6},{8,9},{11,10},{12,13},{15,14},{16,17},{19,... | collective-permute-start | bytes 1179656 | tf_op jit(solution)/shard_map/ppermute | solution.py:137
  53.4 16.6 %collective-permute-start.6 = (bf16[512,384]{1,0:T(8,128)(2,1)S(1)}, bf16[512,384]{1,0:T(8,128)(2,1)S(1)}, u32[]{:S(2)}, u32[]{:S(2)}) collective-permute-start(bf16[512,384]{1,0:T(8,128)(2,1)S(1)} %get-tuple-element.36), channel_id=1, source_target_pairs={{0,1},{3,2},{4,5},{7,6},{8,9},{11,10},{12,13},{15,14},{16,17},{19,... | collective-permute-start | bytes 1179656 | tf_op jit(solution)/shard_map/ppermute | solution.py:137
  54.9 22.5 %collective-permute-start.17 = (bf16[512,384]{1,0:T(8,128)(2,1)S(1)}, bf16[512,384]{1,0:T(8,128)(2,1)S(1)}, u32[]{:S(2)}, u32[]{:S(2)}) collective-permute-start(bf16[512,384]{1,0:T(8,128)(2,1)S(1)} %slice.16), channel_id=1, source_target_pairs={{0,16},{4,20},{8,24},{12,28},{16,0},{20,4},{24,8},{28,12},{1,17},{... | collective-permute-start | bytes 1179656 | tf_op jit(solution)/shard_map/ppermute | solution.py:94
  58.7 17.9 %collective-permute-start.14 = (bf16[512,384]{1,0:T(8,128)(2,1)S(1)}, bf16[512,384]{1,0:T(8,128)(2,1)S(1)}, u32[]{:S(2)}, u32[]{:S(2)}) collective-permute-start(bf16[512,384]{1,0:T(8,128)(2,1)S(1)} %get-tuple-element.42), channel_id=1, source_target_pairs={{0,1},{3,2},{4,5},{7,6},{8,9},{11,10},{12,13},{15,14},{16,17},{19,... | collective-permute-start | bytes 1179656 | tf_op jit(solution)/shard_map/ppermute | solution.py:137
  60.1 17.3 %collective-permute-start.18 = (bf16[512,384]{1,0:T(8,128)(2,1)S(1)}, bf16[512,384]{1,0:T(8,128)(2,1)S(1)}, u32[]{:S(2)}, u32[]{:S(2)}) collective-permute-start(bf16[512,384]{1,0:T(8,128)(2,1)S(1)} %slice.17), channel_id=1, source_target_pairs={{0,8},{4,12},{8,0},{12,4},{16,24},{20,28},{24,16},{28,20},{1,9},{5... | collective-permute-start | bytes 1179656 | tf_op jit(solution)/shard_map/ppermute | solution.py:94
  61.8 22.7 %collective-permute-start.11 = (bf16[512,384]{1,0:T(8,128)(2,1)S(1)}, bf16[512,384]{1,0:T(8,128)(2,1)S(1)}, u32[]{:S(2)}, u32[]{:S(2)}) collective-permute-start(bf16[512,384]{1,0:T(8,128)(2,1)S(1)} %fusion.4), channel_id=1, source_target_pairs={{1,2},{2,1},{5,6},{6,5},{9,10},{10,9},{13,14},{14,13},{17,18},{18,... | collective-permute-start | bytes 1179656 | tf_op jit(solution)/shard_map/ppermute | solution.py:140
  70.2 15.7 %collective-permute-start.7 = (bf16[512,384]{1,0:T(8,128)(2,1)S(1)}, bf16[512,384]{1,0:T(8,128)(2,1)S(1)}, u32[]{:S(2)}, u32[]{:S(2)}) collective-permute-start(bf16[512,384]{1,0:T(8,128)(2,1)S(1)} %fusion.3), channel_id=1, source_target_pairs={{1,2},{2,1},{5,6},{6,5},{9,10},{10,9},{13,14},{14,13},{17,18},{18,... | collective-permute-start | bytes 1179656 | tf_op jit(solution)/shard_map/ppermute | solution.py:140
  76.7 10.7 %collective-permute-start.15 = (bf16[512,384]{1,0:T(8,128)(2,1)S(1)}, bf16[512,384]{1,0:T(8,128)(2,1)S(1)}, u32[]{:S(2)}, u32[]{:S(2)}) collective-permute-start(bf16[512,384]{1,0:T(8,128)(2,1)S(1)} %fusion.5), channel_id=1, source_target_pairs={{1,2},{2,1},{5,6},{6,5},{9,10},{10,9},{13,14},{14,13},{17,18},{18,... | collective-permute-start | bytes 1179656 | tf_op jit(solution)/shard_map/ppermute | solution.py:140
  78.8 12.4 %collective-permute-start.19 = (bf16[512,384]{1,0:T(8,128)(2,1)S(1)}, bf16[512,384]{1,0:T(8,128)(2,1)S(1)}, u32[]{:S(2)}, u32[]{:S(2)}) collective-permute-start(bf16[512,384]{1,0:T(8,128)(2,1)S(1)} %get-tuple-element.44), channel_id=1, source_target_pairs={{0,1},{3,2},{4,5},{7,6},{8,9},{11,10},{12,13},{15,14},{16,17},{19,... | collective-permute-start | bytes 1179656 | tf_op jit(solution)/shard_map/ppermute | solution.py:137
  84.6 13.9 %collective-permute-start.12 = (bf16[512,384]{1,0:T(8,128)(2,1)S(1)}, bf16[512,384]{1,0:T(8,128)(2,1)S(1)}, u32[]{:S(2)}, u32[]{:S(2)}) collective-permute-start(bf16[512,384]{1,0:T(8,128)(2,1)S(1)} %add_convert_fusion.2), channel_id=1, source_target_pairs={{1,0},{2,3},{5,4},{6,7},{9,8},{10,11},{13,12},{14,15},{17,16},{18,... | collective-permute-start | bytes 1179656 | tf_op jit(solution)/shard_map/ppermute | solution.py:144
  86.1 20.9 %collective-permute-start.8 = (bf16[512,384]{1,0:T(8,128)(2,1)S(1)}, bf16[512,384]{1,0:T(8,128)(2,1)S(1)}, u32[]{:S(2)}, u32[]{:S(2)}) collective-permute-start(bf16[512,384]{1,0:T(8,128)(2,1)S(1)} %add_convert_fusion.3), channel_id=1, source_target_pairs={{1,0},{2,3},{5,4},{6,7},{9,8},{10,11},{13,12},{14,15},{17,16},{18,... | collective-permute-start | bytes 1179656 | tf_op jit(solution)/shard_map/ppermute | solution.py:144
  87.5 24.8 %collective-permute-start.16 = (bf16[512,384]{1,0:T(8,128)(2,1)S(1)}, bf16[512,384]{1,0:T(8,128)(2,1)S(1)}, u32[]{:S(2)}, u32[]{:S(2)}) collective-permute-start(bf16[512,384]{1,0:T(8,128)(2,1)S(1)} %add_convert_fusion.1), channel_id=1, source_target_pairs={{1,0},{2,3},{5,4},{6,7},{9,8},{10,11},{13,12},{14,15},{17,16},{18,... | collective-permute-start | bytes 1179656 | tf_op jit(solution)/shard_map/ppermute | solution.py:144
  91.2 23.2 %collective-permute-start.20 = (bf16[512,384]{1,0:T(8,128)(2,1)S(1)}, bf16[512,384]{1,0:T(8,128)(2,1)S(1)}, u32[]{:S(2)}, u32[]{:S(2)}) collective-permute-start(bf16[512,384]{1,0:T(8,128)(2,1)S(1)} %fusion.6), channel_id=1, source_target_pairs={{1,2},{2,1},{5,6},{6,5},{9,10},{10,9},{13,14},{14,13},{17,18},{18,... | collective-permute-start | bytes 1179656 | tf_op jit(solution)/shard_map/ppermute | solution.py:140
  99.0 16.0 %collective-permute-start.53 = (bf16[384,384]{1,0:T(8,128)(2,1)S(1)}, bf16[384,384]{1,0:T(8,128)(2,1)S(1)}, u32[]{:S(2)}, u32[]{:S(2)}) collective-permute-start(bf16[384,384]{1,0:T(8,128)(2,1)S(1)} %shard_map.124.refs_2_), channel_id=1, source_target_pairs={{0,4},{4,0},{8,12},{12,8},{16,20},{20,16},{24,28},{28,24},{1,5},{5... | collective-permute-start | bytes 884744 | tf_op jit(solution)/shard_map/ppermute | solution.py:107
  107.4 9.7 %collective-permute-start.52 = (bf16[384,384]{1,0:T(8,128)(2,1)S(1)}, bf16[384,384]{1,0:T(8,128)(2,1)S(1)}, u32[]{:S(2)}, u32[]{:S(2)}) collective-permute-start(bf16[384,384]{1,0:T(8,128)(2,1)S(1)} %shard_map.123.refs_0_), channel_id=1, source_target_pairs={{0,4},{4,0},{8,12},{12,8},{16,20},{20,16},{24,28},{28,24},{1,5},{5... | collective-permute-start | bytes 884744 | tf_op jit(solution)/shard_map/ppermute | solution.py:107
  112.8 8.2 %collective-permute-start.51 = (bf16[384,384]{1,0:T(8,128)(2,1)S(1)}, bf16[384,384]{1,0:T(8,128)(2,1)S(1)}, u32[]{:S(2)}, u32[]{:S(2)}) collective-permute-start(bf16[384,384]{1,0:T(8,128)(2,1)S(1)} %shard_map.122.refs_0_), channel_id=1, source_target_pairs={{0,4},{4,0},{8,12},{12,8},{16,20},{20,16},{24,28},{28,24},{1,5},{5... | collective-permute-start | bytes 884744 | tf_op jit(solution)/shard_map/ppermute | solution.py:107
  112.9 10.0 %collective-permute-start.48 = (bf16[384,384]{1,0:T(8,128)(2,1)S(1)}, bf16[384,384]{1,0:T(8,128)(2,1)}, u32[]{:S(2)}, u32[]{:S(2)}) collective-permute-start(bf16[384,384]{1,0:T(8,128)(2,1)S(1)} %shard_map.124.refs_2_), channel_id=1, source_target_pairs={{0,8},{4,12},{8,0},{12,4},{16,24},{20,28},{24,16},{28,20},{1,9},{5... | collective-permute-start | bytes 884744 | tf_op jit(solution)/shard_map/ppermute | solution.py:94
  114.4 14.6 %collective-permute-start.32 = (bf16[384,384]{1,0:T(8,128)(2,1)S(1)}, bf16[384,384]{1,0:T(8,128)(2,1)S(1)}, u32[]{:S(2)}, u32[]{:S(2)}) collective-permute-start(bf16[384,384]{1,0:T(8,128)(2,1)S(1)} %shard_map.123.refs_0_), channel_id=1, source_target_pairs={{0,8},{4,12},{8,0},{12,4},{16,24},{20,28},{24,16},{28,20},{1,9},{5... | collective-permute-start | bytes 884744 | tf_op jit(solution)/shard_map/ppermute | solution.py:94
  115.7 19.3 %collective-permute-start.29 = (bf16[384,384]{1,0:T(8,128)(2,1)S(1)}, bf16[384,384]{1,0:T(8,128)(2,1)S(1)}, u32[]{:S(2)}, u32[]{:S(2)}) collective-permute-start(bf16[384,384]{1,0:T(8,128)(2,1)S(1)} %shard_map.122.refs_0_), channel_id=1, source_target_pairs={{0,8},{4,12},{8,0},{12,4},{16,24},{20,28},{24,16},{28,20},{1,9},{5... | collective-permute-start | bytes 884744 | tf_op jit(solution)/shard_map/ppermute | solution.py:94
  117.2 17.8 %collective-permute-start.35 = (bf16[384,384]{1,0:T(8,128)(2,1)S(1)}, bf16[384,384]{1,0:T(8,128)(2,1)}, u32[]{:S(2)}, u32[]{:S(2)}) collective-permute-start(bf16[384,384]{1,0:T(8,128)(2,1)S(1)} %shard_map.124.refs_2_), channel_id=1, source_target_pairs={{0,16},{4,20},{8,24},{12,28},{16,0},{20,4},{24,8},{28,12},{1,17},{... | collective-permute-start | bytes 884744 | tf_op jit(solution)/shard_map/ppermute | solution.py:94
  120.9 18.6 %collective-permute-start.21 = (bf16[512,384]{1,0:T(8,128)(2,1)}, bf16[512,384]{1,0:T(8,128)(2,1)}, u32[]{:S(2)}, u32[]{:S(2)}) collective-permute-start(bf16[512,384]{1,0:T(8,128)(2,1)} %add_convert_fusion), channel_id=1, source_target_pairs={{1,0},{2,3},{5,4},{6,7},{9,8},{10,11},{13,12},{14,15},{17,16},{18,... | collective-permute-start | bytes 1179656 | tf_op jit(solution)/shard_map/ppermute | solution.py:144
  122.8 12.7 %collective-permute-start.41 = (bf16[384,384]{1,0:T(8,128)(2,1)S(1)}, bf16[384,384]{1,0:T(8,128)(2,1)}, u32[]{:S(2)}, u32[]{:S(2)}) collective-permute-start(bf16[384,384]{1,0:T(8,128)(2,1)S(1)} %shard_map.123.refs_0_), channel_id=1, source_target_pairs={{0,16},{4,20},{8,24},{12,28},{16,0},{20,4},{24,8},{28,12},{1,17},{... | collective-permute-start | bytes 884744 | tf_op jit(solution)/shard_map/ppermute | solution.py:94
  129.0 10.4 %collective-permute-start.39 = (bf16[384,384]{1,0:T(8,128)(2,1)S(1)}, bf16[384,384]{1,0:T(8,128)(2,1)S(1)}, u32[]{:S(2)}, u32[]{:S(2)}) collective-permute-start(bf16[384,384]{1,0:T(8,128)(2,1)S(1)} %shard_map.122.refs_0_), channel_id=1, source_target_pairs={{0,16},{4,20},{8,24},{12,28},{16,0},{20,4},{24,8},{28,12},{1,17},{... | collective-permute-start | bytes 884744 | tf_op jit(solution)/shard_map/ppermute | solution.py:94
  134.9 9.7 %copy-start.12 = (bf16[384,384]{1,0:T(8,128)(2,1)}, bf16[384,384]{1,0:T(8,128)(2,1)S(1)}, u32[]{:S(2)}) copy-start(bf16[384,384]{1,0:T(8,128)(2,1)S(1)} %collective-permute-done.29.refs_0_) | copy-start | bytes 884740
  134.9 5.1 %collective-permute-start.49 = (bf16[384,384]{1,0:T(8,128)(2,1)}, bf16[384,384]{1,0:T(8,128)(2,1)}, u32[]{:S(2)}, u32[]{:S(2)}) collective-permute-start(bf16[384,384]{1,0:T(8,128)(2,1)} %collective-permute-done.48.refs_2_), channel_id=1, source_target_pairs={{0,4},{4,0},{8,12},{12,8},{16,20},{20,16},{24,28},{28,24},{1,5},{5... | collective-permute-start | bytes 884744 | tf_op jit(solution)/shard_map/ppermute | solution.py:107
  135.0 6.9 %collective-permute-start.47 = (bf16[384,384]{1,0:T(8,128)(2,1)}, bf16[384,384]{1,0:T(8,128)(2,1)S(1)}, u32[]{:S(2)}, u32[]{:S(2)}) collective-permute-start(bf16[384,384]{1,0:T(8,128)(2,1)} %copy-done.24), channel_id=1, source_target_pairs={{0,4},{4,0},{8,12},{12,8},{16,20},{20,16},{24,28},{28,24},{1,5},{5... | collective-permute-start | bytes 884744 | tf_op jit(solution)/shard_map/ppermute | solution.py:107
  135.5 8.1 %collective-permute-start.46 = (bf16[384,384]{1,0:T(8,128)(2,1)S(1)}, bf16[384,384]{1,0:T(8,128)(2,1)S(1)}, u32[]{:S(2)}, u32[]{:S(2)}) collective-permute-start(bf16[384,384]{1,0:T(8,128)(2,1)S(1)} %collective-permute-done.29.refs_0_), channel_id=1, source_target_pairs={{0,4},{4,0},{8,12},{12,8},{16,20},{20,16},{24,28},{28,24},{1,5},{5... | collective-permute-start | bytes 884744 | tf_op jit(solution)/shard_map/ppermute | solution.py:107
  139.5 4.8 %collective-permute-start.43 = (bf16[384,384]{1,0:T(8,128)(2,1)}, bf16[384,384]{1,0:T(8,128)(2,1)S(1)}, u32[]{:S(2)}, u32[]{:S(2)}) collective-permute-start(bf16[384,384]{1,0:T(8,128)(2,1)} %collective-permute-done.35.refs_2_), channel_id=1, source_target_pairs={{0,4},{4,0},{8,12},{12,8},{16,20},{20,16},{24,28},{28,24},{1,5},{5... | collective-permute-start | bytes 884744 | tf_op jit(solution)/shard_map/ppermute | solution.py:107
  139.5 5.1 %collective-permute-start.42 = (bf16[384,384]{1,0:T(8,128)(2,1)}, bf16[384,384]{1,0:T(8,128)(2,1)S(1)}, u32[]{:S(2)}, u32[]{:S(2)}) collective-permute-start(bf16[384,384]{1,0:T(8,128)(2,1)} %collective-permute-done.41.refs_0_), channel_id=1, source_target_pairs={{0,4},{4,0},{8,12},{12,8},{16,20},{20,16},{24,28},{28,24},{1,5},{5... | collective-permute-start | bytes 884744 | tf_op jit(solution)/shard_map/ppermute | solution.py:107
  140.0 6.4 %collective-permute-start.40 = (bf16[384,384]{1,0:T(8,128)(2,1)S(1)}, bf16[384,384]{1,0:T(8,128)(2,1)S(1)}, u32[]{:S(2)}, u32[]{:S(2)}) collective-permute-start(bf16[384,384]{1,0:T(8,128)(2,1)S(1)} %collective-permute-done.39.refs_0_), channel_id=1, source_target_pairs={{0,4},{4,0},{8,12},{12,8},{16,20},{20,16},{24,28},{28,24},{1,5},{5... | collective-permute-start | bytes 884744 | tf_op jit(solution)/shard_map/ppermute | solution.py:107
  141.1 19.6 %copy-start.21 = (bf16[384,384]{1,0:T(8,128)(2,1)S(1)}, bf16[384,384]{1,0:T(8,128)(2,1)}, u32[]{:S(2)}) copy-start(bf16[384,384]{1,0:T(8,128)(2,1)} %copy-done.20) | copy-start | bytes 884740
  141.1 19.6 %copy-start.23 = (bf16[384,384]{1,0:T(8,128)(2,1)S(1)}, bf16[384,384]{1,0:T(8,128)(2,1)}, u32[]{:S(2)}) copy-start(bf16[384,384]{1,0:T(8,128)(2,1)} %copy-done.22) | copy-start | bytes 884740
  141.9 18.3 %collective-permute-start.26 = (bf16[384,512]{1,0:T(8,128)(2,1)S(1)}, bf16[384,512]{1,0:T(8,128)(2,1)}, u32[]{:S(2)}, u32[]{:S(2)}) collective-permute-start(bf16[384,512]{1,0:T(8,128)(2,1)S(1)} %shard_map.121.refs_0_), channel_id=1, source_target_pairs={{0,16},{4,20},{8,24},{12,28},{16,0},{20,4},{24,8},{28,12},{1,17},{... | collective-permute-start | bytes 1179656 | tf_op jit(solution)/shard_map/ppermute | solution.py:94
  143.7 10.1 %collective-permute-start.36 = (bf16[384,384]{1,0:T(8,128)(2,1)}, bf16[384,384]{1,0:T(8,128)(2,1)S(1)}, u32[]{:S(2)}, u32[]{:S(2)}) collective-permute-start(bf16[384,384]{1,0:T(8,128)(2,1)} %collective-permute-done.35.refs_2_), channel_id=1, source_target_pairs={{0,8},{4,12},{8,0},{12,4},{16,24},{20,28},{24,16},{28,20},{1,9},{5... | collective-permute-start | bytes 884744 | tf_op jit(solution)/shard_map/ppermute | solution.py:94
  144.3 15.9 %collective-permute-start.33 = (bf16[384,384]{1,0:T(8,128)(2,1)S(1)}, bf16[384,384]{1,0:T(8,128)(2,1)S(1)}, u32[]{:S(2)}, u32[]{:S(2)}) collective-permute-start(bf16[384,384]{1,0:T(8,128)(2,1)S(1)} %copy-done.25), channel_id=1, source_target_pairs={{0,16},{4,20},{8,24},{12,28},{16,0},{20,4},{24,8},{28,12},{1,17},{... | collective-permute-start | bytes 884744 | tf_op jit(solution)/shard_map/ppermute | solution.py:94
  144.6 21.4 %collective-permute-start.30 = (bf16[384,384]{1,0:T(8,128)(2,1)S(1)}, bf16[384,384]{1,0:T(8,128)(2,1)S(1)}, u32[]{:S(2)}, u32[]{:S(2)}) collective-permute-start(bf16[384,384]{1,0:T(8,128)(2,1)S(1)} %collective-permute-done.29.refs_0_), channel_id=1, source_target_pairs={{0,16},{4,20},{8,24},{12,28},{16,0},{20,4},{24,8},{28,12},{1,17},{... | collective-permute-start | bytes 884744 | tf_op jit(solution)/shard_map/ppermute | solution.py:94
  146.4 14.3 %copy-start.16 = (bf16[384,384]{1,0:T(8,128)(2,1)}, bf16[384,384]{1,0:T(8,128)(2,1)S(1)}, u32[]{:S(2)}) copy-start(bf16[384,384]{1,0:T(8,128)(2,1)S(1)} %collective-permute-done.40.refs_1_) | copy-start | bytes 884740
  146.4 30.3 %collective-permute-start.44 = (bf16[384,512]{1,0:T(8,128)(2,1)S(1)}, bf16[384,512]{1,0:T(8,128)(2,1)}, u32[]{:S(2)}, u32[]{:S(2)}) collective-permute-start(bf16[384,512]{1,0:T(8,128)(2,1)S(1)} %shard_map.121.refs_0_), channel_id=1, source_target_pairs={{0,8},{4,12},{8,0},{12,4},{16,24},{20,28},{24,16},{28,20},{1,9},{5... | collective-permute-start | bytes 1179656 | tf_op jit(solution)/shard_map/ppermute | solution.py:94
  153.8 28.0 %collective-permute-start.50 = (bf16[384,512]{1,0:T(8,128)(2,1)S(1)}, bf16[384,512]{1,0:T(8,128)(2,1)S(1)}, u32[]{:S(2)}, u32[]{:S(2)}) collective-permute-start(bf16[384,512]{1,0:T(8,128)(2,1)S(1)} %shard_map.121.refs_0_), channel_id=1, source_target_pairs={{0,4},{4,0},{8,12},{12,8},{16,20},{20,16},{24,28},{28,24},{1,5},{5... | collective-permute-start | bytes 1179656 | tf_op jit(solution)/shard_map/ppermute | solution.py:107
  160.2 16.0 %collective-permute-start.22 = (bf16[64,1536]{1,0:T(8,128)(2,1)S(1)}, bf16[64,1536]{1,0:T(8,128)(2,1)S(1)}, u32[]{:S(2)}, u32[]{:S(2)}) collective-permute-start(bf16[64,1536]{1,0:T(8,128)(2,1)S(1)} %pad_maximum_fusion.1), channel_id=1, source_target_pairs={{0,4},{4,0},{8,12},{12,8},{16,20},{20,16},{24,28},{28,24},{1,5},{5... | collective-permute-start | bytes 589832 | tf_op jit(solution)/shard_map/ppermute | solution.py:465
  160.2 25.5 %collective-permute-start.27 = (bf16[384,512]{1,0:T(8,128)(2,1)}, bf16[384,512]{1,0:T(8,128)(2,1)}, u32[]{:S(2)}, u32[]{:S(2)}) collective-permute-start(bf16[384,512]{1,0:T(8,128)(2,1)} %collective-permute-done.26.refs_0_), channel_id=1, source_target_pairs={{0,8},{4,12},{8,0},{12,4},{16,24},{20,28},{24,16},{28,20},{1,9},{5... | collective-permute-start | bytes 1179656 | tf_op jit(solution)/shard_map/ppermute | solution.py:94
  166.0 15.8 %copy-start.18 = (bf16[384,384]{1,0:T(8,128)(2,1)}, bf16[384,384]{1,0:T(8,128)(2,1)S(1)}, u32[]{:S(2)}) copy-start(bf16[384,384]{1,0:T(8,128)(2,1)S(1)} %collective-permute-done.30.refs_0_) | copy-start | bytes 884740
  166.0 16.3 %collective-permute-start.37 = (bf16[384,384]{1,0:T(8,128)(2,1)S(1)}, bf16[384,384]{1,0:T(8,128)(2,1)S(1)}, u32[]{:S(2)}, u32[]{:S(2)}) collective-permute-start(bf16[384,384]{1,0:T(8,128)(2,1)S(1)} %collective-permute-done.36.refs_2_), channel_id=1, source_target_pairs={{0,4},{4,0},{8,12},{12,8},{16,20},{20,16},{24,28},{28,24},{1,5},{5... | collective-permute-start | bytes 884744 | tf_op jit(solution)/shard_map/ppermute | solution.py:107
  176.1 19.5 %collective-permute-start.34 = (bf16[384,384]{1,0:T(8,128)(2,1)S(1)}, bf16[384,384]{1,0:T(8,128)(2,1)S(1)}, u32[]{:S(2)}, u32[]{:S(2)}) collective-permute-start(bf16[384,384]{1,0:T(8,128)(2,1)S(1)} %collective-permute-done.33.refs_0_), channel_id=1, source_target_pairs={{0,4},{4,0},{8,12},{12,8},{16,20},{20,16},{24,28},{28,24},{1,5},{5... | collective-permute-start | bytes 884744 | tf_op jit(solution)/shard_map/ppermute | solution.py:107
  176.7 27.4 %collective-permute-start.45 = (bf16[384,512]{1,0:T(8,128)(2,1)}, bf16[384,512]{1,0:T(8,128)(2,1)S(1)}, u32[]{:S(2)}, u32[]{:S(2)}) collective-permute-start(bf16[384,512]{1,0:T(8,128)(2,1)} %collective-permute-done.44.refs_0_), channel_id=1, source_target_pairs={{0,4},{4,0},{8,12},{12,8},{16,20},{20,16},{24,28},{28,24},{1,5},{5... | collective-permute-start | bytes 1179656 | tf_op jit(solution)/shard_map/ppermute | solution.py:107
  181.8 18.7 %collective-permute-start.31 = (bf16[384,384]{1,0:T(8,128)(2,1)S(1)}, bf16[384,384]{1,0:T(8,128)(2,1)S(1)}, u32[]{:S(2)}, u32[]{:S(2)}) collective-permute-start(bf16[384,384]{1,0:T(8,128)(2,1)S(1)} %collective-permute-done.30.refs_0_), channel_id=1, source_target_pairs={{0,4},{4,0},{8,12},{12,8},{16,20},{20,16},{24,28},{28,24},{1,5},{5... | collective-permute-start | bytes 884744 | tf_op jit(solution)/shard_map/ppermute | solution.py:107
  182.3 26.2 %collective-permute-start.38 = (bf16[384,512]{1,0:T(8,128)(2,1)}, bf16[384,512]{1,0:T(8,128)(2,1)S(1)}, u32[]{:S(2)}, u32[]{:S(2)}) collective-permute-start(bf16[384,512]{1,0:T(8,128)(2,1)} %collective-permute-done.26.refs_0_), channel_id=1, source_target_pairs={{0,4},{4,0},{8,12},{12,8},{16,20},{20,16},{24,28},{28,24},{1,5},{5... | collective-permute-start | bytes 1179656 | tf_op jit(solution)/shard_map/ppermute | solution.py:107
  185.7 27.2 %collective-permute-start.28 = (bf16[384,512]{1,0:T(8,128)(2,1)}, bf16[384,512]{1,0:T(8,128)(2,1)}, u32[]{:S(2)}, u32[]{:S(2)}) collective-permute-start(bf16[384,512]{1,0:T(8,128)(2,1)} %collective-permute-done.27.refs_0_), channel_id=1, source_target_pairs={{0,4},{4,0},{8,12},{12,8},{16,20},{20,16},{24,28},{28,24},{1,5},{5... | collective-permute-start | bytes 1179656 | tf_op jit(solution)/shard_map/ppermute | solution.py:107
  (20 other events, 78.3 us)

commit v3 on v2

v3 whole, which is shorter than its diff:
```python
import functools

import jax
import jax.numpy as jnp
from jax import lax
from jax.experimental import pallas as pl
from jax.experimental.pallas import tpu as pltpu
from jax.sharding import PartitionSpec as P

GROUPS = 4
BF16 = jnp.bfloat16
F32 = jnp.float32
NT = (((1,), (1,)), ((), ()))
TN = (((0,), (0,)), ((), ()))
NN = (((1,), (0,)), ((), ()))


def dot(a, b, dims):
    return lax.dot_general(a, b, dims, preferred_element_type=F32)


def halves(x):
    high = x.astype(BF16)
    return high, (x - high.astype(F32)).astype(BF16)


def call(kernel, out_shape, operands, flops, exps=0, deps=(), specs=None, limit=12, **kwargs):
    count, extra = len(operands), len(deps)

    def body(*refs):
        kernel(*refs[:count], *refs[count + extra :])

    shapes = out_shape if isinstance(out_shape, (list, tuple)) else [out_shape]
    nbytes = sum(x.size * x.dtype.itemsize for x in list(operands) + list(shapes))
    kwargs.setdefault("out_specs", jax.tree.map(lambda _: VM, out_shape))
    return pl.pallas_call(
        body,
        out_shape=out_shape,
        in_specs=list(specs or [VM] * count) + [ANY] * extra,
        compiler_params=pltpu.CompilerParams(vmem_limit_bytes=limit * 1024 * 1024),
        cost_estimate=pl.CostEstimate(
            flops=int(flops), bytes_accessed=int(nbytes), transcendentals=int(exps)
        ),
        **kwargs,
    )(*operands, *deps)


VM = pl.BlockSpec(memory_space=pltpu.VMEM)
SM = pl.BlockSpec(memory_space=pltpu.SMEM)
ANY = pl.BlockSpec(memory_space=pl.ANY)


def fresh_kernel(place_ref, rate_ref, k_ref, v_ref, *outs):
    part, size = outs[0].shape[0], outs[0].shape[1]
    length = k_ref.shape[0]
    left = length - lax.broadcasted_iota(jnp.int32, (length, size), 0).astype(F32)
    for a, out_ref in enumerate(outs):
        first = lax.rem(place_ref[1] + a, len(outs)) * part
        for j in range(part):
            cols = pl.ds(pl.multiple_of((first + j) * size, size), size)
            tail = jnp.exp(-rate_ref[first + j] * left)
            high, low = halves(k_ref[:, cols].astype(F32) * tail)
            v = v_ref[:, cols]
            out_ref[j] = dot(high, v, TN) + dot(low, v, TN)


def local_kernel(rate_ref, q_ref, k_ref, v_ref, out_ref):
    heads = rate_ref.shape[0]
    length = k_ref.shape[0]
    size = k_ref.shape[1] // heads
    rows = lax.broadcasted_iota(jnp.int32, (length, length), 0)
    cols = lax.broadcasted_iota(jnp.int32, (length, length), 1)
    offset = (rows - cols).astype(F32)
    keep = offset >= 0
    offset = jnp.maximum(offset, 0.0)
    for h in range(heads):
        at = slice(h * size, (h + 1) * size)
        masked = jnp.where(keep, jnp.exp(-rate_ref[h] * offset), 0.0)
        weighted = (dot(q_ref[:, at], k_ref[:, at], NT) * masked).astype(BF16)
        out_ref[:, at] = dot(weighted, v_ref[:, at], NN)


def fade(rate_ref, head, positions):
    return jnp.exp(-(rate_ref[head] * positions) + jnp.zeros((1, 128), F32))


def pair_kernel(length, place_ref, rate_ref, mine_ref, got_ref, early_ref, total_ref):
    part = mine_ref.shape[0]
    first = place_ref[1] == 0
    for j in range(part):
        mine, got = mine_ref[j], got_ref[j]
        early = jnp.where(first, mine, got)
        early_ref[j] = early
        late = jnp.where(first, got, mine)
        total_ref[j] = fade(rate_ref, place_ref[1] * part + j, float(length)) * early + late


def scan_kernel(length, step, place_ref, rate_ref, *refs):
    old_ref = refs[0] if step > 1 else None
    total_ref, got_ref, state_ref, out_ref = refs[-4:]
    part = total_ref.shape[0]
    upper = (place_ref[0] & step) != 0
    behind = (place_ref[0] & (step - 1)).astype(F32) * (2.0 * length)
    for j in range(part):
        head = place_ref[1] * part + j
        got, total = got_ref[j], total_ref[j]
        state = jnp.where(upper, fade(rate_ref, head, behind) * got, 0.0)
        state_ref[j] = state if old_ref is None else old_ref[j] + state
        span = fade(rate_ref, head, 2.0 * length * step)
        out_ref[j] = jnp.where(upper, span * got + total, span * total + got)


def final_scan_kernel(length, step, place_ref, rate_ref, old_ref, got_ref, early_ref, keep_ref, give_ref):
    part = old_ref.shape[0]
    first = place_ref[1] == 0
    upper = (place_ref[0] & step) != 0
    behind = (place_ref[0] & (step - 1)).astype(F32) * (2.0 * length)
    for j in range(part):
        head = place_ref[1] * part + j
        state = old_ref[j] + jnp.where(upper, fade(rate_ref, head, behind) * got_ref[j], 0.0)
        late = fade(rate_ref, head, float(length)) * state + early_ref[j]
        keep_ref[j] = jnp.where(first, state, late)
        give_ref[j] = jnp.where(first, late, state)


def head_kernel(place_ref, rate_ref, q_ref, local_ref, *refs):
    states, out_ref = refs[:-1], refs[-1]
    part, size = states[0].shape[0], states[0].shape[1]
    length = q_ref.shape[0]
    pos = lax.broadcasted_iota(jnp.int32, (length, size), 0).astype(F32)
    for a, state_ref in enumerate(states):
        first = lax.rem(place_ref[1] + a, len(states)) * part
        for j in range(part):
            at = pl.ds(pl.multiple_of((first + j) * size, size), size)
            high, low = halves(state_ref[j])
            q = q_ref[:, at]
            carried = dot(q, high, NN) + dot(q, low, NN)
            carried = carried * jnp.exp(-rate_ref[first + j] * pos)
            attended = local_ref[:, at] + carried
            scale = lax.rsqrt(jnp.mean(attended * attended, axis=-1, keepdims=True) + 1e-05)
            out_ref[:, at] = (attended * scale).astype(BF16)


def xor_permute(x, step):
    n = lax.axis_size("ctx")
    return lax.ppermute(x, "ctx", [(d, d ^ step) for d in range(n)])


def within_group(x):
    n = lax.axis_size("ctx")
    low = n // GROUPS
    got = [x]
    for step in range(1, low):
        got.append(
            lax.ppermute(
                x, "ctx", [(d, d // low * low + (d % low - step) % low) for d in range(n)]
            )
        )
    return got


def in_order(pieces, first, axis):
    n, width = len(pieces), pieces[0].shape[axis]
    ring = jnp.concatenate(pieces + pieces[:-1], axis=axis)
    return lax.dynamic_slice_in_dim(ring, lax.rem(n - first, n) * width, n * width, axis)


def gather_doubling(x, axis, count, place):
    n = lax.axis_size(axis)
    step = 1
    while step < count:
        got = lax.ppermute(x, axis, [(d, d ^ step) for d in range(n)])
        upper = (place & step) != 0
        x = jnp.where(
            upper, jnp.concatenate([got, x], axis=1), jnp.concatenate([x, got], axis=1)
        )
        step *= 2
    return x


def project_kernel(low, halves_of_w, place_ref, *refs):
    heads, rests = refs[:low], refs[low + halves_of_w : 2 * low + halves_of_w]
    weights = refs[low : low + halves_of_w]
    sum_ref, sent_ref = refs[2 * low + halves_of_w :]
    length, tokens = heads[0].shape[0], rests[0].shape[0]
    for a in range(low):
        first = lax.rem(place_ref[1] + a, low) * length
        at = pl.ds(pl.multiple_of(first, length), length)
        total, start = 0.0, 0
        for w_ref in weights:
            depth = w_ref.shape[0]
            total = total + dot(heads[a][:, start : start + depth], w_ref[...], NN)
            start += depth
        sum_ref[at, :] = total
        own = pl.ds(pl.multiple_of(first + place_ref[2] * tokens, tokens), tokens)
        sum_ref[own, :] += rests[a][...].astype(F32)
        sent_ref[at, :] = sum_ref[at, :].astype(BF16)


def add_kernel(part_ref, got_ref, *outs):
    total = part_ref[...] + got_ref[...].astype(F32)
    for out_ref in outs:
        out_ref[...] = total.astype(out_ref.dtype)


def dispatch_kernel(count, others, edges, place_ref, got_ref, *refs):
    mixed, (gain_ref, picks_ref, out_ref, mixed_ref), gives = (
        refs[:count],
        refs[count : count + 4],
        refs[count + 4 :],
    )
    cols = gain_ref.shape[1]
    if edges is None:
        mixed_ref[...] = mixed[-1][...]
    else:
        outer = (place_ref[2] == edges[0]) | (place_ref[2] == edges[1])
        mixed_ref[...] = jnp.where(outer, got_ref[...], mixed[-1][...])
    value = mixed_ref[...].astype(F32)
    rows = (value * gain_ref[...]).astype(BF16)
    out_ref[:, :cols] = dot(picks_ref[...], rows, NN).astype(BF16)
    if count == 1:
        return
    mixed = list(mixed[:-1]) + [mixed_ref]
    squares = jnp.sum(value * value, axis=1, keepdims=True)
    for ref in mixed[:-1]:
        value = ref[...].astype(F32)
        squares = squares + jnp.sum(value * value, axis=1, keepdims=True)
    lane = lax.broadcasted_iota(jnp.int32, (squares.shape[0], 128), 1)
    rest, extra = squares, jnp.zeros((squares.shape[0], 128), F32)
    for place in range(3):
        high = rest.astype(BF16).astype(F32)
        extra = jnp.where(lane == place, high, extra)
        rest = rest - high
    extra = dot(picks_ref[...], extra.astype(BF16), NN).astype(BF16)
    out_ref[:, out_ref.shape[1] - 128 :] = extra
    for a, give_ref in enumerate(gives, 1):
        tokens = give_ref.shape[0]
        first = lax.rem(place_ref[1] + a, others + 1) * (mixed_ref.shape[0] // (others + 1))
        rows = pl.ds(pl.multiple_of(first + place_ref[2] * tokens, tokens), tokens)
        for t, ref in enumerate(mixed):
            give_ref[:, t * cols : (t + 1) * cols] = ref[rows, :]


def mixed_kernel(low, place_ref, *refs):
    out_ref = refs[-1]
    cols = refs[0].shape[1]
    tokens = out_ref.shape[0]
    length = refs[0].shape[0] // low
    for t in range(GROUPS):
        block = (place_ref[0] ^ t) * low
        own = pl.ds(pl.multiple_of(place_ref[1] * length + place_ref[2] * tokens, tokens), tokens)
        at = pl.multiple_of((block + place_ref[1]) * cols, cols)
        out_ref[:, pl.ds(at, cols)] = refs[t][own, :]
        for a in range(1, low):
            at = pl.multiple_of((block + lax.rem(place_ref[1] + a, low)) * cols, cols)
            got = refs[GROUPS + a - 1]
            out_ref[:, pl.ds(at, cols)] = got[:, t * cols : (t + 1) * cols]


def expert_kernel(t, spans, count, mode, model, place_ref, gate_ref, up_ref, *refs):
    refs = list(refs)
    pieces = [[refs.pop(0) for _ in range(count)] for _ in spans]
    sums = [[refs.pop(0), refs.pop(0)] for _ in spans] if t > 0 else None
    if mode == "next":
        refs.pop(0)
    outs, scratch = (refs[0], refs[1:]) if mode else (refs[: 2 * len(spans)], refs[2 * len(spans) :])
    width = scratch[0].shape[2]
    part = width // count
    copies = []
    for n, s in enumerate(spans):
        extras, held = [], scratch[0].at[n]
        for a, piece in enumerate(pieces[n]):
            member = lax.rem(place_ref[1] + a, count) if count > 1 else 0
            at = pl.multiple_of(member * part, part) if count > 1 else 0
            held[:, pl.ds(at, part)] = piece[:, :part]
            if mode:
                extras.append(piece[:, part:])
        x = held[...]
        cols = pl.ds(pl.multiple_of((place_ref[0] ^ (s ^ t)) * width, width), width)
        gated = dot(gate_ref[:, cols], x, NT)
        lifted = dot(up_ref[:, cols], x, NT)
        if sums is not None:
            gated = gated + sums[n][0][...]
            lifted = lifted + sums[n][1][...]
        if mode is None:
            outs[2 * n][...] = gated
            outs[2 * n + 1][...] = lifted
            continue
        squares = 0.0
        for extra in extras:
            lane = lax.broadcasted_iota(jnp.int32, (8, extra.shape[1]), 1)
            squares = squares + dot((lax.rem(lane, 128) < 3).astype(BF16), extra, NT)[0:1, :]
        scale = lax.rsqrt(squares / model + 1e-05)
        gated, lifted = gated * scale, lifted * scale
        ready, sems = scratch[1], scratch[2]
        ready[n] = (gated / (1.0 + jnp.exp(-gated)) * lifted).astype(BF16)
        slots = ready.shape[2]
        at = pl.ds(pl.multiple_of((place_ref[0] ^ s) * slots, slots), slots)
        copies.append(pltpu.make_async_copy(ready.at[n], outs.at[:, at], sems.at[n]))
        copies[-1].start()
    for copy in copies:
        copy.wait()


def expert_step(place, t, spans, pieces, gate, up, sums, hidden, final, deps):
    hid, model = gate.shape
    count, slots = len(pieces[0]), pieces[0][0].shape[0]
    width = model // GROUPS
    operands = [place, gate, up] + [x for per in pieces for x in per]
    if t > 0:
        operands += [x for s in spans for x in sums[s]]
    specs = [SM] + [VM] * (len(operands) - 1)
    scratch = [pltpu.VMEM((len(spans), slots, width), BF16)]
    kwargs, mode = {}, None
    if final:
        mode = "first" if hidden is None else "next"
        if hidden is not None:
            kwargs["input_output_aliases"] = {len(operands): 0}
            operands.append(hidden)
            specs.append(ANY)
        out_shape = jax.ShapeDtypeStruct((hid, slots * GROUPS), BF16)
        kwargs["out_specs"] = ANY
        scratch += [
            pltpu.VMEM((len(spans), hid, slots), BF16),
            pltpu.SemaphoreType.DMA((len(spans),)),
        ]
    else:
        out_shape = [jax.ShapeDtypeStruct((hid, slots), F32)] * (2 * len(spans))
    return call(
        functools.partial(expert_kernel, t, spans, count, mode, model),
        out_shape,
        operands,
        4 * hid * slots * width * len(spans),
        hid * slots * len(spans) if final else 0,
        deps,
        specs,
        20,
        scratch_shapes=scratch,
        **kwargs,
    )


def exchange_states(place, rate, mine, theirs, length, deps_one, deps_two):
    like = jax.ShapeDtypeStruct(mine.shape, F32)
    got = xor_permute(theirs, 1)
    early, total = call(
        functools.partial(pair_kernel, length), [like] * 2, [place, rate, mine, got], 0,
        specs=[SM, SM, VM, VM],
    )
    marks = [total]
    state, step = [], 1
    while 2 * step < GROUPS:
        got = xor_permute(total, 2 * step)
        state, total = call(
            functools.partial(scan_kernel, length, step),
            [like] * 2,
            [place, rate] + ([state] if step > 1 else []) + [total, got],
            0,
            deps=deps_one(marks[-1]),
            specs=[SM, SM] + [VM] * (3 if step > 1 else 2),
        )
        marks.append(total)
        step *= 2
    got = lax.ppermute(total, "ctx", [(d, d + 2 * step) for d in range(2 * step)])
    keep, give = call(
        functools.partial(final_scan_kernel, length, step),
        [like] * 2,
        [place, rate, state, got, early],
        0,
        deps=deps_two(marks[-1]),
        specs=[SM, SM, VM, VM, VM],
    )
    return [keep, xor_permute(give, 1)], keep


def states_by_steps(ctx, decay_rate, total, length):
    n_ctx = lax.axis_size("ctx")

    def faded(blocks):
        return jnp.exp(-decay_rate * (length * blocks))[:, None, None]

    state, step = jnp.zeros_like(total), 1
    while step < n_ctx:
        upper = (ctx & step) != 0
        got = xor_permute(total, step)
        state = state + jnp.where(upper, faded((ctx & (step - 1)).astype(F32)), 0.0) * got
        span = faded(float(step))
        total = jnp.where(upper, span * got + total, span * total + got)
        step *= 2
    return [state]


def tie(x, *deps):
    return call(
        lambda i, o: None, jax.ShapeDtypeStruct(x.shape, x.dtype), [x], 0,
        deps=deps, specs=[ANY], out_specs=ANY, input_output_aliases={0: 0},
    )


def per_device(
    queries,
    key_rows,
    value_rows,
    decay_rate,
    out_weight,
    residual,
    moe_gain,
    expert_ids,
    gate_weight,
    up_weight,
):
    n_ctx, n_exp = lax.axis_size("ctx"), lax.axis_size("exp")
    low = n_ctx // GROUPS
    ctx, exp = lax.axis_index("ctx"), lax.axis_index("exp")
    group, member = ctx // low, lax.rem(ctx, low)
    place = jnp.stack([group, member, exp]).astype(jnp.int32)
    length, here = queries.shape
    heads = decay_rate.shape[0]
    size = here // heads
    model = residual.shape[1]
    cols = model // n_ctx
    tokens = length // n_exp
    capacity = max(2, 3 * tokens // n_exp)
    aligned = cols % 128 == 0
    pairs = low == 2 and heads % 2 == 0
    every = low * length
    slots = low * n_exp * capacity

    cut = out_weight.shape[0] // 2
    w_top, w_bottom = out_weight[:cut], out_weight[cut:]
    two_top, two_bottom = xor_permute(w_top, 2 * low), xor_permute(w_bottom, 2 * low)
    one_top = xor_permute(w_top, low)
    ids = expert_ids.T

    fresh = call(
        fresh_kernel,
        [jax.ShapeDtypeStruct((heads // 2, size, size), F32)] * 2
        if pairs
        else [jax.ShapeDtypeStruct((heads, size, size), F32)],
        [place, decay_rate, key_rows, value_rows],
        4 * heads * length * size * size,
        heads * length * size,
        specs=[SM, SM, VM, VM],
    )

    def run_local(*deps):
        return call(
            local_kernel,
            jax.ShapeDtypeStruct((length, here), F32),
            [decay_rate, queries, key_rows, value_rows],
            4 * heads * length * length * size,
            heads * length * length,
            deps,
            [SM, VM, VM, VM],
        )

    if pairs:
        side = {}

        def deps_one(total):
            side["ids"] = gather_doubling(ids, "exp", n_exp, exp)
            side["local"] = run_local(total)
            side["rest"] = within_group(residual)
            return [side["local"], one_top, side["rest"][1]]

        def deps_two(total):
            side["one_bottom"] = xor_permute(tie(w_bottom, total), low)
            return [side["ids"], two_top, two_bottom]

        states, kept = exchange_states(
            place, decay_rate, fresh[0], fresh[1], length, deps_one, deps_two
        )
        ids, local, rest_rows, one_bottom = (
            side["ids"], side["local"], side["rest"], side["one_bottom"]
        )
        ids = gather_doubling(tie(ids, kept), "ctx", low, member)
        three_top = xor_permute(tie(one_top, kept), 2 * low)
        deps = [ids, one_bottom]
    else:
        states = states_by_steps(ctx, decay_rate, fresh[0], length)
        local, rest_rows = run_local(), within_group(residual)
        ids = gather_doubling(gather_doubling(ids, "exp", n_exp, exp), "ctx", low, member)
        one_bottom = xor_permute(w_bottom, low)
        three_top = xor_permute(one_top, 2 * low)
        deps = []

    head_out = call(
        head_kernel,
        jax.ShapeDtypeStruct((length, here), BF16),
        [place, decay_rate, queries, local] + states,
        4 * heads * length * size * size,
        heads * length * size,
        deps,
        [SM, SM] + [VM] * (2 + len(states)),
    )
    group_heads = within_group(head_out)
    three_bottom = xor_permute(tie(two_bottom, head_out), low)
    columns = [
        [out_weight], [one_top, one_bottom], [two_top, two_bottom], [three_top, three_bottom]
    ]

    named = (ids[0] == exp) | (ids[1] == exp)
    token = jnp.arange(every, dtype=jnp.int32)
    earlier = (token[:, None] < token[None, :]) & (
        token[:, None] // tokens == token[None, :] // tokens
    )
    rank = jnp.sum((earlier & named[:, None]).astype(jnp.int32), axis=0)
    row = jnp.where(named & (rank < capacity), token // tokens * capacity + rank, -1)
    picks = (jnp.arange(slots, dtype=jnp.int32)[:, None] == row[None, :]).astype(BF16)

    gains, rests = [], []
    for t in range(GROUPS):
        start = (((group ^ t) * low + member) * cols).astype(jnp.int32)
        gains.append(lax.dynamic_slice(moe_gain, (start,), (cols,))[None])
        rests.append(
            [lax.dynamic_slice(r, (jnp.int32(0), start), (tokens, cols)) for r in rest_rows]
        )
    gate, up = gate_weight[0], up_weight[0]

    chunk_f32 = jax.ShapeDtypeStruct((every, cols), F32)
    chunk_b16 = jax.ShapeDtypeStruct((every, cols), BF16)
    half = n_exp // 2
    mixed, received = [None] * GROUPS, [None] * GROUPS
    sums, gives, hidden = [None] * GROUPS, [], None
    links, last = [None] * GROUPS, [head_out]

    def chunk(t):
        final = t == GROUPS - 1
        part, sent = call(
            functools.partial(project_kernel, low, len(columns[t])),
            [chunk_f32, chunk_b16],
            [place] + group_heads + columns[t] + rests[t],
            2 * every * here * cols,
            deps=last[:],
            specs=[SM] + [VM] * (2 * low + len(columns[t])),
        )
        last[:] = [sent]
        for hop in range(half - 1):
            got = lax.ppermute(sent, "exp", [(hop, hop + 1), (n_exp - 1 - hop, n_exp - 2 - hop)])
            yield
            part, sent = call(
                add_kernel, [chunk_f32, chunk_b16], [part, got], every * cols, deps=last[:]
            )
            last[:] = [sent]
        got = lax.ppermute(sent, "exp", [(half - 1, half), (half, half - 1)])
        yield
        total = call(add_kernel, chunk_b16, [part, got], every * cols, deps=last[:])
        last[:] = [total]
        edges = None
        for hop in range(half - 1):
            if edges is not None:
                total = jnp.where((exp == edges[0]) | (exp == edges[1]), got, total)
            here_, there = half - 1 - hop, half + hop
            got = lax.ppermute(total, "exp", [(here_, here_ - 1), (there, there + 1)])
            edges = (here_ - 1, there + 1)
            yield
        wide = (cols + 127) // 128 * 128 + 128 if final else cols
        known = mixed[:t] if final else []
        outs = [jax.ShapeDtypeStruct((slots, wide), BF16), chunk_b16]
        if final and aligned:
            outs += [jax.ShapeDtypeStruct((tokens, GROUPS * cols), BF16)] * (low - 1)
        x, mixed[t], *gives[:] = call(
            functools.partial(dispatch_kernel, len(known) + 1, low - 1, edges),
            outs,
            [place, got] + known + [total, gains[t], picks],
            2 * slots * every * wide,
            deps=last[:] + (links[t - 1] or [] if t > 0 else []),
            specs=[SM] + [VM] * (len(known) + 4),
        )
        last[:] = [x]
        one, two = xor_permute(x, low), xor_permute(x, 2 * low)
        got = [within_group(x)]
        links[t] = [one, two]
        yield
        three = xor_permute(one, 2 * low) if t % 2 == 0 else xor_permute(two, low)
        got += [within_group(one), within_group(two)]
        if final:
            last[:] = last[:] + [one, two]
        yield
        got += [within_group(three)]
        if final:
            last[:] = last[:] + [three]
        if not aligned:
            joined = []
            for per in got:
                whole = in_order([y[:, :cols] for y in per], member, 1)
                if final:
                    whole = jnp.concatenate([whole] + [y[:, wide - 128 :] for y in per], axis=1)
                joined.append([whole])
            got = joined
        received[t] = got
        yield

    def experts(t, spans):
        nonlocal hidden
        final = t == GROUPS - 1
        pieces = [received[t][s] for s in spans]
        out = expert_step(
            place, t, spans, pieces, gate, up, sums, hidden, final, last[:]
        )
        if final:
            hidden = out
            last[:] = []
        else:
            for n, s in enumerate(spans):
                sums[s] = out[2 * n : 2 * n + 2]
            last[:] = [out[0]]

    running, waiting = [], list(range(GROUPS))
    everyone = list(range(GROUPS))
    done = []
    while running or waiting:
        if waiting:
            running.insert(0, (waiting[0], chunk(waiting.pop(0))))
        for t, work in list(running):
            if next(work, "end") == "end":
                running.remove((t, work))
                if t < GROUPS - 1:
                    experts(t, everyone)

    own = exp * tokens
    gotten = []
    for a in range(1, low):
        if aligned:
            give = gives[a - 1]
        else:
            first = lax.rem(member + a, low) * length + own
            rows = [lax.dynamic_slice_in_dim(m, first, tokens, 0) for m in mixed]
            give = jnp.concatenate(rows, axis=1)
        gotten.append(
            lax.ppermute(
                give, "ctx", [(d, d // low * low + (d % low + a) % low) for d in range(n_ctx)]
            )
        )
    gotten = gotten[::-1]
    if aligned:
        mixed_out = call(
            functools.partial(mixed_kernel, low),
            jax.ShapeDtypeStruct((tokens, model), BF16),
            [place] + mixed + gotten,
            0,
            deps=last[:],
            specs=[SM] + [VM] * (GROUPS + low - 1),
        )
        last[:] = [mixed_out]
    else:
        rows = [lax.dynamic_slice_in_dim(m, member * length + own, tokens, 0) for m in mixed]
        parts = [jnp.concatenate(rows, axis=1)] + gotten
        mixed_out = jnp.zeros((tokens, model), BF16)
        for a, part in enumerate(parts):
            for t in range(GROUPS):
                start = ((group ^ t) * low + lax.rem(member + a, low)) * cols
                mixed_out = lax.dynamic_update_slice_in_dim(
                    mixed_out, part[:, t * cols : (t + 1) * cols], start, 1
                )
    experts(GROUPS - 1, everyone[:-1])
    experts(GROUPS - 1, everyone[-1:])
    return (mixed_out, hidden[None])


def solution(mesh):
    in_specs = (
        P("ctx", "exp"),
        P("ctx", "exp"),
        P("ctx", "exp"),
        P("exp"),
        P("exp", "ctx"),
        P(("ctx", "exp"), None),
        P(),
        P(("ctx", "exp"), None),
        P("exp", "ctx", None),
        P("exp", "ctx", None),
    )
    out_specs = (P(("ctx", "exp"), None), P("exp", "ctx", None))
    return jax.shard_map(
        per_device, mesh=mesh, in_specs=in_specs, out_specs=out_specs, check_vma=False
    )
```

time: 218 us -> 170 us (0.78)
  waiting for transfers between devices: 81.3 us -> 55.4 us
  Pallas kernels: 63.1 us -> 42.6 us
  local copies, waits for them, and re-layouts: 5.71 us -> 16.9 us
  starting transfers between devices: 61.9 us -> 52.5 us
  other arithmetic: 3.93 us -> 0.52 us
    ppermute x14, waiting for transfers between devices: 36.6 us -> 15.6 us  [the longest x4 9.42 us: chunk(): got = lax.ppermute(total, 'exp', [(here_, here_ - 1), (there, there + 1)])]
    pallas_call x24 -> x32, Pallas kernels: 63.1 us -> 42.6 us  [call(): pl.pallas_call(body, out_shape=out_shape, in_specs=list(specs or [VM] * c...]
    ppermute x19 -> x21, starting transfers between devices: 30.3 us -> 15.1 us  [xor_permute(): return lax.ppermute(x, 'ctx', [(d, d ^ step) for d in range(n)])]
    ppermute x19 -> x21, waiting for transfers between devices: 44 us -> 35.9 us  [xor_permute(): return lax.ppermute(x, 'ctx', [(d, d ^ step) for d in range(n)])]
    unnamed x60 -> x48, local copies, waits for them, and re-layouts: 5.44 us -> 12.9 us
    ppermute x14, starting transfers between devices: 23.6 us -> 30.3 us  [the longest x4 17.8 us: chunk(): lax.ppermute(sent, 'exp', [(hop, hop + 1), (n_exp - 1 - hop, n_exp - 2 -...]
    ppermute x3, waiting for transfers between devices: 0.57 us -> 3.2 us  [gather_doubling(): got = lax.ppermute(x, axis, [(d, d ^ step) for d in range(n)])]
  transfers between devices with their start and end apart: 54 -> 56, of which waited for: 19 -> 19; matrix products, arithmetic and copies ran while one was open for 2% -> 3% of each run, Pallas kernels for 26% -> 21%
where the time goes in v3:
time: 170 us; the launch traced here: 169 us
  waiting for transfers between devices  55.4 us (33%)
  starting transfers between devices  52.5 us (31%)
  Pallas kernels  42.6 us (25%)
  local copies, waits for them, and re-layouts  16.9 us (10%)
    pallas_call x32, Pallas kernels, call(): pl.pallas_call(body, out_shape=out_shape, in_specs=list(specs or [VM] * c...  42.6 us
    ppermute x21, waiting for transfers between devices, xor_permute(): return lax.ppermute(x, 'ctx', [(d, d ^ step) for d in range(n)])  35.9 us
    ppermute x4, starting transfers between devices, chunk(): lax.ppermute(sent, 'exp', [(hop, hop + 1), (n_exp - 1 - hop, n_exp - 2 -...  17.8 us
    ppermute x21, starting transfers between devices, xor_permute(): return lax.ppermute(x, 'ctx', [(d, d ^ step) for d in range(n)])  15.1 us
    unnamed x48, local copies, waits for them, and re-layouts  12.9 us
    ppermute x4, waiting for transfers between devices, chunk(): got = lax.ppermute(total, 'exp', [(here_, here_ - 1), (there, there + 1)])  9.42 us
    ppermute x4, waiting for transfers between devices, chunk(): lax.ppermute(sent, 'exp', [(hop, hop + 1), (n_exp - 1 - hop, n_exp - 2 -...  6.15 us
    ppermute x4, starting transfers between devices, chunk(): got = lax.ppermute(total, 'exp', [(here_, here_ - 1), (there, there + 1)])  5.61 us
  transfers between devices with their start and end apart: 56, of which 19 were waited for; matrix products, arithmetic and copies ran while one was open for 3% of the time, Pallas kernels for 21%

profile of v3, /device:TPU:0, one launch (start us, length us, event | category | flops | bytes accessed | tf_op | source)
XLA Modules:
  0.0 169.2 jit_solution(3314031995918226083)
XLA Ops:
  0.7 1.0 copy-done.3
  1.8 1.0 copy-done.5
  3.5 1.1 shard_map.113
  5.1 2.1 %fusion.9 = (bf16[512,384]{1,0:T(8,128)(2,1)}, bf16[512,384]{1,0:T(8,128)(2,1)}) fusion(bf16[1024,384]{1,0:T(8,128)(2,1)} %refs_3_.5), kind=kLoop, calls=%fused_computation.34 | loop fusion | bytes 1572864 | tf_op jit(solution)/shard_map/slice | solution.py:430
  7.2 2.5 %collective-permute-start.2 = (bf16[512,384]{1,0:T(8,128)(2,1)}, bf16[512,384]{1,0:T(8,128)(2,1)S(1)}, u32[]{:S(2)}, u32[]{:S(2)}) collective-permute-start(bf16[512,384]{1,0:T(8,128)(2,1)} %get-tuple-element.119), channel_id=1, source_target_pairs={{0,8},{4,12},{8,0},{12,4},{16,24},{20,28},{24,16},{28,20},{1,9},{5... | collective-permute-start | bytes 1179656 | tf_op jit(solution)/shard_map/ppermute | solution.py:146
  9.9 1.5 collective-permute-start.8
  13.6 1.0 copy-done.4
  14.6 1.0 copy-done.6
  15.6 1.0 copy-done.7
  16.7 1.5 shard_map.115.refs_4_.refs_3_
  18.2 1.6 collective-permute-done.2.refs_5_.refs_3_.refs_0_
  19.9 5.4 %collective-permute-done.1.refs_3_ = f32[4,128,128]{2,1,0:T(8,128)S(1)} collective-permute-done((f32[4,128,128]{2,1,0:T(8,128)S(1)}, f32[4,128,128]{2,1,0:T(8,128)S(1)}, u32[]{:S(2)}, u32[]{:S(2)}) %collective-permute-start.1) | collective-permute-done | bytes 262176 | tf_op jit(solution)/shard_map/ppermute | solution.py:146
  25.3 1.3 shard_map.116
  27.3 3.8 %collective-permute-start.4 = (f32[4,128,128]{2,1,0:T(8,128)}, f32[4,128,128]{2,1,0:T(8,128)S(1)}, u32[]{:S(2)}, u32[]{:S(2)}) collective-permute-start(f32[4,128,128]{2,1,0:T(8,128)} %get-tuple-element.63.refs_1_), channel_id=1, source_target_pairs={{0,16},{4,20},{8,24},{12,28},{1,17},{5,21},{9,25},{13,29},{2,18},{... | collective-permute-start | bytes 786440 | tf_op jit(solution)/shard_map/ppermute | solution.py:364
  31.2 1.6 collective-permute-start.5
  32.8 1.5 collective-permute-start.11
  34.9 2.6 %collective-permute-start.6 = (s32[2,128]{1,0:T(2,128)S(1)}, s32[2,128]{1,0:T(2,128)S(1)}, u32[]{:S(2)}, u32[]{:S(2)}) collective-permute-start(s32[2,128]{1,0:T(2,128)S(1)} %add_select_fusion.3), channel_id=1, source_target_pairs={{0,2},{1,3},{2,0},{3,1},{4,6},{5,7},{6,4},{7,5},{8,10},{9,11},{10,... | collective-permute-start | bytes 3080 | tf_op jit(solution)/shard_map/ppermute | solution.py:172
  37.5 1.9 %collective-permute-done.6 = s32[2,128]{1,0:T(2,128)S(1)} collective-permute-done((s32[2,128]{1,0:T(2,128)S(1)}, s32[2,128]{1,0:T(2,128)S(1)}, u32[]{:S(2)}, u32[]{:S(2)}) %collective-permute-start.6) | collective-permute-done | bytes 1056 | tf_op jit(solution)/shard_map/ppermute | solution.py:172
  40.1 0.9 copy-done.14
  41.1 0.9 copy-done.16
  42.0 0.9 copy-done.18
  43.0 1.3 shard_map.117
  46.2 1.0 copy-done.8
  47.2 1.6 shard_map.120.refs_1_.refs_6_
  49.1 0.9 constant_dynamic-slice_fusion.1
  50.0 0.9 constant_dynamic-slice_fusion
  50.9 1.3 shard_map.121
  52.2 3.5 %collective-permute-start.13 = (bf16[512,384]{1,0:T(8,128)(2,1)S(1)}, bf16[512,384]{1,0:T(8,128)(2,1)S(1)}, u32[]{:S(2)}, u32[]{:S(2)}) collective-permute-start(bf16[512,384]{1,0:T(8,128)(2,1)S(1)} %get-tuple-element.68.refs_7_), channel_id=1, source_target_pairs={{0,1},{3,2},{4,5},{7,6},{8,9},{11,10},{12,13},{15,14},{16,17},{19,... | collective-permute-start | bytes 1179656 | tf_op jit(solution)/shard_map/ppermute | solution.py:539
  55.7 1.7 %shard_map.122 = (f32[512,384]{1,0:T(8,128)S(1)}, bf16[512,384]{1,0:T(8,128)(2,1)S(1)}) custom-call(s32[3]{0:T(128)S(1)} %pad_add_fusion.refs_0_, bf16[256,1024]{1,0:T(8,128)(2,1)S(1)} %shard_map.120.refs_1_.refs_6_, bf16[256,1024]{1,0:T(8,128)(2,1)S(1)} %collective-permute-done.12.refs_2_, ...), custom_call_target="tpu_custom_call" | custom-call | flops 402653184 | bytes 3112972 | tf_op jit(solution)/shard_map/pallas_call | solution.py:36
  57.5 1.3 collective-permute-start.15
  59.0 6.1 %collective-permute-done.13.refs_1_ = bf16[512,384]{1,0:T(8,128)(2,1)S(1)} collective-permute-done((bf16[512,384]{1,0:T(8,128)(2,1)S(1)}, bf16[512,384]{1,0:T(8,128)(2,1)S(1)}, u32[]{:S(2)}, u32[]{:S(2)}) %collective-permute-start.13) | collective-permute-done | bytes 393248 | tf_op jit(solution)/shard_map/ppermute | solution.py:539
  66.0 1.3 shard_map.124
  67.3 1.6 collective-permute-start.20
  68.9 7.2 %collective-permute-start.18 = (bf16[512,384]{1,0:T(8,128)(2,1)S(1)}, bf16[512,384]{1,0:T(8,128)(2,1)S(1)}, u32[]{:S(2)}, u32[]{:S(2)}) collective-permute-start(bf16[512,384]{1,0:T(8,128)(2,1)S(1)} %get-tuple-element.73.refs_2_), channel_id=1, source_target_pairs={{0,1},{3,2},{4,5},{7,6},{8,9},{11,10},{12,13},{15,14},{16,17},{19,... | collective-permute-start | bytes 1179656 | tf_op jit(solution)/shard_map/ppermute | solution.py:539
  77.2 1.3 collective-permute-start.16
  78.6 1.3 shard_map.129
  79.9 5.7 %collective-permute-start.23 = (bf16[512,384]{1,0:T(8,128)(2,1)S(1)}, bf16[512,384]{1,0:T(8,128)(2,1)S(1)}, u32[]{:S(2)}, u32[]{:S(2)}) collective-permute-start(bf16[512,384]{1,0:T(8,128)(2,1)S(1)} %get-tuple-element.77.refs_2_), channel_id=1, source_target_pairs={{0,1},{3,2},{4,5},{7,6},{8,9},{11,10},{12,13},{15,14},{16,17},{19,... | collective-permute-start | bytes 1179656 | tf_op jit(solution)/shard_map/ppermute | solution.py:539
  86.6 1.3 collective-permute-start.21
  88.0 1.5 collective-permute-done.16.refs_1_
  89.5 1.0 shard_map.132
  90.5 1.6 collective-permute-start.24
  93.0 1.3 collective-permute-start.26
  94.3 5.0 %collective-permute-done.21.refs_1_ = bf16[512,384]{1,0:T(8,128)(2,1)S(1)} collective-permute-done((bf16[512,384]{1,0:T(8,128)(2,1)S(1)}, bf16[512,384]{1,0:T(8,128)(2,1)S(1)}, u32[]{:S(2)}, u32[]{:S(2)}) %collective-permute-start.21) | collective-permute-done | bytes 393248 | tf_op jit(solution)/shard_map/ppermute | solution.py:554
  99.3 1.0 shard_map.135
  100.3 1.1 collective-permute-start.28
  101.5 1.7 %collective-permute-start.30 = (bf16[512,384]{1,0:T(8,128)(2,1)S(1)}, bf16[512,384]{1,0:T(8,128)(2,1)S(1)}, u32[]{:S(2)}, u32[]{:S(2)}) collective-permute-start(bf16[512,384]{1,0:T(8,128)(2,1)S(1)} %shard_map.136.refs_5_), channel_id=1, source_target_pairs={{1,0},{2,3},{5,4},{6,7},{9,8},{10,11},{13,12},{14,15},{17,16},{18,... | collective-permute-start | bytes 1179656 | tf_op jit(solution)/shard_map/ppermute | solution.py:554
  103.3 2.9 %collective-permute-done.26.refs_1_ = bf16[512,384]{1,0:T(8,128)(2,1)S(1)} collective-permute-done((bf16[512,384]{1,0:T(8,128)(2,1)S(1)}, bf16[512,384]{1,0:T(8,128)(2,1)S(1)}, u32[]{:S(2)}, u32[]{:S(2)}) %collective-permute-start.26) | collective-permute-done | bytes 393248 | tf_op jit(solution)/shard_map/ppermute | solution.py:554
  107.1 2.4 %collective-permute-done.29.refs_7_ = bf16[384,384]{1,0:T(8,128)(2,1)S(1)} collective-permute-done((bf16[384,384]{1,0:T(8,128)(2,1)S(1)}, bf16[384,384]{1,0:T(8,128)(2,1)S(1)}, u32[]{:S(2)}, u32[]{:S(2)}) %collective-permute-start.29) | collective-permute-done | bytes 294944 | tf_op jit(solution)/shard_map/ppermute | solution.py:146
  109.5 1.0 shard_map.137
  111.2 3.3 %collective-permute-done.47.refs_9_ = bf16[384,384]{1,0:T(8,128)(2,1)S(1)} collective-permute-done((bf16[384,384]{1,0:T(8,128)(2,1)S(1)}, bf16[384,384]{1,0:T(8,128)(2,1)S(1)}, u32[]{:S(2)}, u32[]{:S(2)}) %collective-permute-start.47) | collective-permute-done | bytes 294944 | tf_op jit(solution)/shard_map/ppermute | solution.py:146
  115.3 1.0 collective-permute-start.42
  116.3 4.0 %collective-permute-done.31.refs_9_.refs_5_ = bf16[384,384]{1,0:T(8,128)(2,1)S(1)} collective-permute-done((bf16[384,384]{1,0:T(8,128)(2,1)S(1)}, bf16[384,384]{1,0:T(8,128)(2,1)S(1)}, u32[]{:S(2)}, u32[]{:S(2)}) %collective-permute-start.31) | collective-permute-done | bytes 294944 | tf_op jit(solution)/shard_map/ppermute | solution.py:146
  120.3 1.5 collective-permute-done.32.refs_10_.refs_7_
  121.8 1.4 shard_map.138
  123.8 2.4 %collective-permute-done.42.refs_9_ = bf16[384,384]{1,0:T(8,128)(2,1)S(1)} collective-permute-done((bf16[384,384]{1,0:T(8,128)(2,1)S(1)}, bf16[384,384]{1,0:T(8,128)(2,1)S(1)}, u32[]{:S(2)}, u32[]{:S(2)}) %collective-permute-start.42) | collective-permute-done | bytes 294944 | tf_op jit(solution)/shard_map/ppermute | solution.py:146
  128.0 13.1 %collective-permute-done.37.refs_9_ = bf16[384,384]{1,0:T(8,128)(2,1)S(1)} collective-permute-done((bf16[384,384]{1,0:T(8,128)(2,1)S(1)}, bf16[384,384]{1,0:T(8,128)(2,1)S(1)}, u32[]{:S(2)}, u32[]{:S(2)}) %collective-permute-start.37) | collective-permute-done | bytes 294944 | tf_op jit(solution)/shard_map/ppermute | solution.py:146
  141.5 4.5 %shard_map.139 = (f32[576,384]{1,0:T(8,128)S(1)}, f32[576,384]{1,0:T(8,128)S(1)}, f32[576,384]{1,0:T(8,128)S(1)}, f32[576,384]{1,0:T(8,128)S(1)}, f32[576,384]{1...) custom-call(s32[3]{0:T(128)S(1)} %pad_add_fusion.refs_0_, ...), custom_call_target="tpu_custom_call" | custom-call | flops 2717908992 | bytes 16515084 | tf_op jit(solution)/shard_map/pallas_call | solution.py:36
  146.8 4.5 %shard_map.140 = (f32[576,384]{1,0:T(8,128)S(1)}, f32[576,384]{1,0:T(8,128)S(1)}, f32[576,384]{1,0:T(8,128)S(1)}, f32[576,384]{1,0:T(8,128)S(1)}, f32[576,384]{1...) custom-call(s32[3]{0:T(128)S(1)} %pad_add_fusion.refs_0_, ...), custom_call_target="tpu_custom_call" | custom-call | flops 2717908992 | bytes 23592972 | tf_op jit(solution)/shard_map/pallas_call | solution.py:36
  151.7 0.9 collective-permute-done.51.refs_20_.refs_3_
  152.6 4.5 %shard_map.141 = (f32[576,384]{1,0:T(8,128)S(1)}, f32[576,384]{1,0:T(8,128)S(1)}, f32[576,384]{1,0:T(8,128)S(1)}, f32[576,384]{1,0:T(8,128)S(1)}, f32[576,384]{1...) custom-call(s32[3]{0:T(128)S(1)} %pad_add_fusion.refs_0_, ...), custom_call_target="tpu_custom_call" | custom-call | flops 2717908992 | bytes 23592972 | tf_op jit(solution)/shard_map/pallas_call | solution.py:36
  157.2 1.3 shard_map.142.refs_15_
  158.5 1.0 copy-done.11
  159.5 6.5 %shard_map.143.refs_7_ = bf16[576,1536]{1,0:T(8,128)(2,1)} custom-call(s32[3]{0:T(128)S(1)} %pad_add_fusion.refs_0_, bf16[576,3072]{1,0:T(8,128)(2,1)S(1)} %bitcast.12, bf16[576,3072]{1,0:T(8,128)(2,1)S(1)} %bitcast.17, bf16[384,512]{1,0:T(8,128)(2,1)S(1)} %get-tuple-element.91.refs_11_.refs_3_, bf16[384,512]{1,0:T(8,128)(2,1)S(1)} %collective-permute-done.53.refs_4_, ...), custom_call_target="tpu_custom_call" | custom-call | flops 2038431744 | bytes 16515084 | tf_op jit(solution)/shard_map/pallas_call | solution.py:36
  166.0 3.1 %shard_map.144 = bf16[576,1536]{1,0:T(8,128)(2,1)} custom-call(s32[3]{0:T(128)S(1)} %pad_add_fusion.refs_0_, bf16[576,3072]{1,0:T(8,128)(2,1)S(1)} %bitcast.13, bf16[576,3072]{1,0:T(8,128)(2,1)S(1)} %bitcast.18, bf16[384,512]{1,0:T(8,128)(2,1)S(1)} %collective-permute-done.51.refs_20_.refs_3_, ...), custom_call_target="tpu_custom_call", output_to_operand_aliasing={{}: (7, {})} | custom-call | flops 679477248 | bytes 13172748 | tf_op jit(solution)/shard_map/pallas_call | solution.py:36
  (145 shorter events, 18.4 us)
Async XLA Ops:
  4.6 26.6 %copy-start.23 = (s32[64,2]{0,1:T(2,128)S(1)}, s32[64,2]{0,1:T(2,128)}, u32[]{:S(2)}) copy-start(s32[64,2]{0,1:T(2,128)} %param.17) | copy-start | bytes 1540
  4.6 6.8 %collective-permute-start = (f32[4,128,128]{2,1,0:T(8,128)S(1)}, f32[4,128,128]{2,1,0:T(8,128)S(1)}, u32[]{:S(2)}, u32[]{:S(2)}) collective-permute-start(f32[4,128,128]{2,1,0:T(8,128)S(1)} %get-tuple-element.60), channel_id=1, source_target_pairs={{0,4},{4,0},{8,12},{12,8},{16,20},{20,16},{24,28},{28,24},{1,5},{5... | collective-permute-start | bytes 786440 | tf_op jit(solution)/shard_map/ppermute | solution.py:146
  7.2 32.9 %copy-start.21 = (f32[8]{0:T(128)S(1)}, f32[8]{0:T(128)}, u32[]{:S(2)}) copy-start(f32[8]{0:T(128)} %refs_1_.11) | copy-start | bytes 100
  7.2 12.7 %collective-permute-start.2 = (bf16[512,384]{1,0:T(8,128)(2,1)}, bf16[512,384]{1,0:T(8,128)(2,1)S(1)}, u32[]{:S(2)}, u32[]{:S(2)}) collective-permute-start(bf16[512,384]{1,0:T(8,128)(2,1)} %get-tuple-element.119), channel_id=1, source_target_pairs={{0,8},{4,12},{8,0},{12,4},{16,24},{20,28},{24,16},{28,20},{1,9},{5... | collective-permute-start | bytes 1179656 | tf_op jit(solution)/shard_map/ppermute | solution.py:146
  9.7 10.2 %collective-permute-start.3 = (bf16[64,3072]{1,0:T(8,128)(2,1)}, bf16[64,3072]{1,0:T(8,128)(2,1)S(1)}, u32[]{:S(2)}, u32[]{:S(2)}) collective-permute-start(bf16[64,3072]{1,0:T(8,128)(2,1)} %param.15), channel_id=1, source_target_pairs={{0,4},{4,0},{8,12},{12,8},{16,20},{20,16},{24,28},{28,24},{1,5},{5... | collective-permute-start | bytes 1179656 | tf_op jit(solution)/shard_map/ppermute | solution.py:155
  9.9 22.9 %collective-permute-start.8 = (bf16[512,384]{1,0:T(8,128)(2,1)}, bf16[512,384]{1,0:T(8,128)(2,1)S(1)}, u32[]{:S(2)}, u32[]{:S(2)}) collective-permute-start(bf16[512,384]{1,0:T(8,128)(2,1)} %get-tuple-element.118.refs_0_), channel_id=1, source_target_pairs={{0,16},{4,20},{8,24},{12,28},{16,0},{20,4},{24,8},{28,12},{1,17},{... | collective-permute-start | bytes 1179656 | tf_op jit(solution)/shard_map/ppermute | solution.py:146
  12.7 7.2 %copy-start.13 = (f32[4,128,128]{2,1,0:T(8,128)}, f32[4,128,128]{2,1,0:T(8,128)S(1)}, u32[]{:S(2)}) copy-start(f32[4,128,128]{2,1,0:T(8,128)S(1)} %get-tuple-element.64.refs_4_) | copy-start | bytes 786436
  12.7 12.6 %collective-permute-start.1 = (f32[4,128,128]{2,1,0:T(8,128)S(1)}, f32[4,128,128]{2,1,0:T(8,128)S(1)}, u32[]{:S(2)}, u32[]{:S(2)}) collective-permute-start(f32[4,128,128]{2,1,0:T(8,128)S(1)} %get-tuple-element.61.refs_4_.refs_2_), channel_id=1, source_target_pairs={{0,8},{4,12},{8,0},{12,4},{16,24},{20,28},{24,16},{28,20},{1,9},{5... | collective-permute-start | bytes 786440 | tf_op jit(solution)/shard_map/ppermute | solution.py:146
  13.3 26.0 %collective-permute-start.7 = (bf16[512,384]{1,0:T(8,128)(2,1)}, bf16[512,384]{1,0:T(8,128)(2,1)S(1)}, u32[]{:S(2)}, u32[]{:S(2)}) collective-permute-start(bf16[512,384]{1,0:T(8,128)(2,1)} %get-tuple-element.119), channel_id=1, source_target_pairs={{0,16},{4,20},{8,24},{12,28},{16,0},{20,4},{24,8},{28,12},{1,17},{... | collective-permute-start | bytes 1179656 | tf_op jit(solution)/shard_map/ppermute | solution.py:146
  27.3 23.6 %copy-start.2 = (bf16[1024,384]{1,0:T(8,128)(2,1)S(1)}, bf16[1024,384]{1,0:T(8,128)(2,1)}, u32[]{:S(2)}) copy-start(bf16[1024,384]{1,0:T(8,128)(2,1)} %refs_3_.5) | copy-start | bytes 2359300
  27.3 12.0 %collective-permute-start.4 = (f32[4,128,128]{2,1,0:T(8,128)}, f32[4,128,128]{2,1,0:T(8,128)S(1)}, u32[]{:S(2)}, u32[]{:S(2)}) collective-permute-start(f32[4,128,128]{2,1,0:T(8,128)} %get-tuple-element.63.refs_1_), channel_id=1, source_target_pairs={{0,16},{4,20},{8,24},{12,28},{1,17},{5,21},{9,25},{13,29},{2,18},{... | collective-permute-start | bytes 786440 | tf_op jit(solution)/shard_map/ppermute | solution.py:364
  31.2 3.6 %collective-permute-start.5 = (s32[2,64]{1,0:T(2,128)S(1)}, s32[2,64]{1,0:T(2,128)S(1)}, u32[]{:S(2)}, u32[]{:S(2)}) collective-permute-start(s32[2,64]{1,0:T(2,128)S(1)} %bitcast.22), channel_id=1, source_target_pairs={{0,1},{1,0},{2,3},{3,2},{4,5},{5,4},{6,7},{7,6},{8,9},{9,8},{10,11... | collective-permute-start | bytes 1544 | tf_op jit(solution)/shard_map/ppermute | solution.py:172
  32.8 12.9 %collective-permute-start.11 = (bf16[512,384]{1,0:T(8,128)(2,1)}, bf16[512,384]{1,0:T(8,128)(2,1)}, u32[]{:S(2)}, u32[]{:S(2)}) collective-permute-start(bf16[512,384]{1,0:T(8,128)(2,1)} %shard_map.119), channel_id=1, source_target_pairs={{0,8},{4,12},{8,0},{12,4},{16,24},{20,28},{24,16},{28,20},{1,9},{5... | collective-permute-start | bytes 1179656 | tf_op jit(solution)/shard_map/ppermute | solution.py:146
  34.9 4.5 %collective-permute-start.6 = (s32[2,128]{1,0:T(2,128)S(1)}, s32[2,128]{1,0:T(2,128)S(1)}, u32[]{:S(2)}, u32[]{:S(2)}) collective-permute-start(s32[2,128]{1,0:T(2,128)S(1)} %add_select_fusion.3), channel_id=1, source_target_pairs={{0,2},{1,3},{2,0},{3,1},{4,6},{5,7},{6,4},{7,5},{8,10},{9,11},{10,... | collective-permute-start | bytes 3080 | tf_op jit(solution)/shard_map/ppermute | solution.py:172
  44.3 1.9 %collective-permute-start.9 = (f32[4,128,128]{2,1,0:T(8,128)}, f32[4,128,128]{2,1,0:T(8,128)}, u32[]{:S(2)}, u32[]{:S(2)}) collective-permute-start(f32[4,128,128]{2,1,0:T(8,128)} %get-tuple-element.66), channel_id=1, source_target_pairs={{0,4},{4,0},{8,12},{12,8},{16,20},{20,16},{24,28},{28,24},{1,5},{5... | collective-permute-start | bytes 786440 | tf_op jit(solution)/shard_map/ppermute | solution.py:146
  44.3 1.3 collective-permute-start.10
  48.9 9.9 %copy-start.22 = (f32[3072]{0:T(1024)S(1)}, f32[3072]{0:T(1024)}, u32[]{:S(2)}) copy-start(f32[3072]{0:T(1024)} %param.16) | copy-start | bytes 36868
  48.9 2.0 %collective-permute-start.12 = (bf16[256,1024]{1,0:T(8,128)(2,1)S(1)}, bf16[256,1024]{1,0:T(8,128)(2,1)S(1)}, u32[]{:S(2)}, u32[]{:S(2)}) collective-permute-start(bf16[256,1024]{1,0:T(8,128)(2,1)S(1)} %shard_map.120.refs_1_.refs_6_), channel_id=1, source_target_pairs={{0,4},{4,0},{8,12},{12,8},{16,20},{20,16},{24,28},{28,24},{1,5},{5... | collective-permute-start | bytes 1572872 | tf_op jit(solution)/shard_map/ppermute | solution.py:155
  50.9 15.1 %copy-start.10 = (bf16[512,384]{1,0:T(8,128)(2,1)S(1)}, bf16[512,384]{1,0:T(8,128)(2,1)}, u32[]{:S(2)}) copy-start(bf16[512,384]{1,0:T(8,128)(2,1)} %copy-done.9) | copy-start | bytes 1179652
  52.2 12.9 %collective-permute-start.13 = (bf16[512,384]{1,0:T(8,128)(2,1)S(1)}, bf16[512,384]{1,0:T(8,128)(2,1)S(1)}, u32[]{:S(2)}, u32[]{:S(2)}) collective-permute-start(bf16[512,384]{1,0:T(8,128)(2,1)S(1)} %get-tuple-element.68.refs_7_), channel_id=1, source_target_pairs={{0,1},{3,2},{4,5},{7,6},{8,9},{11,10},{12,13},{15,14},{16,17},{19,... | collective-permute-start | bytes 1179656 | tf_op jit(solution)/shard_map/ppermute | solution.py:539
  57.5 18.6 %collective-permute-start.15 = (bf16[512,384]{1,0:T(8,128)(2,1)S(1)}, bf16[512,384]{1,0:T(8,128)(2,1)S(1)}, u32[]{:S(2)}, u32[]{:S(2)}) collective-permute-start(bf16[512,384]{1,0:T(8,128)(2,1)S(1)} %get-tuple-element.69.refs_2_), channel_id=1, source_target_pairs={{0,1},{3,2},{4,5},{7,6},{8,9},{11,10},{12,13},{15,14},{16,17},{19,... | collective-permute-start | bytes 1179656 | tf_op jit(solution)/shard_map/ppermute | solution.py:539
  58.9 19.6 %collective-permute-start.19 = (bf16[512,384]{1,0:T(8,128)(2,1)S(1)}, bf16[512,384]{1,0:T(8,128)(2,1)S(1)}, u32[]{:S(2)}, u32[]{:S(2)}) collective-permute-start(bf16[512,384]{1,0:T(8,128)(2,1)S(1)} %shard_map.127), channel_id=1, source_target_pairs={{0,16},{4,20},{8,24},{12,28},{16,0},{20,4},{24,8},{28,12},{1,17},{... | collective-permute-start | bytes 1179656 | tf_op jit(solution)/shard_map/ppermute | solution.py:146
  65.3 11.9 %collective-permute-start.14 = (bf16[512,384]{1,0:T(8,128)(2,1)S(1)}, bf16[512,384]{1,0:T(8,128)(2,1)S(1)}, u32[]{:S(2)}, u32[]{:S(2)}) collective-permute-start(bf16[512,384]{1,0:T(8,128)(2,1)S(1)} %get-tuple-element.71.refs_7_), channel_id=1, source_target_pairs={{1,2},{2,1},{5,6},{6,5},{9,10},{10,9},{13,14},{14,13},{17,18},{18,... | collective-permute-start | bytes 1179656 | tf_op jit(solution)/shard_map/ppermute | solution.py:545
  67.3 11.3 %collective-permute-start.20 = (bf16[512,384]{1,0:T(8,128)(2,1)S(1)}, bf16[512,384]{1,0:T(8,128)(2,1)S(1)}, u32[]{:S(2)}, u32[]{:S(2)}) collective-permute-start(bf16[512,384]{1,0:T(8,128)(2,1)S(1)} %shard_map.128), channel_id=1, source_target_pairs={{0,8},{4,12},{8,0},{12,4},{16,24},{20,28},{24,16},{28,20},{1,9},{5... | collective-permute-start | bytes 1179656 | tf_op jit(solution)/shard_map/ppermute | solution.py:146
  68.9 16.8 %collective-permute-start.18 = (bf16[512,384]{1,0:T(8,128)(2,1)S(1)}, bf16[512,384]{1,0:T(8,128)(2,1)S(1)}, u32[]{:S(2)}, u32[]{:S(2)}) collective-permute-start(bf16[512,384]{1,0:T(8,128)(2,1)S(1)} %get-tuple-element.73.refs_2_), channel_id=1, source_target_pairs={{0,1},{3,2},{4,5},{7,6},{8,9},{11,10},{12,13},{15,14},{16,17},{19,... | collective-permute-start | bytes 1179656 | tf_op jit(solution)/shard_map/ppermute | solution.py:539
  76.2 10.2 %collective-permute-start.17 = (bf16[512,384]{1,0:T(8,128)(2,1)S(1)}, bf16[512,384]{1,0:T(8,128)(2,1)S(1)}, u32[]{:S(2)}, u32[]{:S(2)}) collective-permute-start(bf16[512,384]{1,0:T(8,128)(2,1)S(1)} %get-tuple-element.74.refs_2_), channel_id=1, source_target_pairs={{1,2},{2,1},{5,6},{6,5},{9,10},{10,9},{13,14},{14,13},{17,18},{18,... | collective-permute-start | bytes 1179656 | tf_op jit(solution)/shard_map/ppermute | solution.py:545
  77.2 12.3 %collective-permute-start.16 = (bf16[512,384]{1,0:T(8,128)(2,1)S(1)}, bf16[512,384]{1,0:T(8,128)(2,1)S(1)}, u32[]{:S(2)}, u32[]{:S(2)}) collective-permute-start(bf16[512,384]{1,0:T(8,128)(2,1)S(1)} %shard_map.126.refs_7_.refs_2_), channel_id=1, source_target_pairs={{1,0},{2,3},{5,4},{6,7},{9,8},{10,11},{13,12},{14,15},{17,16},{18,... | collective-permute-start | bytes 1179656 | tf_op jit(solution)/shard_map/ppermute | solution.py:554
  79.9 12.2 %collective-permute-start.23 = (bf16[512,384]{1,0:T(8,128)(2,1)S(1)}, bf16[512,384]{1,0:T(8,128)(2,1)S(1)}, u32[]{:S(2)}, u32[]{:S(2)}) collective-permute-start(bf16[512,384]{1,0:T(8,128)(2,1)S(1)} %get-tuple-element.77.refs_2_), channel_id=1, source_target_pairs={{0,1},{3,2},{4,5},{7,6},{8,9},{11,10},{12,13},{15,14},{16,17},{19,... | collective-permute-start | bytes 1179656 | tf_op jit(solution)/shard_map/ppermute | solution.py:539
  85.8 7.1 %collective-permute-start.22 = (bf16[512,384]{1,0:T(8,128)(2,1)S(1)}, bf16[512,384]{1,0:T(8,128)(2,1)S(1)}, u32[]{:S(2)}, u32[]{:S(2)}) collective-permute-start(bf16[512,384]{1,0:T(8,128)(2,1)S(1)} %get-tuple-element.78.refs_2_), channel_id=1, source_target_pairs={{1,2},{2,1},{5,6},{6,5},{9,10},{10,9},{13,14},{14,13},{17,18},{18,... | collective-permute-start | bytes 1179656 | tf_op jit(solution)/shard_map/ppermute | solution.py:545
  86.6 12.7 %collective-permute-start.21 = (bf16[512,384]{1,0:T(8,128)(2,1)S(1)}, bf16[512,384]{1,0:T(8,128)(2,1)S(1)}, u32[]{:S(2)}, u32[]{:S(2)}) collective-permute-start(bf16[512,384]{1,0:T(8,128)(2,1)S(1)} %shard_map.131.refs_5_.refs_2_), channel_id=1, source_target_pairs={{1,0},{2,3},{5,4},{6,7},{9,8},{10,11},{13,12},{14,15},{17,16},{18,... | collective-permute-start | bytes 1179656 | tf_op jit(solution)/shard_map/ppermute | solution.py:554
  90.5 8.8 %collective-permute-start.24 = (bf16[384,384]{1,0:T(8,128)(2,1)S(1)}, bf16[384,384]{1,0:T(8,128)(2,1)S(1)}, u32[]{:S(2)}, u32[]{:S(2)}) collective-permute-start(bf16[384,384]{1,0:T(8,128)(2,1)S(1)} %get-tuple-element.82.refs_2_.refs_3_), channel_id=1, source_target_pairs={{0,8},{4,12},{8,0},{12,4},{16,24},{20,28},{24,16},{28,20},{1,9},{5... | collective-permute-start | bytes 884744 | tf_op jit(solution)/shard_map/ppermute | solution.py:146
  92.0 7.3 %collective-permute-start.25 = (bf16[384,384]{1,0:T(8,128)(2,1)S(1)}, bf16[384,384]{1,0:T(8,128)(2,1)S(1)}, u32[]{:S(2)}, u32[]{:S(2)}) collective-permute-start(bf16[384,384]{1,0:T(8,128)(2,1)S(1)} %get-tuple-element.82.refs_2_.refs_3_), channel_id=1, source_target_pairs={{0,16},{4,20},{8,24},{12,28},{16,0},{20,4},{24,8},{28,12},{1,17},{... | collective-permute-start | bytes 884744 | tf_op jit(solution)/shard_map/ppermute | solution.py:146
  92.2 9.2 %collective-permute-start.27 = (bf16[512,384]{1,0:T(8,128)(2,1)S(1)}, bf16[512,384]{1,0:T(8,128)(2,1)S(1)}, u32[]{:S(2)}, u32[]{:S(2)}) collective-permute-start(bf16[512,384]{1,0:T(8,128)(2,1)S(1)} %get-tuple-element.83.refs_2_), channel_id=1, source_target_pairs={{1,2},{2,1},{5,6},{6,5},{9,10},{10,9},{13,14},{14,13},{17,18},{18,... | collective-permute-start | bytes 1179656 | tf_op jit(solution)/shard_map/ppermute | solution.py:545
  93.0 13.2 %collective-permute-start.26 = (bf16[512,384]{1,0:T(8,128)(2,1)S(1)}, bf16[512,384]{1,0:T(8,128)(2,1)S(1)}, u32[]{:S(2)}, u32[]{:S(2)}) collective-permute-start(bf16[512,384]{1,0:T(8,128)(2,1)S(1)} %shard_map.134.refs_5_.refs_2_), channel_id=1, source_target_pairs={{1,0},{2,3},{5,4},{6,7},{9,8},{10,11},{13,12},{14,15},{17,16},{18,... | collective-permute-start | bytes 1179656 | tf_op jit(solution)/shard_map/ppermute | solution.py:554
  100.3 6.8 %collective-permute-start.28 = (bf16[384,384]{1,0:T(8,128)(2,1)S(1)}, bf16[384,384]{1,0:T(8,128)(2,1)S(1)}, u32[]{:S(2)}, u32[]{:S(2)}) collective-permute-start(bf16[384,384]{1,0:T(8,128)(2,1)S(1)} %get-tuple-element.86.refs_2_.refs_3_), channel_id=1, source_target_pairs={{0,8},{4,12},{8,0},{12,4},{16,24},{20,28},{24,16},{28,20},{1,9},{5... | collective-permute-start | bytes 884744 | tf_op jit(solution)/shard_map/ppermute | solution.py:146
  101.4 8.1 %collective-permute-start.29 = (bf16[384,384]{1,0:T(8,128)(2,1)S(1)}, bf16[384,384]{1,0:T(8,128)(2,1)S(1)}, u32[]{:S(2)}, u32[]{:S(2)}) collective-permute-start(bf16[384,384]{1,0:T(8,128)(2,1)S(1)} %get-tuple-element.86.refs_2_.refs_3_), channel_id=1, source_target_pairs={{0,16},{4,20},{8,24},{12,28},{16,0},{20,4},{24,8},{28,12},{1,17},{... | collective-permute-start | bytes 884744 | tf_op jit(solution)/shard_map/ppermute | solution.py:146
  101.4 9.0 %collective-permute-start.44 = (bf16[384,384]{1,0:T(8,128)(2,1)S(1)}, bf16[384,384]{1,0:T(8,128)(2,1)S(1)}, u32[]{:S(2)}, u32[]{:S(2)}) collective-permute-start(bf16[384,384]{1,0:T(8,128)(2,1)S(1)} %get-tuple-element.82.refs_2_.refs_3_), channel_id=1, source_target_pairs={{0,4},{4,0},{8,12},{12,8},{16,20},{20,16},{24,28},{28,24},{1,5},{5... | collective-permute-start | bytes 884744 | tf_op jit(solution)/shard_map/ppermute | solution.py:155
  101.4 40.1 %copy-start = (bf16[1,576,3072]{2,1,0:T(8,128)(2,1)S(1)}, bf16[1,576,3072]{2,1,0:T(8,128)(2,1)}, u32[]{:S(2)}) copy-start(bf16[1,576,3072]{2,1,0:T(8,128)(2,1)} %param.18) | copy-start | bytes 10616836
  101.4 40.1 %copy-start.1 = (bf16[1,576,3072]{2,1,0:T(8,128)(2,1)S(1)}, bf16[1,576,3072]{2,1,0:T(8,128)(2,1)}, u32[]{:S(2)}) copy-start(bf16[1,576,3072]{2,1,0:T(8,128)(2,1)} %param.19) | copy-start | bytes 10616836
  101.5 13.8 %collective-permute-start.30 = (bf16[512,384]{1,0:T(8,128)(2,1)S(1)}, bf16[512,384]{1,0:T(8,128)(2,1)S(1)}, u32[]{:S(2)}, u32[]{:S(2)}) collective-permute-start(bf16[512,384]{1,0:T(8,128)(2,1)S(1)} %shard_map.136.refs_5_), channel_id=1, source_target_pairs={{1,0},{2,3},{5,4},{6,7},{9,8},{10,11},{13,12},{14,15},{17,16},{18,... | collective-permute-start | bytes 1179656 | tf_op jit(solution)/shard_map/ppermute | solution.py:554
  106.1 8.3 %collective-permute-start.47 = (bf16[384,384]{1,0:T(8,128)(2,1)S(1)}, bf16[384,384]{1,0:T(8,128)(2,1)S(1)}, u32[]{:S(2)}, u32[]{:S(2)}) collective-permute-start(bf16[384,384]{1,0:T(8,128)(2,1)S(1)} %collective-permute-done.24.refs_6_.refs_5_), channel_id=1, source_target_pairs={{0,16},{4,20},{8,24},{12,28},{16,0},{20,4},{24,8},{28,12},{1,17},{... | collective-permute-start | bytes 884744 | tf_op jit(solution)/shard_map/ppermute | solution.py:146
  107.1 7.7 %collective-permute-start.45 = (bf16[384,384]{1,0:T(8,128)(2,1)S(1)}, bf16[384,384]{1,0:T(8,128)(2,1)S(1)}, u32[]{:S(2)}, u32[]{:S(2)}) collective-permute-start(bf16[384,384]{1,0:T(8,128)(2,1)S(1)} %collective-permute-done.24.refs_6_.refs_5_), channel_id=1, source_target_pairs={{0,4},{4,0},{8,12},{12,8},{16,20},{20,16},{24,28},{28,24},{1,5},{5... | collective-permute-start | bytes 884744 | tf_op jit(solution)/shard_map/ppermute | solution.py:155
  109.5 5.3 %collective-permute-start.46 = (bf16[384,384]{1,0:T(8,128)(2,1)S(1)}, bf16[384,384]{1,0:T(8,128)(2,1)S(1)}, u32[]{:S(2)}, u32[]{:S(2)}) collective-permute-start(bf16[384,384]{1,0:T(8,128)(2,1)S(1)} %collective-permute-done.25.refs_7_), channel_id=1, source_target_pairs={{0,4},{4,0},{8,12},{12,8},{16,20},{20,16},{24,28},{28,24},{1,5},{5... | collective-permute-start | bytes 884744 | tf_op jit(solution)/shard_map/ppermute | solution.py:155
  110.5 9.9 %collective-permute-start.31 = (bf16[384,384]{1,0:T(8,128)(2,1)S(1)}, bf16[384,384]{1,0:T(8,128)(2,1)S(1)}, u32[]{:S(2)}, u32[]{:S(2)}) collective-permute-start(bf16[384,384]{1,0:T(8,128)(2,1)S(1)} %get-tuple-element.88.refs_8_.refs_3_), channel_id=1, source_target_pairs={{0,8},{4,12},{8,0},{12,4},{16,24},{20,28},{24,16},{28,20},{1,9},{5... | collective-permute-start | bytes 884744 | tf_op jit(solution)/shard_map/ppermute | solution.py:146
  114.4 7.4 %collective-permute-start.32 = (bf16[384,384]{1,0:T(8,128)(2,1)S(1)}, bf16[384,384]{1,0:T(8,128)(2,1)S(1)}, u32[]{:S(2)}, u32[]{:S(2)}) collective-permute-start(bf16[384,384]{1,0:T(8,128)(2,1)S(1)} %get-tuple-element.88.refs_8_.refs_3_), channel_id=1, source_target_pairs={{0,16},{4,20},{8,24},{12,28},{16,0},{20,4},{24,8},{28,12},{1,17},{... | collective-permute-start | bytes 884744 | tf_op jit(solution)/shard_map/ppermute | solution.py:146
  114.8 8.4 %collective-permute-start.39 = (bf16[384,384]{1,0:T(8,128)(2,1)S(1)}, bf16[384,384]{1,0:T(8,128)(2,1)S(1)}, u32[]{:S(2)}, u32[]{:S(2)}) collective-permute-start(bf16[384,384]{1,0:T(8,128)(2,1)S(1)} %get-tuple-element.86.refs_2_.refs_3_), channel_id=1, source_target_pairs={{0,4},{4,0},{8,12},{12,8},{16,20},{20,16},{24,28},{28,24},{1,5},{5... | collective-permute-start | bytes 884744 | tf_op jit(solution)/shard_map/ppermute | solution.py:155
  114.8 8.8 %collective-permute-start.48 = (bf16[384,384]{1,0:T(8,128)(2,1)S(1)}, bf16[384,384]{1,0:T(8,128)(2,1)S(1)}, u32[]{:S(2)}, u32[]{:S(2)}) collective-permute-start(bf16[384,384]{1,0:T(8,128)(2,1)S(1)} %collective-permute-done.47.refs_9_), channel_id=1, source_target_pairs={{0,4},{4,0},{8,12},{12,8},{16,20},{20,16},{24,28},{28,24},{1,5},{5... | collective-permute-start | bytes 884744 | tf_op jit(solution)/shard_map/ppermute | solution.py:155
  115.3 11.0 %collective-permute-start.42 = (bf16[384,384]{1,0:T(8,128)(2,1)S(1)}, bf16[384,384]{1,0:T(8,128)(2,1)S(1)}, u32[]{:S(2)}, u32[]{:S(2)}) collective-permute-start(bf16[384,384]{1,0:T(8,128)(2,1)S(1)} %collective-permute-done.29.refs_7_), channel_id=1, source_target_pairs={{0,8},{4,12},{8,0},{12,4},{16,24},{20,28},{24,16},{28,20},{1,9},{5... | collective-permute-start | bytes 884744 | tf_op jit(solution)/shard_map/ppermute | solution.py:146
  120.3 5.9 %collective-permute-start.40 = (bf16[384,384]{1,0:T(8,128)(2,1)S(1)}, bf16[384,384]{1,0:T(8,128)(2,1)S(1)}, u32[]{:S(2)}, u32[]{:S(2)}) collective-permute-start(bf16[384,384]{1,0:T(8,128)(2,1)S(1)} %collective-permute-done.28.refs_6_.refs_5_), channel_id=1, source_target_pairs={{0,4},{4,0},{8,12},{12,8},{16,20},{20,16},{24,28},{28,24},{1,5},{5... | collective-permute-start | bytes 884744 | tf_op jit(solution)/shard_map/ppermute | solution.py:155
  121.8 4.5 %collective-permute-start.41 = (bf16[384,384]{1,0:T(8,128)(2,1)S(1)}, bf16[384,384]{1,0:T(8,128)(2,1)S(1)}, u32[]{:S(2)}, u32[]{:S(2)}) collective-permute-start(bf16[384,384]{1,0:T(8,128)(2,1)S(1)} %collective-permute-done.29.refs_7_), channel_id=1, source_target_pairs={{0,4},{4,0},{8,12},{12,8},{16,20},{20,16},{24,28},{28,24},{1,5},{5... | collective-permute-start | bytes 884744 | tf_op jit(solution)/shard_map/ppermute | solution.py:155
  123.2 17.9 %collective-permute-start.50 = (bf16[384,512]{1,0:T(8,128)(2,1)S(1)}, bf16[384,512]{1,0:T(8,128)(2,1)S(1)}, u32[]{:S(2)}, u32[]{:S(2)}) collective-permute-start(bf16[384,512]{1,0:T(8,128)(2,1)S(1)} %get-tuple-element.91.refs_11_.refs_3_), channel_id=1, source_target_pairs={{0,16},{4,20},{8,24},{12,28},{16,0},{20,4},{24,8},{28,12},{1,17},{... | collective-permute-start | bytes 1179656 | tf_op jit(solution)/shard_map/ppermute | solution.py:146
  123.6 3.4 %collective-permute-start.34 = (bf16[384,384]{1,0:T(8,128)(2,1)S(1)}, bf16[384,384]{1,0:T(8,128)(2,1)S(1)}, u32[]{:S(2)}, u32[]{:S(2)}) collective-permute-start(bf16[384,384]{1,0:T(8,128)(2,1)S(1)} %get-tuple-element.88.refs_8_.refs_3_), channel_id=1, source_target_pairs={{0,4},{4,0},{8,12},{12,8},{16,20},{20,16},{24,28},{28,24},{1,5},{5... | collective-permute-start | bytes 884744 | tf_op jit(solution)/shard_map/ppermute | solution.py:155
  126.3 1.6 collective-permute-start.43
  126.3 14.8 %collective-permute-start.37 = (bf16[384,384]{1,0:T(8,128)(2,1)S(1)}, bf16[384,384]{1,0:T(8,128)(2,1)S(1)}, u32[]{:S(2)}, u32[]{:S(2)}) collective-permute-start(bf16[384,384]{1,0:T(8,128)(2,1)S(1)} %collective-permute-done.31.refs_9_.refs_5_), channel_id=1, source_target_pairs={{0,16},{4,20},{8,24},{12,28},{16,0},{20,4},{24,8},{28,12},{1,17},{... | collective-permute-start | bytes 884744 | tf_op jit(solution)/shard_map/ppermute | solution.py:146
  126.3 20.3 %collective-permute-start.49 = (bf16[384,512]{1,0:T(8,128)(2,1)S(1)}, bf16[384,512]{1,0:T(8,128)(2,1)S(1)}, u32[]{:S(2)}, u32[]{:S(2)}) collective-permute-start(bf16[384,512]{1,0:T(8,128)(2,1)S(1)} %get-tuple-element.91.refs_11_.refs_3_), channel_id=1, source_target_pairs={{0,8},{4,12},{8,0},{12,4},{16,24},{20,28},{24,16},{28,20},{1,9},{5... | collective-permute-start | bytes 1179656 | tf_op jit(solution)/shard_map/ppermute | solution.py:146
  127.0 19.0 %collective-permute-start.35 = (bf16[384,384]{1,0:T(8,128)(2,1)S(1)}, bf16[384,384]{1,0:T(8,128)(2,1)S(1)}, u32[]{:S(2)}, u32[]{:S(2)}) collective-permute-start(bf16[384,384]{1,0:T(8,128)(2,1)S(1)} %collective-permute-done.31.refs_9_.refs_5_), channel_id=1, source_target_pairs={{0,4},{4,0},{8,12},{12,8},{16,20},{20,16},{24,28},{28,24},{1,5},{5... | collective-permute-start | bytes 884744 | tf_op jit(solution)/shard_map/ppermute | solution.py:155
  127.8 18.5 %collective-permute-start.36 = (bf16[384,384]{1,0:T(8,128)(2,1)S(1)}, bf16[384,384]{1,0:T(8,128)(2,1)S(1)}, u32[]{:S(2)}, u32[]{:S(2)}) collective-permute-start(bf16[384,384]{1,0:T(8,128)(2,1)S(1)} %collective-permute-done.32.refs_10_.refs_7_), channel_id=1, source_target_pairs={{0,4},{4,0},{8,12},{12,8},{16,20},{20,16},{24,28},{28,24},{1,5},{5... | collective-permute-start | bytes 884744 | tf_op jit(solution)/shard_map/ppermute | solution.py:155
  141.1 10.3 %collective-permute-start.38 = (bf16[384,384]{1,0:T(8,128)(2,1)S(1)}, bf16[384,384]{1,0:T(8,128)(2,1)S(1)}, u32[]{:S(2)}, u32[]{:S(2)}) collective-permute-start(bf16[384,384]{1,0:T(8,128)(2,1)S(1)} %collective-permute-done.37.refs_9_), channel_id=1, source_target_pairs={{0,4},{4,0},{8,12},{12,8},{16,20},{20,16},{24,28},{28,24},{1,5},{5... | collective-permute-start | bytes 884744 | tf_op jit(solution)/shard_map/ppermute | solution.py:155
  141.1 11.5 %collective-permute-start.51 = (bf16[384,512]{1,0:T(8,128)(2,1)S(1)}, bf16[384,512]{1,0:T(8,128)(2,1)S(1)}, u32[]{:S(2)}, u32[]{:S(2)}) collective-permute-start(bf16[384,512]{1,0:T(8,128)(2,1)S(1)} %collective-permute-done.50.refs_21_.refs_7_), channel_id=1, source_target_pairs={{0,8},{4,12},{8,0},{12,4},{16,24},{20,28},{24,16},{28,20},{1,9},{5... | collective-permute-start | bytes 1179656 | tf_op jit(solution)/shard_map/ppermute | solution.py:146
  146.0 12.5 %collective-permute-start.53 = (bf16[384,512]{1,0:T(8,128)(2,1)S(1)}, bf16[384,512]{1,0:T(8,128)(2,1)S(1)}, u32[]{:S(2)}, u32[]{:S(2)}) collective-permute-start(bf16[384,512]{1,0:T(8,128)(2,1)S(1)} %get-tuple-element.91.refs_11_.refs_3_), channel_id=1, source_target_pairs={{0,4},{4,0},{8,12},{12,8},{16,20},{20,16},{24,28},{28,24},{1,5},{5... | collective-permute-start | bytes 1179656 | tf_op jit(solution)/shard_map/ppermute | solution.py:155
  146.3 12.2 %collective-permute-start.55 = (bf16[384,512]{1,0:T(8,128)(2,1)S(1)}, bf16[384,512]{1,0:T(8,128)(2,1)S(1)}, u32[]{:S(2)}, u32[]{:S(2)}) collective-permute-start(bf16[384,512]{1,0:T(8,128)(2,1)S(1)} %collective-permute-done.50.refs_21_.refs_7_), channel_id=1, source_target_pairs={{0,4},{4,0},{8,12},{12,8},{16,20},{20,16},{24,28},{28,24},{1,5},{5... | collective-permute-start | bytes 1179656 | tf_op jit(solution)/shard_map/ppermute | solution.py:155
  146.6 11.9 %collective-permute-start.54 = (bf16[384,512]{1,0:T(8,128)(2,1)S(1)}, bf16[384,512]{1,0:T(8,128)(2,1)S(1)}, u32[]{:S(2)}, u32[]{:S(2)}) collective-permute-start(bf16[384,512]{1,0:T(8,128)(2,1)S(1)} %collective-permute-done.49.refs_20_.refs_5_), channel_id=1, source_target_pairs={{0,4},{4,0},{8,12},{12,8},{16,20},{20,16},{24,28},{28,24},{1,5},{5... | collective-permute-start | bytes 1179656 | tf_op jit(solution)/shard_map/ppermute | solution.py:155
  151.4 5.8 %collective-permute-start.33 = (bf16[64,1536]{1,0:T(8,128)(2,1)S(1)}, bf16[64,1536]{1,0:T(8,128)(2,1)S(1)}, u32[]{:S(2)}, u32[]{:S(2)}) collective-permute-start(bf16[64,1536]{1,0:T(8,128)(2,1)S(1)} %get-tuple-element.90), channel_id=1, source_target_pairs={{0,4},{4,0},{8,12},{12,8},{16,20},{20,16},{24,28},{28,24},{1,5},{5... | collective-permute-start | bytes 589832 | tf_op jit(solution)/shard_map/ppermute | solution.py:631
  152.6 13.3 %collective-permute-start.52 = (bf16[384,512]{1,0:T(8,128)(2,1)S(1)}, bf16[384,512]{1,0:T(8,128)(2,1)S(1)}, u32[]{:S(2)}, u32[]{:S(2)}) collective-permute-start(bf16[384,512]{1,0:T(8,128)(2,1)S(1)} %collective-permute-done.51.refs_20_.refs_3_), channel_id=1, source_target_pairs={{0,4},{4,0},{8,12},{12,8},{16,20},{20,16},{24,28},{28,24},{1,5},{5... | collective-permute-start | bytes 1179656 | tf_op jit(solution)/shard_map/ppermute | solution.py:155
  (16 other events, 26.0 us)

commit v4 on v3

--- a/solution.py
+++ b/solution.py
@@ -50,77 +50,57 @@
 ANY = pl.BlockSpec(memory_space=pl.ANY)
 
 
-def fresh_kernel(place_ref, rate_ref, k_ref, v_ref, *outs):
+def fresh_kernel(place_ref, rate_ref, k_in, v_in, *refs):
+    outs, (k_ref, v_ref, sems) = refs[:-3], refs[-3:]
     part, size = outs[0].shape[0], outs[0].shape[1]
     length = k_ref.shape[0]
     left = length - lax.broadcasted_iota(jnp.int32, (length, size), 0).astype(F32)
-    for a, out_ref in enumerate(outs):
-        first = lax.rem(place_ref[1] + a, len(outs)) * part
+    waits = []
+    for a in range(len(outs)):
+        first = lax.rem(place_ref[1] + len(outs) - 1 - a, len(outs)) * part
+        at = pl.ds(pl.multiple_of(first * size, part * size), part * size)
+        pair = []
+        for n, (source, target) in enumerate(((k_in, k_ref), (v_in, v_ref))):
+            pair.append(pltpu.make_async_copy(source.at[:, at], target.at[:, at], sems.at[2 * a + n]))
+            pair[-1].start()
+        waits.append((first, pair))
+    for a, out_ref in enumerate(outs[::-1]):
+        first, pair = waits[a]
+        for copy in pair:
+            copy.wait()
         for j in range(part):
             cols = pl.ds(pl.multiple_of((first + j) * size, size), size)
-            tail = jnp.exp(-rate_ref[first + j] * left)
+            tail = jnp.exp(rate_ref[first + j][:, :size] * left)
             high, low = halves(k_ref[:, cols].astype(F32) * tail)
             v = v_ref[:, cols]
             out_ref[j] = dot(high, v, TN) + dot(low, v, TN)
 
 
-def local_kernel(rate_ref, q_ref, k_ref, v_ref, out_ref):
+def local_kernel(rate_ref, q_in, k_ref, v_ref, out_ref, q_ref, sem):
     heads = rate_ref.shape[0]
     length = k_ref.shape[0]
     size = k_ref.shape[1] // heads
+    copy = pltpu.make_async_copy(q_in, q_ref, sem)
+    copy.start()
     rows = lax.broadcasted_iota(jnp.int32, (length, length), 0)
     cols = lax.broadcasted_iota(jnp.int32, (length, length), 1)
     offset = (rows - cols).astype(F32)
     keep = offset >= 0
     offset = jnp.maximum(offset, 0.0)
+    copy.wait()
     for h in range(heads):
         at = slice(h * size, (h + 1) * size)
-        masked = jnp.where(keep, jnp.exp(-rate_ref[h] * offset), 0.0)
+        masked = jnp.where(keep, jnp.exp(rate_ref[h] * offset), 0.0)
         weighted = (dot(q_ref[:, at], k_ref[:, at], NT) * masked).astype(BF16)
         out_ref[:, at] = dot(weighted, v_ref[:, at], NN)
 
 
-def fade(rate_ref, head, positions):
-    return jnp.exp(-(rate_ref[head] * positions) + jnp.zeros((1, 128), F32))
-
-
-def pair_kernel(length, place_ref, rate_ref, mine_ref, got_ref, early_ref, total_ref):
-    part = mine_ref.shape[0]
-    first = place_ref[1] == 0
-    for j in range(part):
-        mine, got = mine_ref[j], got_ref[j]
-        early = jnp.where(first, mine, got)
-        early_ref[j] = early
-        late = jnp.where(first, got, mine)
-        total_ref[j] = fade(rate_ref, place_ref[1] * part + j, float(length)) * early + late
-
-
-def scan_kernel(length, step, place_ref, rate_ref, *refs):
-    old_ref = refs[0] if step > 1 else None
-    total_ref, got_ref, state_ref, out_ref = refs[-4:]
-    part = total_ref.shape[0]
-    upper = (place_ref[0] & step) != 0
-    behind = (place_ref[0] & (step - 1)).astype(F32) * (2.0 * length)
-    for j in range(part):
-        head = place_ref[1] * part + j
-        got, total = got_ref[j], total_ref[j]
-        state = jnp.where(upper, fade(rate_ref, head, behind) * got, 0.0)
-        state_ref[j] = state if old_ref is None else old_ref[j] + state
-        span = fade(rate_ref, head, 2.0 * length * step)
-        out_ref[j] = jnp.where(upper, span * got + total, span * total + got)
-
-
-def final_scan_kernel(length, step, place_ref, rate_ref, old_ref, got_ref, early_ref, keep_ref, give_ref):
-    part = old_ref.shape[0]
-    first = place_ref[1] == 0
-    upper = (place_ref[0] & step) != 0
-    behind = (place_ref[0] & (step - 1)).astype(F32) * (2.0 * length)
-    for j in range(part):
-        head = place_ref[1] * part + j
-        state = old_ref[j] + jnp.where(upper, fade(rate_ref, head, behind) * got_ref[j], 0.0)
-        late = fade(rate_ref, head, float(length)) * state + early_ref[j]
-        keep_ref[j] = jnp.where(first, state, late)
-        give_ref[j] = jnp.where(first, late, state)
+def mix_kernel(recipe, coef_ref, *refs):
+    count = 1 + max(i for terms in recipe for i, _ in terms)
+    for j in range(refs[0].shape[0]):
+        values = [refs[i][j] for i in range(count)]
+        for out_ref, terms in zip(refs[count:], recipe):
+            out_ref[j] = sum(values[i] * coef_ref[row, j] for i, row in terms)
 
 
 def head_kernel(place_ref, rate_ref, q_ref, local_ref, *refs):
@@ -135,7 +115,7 @@
             high, low = halves(state_ref[j])
             q = q_ref[:, at]
             carried = dot(q, high, NN) + dot(q, low, NN)
-            carried = carried * jnp.exp(-rate_ref[first + j] * pos)
+            carried = carried * jnp.exp(rate_ref[first + j][:, :size] * pos)
             attended = local_ref[:, at] + carried
             scale = lax.rsqrt(jnp.mean(attended * attended, axis=-1, keepdims=True) + 1e-05)
             out_ref[:, at] = (attended * scale).astype(BF16)
@@ -165,9 +145,8 @@
     return lax.dynamic_slice_in_dim(ring, lax.rem(n - first, n) * width, n * width, axis)
 
 
-def gather_doubling(x, axis, count, place):
+def gather_doubling(x, axis, count, place, step=1):
     n = lax.axis_size(axis)
-    step = 1
     while step < count:
         got = lax.ppermute(x, axis, [(d, d ^ step) for d in range(n)])
         upper = (place & step) != 0
@@ -340,35 +319,65 @@
     )
 
 
-def exchange_states(place, rate, mine, theirs, length, deps_one, deps_two):
+def exchange_states(ctx, rate, mine, theirs, length, deps_one, deps_two):
     like = jax.ShapeDtypeStruct(mine.shape, F32)
+    group, member = ctx // 2, lax.rem(ctx, 2)
+    part = mine.shape[0]
+    rates = lax.dynamic_slice(rate, (member * part,), (part,))
+
+    def fade(blocks):
+        return jnp.exp(-rates * (length * blocks))
+
+    one, none = jnp.ones_like(rates), jnp.zeros_like(rates)
+    first = member == 0
+    rows = [
+        jnp.where(first, one, none),
+        jnp.where(first, none, one),
+        jnp.where(first, fade(1.0), one),
+        jnp.where(first, one, fade(1.0)),
+    ]
+    step = 1
+    while step < GROUPS:
+        upper = (group & step) != 0
+        span = fade(2.0 * step)
+        rows += [
+            jnp.where(upper, fade(2.0 * (group & (step - 1)).astype(F32)), none),
+            jnp.where(upper, span, one),
+            jnp.where(upper, one, span),
+        ]
+        step *= 2
+    rows += [
+        jnp.where(first, one, fade(1.0)),
+        jnp.where(first, fade(1.0), one),
+        jnp.where(first, none, one),
+        jnp.where(first, one, none),
+        one,
+    ]
+    size = mine.shape[2]
+    coef = jnp.broadcast_to(jnp.stack(rows)[:, :, None, None], (len(rows), part, 1, size))
+
+    def mix(recipe, values, deps=()):
+        return call(
+            functools.partial(mix_kernel, recipe), [like] * len(recipe), [coef] + values, 0, deps=deps
+        )
+
     got = xor_permute(theirs, 1)
-    early, total = call(
-        functools.partial(pair_kernel, length), [like] * 2, [place, rate, mine, got], 0,
-        specs=[SM, SM, VM, VM],
-    )
-    marks = [total]
-    state, step = [], 1
+    early, total = mix([[(0, 0), (1, 1)], [(0, 2), (1, 3)]], [mine, got])
+    state, step, row = None, 1, 4
     while 2 * step < GROUPS:
-        got = xor_permute(total, 2 * step)
-        state, total = call(
-            functools.partial(scan_kernel, length, step),
-            [like] * 2,
-            [place, rate] + ([state] if step > 1 else []) + [total, got],
-            0,
-            deps=deps_one(marks[-1]),
-            specs=[SM, SM] + [VM] * (3 if step > 1 else 2),
-        )
-        marks.append(total)
-        step *= 2
+        mark, got = total, xor_permute(total, 2 * step)
+        recipe = [[(0, row)], [(0, row + 1), (1, row + 2)]]
+        values = [got, total]
+        if state is not None:
+            recipe[0].append((2, len(rows) - 1))
+            values.append(state)
+        state, total = mix(recipe, values, deps_one(mark, got))
+        step, row = 2 * step, row + 3
     got = lax.ppermute(total, "ctx", [(d, d + 2 * step) for d in range(2 * step)])
-    keep, give = call(
-        functools.partial(final_scan_kernel, length, step),
-        [like] * 2,
-        [place, rate, state, got, early],
-        0,
-        deps=deps_two(marks[-1]),
-        specs=[SM, SM, VM, VM, VM],
+    end = len(rows) - 5
+    final = mix([[(0, len(rows) - 1), (1, row)]], [state, got], deps_two(total))[0]
+    keep, give = mix(
+        [[(0, end), (1, end + 2)], [(0, end + 1), (1, end + 3)]], [final, early]
     )
     return [keep, xor_permute(give, 1)], keep
 
@@ -391,10 +400,17 @@
 
 
 def tie(x, *deps):
-    return call(
-        lambda i, o: None, jax.ShapeDtypeStruct(x.shape, x.dtype), [x], 0,
-        deps=deps, specs=[ANY], out_specs=ANY, input_output_aliases={0: 0},
-    )
+    def copy_kernel(in_ref, out_ref):
+        out_ref[...] = in_ref[...]
+
+    return call(copy_kernel, jax.ShapeDtypeStruct(x.shape, x.dtype), [x], 0, deps=deps)
+
+
+def split_kernel(in_ref, *outs):
+    start = 0
+    for out_ref in outs:
+        out_ref[...] = in_ref[start : start + out_ref.shape[0], :]
+        start += out_ref.shape[0]
 
 
 def per_device(
@@ -427,77 +443,97 @@
     slots = low * n_exp * capacity
 
     cut = out_weight.shape[0] // 2
-    w_top, w_bottom = out_weight[:cut], out_weight[cut:]
-    two_top, two_bottom = xor_permute(w_top, 2 * low), xor_permute(w_bottom, 2 * low)
-    one_top = xor_permute(w_top, low)
+    half_w = jax.ShapeDtypeStruct((cut, cols), BF16)
+
+    def split(*deps):
+        return call(split_kernel, [half_w] * 2, [out_weight], 0, deps=deps)
+
     ids = expert_ids.T
-
-    fresh = call(
-        fresh_kernel,
+    rate = jnp.broadcast_to(-decay_rate[:, None, None], (heads, 1, length))
+
+    wide_b16 = jax.ShapeDtypeStruct((length, here), BF16)
+    outs = (
         [jax.ShapeDtypeStruct((heads // 2, size, size), F32)] * 2
         if pairs
-        else [jax.ShapeDtypeStruct((heads, size, size), F32)],
-        [place, decay_rate, key_rows, value_rows],
+        else [jax.ShapeDtypeStruct((heads, size, size), F32)]
+    )
+    *fresh, keys, values = call(
+        fresh_kernel,
+        outs + [wide_b16] * 2,
+        [place, rate, key_rows, value_rows],
         4 * heads * length * size * size,
         heads * length * size,
-        specs=[SM, SM, VM, VM],
+        specs=[SM, VM, ANY, ANY],
+        scratch_shapes=[pltpu.SemaphoreType.DMA((2 * len(outs),))],
     )
 
     def run_local(*deps):
         return call(
             local_kernel,
-            jax.ShapeDtypeStruct((length, here), F32),
-            [decay_rate, queries, key_rows, value_rows],
+            [jax.ShapeDtypeStruct((length, here), F32), wide_b16],
+            [rate, queries, keys, values],
             4 * heads * length * length * size,
             heads * length * length,
             deps,
-            [SM, VM, VM, VM],
+            [VM, ANY, VM, VM],
+            scratch_shapes=[pltpu.SemaphoreType.DMA(())],
         )
 
     if pairs:
         side = {}
 
-        def deps_one(total):
-            side["ids"] = gather_doubling(ids, "exp", n_exp, exp)
+        def deps_one(total, got):
+            side["ids"] = gather_doubling(ids, "exp", 2, exp)
             side["local"] = run_local(total)
             side["rest"] = within_group(residual)
-            return [side["local"], one_top, side["rest"][1]]
+            side["w"] = split(got)
+            side["one"] = [xor_permute(w, low) for w in side["w"]]
+            return [side["local"][0], side["ids"], side["rest"][1]]
 
         def deps_two(total):
-            side["one_bottom"] = xor_permute(tie(w_bottom, total), low)
-            return [side["ids"], two_top, two_bottom]
+            side["ids"] = gather_doubling(tie(side["ids"], total), "exp", n_exp, exp, 2)
+            return [side["ids"]]
 
         states, kept = exchange_states(
-            place, decay_rate, fresh[0], fresh[1], length, deps_one, deps_two
-        )
-        ids, local, rest_rows, one_bottom = (
-            side["ids"], side["local"], side["rest"], side["one_bottom"]
-        )
-        ids = gather_doubling(tie(ids, kept), "ctx", low, member)
-        three_top = xor_permute(tie(one_top, kept), 2 * low)
-        deps = [ids, one_bottom]
+            ctx, decay_rate, fresh[0], fresh[1], length, deps_one, deps_two
+        )
+        ids, (local, queries_here), rest_rows, one = (
+            side["ids"], side["local"], side["rest"], side["one"]
+        )
+        deps = [one[0]]
     else:
         states = states_by_steps(ctx, decay_rate, fresh[0], length)
-        local, rest_rows = run_local(), within_group(residual)
-        ids = gather_doubling(gather_doubling(ids, "exp", n_exp, exp), "ctx", low, member)
-        one_bottom = xor_permute(w_bottom, low)
-        three_top = xor_permute(one_top, 2 * low)
+        (local, queries_here), rest_rows = run_local(), within_group(residual)
+        ids = gather_doubling(ids, "exp", n_exp, exp)
+        one = [xor_permute(w, low) for w in split()]
         deps = []
 
     head_out = call(
         head_kernel,
-        jax.ShapeDtypeStruct((length, here), BF16),
-        [place, decay_rate, queries, local] + states,
+        wide_b16,
+        [place, rate, queries_here, local] + states,
         4 * heads * length * size * size,
         heads * length * size,
         deps,
-        [SM, SM] + [VM] * (2 + len(states)),
+        [SM] + [VM] * (3 + len(states)),
     )
     group_heads = within_group(head_out)
-    three_bottom = xor_permute(tie(two_bottom, head_out), low)
-    columns = [
-        [out_weight], [one_top, one_bottom], [two_top, two_bottom], [three_top, three_bottom]
-    ]
+
+    w_top, w_bottom = split(head_out)
+    two = [xor_permute(w_top, 2 * low), None]
+    columns = [[out_weight], one, two, [None, None]]
+    ids = gather_doubling(tie(ids, head_out), "ctx", low, member)
+    pins = {}
+
+    def after_kernel(name, t, out):
+        if (name, t) == ("project", 0):
+            pins["add", 0] = [two[0], ids]
+            two[1] = xor_permute(tie(w_bottom, out), 2 * low)
+        if (name, t) == ("add", 0):
+            columns[3][0] = xor_permute(tie(one[0], out), 2 * low)
+        if (name, t) == ("project", 2):
+            pins["dispatch", 0] = [columns[3][0]]
+            columns[3][1] = xor_permute(tie(two[1], out), low)
 
     named = (ids[0] == exp) | (ids[1] == exp)
     token = jnp.arange(every, dtype=jnp.int32)
@@ -531,17 +567,24 @@
             [chunk_f32, chunk_b16],
             [place] + group_heads + columns[t] + rests[t],
             2 * every * here * cols,
-            deps=last[:],
+            deps=last[:] + (one[1:] if t == 0 else []),
             specs=[SM] + [VM] * (2 * low + len(columns[t])),
         )
         last[:] = [sent]
+        after_kernel("project", t, sent)
         for hop in range(half - 1):
             got = lax.ppermute(sent, "exp", [(hop, hop + 1), (n_exp - 1 - hop, n_exp - 2 - hop)])
             yield
             part, sent = call(
-                add_kernel, [chunk_f32, chunk_b16], [part, got], every * cols, deps=last[:]
+                add_kernel,
+                [chunk_f32, chunk_b16],
+                [part, got],
+                every * cols,
+                deps=last[:] + (pins.get(("add", t), []) if hop == 0 else []),
             )
             last[:] = [sent]
+            if hop == 0:
+                after_kernel("add", t, sent)
         got = lax.ppermute(sent, "exp", [(half - 1, half), (half, half - 1)])
         yield
         total = call(add_kernel, chunk_b16, [part, got], every * cols, deps=last[:])
@@ -564,32 +607,34 @@
             outs,
             [place, got] + known + [total, gains[t], picks],
             2 * slots * every * wide,
-            deps=last[:] + (links[t - 1] or [] if t > 0 else []),
+            deps=last[:] + (links[t - 1] if t > 0 else []) + pins.get(("dispatch", t), []),
             specs=[SM] + [VM] * (len(known) + 4),
         )
         last[:] = [x]
-        one, two = xor_permute(x, low), xor_permute(x, 2 * low)
+        near, far = xor_permute(x, low), xor_permute(x, 2 * low)
         got = [within_group(x)]
-        links[t] = [one, two]
+        links[t] = [near, far]
         yield
-        three = xor_permute(one, 2 * low) if t % 2 == 0 else xor_permute(two, low)
-        got += [within_group(one), within_group(two)]
-        if final:
-            last[:] = last[:] + [one, two]
+        if t % 2 == 0:
+            diagonal = xor_permute(tie(near, *last) if t > 1 else near, 2 * low)
+        else:
+            diagonal = xor_permute(tie(far, *last) if t > 1 else far, low)
+        got += [within_group(near), within_group(far)]
+        received[t] = [in_columns(per, t) for per in got]
         yield
-        got += [within_group(three)]
-        if final:
-            last[:] = last[:] + [three]
-        if not aligned:
-            joined = []
-            for per in got:
-                whole = in_order([y[:, :cols] for y in per], member, 1)
-                if final:
-                    whole = jnp.concatenate([whole] + [y[:, wide - 128 :] for y in per], axis=1)
-                joined.append([whole])
-            got = joined
-        received[t] = got
+        experts(t, everyone[:-1])
+        received[t].append(in_columns(within_group(tie(diagonal, *last)), t))
         yield
+        experts(t, everyone[-1:])
+        yield
+
+    def in_columns(per, t):
+        if aligned:
+            return per
+        whole = in_order([y[:, :cols] for y in per], member, 1)
+        if t == GROUPS - 1:
+            whole = jnp.concatenate([whole] + [y[:, -128:] for y in per], axis=1)
+        return [whole]
 
     def experts(t, spans):
         nonlocal hidden
@@ -600,23 +645,19 @@
         )
         if final:
             hidden = out
-            last[:] = []
         else:
             for n, s in enumerate(spans):
                 sums[s] = out[2 * n : 2 * n + 2]
             last[:] = [out[0]]
 
-    running, waiting = [], list(range(GROUPS))
     everyone = list(range(GROUPS))
-    done = []
+    running, waiting = [], everyone[:]
     while running or waiting:
         if waiting:
-            running.insert(0, (waiting[0], chunk(waiting.pop(0))))
-        for t, work in list(running):
+            running.insert(0, chunk(waiting.pop(0)))
+        for work in list(running):
             if next(work, "end") == "end":
-                running.remove((t, work))
-                if t < GROUPS - 1:
-                    experts(t, everyone)
+                running.remove(work)
 
     own = exp * tokens
     gotten = []
@@ -639,10 +680,8 @@
             jax.ShapeDtypeStruct((tokens, model), BF16),
             [place] + mixed + gotten,
             0,
-            deps=last[:],
             specs=[SM] + [VM] * (GROUPS + low - 1),
         )
-        last[:] = [mixed_out]
     else:
         rows = [lax.dynamic_slice_in_dim(m, member * length + own, tokens, 0) for m in mixed]
         parts = [jnp.concatenate(rows, axis=1)] + gotten
@@ -653,8 +692,6 @@
                 mixed_out = lax.dynamic_update_slice_in_dim(
                     mixed_out, part[:, t * cols : (t + 1) * cols], start, 1
                 )
-    experts(GROUPS - 1, everyone[:-1])
-    experts(GROUPS - 1, everyone[-1:])
     return (mixed_out, hidden[None])
 
 

time: 170 us -> 169 us (level)
  waiting for transfers between devices: 55.4 us -> 39.7 us
  starting transfers between devices: 52.5 us -> 60.1 us
  Pallas kernels: 42.6 us -> 47.6 us
  other arithmetic: 0.52 us -> 2.74 us
    ppermute x21, starting transfers between devices: 15.1 us -> 22.9 us  [xor_permute(): return lax.ppermute(x, 'ctx', [(d, d ^ step) for d in range(n)])]
    ppermute x21, waiting for transfers between devices: 35.9 us -> 28.2 us  [xor_permute(): return lax.ppermute(x, 'ctx', [(d, d ^ step) for d in range(n)])]
    ppermute x4, waiting for transfers between devices: 9.42 us -> 3.86 us  [chunk(): got = lax.ppermute(total, 'exp', [(here_, here_ - 1), (there, there + 1)])]
    pallas_call x32 -> x45, Pallas kernels: 42.6 us -> 47.6 us  [call(): pl.pallas_call(body, out_shape=out_shape, in_specs=list(specs or [VM] * c...]
    ppermute x4, waiting for transfers between devices: 6.15 us -> 3.49 us  [chunk(): lax.ppermute(sent, 'exp', [(hop, hop + 1), (n_exp - 1 - hop, n_exp - 2 -...]
    slice x1 -> x0, local copies, waits for them, and re-layouts: 2.07 us -> none  [per_device(): w_top, w_bottom = (out_weight[:cut], out_weight[cut:])]
    unnamed x48 -> x38, local copies, waits for them, and re-layouts: 12.9 us -> 12.5 us
  transfers between devices with their start and end apart: 56 -> 56, of which waited for: 19 -> 17; matrix products, arithmetic and copies ran while one was open for 3% -> 3% of each run, Pallas kernels for 21% -> 24%
where the time goes in v4:
time: 169 us; the launch traced here: 168 us
  starting transfers between devices  60.1 us (36%)
  Pallas kernels  47.6 us (28%)
  waiting for transfers between devices  39.7 us (23%)
  local copies, waits for them, and re-layouts  15.9 us (9%)
  other arithmetic  2.74 us (2%)
    pallas_call x45, Pallas kernels, call(): pl.pallas_call(body, out_shape=out_shape, in_specs=list(specs or [VM] * c...  47.6 us
    ppermute x21, waiting for transfers between devices, xor_permute(): return lax.ppermute(x, 'ctx', [(d, d ^ step) for d in range(n)])  28.2 us
    ppermute x21, starting transfers between devices, xor_permute(): return lax.ppermute(x, 'ctx', [(d, d ^ step) for d in range(n)])  22.9 us
    ppermute x4, starting transfers between devices, chunk(): lax.ppermute(sent, 'exp', [(hop, hop + 1), (n_exp - 1 - hop, n_exp - 2 -...  16.9 us
    unnamed x38, local copies, waits for them, and re-layouts  12.5 us
    ppermute x4, starting transfers between devices, chunk(): got = lax.ppermute(total, 'exp', [(here_, here_ - 1), (there, there + 1)])  5.61 us
    ppermute x3, starting transfers between devices, gather_doubling(): got = lax.ppermute(x, axis, [(d, d ^ step) for d in range(n)])  4.18 us
    ppermute x1, starting transfers between devices, exchange_states(): lax.ppermute(total, 'ctx', [(d, d + 2 * step) for d in range(2 * step)])  4.12 us
  transfers between devices with their start and end apart: 56, of which 17 were waited for; matrix products, arithmetic and copies ran while one was open for 3% of the time, Pallas kernels for 24%

profile of v4, /device:TPU:0, one launch (start us, length us, event | category | flops | bytes accessed | tf_op | source)
XLA Modules:
  0.0 167.6 jit_solution(5007382464961256615)
XLA Ops:
  1.5 1.0 copy-done.8
  2.6 1.0 copy-done.9
  3.6 1.4 shard_map.113
  8.4 3.2 %collective-permute-start.1 = (f32[4,128,128]{2,1,0:T(8,128)S(1)}, f32[4,128,128]{2,1,0:T(8,128)S(1)}, u32[]{:S(2)}, u32[]{:S(2)}) collective-permute-start(f32[4,128,128]{2,1,0:T(8,128)S(1)} %get-tuple-element.71.refs_4_.refs_2_), channel_id=1, source_target_pairs={{0,8},{4,12},{8,0},{12,4},{16,24},{20,28},{24,16},{28,20},{1,9},{5... | collective-permute-start | bytes 786440 | tf_op jit(solution)/shard_map/ppermute | solution.py:126
  11.6 1.6 collective-permute-start.2
  13.1 2.2 %collective-permute-done.2 = s32[2,64]{1,0:T(2,128)S(1)} collective-permute-done((s32[2,64]{1,0:T(2,128)}, s32[2,64]{1,0:T(2,128)S(1)}, u32[]{:S(2)}, u32[]{:S(2)}) %collective-permute-start.2) | collective-permute-done | bytes 544 | tf_op jit(solution)/shard_map/ppermute | solution.py:151
  16.2 1.0 copy-done.3
  17.2 1.0 copy-done.5
  18.3 1.1 shard_map.115
  20.9 4.1 %collective-permute-start.4 = (f32[4,128,128]{2,1,0:T(8,128)}, f32[4,128,128]{2,1,0:T(8,128)}, u32[]{:S(2)}, u32[]{:S(2)}) collective-permute-start(f32[4,128,128]{2,1,0:T(8,128)} %get-tuple-element.75.refs_1_), channel_id=1, source_target_pairs={{0,16},{4,20},{8,24},{12,28},{1,17},{5,21},{9,25},{13,29},{2,18},{... | collective-permute-start | bytes 786440 | tf_op jit(solution)/shard_map/ppermute | solution.py:376
  25.1 1.0 shard_map.120
  26.6 2.6 %collective-permute-start.5 = (s32[2,128]{1,0:T(2,128)S(1)}, s32[2,128]{1,0:T(2,128)S(1)}, u32[]{:S(2)}, u32[]{:S(2)}) collective-permute-start(s32[2,128]{1,0:T(2,128)S(1)} %shard_map.117), channel_id=1, source_target_pairs={{0,2},{1,3},{2,0},{3,1},{4,6},{5,7},{6,4},{7,5},{8,10},{9,11},{10,... | collective-permute-start | bytes 3080 | tf_op jit(solution)/shard_map/ppermute | solution.py:151
  29.2 1.9 %collective-permute-done.5 = s32[2,128]{1,0:T(2,128)S(1)} collective-permute-done((s32[2,128]{1,0:T(2,128)S(1)}, s32[2,128]{1,0:T(2,128)S(1)}, u32[]{:S(2)}, u32[]{:S(2)}) %collective-permute-start.5) | collective-permute-done | bytes 1056 | tf_op jit(solution)/shard_map/ppermute | solution.py:151
  31.1 0.9 copy-done.11
  32.0 1.0 shard_map.118.refs_1_
  34.1 1.9 %collective-permute-done.7.refs_6_.refs_3_.refs_0_ = bf16[512,384]{1,0:T(8,128)(2,1)S(1)} collective-permute-done((bf16[512,384]{1,0:T(8,128)(2,1)}, bf16[512,384]{1,0:T(8,128)(2,1)S(1)}, u32[]{:S(2)}, u32[]{:S(2)}) %collective-permute-start.7) | collective-permute-done | bytes 393248 | tf_op jit(solution)/shard_map/ppermute | solution.py:126
  36.0 1.0 copy-done.7
  37.1 1.2 shard_map.121.refs_1_.refs_6_
  38.4 1.2 collective-permute-start.9
  39.6 1.5 constant_dynamic-slice_fusion.1
  41.2 1.5 constant_dynamic-slice_fusion
  43.5 6.6 %collective-permute-done.9.refs_7_.refs_4_ = bf16[512,384]{1,0:T(8,128)(2,1)S(1)} collective-permute-done((bf16[512,384]{1,0:T(8,128)(2,1)}, bf16[512,384]{1,0:T(8,128)(2,1)S(1)}, u32[]{:S(2)}, u32[]{:S(2)}) %collective-permute-start.9) | collective-permute-done | bytes 393248 | tf_op jit(solution)/shard_map/ppermute | solution.py:126
  50.1 2.0 %shard_map.122 = (f32[512,384]{1,0:T(8,128)S(1)}, bf16[512,384]{1,0:T(8,128)(2,1)}) custom-call(s32[3]{0:T(128)S(1)} %pad_add_fusion.refs_0_, bf16[256,1024]{1,0:T(8,128)(2,1)S(1)} %shard_map.121.refs_1_.refs_6_, bf16[256,1024]{1,0:T(8,128)(2,1)S(1)} %collective-permute-done.8.refs_2_, bf16[1024,384]{1,0:T(8,128)(2,1)S(1)} %copy-done.2, ...), custom_call_target="tpu_custom_call" | custom-call | flops 402653184 | bytes 3112972 | tf_op jit(solution)/shard_map/pallas_call | solution.py:36
  52.2 4.3 %collective-permute-start.10 = (bf16[512,384]{1,0:T(8,128)(2,1)}, bf16[512,384]{1,0:T(8,128)(2,1)}, u32[]{:S(2)}, u32[]{:S(2)}) collective-permute-start(bf16[512,384]{1,0:T(8,128)(2,1)} %get-tuple-element.82.refs_7_.refs_1_), channel_id=1, source_target_pairs={{0,1},{3,2},{4,5},{7,6},{8,9},{11,10},{12,13},{15,14},{16,17},{19,... | collective-permute-start | bytes 1179656 | tf_op jit(solution)/shard_map/ppermute | solution.py:576
  59.3 1.3 shard_map.123
  60.6 1.3 collective-permute-start.14
  62.0 3.5 %collective-permute-done.10.refs_1_ = bf16[512,384]{1,0:T(8,128)(2,1)} collective-permute-done((bf16[512,384]{1,0:T(8,128)(2,1)}, bf16[512,384]{1,0:T(8,128)(2,1)}, u32[]{:S(2)}, u32[]{:S(2)}) %collective-permute-start.10) | collective-permute-done | bytes 393248 | tf_op jit(solution)/shard_map/ppermute | solution.py:576
  65.5 1.1 shard_map.126
  69.7 1.8 %shard_map.128 = (f32[512,384]{1,0:T(8,128)S(1)}, bf16[512,384]{1,0:T(8,128)(2,1)S(1)}) custom-call(s32[3]{0:T(128)S(1)} %pad_add_fusion.refs_0_, bf16[256,1024]{1,0:T(8,128)(2,1)S(1)} %shard_map.121.refs_1_.refs_6_, bf16[256,1024]{1,0:T(8,128)(2,1)S(1)} %collective-permute-done.8.refs_2_, bf16[512,384]{1,0:T(8,128)(2,1)} %collective-permute-done.11.refs_3_, ...), custom_call_target="tpu_custom_call" | custom-call | flops 402653184 | bytes 3112972 | tf_op jit(solution)/shard_map/pallas_call | solution.py:36
  71.5 1.2 collective-permute-start.20
  72.7 6.5 %collective-permute-start.18 = (bf16[512,384]{1,0:T(8,128)(2,1)S(1)}, bf16[512,384]{1,0:T(8,128)(2,1)S(1)}, u32[]{:S(2)}, u32[]{:S(2)}) collective-permute-start(bf16[512,384]{1,0:T(8,128)(2,1)S(1)} %get-tuple-element.89.refs_2_.refs_1_), channel_id=1, source_target_pairs={{0,1},{3,2},{4,5},{7,6},{8,9},{11,10},{12,13},{15,14},{16,17},{19,... | collective-permute-start | bytes 1179656 | tf_op jit(solution)/shard_map/ppermute | solution.py:576
  80.4 1.3 collective-permute-start.16
  81.7 1.3 shard_map.133
  83.0 4.8 %collective-permute-start.23 = (bf16[512,384]{1,0:T(8,128)(2,1)S(1)}, bf16[512,384]{1,0:T(8,128)(2,1)S(1)}, u32[]{:S(2)}, u32[]{:S(2)}) collective-permute-start(bf16[512,384]{1,0:T(8,128)(2,1)S(1)} %get-tuple-element.93.refs_2_), channel_id=1, source_target_pairs={{0,1},{3,2},{4,5},{7,6},{8,9},{11,10},{12,13},{15,14},{16,17},{19,... | collective-permute-start | bytes 1179656 | tf_op jit(solution)/shard_map/ppermute | solution.py:576
  88.8 1.3 collective-permute-start.21
  91.6 1.2 collective-permute-start.24
  92.8 2.2 %collective-permute-start.25 = (bf16[384,384]{1,0:T(8,128)(2,1)S(1)}, bf16[384,384]{1,0:T(8,128)(2,1)S(1)}, u32[]{:S(2)}, u32[]{:S(2)}) collective-permute-start(bf16[384,384]{1,0:T(8,128)(2,1)S(1)} %get-tuple-element.98.refs_2_.refs_3_), channel_id=1, source_target_pairs={{0,16},{4,20},{8,24},{12,28},{16,0},{20,4},{24,8},{28,12},{1,17},{... | collective-permute-start | bytes 884744 | tf_op jit(solution)/shard_map/ppermute | solution.py:126
  95.9 1.6 collective-permute-start.26
  97.5 3.0 %collective-permute-done.21.refs_1_ = bf16[512,384]{1,0:T(8,128)(2,1)S(1)} collective-permute-done((bf16[512,384]{1,0:T(8,128)(2,1)S(1)}, bf16[512,384]{1,0:T(8,128)(2,1)S(1)}, u32[]{:S(2)}, u32[]{:S(2)}) %collective-permute-start.21) | collective-permute-done | bytes 393248 | tf_op jit(solution)/shard_map/ppermute | solution.py:597
  100.5 1.0 shard_map.139
  101.4 1.2 collective-permute-start.28
  102.7 2.3 %collective-permute-start.29 = (bf16[384,384]{1,0:T(8,128)(2,1)S(1)}, bf16[384,384]{1,0:T(8,128)(2,1)S(1)}, u32[]{:S(2)}, u32[]{:S(2)}) collective-permute-start(bf16[384,384]{1,0:T(8,128)(2,1)S(1)} %get-tuple-element.102.refs_2_.refs_3_), channel_id=1, source_target_pairs={{0,16},{4,20},{8,24},{12,28},{16,0},{20,4},{24,8},{28,12},{1,17},{... | collective-permute-start | bytes 884744 | tf_op jit(solution)/shard_map/ppermute | solution.py:126
  105.1 1.5 collective-permute-start.30
  107.1 1.1 collective-permute-done.28.refs_6_.refs_5_
  108.2 1.4 collective-permute-done.29.refs_7_
  109.7 2.0 %collective-permute-start.38 = (bf16[384,384]{1,0:T(8,128)(2,1)S(1)}, bf16[384,384]{1,0:T(8,128)(2,1)S(1)}, u32[]{:S(2)}, u32[]{:S(2)}) collective-permute-start(bf16[384,384]{1,0:T(8,128)(2,1)S(1)} %collective-permute-done.24.refs_6_.refs_5_), channel_id=1, source_target_pairs={{0,16},{4,20},{8,24},{12,28},{16,0},{20,4},{24,8},{28,12},{1,17},{... | collective-permute-start | bytes 884744 | tf_op jit(solution)/shard_map/ppermute | solution.py:126
  112.7 1.4 collective-permute-start.34
  114.1 5.4 %collective-permute-done.38.refs_0_ = bf16[384,384]{1,0:T(8,128)(2,1)S(1)} collective-permute-done((bf16[384,384]{1,0:T(8,128)(2,1)S(1)}, bf16[384,384]{1,0:T(8,128)(2,1)S(1)}, u32[]{:S(2)}, u32[]{:S(2)}) %collective-permute-start.38) | collective-permute-done | bytes 294944 | tf_op jit(solution)/shard_map/ppermute | solution.py:126
  120.1 1.1 collective-permute-done.34.refs_9_.refs_5_.refs_0_
  121.9 3.5 %shard_map.142 = (f32[576,384]{1,0:T(8,128)S(1)}, f32[576,384]{1,0:T(8,128)S(1)}, f32[576,384]{1,0:T(8,128)S(1)}, f32[576,384]{1,0:T(8,128)S(1)}, f32[576,384]{1,0:T(8,128)S(1)}, /*index=5*/f32[576,384]{1,0:T(8,128)S(1)}) custom-call(s32[3]{0:T(128)S(1)} %pad_add_fusion.refs_0_, bf16[576,3072]{1,0:T(8,128)(2,1)S(1)} %bitcast.25, ...), custom_call_target="tpu_custom_call" | custom-call | flops 2038431744 | bytes 14155788 | tf_op jit(solution)/shard_map/pallas_call | solution.py:36
  125.5 1.3 shard_map.143
  126.9 1.6 collective-permute-start.37
  128.8 3.6 %shard_map.146 = (f32[576,384]{1,0:T(8,128)S(1)}, f32[576,384]{1,0:T(8,128)S(1)}, f32[576,384]{1,0:T(8,128)S(1)}, f32[576,384]{1,0:T(8,128)S(1)}, f32[576,384]{1,0:T(8,128)S(1)}, /*index=5*/f32[576,384]{1,0:T(8,128)S(1)}) custom-call(s32[3]{0:T(128)S(1)} %pad_add_fusion.refs_0_, bf16[576,3072]{1,0:T(8,128)(2,1)S(1)} %bitcast.26, ...), custom_call_target="tpu_custom_call" | custom-call | flops 2038431744 | bytes 19464204 | tf_op jit(solution)/shard_map/pallas_call | solution.py:36
  134.0 4.5 %collective-permute-done.37.refs_0_.refs_7_ = bf16[384,512]{1,0:T(8,128)(2,1)S(1)} collective-permute-done((bf16[384,512]{1,0:T(8,128)(2,1)S(1)}, bf16[384,512]{1,0:T(8,128)(2,1)S(1)}, u32[]{:S(2)}, u32[]{:S(2)}) %collective-permute-start.37) | collective-permute-done | bytes 393248 | tf_op jit(solution)/shard_map/ppermute | solution.py:126
  138.5 1.6 collective-permute-start.50
  140.1 1.7 %shard_map.147 = (f32[576,384]{1,0:T(8,128)S(1)}, f32[576,384]{1,0:T(8,128)S(1)}) custom-call(s32[3]{0:T(128)S(1)} %pad_add_fusion.refs_0_, bf16[576,3072]{1,0:T(8,128)(2,1)S(1)} %bitcast.27, bf16[576,3072]{1,0:T(8,128)(2,1)S(1)} %bitcast.35, bf16[384,384]{1,0:T(8,128)(2,1)S(1)} %shard_map.145.refs_3_, bf16[384,384]{1,0:T(8,128)(2,1)S(1)} %collective-permute-done.39.refs_4_, ...), custom_call_target="tpu_custom_call" | custom-call | flops 679477248 | bytes 9437196 | tf_op jit(solution)/shard_map/pallas_call | solution.py:36
  143.1 4.0 %collective-permute-done.50.refs_0_ = bf16[384,384]{1,0:T(8,128)(2,1)S(1)} collective-permute-done((bf16[384,384]{1,0:T(8,128)(2,1)S(1)}, bf16[384,384]{1,0:T(8,128)(2,1)S(1)}, u32[]{:S(2)}, u32[]{:S(2)}) %collective-permute-start.50) | collective-permute-done | bytes 294944 | tf_op jit(solution)/shard_map/ppermute | solution.py:126
  147.6 3.6 %shard_map.150 = (f32[576,384]{1,0:T(8,128)S(1)}, f32[576,384]{1,0:T(8,128)S(1)}, f32[576,384]{1,0:T(8,128)S(1)}, f32[576,384]{1,0:T(8,128)S(1)}, f32[576,384]{1,0:T(8,128)S(1)}, /*index=5*/f32[576,384]{1,0:T(8,128)S(1)}) custom-call(s32[3]{0:T(128)S(1)} %pad_add_fusion.refs_0_, bf16[576,3072]{1,0:T(8,128)(2,1)S(1)} %bitcast.28, ...), custom_call_target="tpu_custom_call" | custom-call | flops 2038431744 | bytes 19464204 | tf_op jit(solution)/shard_map/pallas_call | solution.py:36
  151.2 1.2 collective-permute-done.43.refs_0_
  152.4 1.7 %shard_map.151 = (f32[576,384]{1,0:T(8,128)S(1)}, f32[576,384]{1,0:T(8,128)S(1)}) custom-call(s32[3]{0:T(128)S(1)} %pad_add_fusion.refs_0_, bf16[576,3072]{1,0:T(8,128)(2,1)S(1)} %bitcast.29, bf16[576,3072]{1,0:T(8,128)(2,1)S(1)} %bitcast.37, bf16[384,384]{1,0:T(8,128)(2,1)S(1)} %shard_map.149.refs_3_, bf16[384,384]{1,0:T(8,128)(2,1)S(1)} %collective-permute-done.45.refs_4_, ...), custom_call_target="tpu_custom_call" | custom-call | flops 679477248 | bytes 11206668 | tf_op jit(solution)/shard_map/pallas_call | solution.py:36
  154.8 1.3 shard_map.144
  156.1 1.9 %shard_map.155 = (f32[576,384]{1,0:T(8,128)S(1)}, f32[576,384]{1,0:T(8,128)S(1)}) custom-call(s32[3]{0:T(128)S(1)} %pad_add_fusion.refs_0_, bf16[576,3072]{1,0:T(8,128)(2,1)S(1)} %bitcast.30, bf16[576,3072]{1,0:T(8,128)(2,1)S(1)} %bitcast.38, bf16[384,384]{1,0:T(8,128)(2,1)S(1)} %shard_map.154.refs_3_, bf16[384,384]{1,0:T(8,128)(2,1)S(1)} %collective-permute-done.51.refs_4_, ...), custom_call_target="tpu_custom_call" | custom-call | flops 679477248 | bytes 11206668 | tf_op jit(solution)/shard_map/pallas_call | solution.py:36
  158.1 6.3 %shard_map.156.refs_7_ = bf16[576,1536]{1,0:T(8,128)(2,1)} custom-call(s32[3]{0:T(128)S(1)} %pad_add_fusion.refs_0_, bf16[576,3072]{1,0:T(8,128)(2,1)S(1)} %bitcast.31, bf16[576,3072]{1,0:T(8,128)(2,1)S(1)} %bitcast.39, bf16[384,512]{1,0:T(8,128)(2,1)S(1)} %get-tuple-element.108.refs_15_.refs_1_.refs_3_, ...), custom_call_target="tpu_custom_call" | custom-call | flops 2038431744 | bytes 16515084 | tf_op jit(solution)/shard_map/pallas_call | solution.py:36
  164.3 3.1 %shard_map.157 = bf16[576,1536]{1,0:T(8,128)(2,1)} custom-call(s32[3]{0:T(128)S(1)} %pad_add_fusion.refs_0_, bf16[576,3072]{1,0:T(8,128)(2,1)S(1)} %bitcast.32, bf16[576,3072]{1,0:T(8,128)(2,1)S(1)} %bitcast.40, bf16[384,512]{1,0:T(8,128)(2,1)S(1)} %shard_map.152.refs_3_, ...), custom_call_target="tpu_custom_call", output_to_operand_aliasing={{}: (7, {})} | custom-call | flops 679477248 | bytes 13172748 | tf_op jit(solution)/shard_map/pallas_call | solution.py:36
  (156 shorter events, 27.0 us)
Async XLA Ops:
  0.6 24.4 %copy-start.2 = (bf16[1024,384]{1,0:T(8,128)(2,1)S(1)}, bf16[1024,384]{1,0:T(8,128)(2,1)}, u32[]{:S(2)}) copy-start(bf16[1024,384]{1,0:T(8,128)(2,1)} %refs_0_.3) | copy-start | bytes 2359300
  1.5 1.0 copy-start.8
  5.8 1.6 collective-permute-start
  6.3 13.1 %collective-permute-start.3 = (bf16[64,3072]{1,0:T(8,128)(2,1)}, bf16[64,3072]{1,0:T(8,128)(2,1)}, u32[]{:S(2)}, u32[]{:S(2)}) collective-permute-start(bf16[64,3072]{1,0:T(8,128)(2,1)} %param.15), channel_id=1, source_target_pairs={{0,4},{4,0},{8,12},{12,8},{16,20},{20,16},{24,28},{28,24},{1,5},{5... | collective-permute-start | bytes 1179656 | tf_op jit(solution)/shard_map/ppermute | solution.py:135
  8.4 11.0 %collective-permute-start.1 = (f32[4,128,128]{2,1,0:T(8,128)S(1)}, f32[4,128,128]{2,1,0:T(8,128)S(1)}, u32[]{:S(2)}, u32[]{:S(2)}) collective-permute-start(f32[4,128,128]{2,1,0:T(8,128)S(1)} %get-tuple-element.71.refs_4_.refs_2_), channel_id=1, source_target_pairs={{0,8},{4,12},{8,0},{12,4},{16,24},{20,28},{24,16},{28,20},{1,9},{5... | collective-permute-start | bytes 786440 | tf_op jit(solution)/shard_map/ppermute | solution.py:126
  11.6 3.8 %collective-permute-start.2 = (s32[2,64]{1,0:T(2,128)}, s32[2,64]{1,0:T(2,128)S(1)}, u32[]{:S(2)}, u32[]{:S(2)}) collective-permute-start(s32[2,64]{1,0:T(2,128)} %bitcast.44), channel_id=1, source_target_pairs={{0,1},{1,0},{2,3},{3,2},{4,5},{5,4},{6,7},{7,6},{8,9},{9,8},{10,11... | collective-permute-start | bytes 1544 | tf_op jit(solution)/shard_map/ppermute | solution.py:151
  16.2 1.0 copy-start.3
  19.4 6.7 %copy-start.6 = (bf16[256,1024]{1,0:T(8,128)(2,1)}, bf16[256,1024]{1,0:T(8,128)(2,1)S(1)}, u32[]{:S(2)}) copy-start(bf16[256,1024]{1,0:T(8,128)(2,1)S(1)} %get-tuple-element.72.refs_2_) | copy-start | bytes 1572868
  20.9 10.1 %collective-permute-start.4 = (f32[4,128,128]{2,1,0:T(8,128)}, f32[4,128,128]{2,1,0:T(8,128)}, u32[]{:S(2)}, u32[]{:S(2)}) collective-permute-start(f32[4,128,128]{2,1,0:T(8,128)} %get-tuple-element.75.refs_1_), channel_id=1, source_target_pairs={{0,16},{4,20},{8,24},{12,28},{1,17},{5,21},{9,25},{13,29},{2,18},{... | collective-permute-start | bytes 786440 | tf_op jit(solution)/shard_map/ppermute | solution.py:376
  26.1 10.0 %collective-permute-start.7 = (bf16[512,384]{1,0:T(8,128)(2,1)}, bf16[512,384]{1,0:T(8,128)(2,1)S(1)}, u32[]{:S(2)}, u32[]{:S(2)}) collective-permute-start(bf16[512,384]{1,0:T(8,128)(2,1)} %get-tuple-element.79), channel_id=1, source_target_pairs={{0,8},{4,12},{8,0},{12,4},{16,24},{20,28},{24,16},{28,20},{1,9},{5... | collective-permute-start | bytes 1179656 | tf_op jit(solution)/shard_map/ppermute | solution.py:126
  26.6 4.5 %collective-permute-start.5 = (s32[2,128]{1,0:T(2,128)S(1)}, s32[2,128]{1,0:T(2,128)S(1)}, u32[]{:S(2)}, u32[]{:S(2)}) collective-permute-start(s32[2,128]{1,0:T(2,128)S(1)} %shard_map.117), channel_id=1, source_target_pairs={{0,2},{1,3},{2,0},{3,1},{4,6},{5,7},{6,4},{7,5},{8,10},{9,11},{10,... | collective-permute-start | bytes 3080 | tf_op jit(solution)/shard_map/ppermute | solution.py:151
  34.0 2.0 %collective-permute-start.6 = (f32[4,128,128]{2,1,0:T(8,128)S(1)}, f32[4,128,128]{2,1,0:T(8,128)S(1)}, u32[]{:S(2)}, u32[]{:S(2)}) collective-permute-start(f32[4,128,128]{2,1,0:T(8,128)S(1)} %get-tuple-element.78), channel_id=1, source_target_pairs={{0,4},{4,0},{8,12},{12,8},{16,20},{20,16},{24,28},{28,24},{1,5},{5... | collective-permute-start | bytes 786440 | tf_op jit(solution)/shard_map/ppermute | solution.py:126
  36.0 1.0 copy-start.7
  38.3 19.3 %copy-start.18 = (f32[3072]{0:T(1024)S(1)}, f32[3072]{0:T(1024)}, u32[]{:S(2)}) copy-start(f32[3072]{0:T(1024)} %param.16) | copy-start | bytes 36868
  38.3 11.8 %collective-permute-start.8 = (bf16[256,1024]{1,0:T(8,128)(2,1)S(1)}, bf16[256,1024]{1,0:T(8,128)(2,1)S(1)}, u32[]{:S(2)}, u32[]{:S(2)}) collective-permute-start(bf16[256,1024]{1,0:T(8,128)(2,1)S(1)} %shard_map.121.refs_1_.refs_6_), channel_id=1, source_target_pairs={{0,4},{4,0},{8,12},{12,8},{16,20},{20,16},{24,28},{28,24},{1,5},{5... | collective-permute-start | bytes 1572872 | tf_op jit(solution)/shard_map/ppermute | solution.py:135
  38.4 11.7 %collective-permute-start.9 = (bf16[512,384]{1,0:T(8,128)(2,1)}, bf16[512,384]{1,0:T(8,128)(2,1)S(1)}, u32[]{:S(2)}, u32[]{:S(2)}) collective-permute-start(bf16[512,384]{1,0:T(8,128)(2,1)} %get-tuple-element.80), channel_id=1, source_target_pairs={{0,8},{4,12},{8,0},{12,4},{16,24},{20,28},{24,16},{28,20},{1,9},{5... | collective-permute-start | bytes 1179656 | tf_op jit(solution)/shard_map/ppermute | solution.py:126
  43.5 18.5 %collective-permute-start.11 = (bf16[512,384]{1,0:T(8,128)(2,1)}, bf16[512,384]{1,0:T(8,128)(2,1)}, u32[]{:S(2)}, u32[]{:S(2)}) collective-permute-start(bf16[512,384]{1,0:T(8,128)(2,1)} %get-tuple-element.84), channel_id=1, source_target_pairs={{0,16},{4,20},{8,24},{12,28},{16,0},{20,4},{24,8},{28,12},{1,17},{... | collective-permute-start | bytes 1179656 | tf_op jit(solution)/shard_map/ppermute | solution.py:126
  52.2 13.3 %collective-permute-start.10 = (bf16[512,384]{1,0:T(8,128)(2,1)}, bf16[512,384]{1,0:T(8,128)(2,1)}, u32[]{:S(2)}, u32[]{:S(2)}) collective-permute-start(bf16[512,384]{1,0:T(8,128)(2,1)} %get-tuple-element.82.refs_7_.refs_1_), channel_id=1, source_target_pairs={{0,1},{3,2},{4,5},{7,6},{8,9},{11,10},{12,13},{15,14},{16,17},{19,... | collective-permute-start | bytes 1179656 | tf_op jit(solution)/shard_map/ppermute | solution.py:576
  57.2 10.9 %collective-permute-start.15 = (bf16[512,384]{1,0:T(8,128)(2,1)}, bf16[512,384]{1,0:T(8,128)(2,1)S(1)}, u32[]{:S(2)}, u32[]{:S(2)}) collective-permute-start(bf16[512,384]{1,0:T(8,128)(2,1)} %shard_map.127), channel_id=1, source_target_pairs={{0,16},{4,20},{8,24},{12,28},{16,0},{20,4},{24,8},{28,12},{1,17},{... | collective-permute-start | bytes 1179656 | tf_op jit(solution)/shard_map/ppermute | solution.py:126
  57.7 4.3 %collective-permute-start.12 = (s32[2,256]{1,0:T(2,128)S(1)}, s32[2,256]{1,0:T(2,128)S(1)}, u32[]{:S(2)}, u32[]{:S(2)}) collective-permute-start(s32[2,256]{1,0:T(2,128)S(1)} %shard_map.125), channel_id=1, source_target_pairs={{0,4},{4,0},{8,12},{12,8},{16,20},{20,16},{24,28},{28,24},{1,5},{5... | collective-permute-start | bytes 6152 | tf_op jit(solution)/shard_map/ppermute | solution.py:151
  60.6 18.6 %collective-permute-start.14 = (bf16[512,384]{1,0:T(8,128)(2,1)S(1)}, bf16[512,384]{1,0:T(8,128)(2,1)S(1)}, u32[]{:S(2)}, u32[]{:S(2)}) collective-permute-start(bf16[512,384]{1,0:T(8,128)(2,1)S(1)} %get-tuple-element.83.refs_2_), channel_id=1, source_target_pairs={{0,1},{3,2},{4,5},{7,6},{8,9},{11,10},{12,13},{15,14},{16,17},{19,... | collective-permute-start | bytes 1179656 | tf_op jit(solution)/shard_map/ppermute | solution.py:576
  66.6 13.7 %collective-permute-start.13 = (bf16[512,384]{1,0:T(8,128)(2,1)S(1)}, bf16[512,384]{1,0:T(8,128)(2,1)S(1)}, u32[]{:S(2)}, u32[]{:S(2)}) collective-permute-start(bf16[512,384]{1,0:T(8,128)(2,1)S(1)} %get-tuple-element.86.refs_7_.refs_1_), channel_id=1, source_target_pairs={{1,2},{2,1},{5,6},{6,5},{9,10},{10,9},{13,14},{14,13},{17,18},{18,... | collective-permute-start | bytes 1179656 | tf_op jit(solution)/shard_map/ppermute | solution.py:588
  67.4 14.3 %collective-permute-start.19 = (bf16[512,384]{1,0:T(8,128)(2,1)S(1)}, bf16[512,384]{1,0:T(8,128)(2,1)S(1)}, u32[]{:S(2)}, u32[]{:S(2)}) collective-permute-start(bf16[512,384]{1,0:T(8,128)(2,1)S(1)} %shard_map.131), channel_id=1, source_target_pairs={{0,16},{4,20},{8,24},{12,28},{16,0},{20,4},{24,8},{28,12},{1,17},{... | collective-permute-start | bytes 1179656 | tf_op jit(solution)/shard_map/ppermute | solution.py:126
  71.5 10.2 %collective-permute-start.20 = (bf16[512,384]{1,0:T(8,128)(2,1)S(1)}, bf16[512,384]{1,0:T(8,128)(2,1)S(1)}, u32[]{:S(2)}, u32[]{:S(2)}) collective-permute-start(bf16[512,384]{1,0:T(8,128)(2,1)S(1)} %shard_map.132), channel_id=1, source_target_pairs={{0,8},{4,12},{8,0},{12,4},{16,24},{20,28},{24,16},{28,20},{1,9},{5... | collective-permute-start | bytes 1179656 | tf_op jit(solution)/shard_map/ppermute | solution.py:126
  72.7 15.1 %collective-permute-start.18 = (bf16[512,384]{1,0:T(8,128)(2,1)S(1)}, bf16[512,384]{1,0:T(8,128)(2,1)S(1)}, u32[]{:S(2)}, u32[]{:S(2)}) collective-permute-start(bf16[512,384]{1,0:T(8,128)(2,1)S(1)} %get-tuple-element.89.refs_2_.refs_1_), channel_id=1, source_target_pairs={{0,1},{3,2},{4,5},{7,6},{8,9},{11,10},{12,13},{15,14},{16,17},{19,... | collective-permute-start | bytes 1179656 | tf_op jit(solution)/shard_map/ppermute | solution.py:576
  79.4 9.3 %collective-permute-start.17 = (bf16[512,384]{1,0:T(8,128)(2,1)S(1)}, bf16[512,384]{1,0:T(8,128)(2,1)S(1)}, u32[]{:S(2)}, u32[]{:S(2)}) collective-permute-start(bf16[512,384]{1,0:T(8,128)(2,1)S(1)} %get-tuple-element.90.refs_2_), channel_id=1, source_target_pairs={{1,2},{2,1},{5,6},{6,5},{9,10},{10,9},{13,14},{14,13},{17,18},{18,... | collective-permute-start | bytes 1179656 | tf_op jit(solution)/shard_map/ppermute | solution.py:588
  80.4 10.3 %collective-permute-start.16 = (bf16[512,384]{1,0:T(8,128)(2,1)S(1)}, bf16[512,384]{1,0:T(8,128)(2,1)S(1)}, u32[]{:S(2)}, u32[]{:S(2)}) collective-permute-start(bf16[512,384]{1,0:T(8,128)(2,1)S(1)} %shard_map.130.refs_7_.refs_2_), channel_id=1, source_target_pairs={{1,0},{2,3},{5,4},{6,7},{9,8},{10,11},{13,12},{14,15},{17,16},{18,... | collective-permute-start | bytes 1179656 | tf_op jit(solution)/shard_map/ppermute | solution.py:597
  83.0 12.0 %collective-permute-start.23 = (bf16[512,384]{1,0:T(8,128)(2,1)S(1)}, bf16[512,384]{1,0:T(8,128)(2,1)S(1)}, u32[]{:S(2)}, u32[]{:S(2)}) collective-permute-start(bf16[512,384]{1,0:T(8,128)(2,1)S(1)} %get-tuple-element.93.refs_2_), channel_id=1, source_target_pairs={{0,1},{3,2},{4,5},{7,6},{8,9},{11,10},{12,13},{15,14},{16,17},{19,... | collective-permute-start | bytes 1179656 | tf_op jit(solution)/shard_map/ppermute | solution.py:576
  88.0 7.8 %collective-permute-start.22 = (bf16[512,384]{1,0:T(8,128)(2,1)S(1)}, bf16[512,384]{1,0:T(8,128)(2,1)S(1)}, u32[]{:S(2)}, u32[]{:S(2)}) collective-permute-start(bf16[512,384]{1,0:T(8,128)(2,1)S(1)} %get-tuple-element.94.refs_2_), channel_id=1, source_target_pairs={{1,2},{2,1},{5,6},{6,5},{9,10},{10,9},{13,14},{14,13},{17,18},{18,... | collective-permute-start | bytes 1179656 | tf_op jit(solution)/shard_map/ppermute | solution.py:588
  88.8 11.7 %collective-permute-start.21 = (bf16[512,384]{1,0:T(8,128)(2,1)S(1)}, bf16[512,384]{1,0:T(8,128)(2,1)S(1)}, u32[]{:S(2)}, u32[]{:S(2)}) collective-permute-start(bf16[512,384]{1,0:T(8,128)(2,1)S(1)} %shard_map.135.refs_5_.refs_2_), channel_id=1, source_target_pairs={{1,0},{2,3},{5,4},{6,7},{9,8},{10,11},{13,12},{14,15},{17,16},{18,... | collective-permute-start | bytes 1179656 | tf_op jit(solution)/shard_map/ppermute | solution.py:597
  91.6 8.9 %collective-permute-start.24 = (bf16[384,384]{1,0:T(8,128)(2,1)S(1)}, bf16[384,384]{1,0:T(8,128)(2,1)S(1)}, u32[]{:S(2)}, u32[]{:S(2)}) collective-permute-start(bf16[384,384]{1,0:T(8,128)(2,1)S(1)} %get-tuple-element.98.refs_2_.refs_3_), channel_id=1, source_target_pairs={{0,8},{4,12},{8,0},{12,4},{16,24},{20,28},{24,16},{28,20},{1,9},{5... | collective-permute-start | bytes 884744 | tf_op jit(solution)/shard_map/ppermute | solution.py:126
  92.8 7.7 %collective-permute-start.25 = (bf16[384,384]{1,0:T(8,128)(2,1)S(1)}, bf16[384,384]{1,0:T(8,128)(2,1)S(1)}, u32[]{:S(2)}, u32[]{:S(2)}) collective-permute-start(bf16[384,384]{1,0:T(8,128)(2,1)S(1)} %get-tuple-element.98.refs_2_.refs_3_), channel_id=1, source_target_pairs={{0,16},{4,20},{8,24},{12,28},{16,0},{20,4},{24,8},{28,12},{1,17},{... | collective-permute-start | bytes 884744 | tf_op jit(solution)/shard_map/ppermute | solution.py:126
  95.1 9.9 %collective-permute-start.27 = (bf16[512,384]{1,0:T(8,128)(2,1)S(1)}, bf16[512,384]{1,0:T(8,128)(2,1)S(1)}, u32[]{:S(2)}, u32[]{:S(2)}) collective-permute-start(bf16[512,384]{1,0:T(8,128)(2,1)S(1)} %get-tuple-element.99.refs_2_), channel_id=1, source_target_pairs={{1,2},{2,1},{5,6},{6,5},{9,10},{10,9},{13,14},{14,13},{17,18},{18,... | collective-permute-start | bytes 1179656 | tf_op jit(solution)/shard_map/ppermute | solution.py:588
  95.8 26.1 %copy-start.1 = (bf16[1,576,3072]{2,1,0:T(8,128)(2,1)S(1)}, bf16[1,576,3072]{2,1,0:T(8,128)(2,1)}, u32[]{:S(2)}) copy-start(bf16[1,576,3072]{2,1,0:T(8,128)(2,1)} %param.19) | copy-start | bytes 10616836
  95.9 26.0 %copy-start = (bf16[1,576,3072]{2,1,0:T(8,128)(2,1)S(1)}, bf16[1,576,3072]{2,1,0:T(8,128)(2,1)}, u32[]{:S(2)}) copy-start(bf16[1,576,3072]{2,1,0:T(8,128)(2,1)} %param.18) | copy-start | bytes 10616836
  95.9 11.0 %collective-permute-start.26 = (bf16[512,384]{1,0:T(8,128)(2,1)S(1)}, bf16[512,384]{1,0:T(8,128)(2,1)S(1)}, u32[]{:S(2)}, u32[]{:S(2)}) collective-permute-start(bf16[512,384]{1,0:T(8,128)(2,1)S(1)} %shard_map.138.refs_5_.refs_2_), channel_id=1, source_target_pairs={{1,0},{2,3},{5,4},{6,7},{9,8},{10,11},{13,12},{14,15},{17,16},{18,... | collective-permute-start | bytes 1179656 | tf_op jit(solution)/shard_map/ppermute | solution.py:597
  101.4 6.8 %collective-permute-start.28 = (bf16[384,384]{1,0:T(8,128)(2,1)S(1)}, bf16[384,384]{1,0:T(8,128)(2,1)S(1)}, u32[]{:S(2)}, u32[]{:S(2)}) collective-permute-start(bf16[384,384]{1,0:T(8,128)(2,1)S(1)} %get-tuple-element.102.refs_2_.refs_3_), channel_id=1, source_target_pairs={{0,8},{4,12},{8,0},{12,4},{16,24},{20,28},{24,16},{28,20},{1,9},{5... | collective-permute-start | bytes 884744 | tf_op jit(solution)/shard_map/ppermute | solution.py:126
  102.7 7.0 %collective-permute-start.29 = (bf16[384,384]{1,0:T(8,128)(2,1)S(1)}, bf16[384,384]{1,0:T(8,128)(2,1)S(1)}, u32[]{:S(2)}, u32[]{:S(2)}) collective-permute-start(bf16[384,384]{1,0:T(8,128)(2,1)S(1)} %get-tuple-element.102.refs_2_.refs_3_), channel_id=1, source_target_pairs={{0,16},{4,20},{8,24},{12,28},{16,0},{20,4},{24,8},{28,12},{1,17},{... | collective-permute-start | bytes 884744 | tf_op jit(solution)/shard_map/ppermute | solution.py:126
  105.0 7.7 %collective-permute-start.31 = (bf16[384,384]{1,0:T(8,128)(2,1)S(1)}, bf16[384,384]{1,0:T(8,128)(2,1)S(1)}, u32[]{:S(2)}, u32[]{:S(2)}) collective-permute-start(bf16[384,384]{1,0:T(8,128)(2,1)S(1)} %get-tuple-element.98.refs_2_.refs_3_), channel_id=1, source_target_pairs={{0,4},{4,0},{8,12},{12,8},{16,20},{20,16},{24,28},{28,24},{1,5},{5... | collective-permute-start | bytes 884744 | tf_op jit(solution)/shard_map/ppermute | solution.py:135
  105.1 14.5 %collective-permute-start.30 = (bf16[512,384]{1,0:T(8,128)(2,1)S(1)}, bf16[512,384]{1,0:T(8,128)(2,1)S(1)}, u32[]{:S(2)}, u32[]{:S(2)}) collective-permute-start(bf16[512,384]{1,0:T(8,128)(2,1)S(1)} %shard_map.140.refs_5_), channel_id=1, source_target_pairs={{1,0},{2,3},{5,4},{6,7},{9,8},{10,11},{13,12},{14,15},{17,16},{18,... | collective-permute-start | bytes 1179656 | tf_op jit(solution)/shard_map/ppermute | solution.py:597
  106.9 7.1 %collective-permute-start.32 = (bf16[384,384]{1,0:T(8,128)(2,1)S(1)}, bf16[384,384]{1,0:T(8,128)(2,1)S(1)}, u32[]{:S(2)}, u32[]{:S(2)}) collective-permute-start(bf16[384,384]{1,0:T(8,128)(2,1)S(1)} %collective-permute-done.24.refs_6_.refs_5_), channel_id=1, source_target_pairs={{0,4},{4,0},{8,12},{12,8},{16,20},{20,16},{24,28},{28,24},{1,5},{5... | collective-permute-start | bytes 884744 | tf_op jit(solution)/shard_map/ppermute | solution.py:135
  108.2 5.8 %collective-permute-start.33 = (bf16[384,384]{1,0:T(8,128)(2,1)S(1)}, bf16[384,384]{1,0:T(8,128)(2,1)S(1)}, u32[]{:S(2)}, u32[]{:S(2)}) collective-permute-start(bf16[384,384]{1,0:T(8,128)(2,1)S(1)} %collective-permute-done.25.refs_7_), channel_id=1, source_target_pairs={{0,4},{4,0},{8,12},{12,8},{16,20},{20,16},{24,28},{28,24},{1,5},{5... | collective-permute-start | bytes 884744 | tf_op jit(solution)/shard_map/ppermute | solution.py:135
  109.7 9.9 %collective-permute-start.38 = (bf16[384,384]{1,0:T(8,128)(2,1)S(1)}, bf16[384,384]{1,0:T(8,128)(2,1)S(1)}, u32[]{:S(2)}, u32[]{:S(2)}) collective-permute-start(bf16[384,384]{1,0:T(8,128)(2,1)S(1)} %collective-permute-done.24.refs_6_.refs_5_), channel_id=1, source_target_pairs={{0,16},{4,20},{8,24},{12,28},{16,0},{20,4},{24,8},{28,12},{1,17},{... | collective-permute-start | bytes 884744 | tf_op jit(solution)/shard_map/ppermute | solution.py:126
  112.7 8.5 %collective-permute-start.34 = (bf16[384,384]{1,0:T(8,128)(2,1)S(1)}, bf16[384,384]{1,0:T(8,128)(2,1)S(1)}, u32[]{:S(2)}, u32[]{:S(2)}) collective-permute-start(bf16[384,384]{1,0:T(8,128)(2,1)S(1)} %get-tuple-element.104.refs_9_.refs_3_), channel_id=1, source_target_pairs={{0,8},{4,12},{8,0},{12,4},{16,24},{20,28},{24,16},{28,20},{1,9},{5... | collective-permute-start | bytes 884744 | tf_op jit(solution)/shard_map/ppermute | solution.py:126
  114.0 11.4 %collective-permute-start.35 = (bf16[384,384]{1,0:T(8,128)(2,1)S(1)}, bf16[384,384]{1,0:T(8,128)(2,1)S(1)}, u32[]{:S(2)}, u32[]{:S(2)}) collective-permute-start(bf16[384,384]{1,0:T(8,128)(2,1)S(1)} %get-tuple-element.104.refs_9_.refs_3_), channel_id=1, source_target_pairs={{0,16},{4,20},{8,24},{12,28},{16,0},{20,4},{24,8},{28,12},{1,17},{... | collective-permute-start | bytes 884744 | tf_op jit(solution)/shard_map/ppermute | solution.py:126
  114.0 12.9 %collective-permute-start.40 = (bf16[384,384]{1,0:T(8,128)(2,1)S(1)}, bf16[384,384]{1,0:T(8,128)(2,1)S(1)}, u32[]{:S(2)}, u32[]{:S(2)}) collective-permute-start(bf16[384,384]{1,0:T(8,128)(2,1)S(1)} %get-tuple-element.102.refs_2_.refs_3_), channel_id=1, source_target_pairs={{0,4},{4,0},{8,12},{12,8},{16,20},{20,16},{24,28},{28,24},{1,5},{5... | collective-permute-start | bytes 884744 | tf_op jit(solution)/shard_map/ppermute | solution.py:135
  119.5 9.0 %collective-permute-start.41 = (bf16[384,384]{1,0:T(8,128)(2,1)S(1)}, bf16[384,384]{1,0:T(8,128)(2,1)S(1)}, u32[]{:S(2)}, u32[]{:S(2)}) collective-permute-start(bf16[384,384]{1,0:T(8,128)(2,1)S(1)} %collective-permute-done.28.refs_6_.refs_5_), channel_id=1, source_target_pairs={{0,4},{4,0},{8,12},{12,8},{16,20},{20,16},{24,28},{28,24},{1,5},{5... | collective-permute-start | bytes 884744 | tf_op jit(solution)/shard_map/ppermute | solution.py:135
  119.5 9.2 %collective-permute-start.42 = (bf16[384,384]{1,0:T(8,128)(2,1)S(1)}, bf16[384,384]{1,0:T(8,128)(2,1)S(1)}, u32[]{:S(2)}, u32[]{:S(2)}) collective-permute-start(bf16[384,384]{1,0:T(8,128)(2,1)S(1)} %collective-permute-done.29.refs_7_), channel_id=1, source_target_pairs={{0,4},{4,0},{8,12},{12,8},{16,20},{20,16},{24,28},{28,24},{1,5},{5... | collective-permute-start | bytes 884744 | tf_op jit(solution)/shard_map/ppermute | solution.py:135
  121.1 11.2 %collective-permute-start.44 = (bf16[384,384]{1,0:T(8,128)(2,1)S(1)}, bf16[384,384]{1,0:T(8,128)(2,1)S(1)}, u32[]{:S(2)}, u32[]{:S(2)}) collective-permute-start(bf16[384,384]{1,0:T(8,128)(2,1)S(1)} %collective-permute-done.29.refs_7_), channel_id=1, source_target_pairs={{0,8},{4,12},{8,0},{12,4},{16,24},{20,28},{24,16},{28,20},{1,9},{5... | collective-permute-start | bytes 884744 | tf_op jit(solution)/shard_map/ppermute | solution.py:126
  125.5 8.0 %collective-permute-start.46 = (bf16[384,384]{1,0:T(8,128)(2,1)S(1)}, bf16[384,384]{1,0:T(8,128)(2,1)S(1)}, u32[]{:S(2)}, u32[]{:S(2)}) collective-permute-start(bf16[384,384]{1,0:T(8,128)(2,1)S(1)} %get-tuple-element.104.refs_9_.refs_3_), channel_id=1, source_target_pairs={{0,4},{4,0},{8,12},{12,8},{16,20},{20,16},{24,28},{28,24},{1,5},{5... | collective-permute-start | bytes 884744 | tf_op jit(solution)/shard_map/ppermute | solution.py:135
  126.9 11.6 %collective-permute-start.37 = (bf16[384,512]{1,0:T(8,128)(2,1)S(1)}, bf16[384,512]{1,0:T(8,128)(2,1)S(1)}, u32[]{:S(2)}, u32[]{:S(2)}) collective-permute-start(bf16[384,512]{1,0:T(8,128)(2,1)S(1)} %get-tuple-element.108.refs_15_.refs_1_.refs_3_), channel_id=1, source_target_pairs={{0,16},{4,20},{8,24},{12,28},{16,0},{20,4},{24,8},{28,12},{1,17},{... | collective-permute-start | bytes 1179656 | tf_op jit(solution)/shard_map/ppermute | solution.py:126
  128.5 4.9 %collective-permute-start.39 = (bf16[384,384]{1,0:T(8,128)(2,1)S(1)}, bf16[384,384]{1,0:T(8,128)(2,1)S(1)}, u32[]{:S(2)}, u32[]{:S(2)}) collective-permute-start(bf16[384,384]{1,0:T(8,128)(2,1)S(1)} %shard_map.145.refs_3_), channel_id=1, source_target_pairs={{0,4},{4,0},{8,12},{12,8},{16,20},{20,16},{24,28},{28,24},{1,5},{5... | collective-permute-start | bytes 884744 | tf_op jit(solution)/shard_map/ppermute | solution.py:135
  132.4 9.4 %collective-permute-start.45 = (bf16[384,384]{1,0:T(8,128)(2,1)S(1)}, bf16[384,384]{1,0:T(8,128)(2,1)S(1)}, u32[]{:S(2)}, u32[]{:S(2)}) collective-permute-start(bf16[384,384]{1,0:T(8,128)(2,1)S(1)} %shard_map.149.refs_3_), channel_id=1, source_target_pairs={{0,4},{4,0},{8,12},{12,8},{16,20},{20,16},{24,28},{28,24},{1,5},{5... | collective-permute-start | bytes 884744 | tf_op jit(solution)/shard_map/ppermute | solution.py:135
  132.8 14.3 %collective-permute-start.53 = (bf16[384,512]{1,0:T(8,128)(2,1)S(1)}, bf16[384,512]{1,0:T(8,128)(2,1)S(1)}, u32[]{:S(2)}, u32[]{:S(2)}) collective-permute-start(bf16[384,512]{1,0:T(8,128)(2,1)S(1)} %get-tuple-element.108.refs_15_.refs_1_.refs_3_), channel_id=1, source_target_pairs={{0,8},{4,12},{8,0},{12,4},{16,24},{20,28},{24,16},{28,20},{1,9},{5... | collective-permute-start | bytes 1179656 | tf_op jit(solution)/shard_map/ppermute | solution.py:126
  133.5 9.1 %collective-permute-start.47 = (bf16[384,384]{1,0:T(8,128)(2,1)S(1)}, bf16[384,384]{1,0:T(8,128)(2,1)S(1)}, u32[]{:S(2)}, u32[]{:S(2)}) collective-permute-start(bf16[384,384]{1,0:T(8,128)(2,1)S(1)} %collective-permute-done.34.refs_9_.refs_5_.refs_0_), channel_id=1, source_target_pairs={{0,4},{4,0},{8,12},{12,8},{16,20},{20,16},{24,28},{28,24},{1,5},{5... | collective-permute-start | bytes 884744 | tf_op jit(solution)/shard_map/ppermute | solution.py:135
  133.5 9.1 %collective-permute-start.48 = (bf16[384,384]{1,0:T(8,128)(2,1)S(1)}, bf16[384,384]{1,0:T(8,128)(2,1)S(1)}, u32[]{:S(2)}, u32[]{:S(2)}) collective-permute-start(bf16[384,384]{1,0:T(8,128)(2,1)S(1)} %collective-permute-done.35.refs_10_.refs_7_), channel_id=1, source_target_pairs={{0,4},{4,0},{8,12},{12,8},{16,20},{20,16},{24,28},{28,24},{1,5},{5... | collective-permute-start | bytes 884744 | tf_op jit(solution)/shard_map/ppermute | solution.py:135
  138.5 8.6 %collective-permute-start.50 = (bf16[384,384]{1,0:T(8,128)(2,1)S(1)}, bf16[384,384]{1,0:T(8,128)(2,1)S(1)}, u32[]{:S(2)}, u32[]{:S(2)}) collective-permute-start(bf16[384,384]{1,0:T(8,128)(2,1)S(1)} %shard_map.153), channel_id=1, source_target_pairs={{0,16},{4,20},{8,24},{12,28},{16,0},{20,4},{24,8},{28,12},{1,17},{... | collective-permute-start | bytes 884744 | tf_op jit(solution)/shard_map/ppermute | solution.py:126
  141.8 10.6 %collective-permute-start.43 = (bf16[384,512]{1,0:T(8,128)(2,1)S(1)}, bf16[384,512]{1,0:T(8,128)(2,1)S(1)}, u32[]{:S(2)}, u32[]{:S(2)}) collective-permute-start(bf16[384,512]{1,0:T(8,128)(2,1)S(1)} %shard_map.148), channel_id=1, source_target_pairs={{0,8},{4,12},{8,0},{12,4},{16,24},{20,28},{24,16},{28,20},{1,9},{5... | collective-permute-start | bytes 1179656 | tf_op jit(solution)/shard_map/ppermute | solution.py:126
  142.6 15.5 %collective-permute-start.52 = (bf16[384,512]{1,0:T(8,128)(2,1)S(1)}, bf16[384,512]{1,0:T(8,128)(2,1)S(1)}, u32[]{:S(2)}, u32[]{:S(2)}) collective-permute-start(bf16[384,512]{1,0:T(8,128)(2,1)S(1)} %get-tuple-element.108.refs_15_.refs_1_.refs_3_), channel_id=1, source_target_pairs={{0,4},{4,0},{8,12},{12,8},{16,20},{20,16},{24,28},{28,24},{1,5},{5... | collective-permute-start | bytes 1179656 | tf_op jit(solution)/shard_map/ppermute | solution.py:135
  142.6 11.6 %collective-permute-start.36 = (bf16[64,1536]{1,0:T(8,128)(2,1)S(1)}, bf16[64,1536]{1,0:T(8,128)(2,1)S(1)}, u32[]{:S(2)}, u32[]{:S(2)}) collective-permute-start(bf16[64,1536]{1,0:T(8,128)(2,1)S(1)} %get-tuple-element.107), channel_id=1, source_target_pairs={{0,4},{4,0},{8,12},{12,8},{16,20},{20,16},{24,28},{28,24},{1,5},{5... | collective-permute-start | bytes 589832 | tf_op jit(solution)/shard_map/ppermute | solution.py:672
  147.1 11.0 %collective-permute-start.55 = (bf16[384,512]{1,0:T(8,128)(2,1)S(1)}, bf16[384,512]{1,0:T(8,128)(2,1)S(1)}, u32[]{:S(2)}, u32[]{:S(2)}) collective-permute-start(bf16[384,512]{1,0:T(8,128)(2,1)S(1)} %collective-permute-done.37.refs_0_.refs_7_), channel_id=1, source_target_pairs={{0,4},{4,0},{8,12},{12,8},{16,20},{20,16},{24,28},{28,24},{1,5},{5... | collective-permute-start | bytes 1179656 | tf_op jit(solution)/shard_map/ppermute | solution.py:135
  147.1 10.9 %collective-permute-start.54 = (bf16[384,512]{1,0:T(8,128)(2,1)S(1)}, bf16[384,512]{1,0:T(8,128)(2,1)S(1)}, u32[]{:S(2)}, u32[]{:S(2)}) collective-permute-start(bf16[384,512]{1,0:T(8,128)(2,1)S(1)} %collective-permute-done.53.refs_5_), channel_id=1, source_target_pairs={{0,4},{4,0},{8,12},{12,8},{16,20},{20,16},{24,28},{28,24},{1,5},{5... | collective-permute-start | bytes 1179656 | tf_op jit(solution)/shard_map/ppermute | solution.py:135
  152.4 3.7 %collective-permute-start.51 = (bf16[384,384]{1,0:T(8,128)(2,1)S(1)}, bf16[384,384]{1,0:T(8,128)(2,1)S(1)}, u32[]{:S(2)}, u32[]{:S(2)}) collective-permute-start(bf16[384,384]{1,0:T(8,128)(2,1)S(1)} %shard_map.154.refs_3_), channel_id=1, source_target_pairs={{0,4},{4,0},{8,12},{12,8},{16,20},{20,16},{24,28},{28,24},{1,5},{5... | collective-permute-start | bytes 884744 | tf_op jit(solution)/shard_map/ppermute | solution.py:135
  154.2 10.1 %collective-permute-start.49 = (bf16[384,512]{1,0:T(8,128)(2,1)S(1)}, bf16[384,512]{1,0:T(8,128)(2,1)S(1)}, u32[]{:S(2)}, u32[]{:S(2)}) collective-permute-start(bf16[384,512]{1,0:T(8,128)(2,1)S(1)} %shard_map.152.refs_3_), channel_id=1, source_target_pairs={{0,4},{4,0},{8,12},{12,8},{16,20},{20,16},{24,28},{28,24},{1,5},{5... | collective-permute-start | bytes 1179656 | tf_op jit(solution)/shard_map/ppermute | solution.py:135
  (11 other events, 9.4 us)

commit v5 on v0

--- a/solution.py
+++ b/solution.py
@@ -1,7 +1,639 @@
+import functools
+
 import jax
 import jax.numpy as jnp
 from jax import lax
+from jax.experimental import pallas as pl
+from jax.experimental.pallas import tpu as pltpu
 from jax.sharding import PartitionSpec as P
+
+GROUPS = 4
+CORES = 2
+LANES = 128
+BF16 = jnp.bfloat16
+F32 = jnp.float32
+NT = (((1,), (1,)), ((), ()))
+TN = (((0,), (0,)), ((), ()))
+NN = (((1,), (0,)), ((), ()))
+VM = pl.BlockSpec(memory_space=pltpu.VMEM)
+SM = pl.BlockSpec(memory_space=pltpu.SMEM)
+HBM = pl.BlockSpec(memory_space=pltpu.HBM)
+ANY = pl.BlockSpec(memory_space=pl.ANY)
+
+
+def dot(a, b, dims):
+    return lax.dot_general(a, b, dims, preferred_element_type=F32)
+
+
+def halves(x):
+    high = x.astype(BF16)
+    return high, (x - high.astype(F32)).astype(BF16)
+
+
+def like(shape, dtype=BF16):
+    return jax.ShapeDtypeStruct(tuple(shape), dtype)
+
+
+def call(kernel, out_shape, operands, flops=0, exps=0, deps=(), specs=None, limit=12, **kwargs):
+    count, extra = len(operands), len(deps)
+
+    def body(*refs):
+        kernel(*refs[:count], *refs[count + extra :])
+
+    shapes = out_shape if isinstance(out_shape, (list, tuple)) else [out_shape]
+    nbytes = sum(x.size * x.dtype.itemsize for x in list(operands) + list(shapes))
+    kwargs.setdefault("out_specs", jax.tree.map(lambda _: VM, out_shape))
+    return pl.pallas_call(
+        body,
+        out_shape=out_shape,
+        in_specs=list(specs or [VM] * count) + [ANY] * extra,
+        compiler_params=pltpu.CompilerParams(vmem_limit_bytes=limit * 1024 * 1024),
+        cost_estimate=pl.CostEstimate(
+            flops=int(flops), bytes_accessed=int(nbytes), transcendentals=int(exps)
+        ),
+        **kwargs,
+    )(*operands, *deps)
+
+
+def tile(index, size):
+    return pl.ds(pl.multiple_of(index * size, size), size)
+
+
+def fresh_kernel(place_ref, rate_ref, k_in, v_in, mine_ref, theirs_ref, k_ref, v_ref, sems):
+    part, size = mine_ref.shape[0], mine_ref.shape[1]
+    length = k_ref.shape[0]
+    left = length - lax.broadcasted_iota(jnp.int32, (length, size), 0).astype(F32)
+    order = ((theirs_ref, 1 - place_ref[1]), (mine_ref, place_ref[1]))
+    copies = []
+    for n, (_, half) in enumerate(order):
+        at = tile(half, part * size)
+        for source, target in ((k_in, k_ref), (v_in, v_ref)):
+            copies.append(
+                pltpu.make_async_copy(source.at[:, at], target.at[:, at], sems.at[len(copies)])
+            )
+            copies[-1].start()
+    for n, (out_ref, half) in enumerate(order):
+        copies[2 * n].wait()
+        copies[2 * n + 1].wait()
+        for j in range(part):
+            head = half * part + j
+            cols = tile(head, size)
+            tail = jnp.exp(rate_ref[head][:, :size] * left)
+            high, low = halves(k_ref[:, cols].astype(F32) * tail)
+            v = v_ref[:, cols]
+            out_ref[j] = dot(high, v, TN) + dot(low, v, TN)
+
+
+def local_kernel(rate_ref, q_in, k_ref, v_ref, out_ref, q_ref, sem):
+    heads = rate_ref.shape[0]
+    length = k_ref.shape[0]
+    size = k_ref.shape[1] // heads
+    copy = pltpu.make_async_copy(q_in, q_ref, sem)
+    copy.start()
+    rows = lax.broadcasted_iota(jnp.int32, (length, length), 0)
+    cols = lax.broadcasted_iota(jnp.int32, (length, length), 1)
+    offset = (rows - cols).astype(F32)
+    keep = offset >= 0
+    offset = jnp.maximum(offset, 0.0)
+    copy.wait()
+    for h in range(heads):
+        at = slice(h * size, (h + 1) * size)
+        masked = jnp.where(keep, jnp.exp(rate_ref[h] * offset), 0.0)
+        weighted = (dot(q_ref[:, at], k_ref[:, at], NT) * masked).astype(BF16)
+        out_ref[:, at] = dot(weighted, v_ref[:, at], NN)
+
+
+def mix_kernel(recipe, coef_ref, *refs):
+    count = 1 + max(i for terms in recipe for i, _ in terms)
+    for j in range(refs[0].shape[0]):
+        values = [refs[i][j] for i in range(count)]
+        for out_ref, terms in zip(refs[count:], recipe):
+            out_ref[j] = sum(values[i] * coef_ref[row, j] for i, row in terms)
+
+
+def scan_rows(chip, core, rate, part, length):
+    rates = lax.dynamic_slice(rate, (core * part,), (part,))
+
+    def fade(blocks):
+        return jnp.exp(-rates * (length * blocks))
+
+    one, none = jnp.ones_like(rates), jnp.zeros_like(rates)
+    first, east, south = core == 0, (chip & 1) != 0, (chip & 2) != 0
+    behind = jnp.where(south, fade(2.0 * (chip & 1).astype(F32)), none)
+    keep, give = jnp.where(first, one, fade(1.0)), jnp.where(first, fade(1.0), one)
+    return [
+        jnp.where(first, one, none),
+        jnp.where(first, none, one),
+        jnp.where(first, fade(1.0), one),
+        jnp.where(first, one, fade(1.0)),
+        jnp.where(east, one, none),
+        jnp.where(east, fade(2.0), one),
+        jnp.where(east, one, fade(2.0)),
+        keep,
+        keep * behind,
+        jnp.where(first, none, one),
+        give,
+        give * behind,
+        jnp.where(first, one, none),
+    ]
+
+
+def head_kernel(place_ref, rate_ref, q_ref, local_ref, keep_ref, got_ref, out_ref):
+    part, size = keep_ref.shape[0], keep_ref.shape[1]
+    length = q_ref.shape[0]
+    pos = lax.broadcasted_iota(jnp.int32, (length, size), 0).astype(F32)
+    for state_ref, half in ((keep_ref, place_ref[1]), (got_ref, 1 - place_ref[1])):
+        for j in range(part):
+            head = half * part + j
+            at = tile(head, size)
+            high, low = halves(state_ref[j])
+            q = q_ref[:, at]
+            carried = dot(q, high, NN) + dot(q, low, NN)
+            carried = carried * jnp.exp(rate_ref[head][:, :size] * pos)
+            attended = local_ref[:, at] + carried
+            scale = lax.rsqrt(jnp.mean(attended * attended, axis=-1, keepdims=True) + 1e-05)
+            out_ref[:, at] = (attended * scale).astype(BF16)
+
+
+def larger_kernel(a_ref, b_ref, out_ref):
+    out_ref[...] = jnp.maximum(a_ref[...], b_ref[...])
+
+
+def stack_kernel(which, place_ref, a_ref, b_ref, out_ref):
+    rows = a_ref.shape[0]
+    upper = (place_ref[which] >> (1 if which == 2 else 0)) & 1
+    out_ref[tile(upper, rows), :] = a_ref[...]
+    out_ref[tile(1 - upper, rows), :] = b_ref[...]
+
+
+def picks_kernel(tokens, capacity, place_ref, own_ref, got_ref, out_ref):
+    slots = out_ref.shape[0]
+    before = lax.broadcasted_iota(jnp.int32, (LANES, LANES), 0)
+    token = lax.broadcasted_iota(jnp.int32, (LANES, LANES), 1)
+    earlier = ((before < token) & (before // tokens == token // tokens)).astype(BF16)
+    lane = lax.broadcasted_iota(jnp.int32, (8, LANES), 1)
+    slot = lax.broadcasted_iota(jnp.int32, (slots, LANES), 0)
+    per = own_ref.shape[0] // 8
+    for ref, half in ((own_ref, place_ref[1]), (got_ref, 1 - place_ref[1])):
+        for n in range(per):
+            first, second = ref[8 * n : 8 * n + 1, :], ref[8 * n + 1 : 8 * n + 2, :]
+            named = (first == place_ref[2]) | (second == place_ref[2])
+            named = jnp.broadcast_to(named.astype(F32), (8, LANES))
+            rank = dot(named.astype(BF16), earlier, NN).astype(jnp.int32)
+            run = half * per + n
+            row = (run * (LANES // tokens) + lane // tokens) * capacity + rank
+            row = jnp.where((named > 0.5) & (rank < capacity), row, -1)
+            out_ref[:, tile(run, LANES)] = (slot == row[0:1, :]).astype(BF16)
+
+
+def project_kernel(t, place_ref, own_ref, got_ref, rest_ref, rest_got_ref, *refs):
+    weights, (sum_ref, sent_ref) = refs[:-2], refs[-2:]
+    length, tokens, cols = own_ref.shape[0], rest_ref.shape[0], sum_ref.shape[1]
+    first = place_ref[1] == 0
+    weight = weights[0][...]
+    if len(weights) > 1:
+        weight = jnp.where(first, weight, weights[1][...])
+    at = tile((place_ref[0] ^ t) * CORES + place_ref[1], cols)
+    for head_ref, row_ref, half in (
+        (own_ref, rest_ref, place_ref[1]),
+        (got_ref, rest_got_ref, 1 - place_ref[1]),
+    ):
+        value = dot(head_ref[...], weight, NN)
+        pieces = []
+        for z in range(length // tokens):
+            piece = value[z * tokens : (z + 1) * tokens, :]
+            pieces.append(
+                jnp.where(place_ref[2] == z, piece + row_ref[:, at].astype(F32), piece)
+            )
+        value = jnp.concatenate(pieces, axis=0)
+        sum_ref[tile(half, length), :] = value
+        sent_ref[tile(half, length), :] = value.astype(BF16)
+
+
+def inward_kernel(part_ref, got_ref, sum_ref, sent_ref):
+    total = part_ref[...] + got_ref[...].astype(F32)
+    sum_ref[...] = total
+    sent_ref[...] = total.astype(BF16)
+
+
+def outer(place_ref):
+    return (place_ref[2] == 0) | (place_ref[2] == 3)
+
+
+def outward_kernel(place_ref, part_ref, got_ref, *refs):
+    total = (part_ref[...] + got_ref[...].astype(F32)).astype(BF16)
+    if len(refs) > 1:
+        total = jnp.where(outer(place_ref), refs[0][...], total)
+    refs[-1][...] = total
+
+
+def dispatch_kernel(t, place_ref, got_ref, given_ref, gain_ref, picks_ref, *refs):
+    earlier, (out_ref, mixed_ref), gives = refs[:-2], refs[-2:], []
+    if t == GROUPS - 1:
+        earlier, (out_ref, mixed_ref, give_ref) = refs[:-3], refs[-3:]
+        gives = [give_ref]
+    cols = mixed_ref.shape[1]
+    mixed = jnp.where(outer(place_ref), got_ref[...], given_ref[...])
+    mixed_ref[...] = mixed
+    value = mixed.astype(F32)
+    gain = gain_ref[:, tile((place_ref[0] ^ t) * CORES + place_ref[1], cols)]
+    out_ref[:, :cols] = dot(picks_ref[...], (value * gain).astype(BF16), NN).astype(BF16)
+    if not gives:
+        return
+    squares = jnp.sum(value * value, axis=1, keepdims=True)
+    for ref in earlier:
+        value = ref[...].astype(F32)
+        squares = squares + jnp.sum(value * value, axis=1, keepdims=True)
+    extra = dot(picks_ref[...], in_three(squares), NN)
+    out_ref[:, cols:] = extra.astype(BF16)
+    tokens = give_ref.shape[0]
+    per = mixed_ref.shape[0] // CORES // tokens
+    rows = tile((1 - place_ref[1]) * per + place_ref[2], tokens)
+    for n, ref in enumerate(list(earlier) + [mixed_ref]):
+        give_ref[:, n * cols : (n + 1) * cols] = ref[rows, :]
+
+
+def in_three(column):
+    lane = lax.broadcasted_iota(jnp.int32, (column.shape[0], LANES), 1)
+    rest, out = column, jnp.zeros((column.shape[0], LANES), F32)
+    for place in range(3):
+        high = rest.astype(BF16).astype(F32)
+        out = jnp.where(lane == place, high, out)
+        rest = rest - high
+    return out.astype(BF16)
+
+
+def join_kernel(cols, place_ref, own_ref, got_ref, out_ref):
+    out_ref[:, tile(place_ref[1], cols)] = own_ref[:, :cols]
+    out_ref[:, tile(1 - place_ref[1], cols)] = got_ref[:, :cols]
+    if own_ref.shape[1] > cols:
+        extra = own_ref[:, cols:].astype(F32) + got_ref[:, cols:].astype(F32)
+        total = jnp.sum(extra, axis=1, keepdims=True)
+        out_ref[:, CORES * cols :] = in_three(total)
+
+
+def half_kernel(place_ref, in_ref, out_ref):
+    out_ref[...] = in_ref[tile(place_ref[1], out_ref.shape[0]), :]
+
+
+def both_kernel(place_ref, own_ref, got_ref, out_ref):
+    rows = own_ref.shape[0]
+    out_ref[tile(place_ref[1], rows), :] = own_ref[...]
+    out_ref[tile(1 - place_ref[1], rows), :] = got_ref[...]
+
+
+def parts_kernel(place_ref, in_ref, keep_ref, give_ref):
+    rows = keep_ref.shape[0]
+    keep_ref[...] = in_ref[tile(place_ref[1], rows), :]
+    give_ref[...] = in_ref[tile(1 - place_ref[1], rows), :]
+
+
+def mixed_kernel(place_ref, got_ref, *refs):
+    mixed, out_ref = refs[:-1], refs[-1]
+    tokens, cols = out_ref.shape[0], mixed[0].shape[1]
+    per = mixed[0].shape[0] // CORES // tokens
+    own = tile(place_ref[1] * per + place_ref[2], tokens)
+    for t, ref in enumerate(mixed):
+        block = (place_ref[0] ^ t) * CORES
+        out_ref[:, tile(block + place_ref[1], cols)] = ref[own, :]
+        out_ref[:, tile(block + 1 - place_ref[1], cols)] = got_ref[:, t * cols : (t + 1) * cols]
+
+
+ROLES = ("own", "mine", "other", "diagonal")
+
+
+def expert_kernel(t, roles, mode, place_ref, gate_ref, up_ref, *refs):
+    refs = list(refs)
+    pieces = [[refs.pop(0) for _ in range(2 if r == "diagonal" else 1)] for r in roles]
+    sums = [[refs.pop(0), refs.pop(0)] for _ in roles] if t > 0 else None
+    if mode == "next":
+        refs.pop(0)
+    model = gate_ref.shape[1]
+    width = model // GROUPS
+    away = {"own": 0, "mine": 1 + place_ref[1], "other": 2 - place_ref[1], "diagonal": 3}
+    if mode is None:
+        outs = refs[: 2 * len(roles)]
+        held = refs[2 * len(roles) :]
+    else:
+        outs, ready, sems = refs[0], refs[1], refs[2]
+        held = refs[3:]
+    copies = []
+    for n, role in enumerate(roles):
+        source = place_ref[0] ^ away[role]
+        ref = pieces[n][0]
+        if role == "diagonal":
+            rows = ref.shape[0]
+            held[0][tile(place_ref[1], rows), :] = ref[...]
+            held[0][tile(1 - place_ref[1], rows), :] = pieces[n][1][...]
+            ref = held[0]
+        x = ref[:, :width]
+        cols = tile(source ^ t, width)
+        gated = dot(gate_ref[:, cols], x, NT)
+        lifted = dot(up_ref[:, cols], x, NT)
+        if sums is not None:
+            gated = gated + sums[n][0][...]
+            lifted = lifted + sums[n][1][...]
+        if mode is None:
+            outs[2 * n][...] = gated
+            outs[2 * n + 1][...] = lifted
+            continue
+        lane = lax.broadcasted_iota(jnp.int32, (8, LANES), 1)
+        squares = dot((lane < 3).astype(BF16), ref[:, width:], NT)[0:1, :]
+        scale = lax.rsqrt(squares / model + 1e-05)
+        gated, lifted = gated * scale, lifted * scale
+        silu = (0.5 * gated) * (1.0 + jnp.tanh(0.5 * gated))
+        ready[n] = (silu * lifted).astype(BF16)
+        at = tile(source, ready.shape[2])
+        copies.append(pltpu.make_async_copy(ready.at[n], outs.at[:, at], sems.at[n]))
+        copies[-1].start()
+    for copy in copies:
+        copy.wait()
+
+
+def expert_step(place, t, roles, pieces, gate, up, sums, hidden, deps):
+    hid, model = gate.shape
+    width = model // GROUPS
+    slots = sum(x.shape[0] for x in pieces[0])
+    operands = [place, gate, up] + [x for per in pieces for x in per]
+    if t > 0:
+        operands += [x for r in roles for x in sums[r]]
+    specs = [SM] + [VM] * (len(operands) - 1)
+    kwargs, mode, scratch = {}, None, []
+    if t == GROUPS - 1:
+        mode = "first" if hidden is None else "next"
+        if hidden is not None:
+            kwargs["input_output_aliases"] = {len(operands): 0}
+            operands.append(hidden)
+            specs.append(ANY)
+        out_shape = like((hid, slots * GROUPS))
+        kwargs["out_specs"] = ANY
+        scratch += [
+            pltpu.VMEM((len(roles), hid, slots), BF16),
+            pltpu.SemaphoreType.DMA((len(roles),)),
+        ]
+    else:
+        out_shape = [like((hid, slots), F32)] * (2 * len(roles))
+    if "diagonal" in roles:
+        wide = pieces[roles.index("diagonal")][0].shape[1]
+        scratch.append(pltpu.VMEM((slots, wide), BF16))
+    out = call(
+        functools.partial(expert_kernel, t, roles, mode),
+        out_shape,
+        operands,
+        4 * hid * slots * width * len(roles),
+        hid * slots * len(roles) if mode else 0,
+        deps,
+        specs,
+        20,
+        scratch_shapes=scratch,
+        **kwargs,
+    )
+    if mode:
+        return out, None
+    for n, r in enumerate(roles):
+        sums[r] = out[2 * n : 2 * n + 2]
+    return hidden, out[0]
+
+
+def send(x, axis, pairs):
+    return lax.ppermute(x, axis, pairs)
+
+
+def swap(x):
+    return send(x, "ctx", [(d, d ^ 1) for d in range(lax.axis_size("ctx"))])
+
+
+def outbound(x):
+    return send(x, "ctx", [(d, d ^ (4 if d % 2 else 2)) for d in range(lax.axis_size("ctx"))])
+
+
+def onward(x):
+    return send(x, "ctx", [(d, d ^ (2 if d % 2 else 4)) for d in range(lax.axis_size("ctx"))])
+
+
+def on_square(
+    queries,
+    key_rows,
+    value_rows,
+    decay_rate,
+    out_weight,
+    residual,
+    moe_gain,
+    expert_ids,
+    gate_weight,
+    up_weight,
+):
+    ctx, exp = lax.axis_index("ctx"), lax.axis_index("exp")
+    chip, core = ctx // CORES, lax.rem(ctx, CORES)
+    place = jnp.stack([chip, core, exp]).astype(jnp.int32)
+    length, here = queries.shape
+    heads = decay_rate.shape[0]
+    size = here // heads
+    part = heads // CORES
+    tokens, model = residual.shape
+    cols = model // GROUPS // CORES
+    capacity = max(2, 3 * tokens // lax.axis_size("exp"))
+    every = CORES * length
+    slots = every // tokens * capacity
+    gate, up = gate_weight[0], up_weight[0]
+    last = []
+
+    def run(kernel, out_shape, operands, *more, deps=(), **kwargs):
+        out = call(kernel, out_shape, operands, *more, deps=list(last) + list(deps), **kwargs)
+        last[:] = [out[0] if isinstance(out, (list, tuple)) else out]
+        return out
+
+    rate = jnp.broadcast_to(-decay_rate[:, None, None], (heads, 1, length))
+    rows = jnp.stack(scan_rows(chip, core, decay_rate, part, length))
+    coef = jnp.broadcast_to(rows[:, :, None, None], rows.shape + (1, size))
+    turned = jnp.tile(expert_ids.T, (1, LANES // tokens))
+    lane = jnp.arange(LANES, dtype=jnp.int32)[None, :]
+    ids = jnp.where(lane // tokens == exp % (LANES // tokens), turned, -1)
+    ids = jnp.pad(ids, ((0, 6), (0, 0)), constant_values=-1)
+    gain = moe_gain[None, :] * 1.0
+
+    state_like = like((part, size, size), F32)
+    mine, theirs, keys, values = run(
+        fresh_kernel,
+        [state_like] * 2 + [like((length, here))] * 2,
+        [place, rate, key_rows, value_rows],
+        4 * heads * length * size * size,
+        heads * length * size,
+        deps=[coef, ids],
+        specs=[SM, VM, HBM, HBM],
+        scratch_shapes=[pltpu.SemaphoreType.DMA((4,))],
+    )
+
+    def mix(recipe, operands, deps=()):
+        return run(
+            functools.partial(mix_kernel, recipe),
+            [state_like] * len(recipe),
+            [coef] + operands,
+            deps=deps,
+        )
+
+    got = swap(theirs)
+    first, total = mix([[(0, 0), (1, 1)], [(0, 2), (1, 3)]], [mine, got])
+    got = send(total, "ctx", [(d, d ^ 2) for d in range(8)])
+    ids_got = send(ids, "exp", [(d, d ^ 1) for d in range(4)])
+    rest_got = swap(residual)
+    weight_got = swap(out_weight)
+    local, queries_here = run(
+        local_kernel,
+        [like((length, here), F32), like((length, here))],
+        [rate, queries, keys, values],
+        4 * heads * length * length * size,
+        heads * length * length,
+        specs=[VM, HBM, VM, VM],
+        scratch_shapes=[pltpu.SemaphoreType.DMA(())],
+    )
+    ids = run(larger_kernel, like(ids.shape, ids.dtype), [ids, ids_got])
+    state, total = mix(
+        [[(0, 4)], [(0, 5), (1, 6)]], [got, total], [rest_got, weight_got]
+    )
+    got = send(total, "ctx", [(d, d + 4) for d in range(4)])
+    ids_got = send(ids, "exp", [(d, d ^ 2) for d in range(4)])
+    ids = run(
+        functools.partial(stack_kernel, 2),
+        like((16, LANES), ids.dtype),
+        [place, ids, ids_got],
+        specs=[SM, VM, VM],
+    )
+    keep, give = mix(
+        [[(0, 7), (1, 8), (2, 9)], [(0, 10), (1, 11), (2, 12)]], [state, got, first]
+    )
+    got = swap(give)
+    ids_got = swap(ids)
+    whole_weight = run(
+        both_kernel,
+        like((CORES * here, cols)),
+        [place, out_weight, weight_got],
+        specs=[SM, VM, VM],
+    )
+    weight_in = outbound(whole_weight)
+    head_out = run(
+        head_kernel,
+        like((length, here)),
+        [place, rate, queries_here, local, keep, got],
+        4 * heads * length * size * size,
+        heads * length * size,
+        specs=[SM] + [VM] * 5,
+    )
+    heads_got = swap(head_out)
+    picks = run(
+        functools.partial(picks_kernel, tokens, capacity),
+        like((slots, every)),
+        [place, ids, ids_got],
+        specs=[SM, VM, VM],
+    )
+
+    chunk_f32, chunk_b16 = like((every, cols), F32), like((every, cols))
+    wide = [cols + LANES * (t == GROUPS - 1) for t in range(GROUPS)]
+    weights = {0: [out_weight]}
+    part_of, sent, mixed, joined, near, far = {}, {}, {}, {}, {}, {}
+    along, across, given = {}, {}, {}
+    sums, hidden, mixed_out = {}, None, None
+
+    def project(t):
+        part_of[t], sent[t] = run(
+            functools.partial(project_kernel, t),
+            [chunk_f32, chunk_b16],
+            [place, head_out, heads_got, residual, rest_got] + weights[t],
+            2 * every * here * cols,
+            specs=[SM] + [VM] * (4 + len(weights[t])),
+        )
+
+    def experts(t, roles, pieces):
+        nonlocal hidden
+        hidden, mark = expert_step(place, t, roles, pieces, gate, up, sums, hidden, last[:])
+        if mark is not None:
+            last[:] = [mark]
+
+    project(0)
+    for k in range(GROUPS + 7):
+        if 1 <= k <= GROUPS:
+            t = k - 1
+            part_of[t], out = run(
+                inward_kernel, [chunk_f32, chunk_b16], [part_of[t], along[t]], every * cols
+            )
+            across[t] = send(out, "exp", [(1, 2), (2, 1)])
+        if k == 1:
+            kept, other = run(
+                parts_kernel, [like((here, cols))] * 2, [place, weight_in], specs=[SM, VM]
+            )
+            other = swap(other)
+            weights[3] = [onward(kept)]
+            weights[1], weights[2] = [kept, other], [other, kept]
+            project(1)
+        if k <= GROUPS + 1:
+            pairs = [(0, 1), (3, 2)] if k < GROUPS else []
+            out = sent.get(k)
+            if k >= 2:
+                t = k - 2
+                pairs = pairs + [(1, 0), (2, 3)]
+                operands = [place, part_of[t], across[t]] + ([out] if k < GROUPS else [])
+                out = run(
+                    outward_kernel,
+                    chunk_b16,
+                    operands,
+                    every * cols,
+                    specs=[SM] + [VM] * (len(operands) - 1),
+                )
+            given[k] = out
+            along[k] = send(out, "exp", pairs)
+        if k in (1, 2):
+            project(k + 1)
+        if 3 <= k <= GROUPS + 2:
+            t = k - 3
+            outs = [like((slots, wide[t])), chunk_b16]
+            known = []
+            if t == GROUPS - 1:
+                outs.append(like((tokens, GROUPS * cols)))
+                known = [mixed[n] for n in range(t)]
+            x, mixed[t], *gives = run(
+                functools.partial(dispatch_kernel, t),
+                outs,
+                [place, along[k - 1], given[k - 1], gain, picks] + known,
+                2 * slots * every * wide[t],
+                specs=[SM] + [VM] * (4 + len(known)),
+            )
+            x_got = swap(x)
+            if gives:
+                mixed_got = swap(gives[0])
+        if 4 <= k <= GROUPS + 3:
+            t = k - 4
+            half = run(
+                half_kernel,
+                like((slots // 2, near[t].shape[1])),
+                [place, near[t]],
+                specs=[SM, VM],
+            )
+            far[t] = onward(half)
+            near[t] = [near[t], swap(near[t])]
+        if 3 <= k <= GROUPS + 2:
+            t = k - 3
+            joined[t] = run(
+                functools.partial(join_kernel, cols),
+                like((slots, wide[t] + cols)),
+                [place, x, x_got],
+                specs=[SM, VM, VM],
+            )
+            near[t] = outbound(joined[t])
+        if 4 <= k <= GROUPS + 3:
+            t = k - 4
+            experts(t, ROLES[:3], [[joined[t]], [near[t][0]], [near[t][1]]])
+        if 5 <= k <= GROUPS + 4:
+            t = k - 5
+            if t == GROUPS - 1:
+                mixed_out = call(
+                    mixed_kernel,
+                    like((tokens, model)),
+                    [place, mixed_got] + [mixed[n] for n in range(GROUPS)],
+                    deps=last[:],
+                    specs=[SM] + [VM] * (GROUPS + 1),
+                )
+            experts(t, ROLES[3:], [[far[t], swap(far[t])]])
+    return (mixed_out, hidden[None])
 
 
 def entering(value, axis, combine, identity):
@@ -43,7 +675,7 @@
     return jnp.einsum("bepr,rt->bept", hits.astype(jnp.float32), to_token)
 
 
-def per_device(
+def on_any_mesh(
     queries,
     key_rows,
     value_rows,
@@ -142,6 +774,14 @@
         P("exp", "ctx", None),
     )
     out_specs = (P(("ctx", "exp"), None), P("exp", "ctx", None))
+    square, line = mesh.shape["ctx"] == GROUPS * CORES, mesh.shape["exp"] == 4
+
+    def per_device(*args):
+        tokens, model = args[5].shape
+        fits = square and line and 2 * tokens == LANES and args[3].shape[0] % CORES == 0
+        fits = fits and model % (GROUPS * CORES * LANES) == 0
+        return (on_square if fits else on_any_mesh)(*args)
+
     return jax.shard_map(
         per_device, mesh=mesh, in_specs=in_specs, out_specs=out_specs, check_vma=False
     )

time: 291 us -> 176 us (0.60)
  waiting for transfers between devices: 158 us -> 69.2 us
  starting transfers between devices: 0.16 us -> 51.2 us
  Pallas kernels: 0 us -> 49.3 us
  blocking collectives: 49 us -> 0 us
  matrix products: 34.8 us -> 0 us
  other arithmetic: 26.3 us -> 1.49 us
  between operations: 14.5 us -> 1.41 us
  local copies, waits for them, and re-layouts: 6.81 us -> 3.19 us
    all_gather x3 -> x0, waiting for transfers between devices: 102 us -> none  [the longest x1 58 us: per_device(): piece = lax.all_gather(received, 'ctx', axis=0, tiled=True)]
    ppermute x0 -> x44, waiting for transfers between devices: none -> 69.2 us  [send(): return lax.ppermute(x, axis, pairs)]
    reduce_scatter x1 -> x0, waiting for transfers between devices: 56 us -> none  [per_device(): lax.psum_scatter(partial_rows, 'exp', scatter_dimension=0, tiled=True)]
    ppermute x0 -> x44, starting transfers between devices: none -> 51.2 us  [send(): return lax.ppermute(x, axis, pairs)]
    pallas_call x0 -> x44, Pallas kernels: none -> 49.3 us  [call(): pl.pallas_call(body, out_shape=out_shape, in_specs=list(specs or [VM] * c...]
    dot_general x7 -> x0, matrix products: 34.8 us -> none  [the longest x1 9.19 us: per_device(): lax.dot_general(gate_here, piece, contract, preferred_element_type=jnp.fl...]
    all_to_all x1 -> x0, blocking collectives: 33 us -> none  [per_device(): lax.all_to_all(buffer, 'exp', split_axis=0, concat_axis=0, tiled=True)]
    select_n x9 -> x1, other arithmetic: 16.9 us -> 0.01 us  [on_square(): ids = jnp.where(lane // tokens == exp % (LANES // tokens), turned, -1)]
  transfers between devices with their start and end apart: 4 -> 44, of which waited for: 4 -> 19; matrix products, arithmetic and copies ran while one was open for 11% -> 1% of each run, Pallas kernels for 0% -> 24%
where the time goes in v5:
time: 176 us
  waiting for transfers between devices  69.2 us (39%)
  starting transfers between devices  51.2 us (29%)
  Pallas kernels  49.3 us (28%)
  local copies, waits for them, and re-layouts  3.19 us (2%)
    ppermute x44, waiting for transfers between devices, send(): return lax.ppermute(x, axis, pairs)  69.2 us
    ppermute x44, starting transfers between devices, send(): return lax.ppermute(x, axis, pairs)  51.2 us
    pallas_call x44, Pallas kernels, call(): pl.pallas_call(body, out_shape=out_shape, in_specs=list(specs or [VM] * c...  49.3 us
  transfers between devices with their start and end apart: 44, of which 19 were waited for; matrix products, arithmetic and copies ran while one was open for 1% of the time, Pallas kernels for 24%

profile of v5, /device:TPU:0, one launch (start us, length us, event | category | flops | bytes accessed | tf_op | source)
XLA Modules:
  0.0 175.7 jit_solution(14314119244842230218)
XLA Ops:
  2.6 0.7 multiply_bitcast_fusion
  3.7 1.1 copy-done.5
  4.8 1.0 copy-done.6
  5.8 1.4 shard_map.113
  7.8 1.0 collective-permute-done.refs_2_
  8.9 2.7 %collective-permute-start.1 = (f32[4,128,128]{2,1,0:T(8,128)S(1)}, f32[4,128,128]{2,1,0:T(8,128)S(1)}, u32[]{:S(2)}, u32[]{:S(2)}) collective-permute-start(f32[4,128,128]{2,1,0:T(8,128)S(1)} %get-tuple-element.72.refs_2_), channel_id=1, source_target_pairs={{0,8},{4,12},{8,0},{12,4},{16,24},{20,28},{24,16},{28,20},{1,9},{5... | collective-permute-start | bytes 786440 | tf_op jit(solution)/shard_map/ppermute | solution.py:399
  11.6 1.6 collective-permute-start.2
  13.2 1.1 shard_map.115
  14.3 0.9 collective-permute-done.2.refs_1_
  15.2 3.2 %collective-permute-done.1.refs_1_ = f32[4,128,128]{2,1,0:T(8,128)S(1)} collective-permute-done((f32[4,128,128]{2,1,0:T(8,128)S(1)}, f32[4,128,128]{2,1,0:T(8,128)S(1)}, u32[]{:S(2)}, u32[]{:S(2)}) %collective-permute-start.1) | collective-permute-done | bytes 262176 | tf_op jit(solution)/shard_map/ppermute | solution.py:399
  18.5 3.7 %collective-permute-start.5 = (f32[4,128,128]{2,1,0:T(8,128)S(1)}, f32[4,128,128]{2,1,0:T(8,128)S(1)}, u32[]{:S(2)}, u32[]{:S(2)}) collective-permute-start(f32[4,128,128]{2,1,0:T(8,128)S(1)} %get-tuple-element.74), channel_id=1, source_target_pairs={{0,16},{4,20},{8,24},{12,28},{1,17},{5,21},{9,25},{13,29},{2,18},{... | collective-permute-start | bytes 786440 | tf_op jit(solution)/shard_map/ppermute | solution.py:399
  22.2 2.7 %collective-permute-start.6 = (s32[8,128]{1,0:T(8,128)S(1)}, s32[8,128]{1,0:T(8,128)S(1)}, u32[]{:S(2)}, u32[]{:S(2)}) collective-permute-start(s32[8,128]{1,0:T(8,128)S(1)} %shard_map.116.refs_3_.refs_1_), channel_id=1, source_target_pairs={{0,2},{1,3},{2,0},{3,1},{4,6},{5,7},{6,4},{7,5},{8,10},{9,11},{10,... | collective-permute-start | bytes 12296 | tf_op jit(solution)/shard_map/ppermute | solution.py:399
  24.9 1.9 %collective-permute-done.6.refs_2_ = s32[8,128]{1,0:T(8,128)S(1)} collective-permute-done((s32[8,128]{1,0:T(8,128)S(1)}, s32[8,128]{1,0:T(8,128)S(1)}, u32[]{:S(2)}, u32[]{:S(2)}) %collective-permute-start.6) | collective-permute-done | bytes 4128 | tf_op jit(solution)/shard_map/ppermute | solution.py:399
  27.6 0.7 shard_map.120.refs_6_
  28.2 1.6 collective-permute-start.9
  29.8 1.5 collective-permute-done.7.refs_5_
  31.3 1.3 shard_map.121.refs_3_.refs_1_
  33.2 1.4 collective-permute-done.10.refs_2_
  34.6 0.8 shard_map.122.refs_6_.refs_4_
  35.5 1.2 shard_map.123
  36.7 3.5 %collective-permute-start.11 = (bf16[512,384]{1,0:T(8,128)(2,1)S(1)}, bf16[512,384]{1,0:T(8,128)(2,1)S(1)}, u32[]{:S(2)}, u32[]{:S(2)}) collective-permute-start(bf16[512,384]{1,0:T(8,128)(2,1)S(1)} %get-tuple-element.78), channel_id=1, source_target_pairs={{0,1},{3,2},{4,5},{7,6},{8,9},{11,10},{12,13},{15,14},{16,17},{19,... | collective-permute-start | bytes 1179656 | tf_op jit(solution)/shard_map/ppermute | solution.py:399
  40.2 8.6 %collective-permute-done.11.refs_1_ = bf16[512,384]{1,0:T(8,128)(2,1)S(1)} collective-permute-done((bf16[512,384]{1,0:T(8,128)(2,1)S(1)}, bf16[512,384]{1,0:T(8,128)(2,1)S(1)}, u32[]{:S(2)}, u32[]{:S(2)}) %collective-permute-start.11) | collective-permute-done | bytes 393248 | tf_op jit(solution)/shard_map/ppermute | solution.py:399
  49.8 2.5 %collective-permute-start.12 = (bf16[1024,384]{1,0:T(8,128)(2,1)S(1)}, bf16[1024,384]{1,0:T(8,128)(2,1)S(1)}, u32[]{:S(2)}, u32[]{:S(2)}) collective-permute-start(bf16[1024,384]{1,0:T(8,128)(2,1)S(1)} %get-tuple-element.80.refs_5_.refs_7_.refs_6_), channel_id=1, source_target_pairs={{0,16},{4,12},{8,24},{12,4},{16,0},{20,28},{24,8},{28,20},{1,17},{... | collective-permute-start | bytes 2359304 | tf_op jit(solution)/shard_map/ppermute | solution.py:399
  52.3 1.3 shard_map.126
  53.6 4.4 %collective-permute-start.15 = (bf16[512,384]{1,0:T(8,128)(2,1)S(1)}, bf16[512,384]{1,0:T(8,128)(2,1)S(1)}, u32[]{:S(2)}, u32[]{:S(2)}) collective-permute-start(bf16[512,384]{1,0:T(8,128)(2,1)S(1)} %get-tuple-element.85), channel_id=1, source_target_pairs={{0,1},{3,2},{4,5},{7,6},{8,9},{11,10},{12,13},{15,14},{16,17},{19,... | collective-permute-start | bytes 1179656 | tf_op jit(solution)/shard_map/ppermute | solution.py:399
  58.0 0.7 collective-permute-start.13
  58.7 1.3 shard_map.127
  60.0 6.4 %collective-permute-done.15.refs_1_ = bf16[512,384]{1,0:T(8,128)(2,1)S(1)} collective-permute-done((bf16[512,384]{1,0:T(8,128)(2,1)S(1)}, bf16[512,384]{1,0:T(8,128)(2,1)S(1)}, u32[]{:S(2)}, u32[]{:S(2)}) %collective-permute-start.15) | collective-permute-done | bytes 393248 | tf_op jit(solution)/shard_map/ppermute | solution.py:399
  67.1 3.7 %collective-permute-start.17 = (bf16[512,384]{1,0:T(8,128)(2,1)S(1)}, bf16[512,384]{1,0:T(8,128)(2,1)S(1)}, u32[]{:S(2)}, u32[]{:S(2)}) collective-permute-start(bf16[512,384]{1,0:T(8,128)(2,1)S(1)} %shard_map.129.refs_6_.refs_2_), channel_id=1, source_target_pairs={{0,1},{3,2},{1,0},{2,3},{4,5},{7,6},{5,4},{6,7},{8,9},{11,10},{9,8... | collective-permute-start | bytes 1179656 | tf_op jit(solution)/shard_map/ppermute | solution.py:399
  71.5 1.2 shard_map.130
  72.8 6.3 %collective-permute-done.17.refs_1_ = bf16[512,384]{1,0:T(8,128)(2,1)S(1)} collective-permute-done((bf16[512,384]{1,0:T(8,128)(2,1)S(1)}, bf16[512,384]{1,0:T(8,128)(2,1)S(1)}, u32[]{:S(2)}, u32[]{:S(2)}) %collective-permute-start.17) | collective-permute-done | bytes 393248 | tf_op jit(solution)/shard_map/ppermute | solution.py:399
  79.9 0.9 shard_map.133
  81.0 3.5 %collective-permute-start.18 = (bf16[512,384]{1,0:T(8,128)(2,1)S(1)}, bf16[512,384]{1,0:T(8,128)(2,1)S(1)}, u32[]{:S(2)}, u32[]{:S(2)}) collective-permute-start(bf16[512,384]{1,0:T(8,128)(2,1)S(1)} %shard_map.132.refs_5_.refs_2_), channel_id=1, source_target_pairs={{0,1},{3,2},{1,0},{2,3},{4,5},{7,6},{5,4},{6,7},{8,9},{11,10},{9,8... | collective-permute-start | bytes 1179656 | tf_op jit(solution)/shard_map/ppermute | solution.py:399
  85.8 1.0 collective-permute-start.21
  86.7 7.5 %collective-permute-done.18.refs_1_ = bf16[512,384]{1,0:T(8,128)(2,1)S(1)} collective-permute-done((bf16[512,384]{1,0:T(8,128)(2,1)S(1)}, bf16[512,384]{1,0:T(8,128)(2,1)S(1)}, u32[]{:S(2)}, u32[]{:S(2)}) %collective-permute-start.18) | collective-permute-done | bytes 393248 | tf_op jit(solution)/shard_map/ppermute | solution.py:399
  95.0 0.9 shard_map.137
  96.6 1.0 collective-permute-done.24.refs_2_
  98.2 1.0 collective-permute-start.29
  99.1 1.8 collective-permute-start.22
  101.5 1.5 collective-permute-start.26
  103.0 5.1 %collective-permute-done.29.refs_1_.refs_4_ = bf16[384,768]{1,0:T(8,128)(2,1)S(1)} collective-permute-done((bf16[384,768]{1,0:T(8,128)(2,1)S(1)}, bf16[384,768]{1,0:T(8,128)(2,1)S(1)}, u32[]{:S(2)}, u32[]{:S(2)}) %collective-permute-start.29) | collective-permute-done | bytes 589856 | tf_op jit(solution)/shard_map/ppermute | solution.py:399
  108.2 2.7 %collective-permute-start.27 = (bf16[192,768]{1,0:T(8,128)(2,1)S(1)}, bf16[192,768]{1,0:T(8,128)(2,1)S(1)}, u32[]{:S(2)}, u32[]{:S(2)}) collective-permute-start(bf16[192,768]{1,0:T(8,128)(2,1)S(1)} %shard_map.138.refs_3_), channel_id=1, source_target_pairs={{0,16},{4,12},{8,24},{12,4},{16,0},{20,28},{24,8},{28,20},{1,17},{... | collective-permute-start | bytes 884744 | tf_op jit(solution)/shard_map/ppermute | solution.py:399
  110.9 3.5 %shard_map.140 = (f32[576,384]{1,0:T(8,128)S(1)}, f32[576,384]{1,0:T(8,128)S(1)}, f32[576,384]{1,0:T(8,128)S(1)}, f32[576,384]{1,0:T(8,128)S(1)}, f32[576,384]{1,0:T(8,128)S(1)}, /*index=5*/f32[576,384]{1,0:T(8,128)S(1)}) custom-call(s32[3]{0:T(128)S(1)} %pad_add_fusion.refs_0_, bf16[576,3072]{1,0:T(8,128)(2,1)S(1)} %bitcast.20, ...), custom_call_target="tpu_custom_call" | custom-call | flops 2038431744 | bytes 14155788 | tf_op jit(solution)/shard_map/pallas_call | solution.py:46
  115.0 3.1 %collective-permute-done.26.refs_1_ = bf16[512,384]{1,0:T(8,128)(2,1)S(1)} collective-permute-done((bf16[512,384]{1,0:T(8,128)(2,1)S(1)}, bf16[512,384]{1,0:T(8,128)(2,1)S(1)}, u32[]{:S(2)}, u32[]{:S(2)}) %collective-permute-start.26) | collective-permute-done | bytes 393248 | tf_op jit(solution)/shard_map/ppermute | solution.py:399
  118.1 0.9 shard_map.142
  119.2 1.3 collective-permute-start.25
  122.8 3.5 %shard_map.145 = (f32[576,384]{1,0:T(8,128)S(1)}, f32[576,384]{1,0:T(8,128)S(1)}, f32[576,384]{1,0:T(8,128)S(1)}, f32[576,384]{1,0:T(8,128)S(1)}, f32[576,384]{1,0:T(8,128)S(1)}, /*index=5*/f32[576,384]{1,0:T(8,128)S(1)}) custom-call(s32[3]{0:T(128)S(1)} %pad_add_fusion.refs_0_, bf16[576,3072]{1,0:T(8,128)(2,1)S(1)} %bitcast.21, ...), custom_call_target="tpu_custom_call" | custom-call | flops 2038431744 | bytes 19464204 | tf_op jit(solution)/shard_map/pallas_call | solution.py:46
  126.3 1.7 shard_map.146
  128.0 4.6 %collective-permute-done.25.refs_1_ = bf16[512,384]{1,0:T(8,128)(2,1)S(1)} collective-permute-done((bf16[512,384]{1,0:T(8,128)(2,1)S(1)}, bf16[512,384]{1,0:T(8,128)(2,1)S(1)}, u32[]{:S(2)}, u32[]{:S(2)}) %collective-permute-start.25) | collective-permute-done | bytes 393248 | tf_op jit(solution)/shard_map/ppermute | solution.py:399
  132.5 1.3 shard_map.147
  134.5 1.1 collective-permute-done.39.refs_2_
  135.6 0.7 shard_map.149.refs_12_.refs_3_
  137.4 1.6 collective-permute-start.36
  139.1 8.3 %collective-permute-done.36.refs_3_ = bf16[192,768]{1,0:T(8,128)(2,1)S(1)} collective-permute-done((bf16[192,768]{1,0:T(8,128)(2,1)S(1)}, bf16[192,768]{1,0:T(8,128)(2,1)S(1)}, u32[]{:S(2)}, u32[]{:S(2)}) %collective-permute-start.36) | collective-permute-done | bytes 294944 | tf_op jit(solution)/shard_map/ppermute | solution.py:399
  147.4 1.6 collective-permute-start.34
  149.0 1.5 collective-permute-done.40.refs_1_.refs_4_
  150.5 3.5 %shard_map.150 = (f32[576,384]{1,0:T(8,128)S(1)}, f32[576,384]{1,0:T(8,128)S(1)}, f32[576,384]{1,0:T(8,128)S(1)}, f32[576,384]{1,0:T(8,128)S(1)}, f32[576,384]{1,0:T(8,128)S(1)}, /*index=5*/f32[576,384]{1,0:T(8,128)S(1)}) custom-call(s32[3]{0:T(128)S(1)} %pad_add_fusion.refs_0_, bf16[576,3072]{1,0:T(8,128)(2,1)S(1)} %bitcast.23, ...), custom_call_target="tpu_custom_call" | custom-call | flops 2038431744 | bytes 19464204 | tf_op jit(solution)/shard_map/pallas_call | solution.py:46
  154.0 1.7 shard_map.151
  156.3 1.3 collective-permute-start.41
  158.0 5.5 %collective-permute-done.41.refs_3_ = bf16[192,896]{1,0:T(8,128)(2,1)S(1)} collective-permute-done((bf16[192,896]{1,0:T(8,128)(2,1)S(1)}, bf16[192,896]{1,0:T(8,128)(2,1)S(1)}, u32[]{:S(2)}, u32[]{:S(2)}) %collective-permute-start.41) | collective-permute-done | bytes 344096 | tf_op jit(solution)/shard_map/ppermute | solution.py:399
  163.6 1.7 shard_map.153
  165.3 1.3 shard_map.154
  166.6 6.0 %shard_map.155.refs_7_ = bf16[576,1536]{1,0:T(8,128)(2,1)} custom-call(s32[3]{0:T(128)S(1)} %pad_add_fusion.refs_0_, bf16[576,3072]{1,0:T(8,128)(2,1)S(1)} %bitcast.26, bf16[576,3072]{1,0:T(8,128)(2,1)S(1)} %bitcast.34, bf16[384,896]{1,0:T(8,128)(2,1)S(1)} %shard_map.149.refs_12_.refs_3_, bf16[384,896]{1,0:T(8,128)(2,1)S(1)} %collective-permute-done.40.refs_1_.refs_4_, ...), custom_call_target="tpu_custom_call" | custom-call | flops 2038431744 | bytes 16220172 | tf_op jit(solution)/shard_map/pallas_call | solution.py:46
  172.6 3.0 %shard_map.156 = bf16[576,1536]{1,0:T(8,128)(2,1)} custom-call(s32[3]{0:T(128)S(1)} %pad_add_fusion.refs_0_, bf16[576,3072]{1,0:T(8,128)(2,1)S(1)} %bitcast.27, bf16[576,3072]{1,0:T(8,128)(2,1)S(1)} %bitcast.35, bf16[192,896]{1,0:T(8,128)(2,1)S(1)} %collective-permute-done.41.refs_3_, ...), custom_call_target="tpu_custom_call", output_to_operand_aliasing={{}: (7, {})} | custom-call | flops 679477248 | bytes 13074444 | tf_op jit(solution)/shard_map/pallas_call | solution.py:46
  (99 shorter events, 17.5 us)
Async XLA Ops:
  0.6 12.6 %copy-start.4 = (bf16[256,1024]{1,0:T(8,128)(2,1)S(1)}, bf16[256,1024]{1,0:T(8,128)(2,1)}, u32[]{:S(2)}) copy-start(bf16[256,1024]{1,0:T(8,128)(2,1)} %refs_1_.2) | copy-start | bytes 1572868
  0.6 17.8 %collective-permute-start.4 = (bf16[1024,384]{1,0:T(8,128)(2,1)}, bf16[1024,384]{1,0:T(8,128)(2,1)S(1)}, u32[]{:S(2)}, u32[]{:S(2)}) collective-permute-start(bf16[1024,384]{1,0:T(8,128)(2,1)} %refs_5_.1), channel_id=1, source_target_pairs={{0,4},{4,0},{8,12},{12,8},{16,20},{20,16},{24,28},{28,24},{1,5},{5... | collective-permute-start | bytes 2359304 | tf_op jit(solution)/shard_map/ppermute | solution.py:399
  3.7 1.1 copy-start.5
  4.8 1.0 copy-start.6
  7.2 1.6 collective-permute-start
  7.4 7.8 %collective-permute-start.3 = (bf16[64,3072]{1,0:T(8,128)(2,1)}, bf16[64,3072]{1,0:T(8,128)(2,1)S(1)}, u32[]{:S(2)}, u32[]{:S(2)}) collective-permute-start(bf16[64,3072]{1,0:T(8,128)(2,1)} %refs_3_.9), channel_id=1, source_target_pairs={{0,4},{4,0},{8,12},{12,8},{16,20},{20,16},{24,28},{28,24},{1,5},{5... | collective-permute-start | bytes 1179656 | tf_op jit(solution)/shard_map/ppermute | solution.py:399
  8.9 9.5 %collective-permute-start.1 = (f32[4,128,128]{2,1,0:T(8,128)S(1)}, f32[4,128,128]{2,1,0:T(8,128)S(1)}, u32[]{:S(2)}, u32[]{:S(2)}) collective-permute-start(f32[4,128,128]{2,1,0:T(8,128)S(1)} %get-tuple-element.72.refs_2_), channel_id=1, source_target_pairs={{0,8},{4,12},{8,0},{12,4},{16,24},{20,28},{24,16},{28,20},{1,9},{5... | collective-permute-start | bytes 786440 | tf_op jit(solution)/shard_map/ppermute | solution.py:399
  11.6 3.6 %collective-permute-start.2 = (s32[8,128]{1,0:T(8,128)S(1)}, s32[8,128]{1,0:T(8,128)S(1)}, u32[]{:S(2)}, u32[]{:S(2)}) collective-permute-start(s32[8,128]{1,0:T(8,128)S(1)} %pad.4.refs_5_.refs_0_), channel_id=1, source_target_pairs={{0,1},{1,0},{2,3},{3,2},{4,5},{5,4},{6,7},{7,6},{8,9},{9,8},{10,11... | collective-permute-start | bytes 12296 | tf_op jit(solution)/shard_map/ppermute | solution.py:399
  15.2 12.3 %copy-start.3 = (bf16[1024,384]{1,0:T(8,128)(2,1)S(1)}, bf16[1024,384]{1,0:T(8,128)(2,1)}, u32[]{:S(2)}) copy-start(bf16[1024,384]{1,0:T(8,128)(2,1)} %refs_5_.1) | copy-start | bytes 2359300
  18.5 8.9 %collective-permute-start.5 = (f32[4,128,128]{2,1,0:T(8,128)S(1)}, f32[4,128,128]{2,1,0:T(8,128)S(1)}, u32[]{:S(2)}, u32[]{:S(2)}) collective-permute-start(f32[4,128,128]{2,1,0:T(8,128)S(1)} %get-tuple-element.74), channel_id=1, source_target_pairs={{0,16},{4,20},{8,24},{12,28},{1,17},{5,21},{9,25},{13,29},{2,18},{... | collective-permute-start | bytes 786440 | tf_op jit(solution)/shard_map/ppermute | solution.py:399
  22.2 4.6 %collective-permute-start.6 = (s32[8,128]{1,0:T(8,128)S(1)}, s32[8,128]{1,0:T(8,128)S(1)}, u32[]{:S(2)}, u32[]{:S(2)}) collective-permute-start(s32[8,128]{1,0:T(8,128)S(1)} %shard_map.116.refs_3_.refs_1_), channel_id=1, source_target_pairs={{0,2},{1,3},{2,0},{3,1},{4,6},{5,7},{6,4},{7,5},{8,10},{9,11},{10,... | collective-permute-start | bytes 12296 | tf_op jit(solution)/shard_map/ppermute | solution.py:399
  28.2 20.8 %collective-permute-start.9 = (bf16[2048,384]{1,0:T(8,128)(2,1)S(1)}, bf16[2048,384]{1,0:T(8,128)(2,1)S(1)}, u32[]{:S(2)}, u32[]{:S(2)}) collective-permute-start(bf16[2048,384]{1,0:T(8,128)(2,1)S(1)} %shard_map.120.refs_6_), channel_id=1, source_target_pairs={{0,8},{4,20},{8,0},{12,28},{16,24},{20,4},{24,16},{28,12},{1,9},{5... | collective-permute-start | bytes 4718600 | tf_op jit(solution)/shard_map/ppermute | solution.py:399
  29.8 1.5 collective-permute-start.7
  31.3 4.1 %copy-start.2 = (bf16[64,3072]{1,0:T(8,128)(2,1)S(1)}, bf16[64,3072]{1,0:T(8,128)(2,1)}, u32[]{:S(2)}) copy-start(bf16[64,3072]{1,0:T(8,128)(2,1)} %refs_3_.9) | copy-start | bytes 1179652
  32.6 2.8 %collective-permute-start.8 = (bf16[256,1024]{1,0:T(8,128)(2,1)S(1)}, bf16[256,1024]{1,0:T(8,128)(2,1)S(1)}, u32[]{:S(2)}, u32[]{:S(2)}) collective-permute-start(bf16[256,1024]{1,0:T(8,128)(2,1)S(1)} %shard_map.121.refs_3_.refs_1_), channel_id=1, source_target_pairs={{0,4},{4,0},{8,12},{12,8},{16,20},{20,16},{24,28},{28,24},{1,5},{5... | collective-permute-start | bytes 1572872 | tf_op jit(solution)/shard_map/ppermute | solution.py:399
  32.8 1.8 %collective-permute-start.10 = (s32[16,128]{1,0:T(8,128)S(1)}, s32[16,128]{1,0:T(8,128)S(1)}, u32[]{:S(2)}, u32[]{:S(2)}) collective-permute-start(s32[16,128]{1,0:T(8,128)S(1)} %shard_map.118.refs_4_.refs_1_), channel_id=1, source_target_pairs={{0,4},{4,0},{8,12},{12,8},{16,20},{20,16},{24,28},{28,24},{1,5},{5... | collective-permute-start | bytes 24584 | tf_op jit(solution)/shard_map/ppermute | solution.py:399
  36.7 12.1 %collective-permute-start.11 = (bf16[512,384]{1,0:T(8,128)(2,1)S(1)}, bf16[512,384]{1,0:T(8,128)(2,1)S(1)}, u32[]{:S(2)}, u32[]{:S(2)}) collective-permute-start(bf16[512,384]{1,0:T(8,128)(2,1)S(1)} %get-tuple-element.78), channel_id=1, source_target_pairs={{0,1},{3,2},{4,5},{7,6},{8,9},{11,10},{12,13},{15,14},{16,17},{19,... | collective-permute-start | bytes 1179656 | tf_op jit(solution)/shard_map/ppermute | solution.py:399
  49.7 2.6 %collective-permute-start.14 = (bf16[1024,384]{1,0:T(8,128)(2,1)S(1)}, bf16[1024,384]{1,0:T(8,128)(2,1)S(1)}, u32[]{:S(2)}, u32[]{:S(2)}) collective-permute-start(bf16[1024,384]{1,0:T(8,128)(2,1)S(1)} %get-tuple-element.82), channel_id=1, source_target_pairs={{0,4},{4,0},{8,12},{12,8},{16,20},{20,16},{24,28},{28,24},{1,5},{5... | collective-permute-start | bytes 2359304 | tf_op jit(solution)/shard_map/ppermute | solution.py:399
  49.8 21.8 %collective-permute-start.12 = (bf16[1024,384]{1,0:T(8,128)(2,1)S(1)}, bf16[1024,384]{1,0:T(8,128)(2,1)S(1)}, u32[]{:S(2)}, u32[]{:S(2)}) collective-permute-start(bf16[1024,384]{1,0:T(8,128)(2,1)S(1)} %get-tuple-element.80.refs_5_.refs_7_.refs_6_), channel_id=1, source_target_pairs={{0,16},{4,12},{8,24},{12,4},{16,0},{20,28},{24,8},{28,20},{1,17},{... | collective-permute-start | bytes 2359304 | tf_op jit(solution)/shard_map/ppermute | solution.py:399
  53.6 12.8 %collective-permute-start.15 = (bf16[512,384]{1,0:T(8,128)(2,1)S(1)}, bf16[512,384]{1,0:T(8,128)(2,1)S(1)}, u32[]{:S(2)}, u32[]{:S(2)}) collective-permute-start(bf16[512,384]{1,0:T(8,128)(2,1)S(1)} %get-tuple-element.85), channel_id=1, source_target_pairs={{0,1},{3,2},{4,5},{7,6},{8,9},{11,10},{12,13},{15,14},{16,17},{19,... | collective-permute-start | bytes 1179656 | tf_op jit(solution)/shard_map/ppermute | solution.py:399
  58.0 8.5 %collective-permute-start.13 = (bf16[512,384]{1,0:T(8,128)(2,1)S(1)}, bf16[512,384]{1,0:T(8,128)(2,1)S(1)}, u32[]{:S(2)}, u32[]{:S(2)}) collective-permute-start(bf16[512,384]{1,0:T(8,128)(2,1)S(1)} %get-tuple-element.81), channel_id=1, source_target_pairs={{1,2},{2,1},{5,6},{6,5},{9,10},{10,9},{13,14},{14,13},{17,18},{18,... | collective-permute-start | bytes 1179656 | tf_op jit(solution)/shard_map/ppermute | solution.py:399
  67.1 12.0 %collective-permute-start.17 = (bf16[512,384]{1,0:T(8,128)(2,1)S(1)}, bf16[512,384]{1,0:T(8,128)(2,1)S(1)}, u32[]{:S(2)}, u32[]{:S(2)}) collective-permute-start(bf16[512,384]{1,0:T(8,128)(2,1)S(1)} %shard_map.129.refs_6_.refs_2_), channel_id=1, source_target_pairs={{0,1},{3,2},{1,0},{2,3},{4,5},{7,6},{5,4},{6,7},{8,9},{11,10},{9,8... | collective-permute-start | bytes 1179656 | tf_op jit(solution)/shard_map/ppermute | solution.py:399
  70.8 8.4 %collective-permute-start.16 = (bf16[512,384]{1,0:T(8,128)(2,1)S(1)}, bf16[512,384]{1,0:T(8,128)(2,1)S(1)}, u32[]{:S(2)}, u32[]{:S(2)}) collective-permute-start(bf16[512,384]{1,0:T(8,128)(2,1)S(1)} %get-tuple-element.89), channel_id=1, source_target_pairs={{1,2},{2,1},{5,6},{6,5},{9,10},{10,9},{13,14},{14,13},{17,18},{18,... | collective-permute-start | bytes 1179656 | tf_op jit(solution)/shard_map/ppermute | solution.py:399
  79.2 0.7 copy-start.7
  80.9 4.3 %collective-permute-start.19 = (bf16[384,384]{1,0:T(8,128)(2,1)S(1)}, bf16[384,384]{1,0:T(8,128)(2,1)S(1)}, u32[]{:S(2)}, u32[]{:S(2)}) collective-permute-start(bf16[384,384]{1,0:T(8,128)(2,1)S(1)} %get-tuple-element.92.refs_1_.refs_3_), channel_id=1, source_target_pairs={{0,4},{4,0},{8,12},{12,8},{16,20},{20,16},{24,28},{28,24},{1,5},{5... | collective-permute-start | bytes 884744 | tf_op jit(solution)/shard_map/ppermute | solution.py:399
  81.0 13.2 %collective-permute-start.18 = (bf16[512,384]{1,0:T(8,128)(2,1)S(1)}, bf16[512,384]{1,0:T(8,128)(2,1)S(1)}, u32[]{:S(2)}, u32[]{:S(2)}) collective-permute-start(bf16[512,384]{1,0:T(8,128)(2,1)S(1)} %shard_map.132.refs_5_.refs_2_), channel_id=1, source_target_pairs={{0,1},{3,2},{1,0},{2,3},{4,5},{7,6},{5,4},{6,7},{8,9},{11,10},{9,8... | collective-permute-start | bytes 1179656 | tf_op jit(solution)/shard_map/ppermute | solution.py:399
  84.5 9.8 %collective-permute-start.23 = (bf16[512,384]{1,0:T(8,128)(2,1)S(1)}, bf16[512,384]{1,0:T(8,128)(2,1)S(1)}, u32[]{:S(2)}, u32[]{:S(2)}) collective-permute-start(bf16[512,384]{1,0:T(8,128)(2,1)S(1)} %get-tuple-element.95), channel_id=1, source_target_pairs={{1,2},{2,1},{5,6},{6,5},{9,10},{10,9},{13,14},{14,13},{17,18},{18,... | collective-permute-start | bytes 1179656 | tf_op jit(solution)/shard_map/ppermute | solution.py:399
  85.8 10.2 %collective-permute-start.21 = (bf16[384,768]{1,0:T(8,128)(2,1)S(1)}, bf16[384,768]{1,0:T(8,128)(2,1)S(1)}, u32[]{:S(2)}, u32[]{:S(2)}) collective-permute-start(bf16[384,768]{1,0:T(8,128)(2,1)S(1)} %shard_map.134.refs_2_.refs_3_), channel_id=1, source_target_pairs={{0,8},{4,20},{8,0},{12,28},{16,24},{20,4},{24,16},{28,12},{1,9},{5... | collective-permute-start | bytes 1769480 | tf_op jit(solution)/shard_map/ppermute | solution.py:399
  94.2 16.7 %copy-start.1 = (bf16[1,576,3072]{2,1,0:T(8,128)(2,1)S(1)}, bf16[1,576,3072]{2,1,0:T(8,128)(2,1)}, u32[]{:S(2)}) copy-start(bf16[1,576,3072]{2,1,0:T(8,128)(2,1)} %param.19) | copy-start | bytes 10616836
  95.0 16.0 %copy-start = (bf16[1,576,3072]{2,1,0:T(8,128)(2,1)S(1)}, bf16[1,576,3072]{2,1,0:T(8,128)(2,1)}, u32[]{:S(2)}) copy-start(bf16[1,576,3072]{2,1,0:T(8,128)(2,1)} %param.18) | copy-start | bytes 10616836
  95.9 1.6 collective-permute-start.24
  98.2 9.9 %collective-permute-start.29 = (bf16[384,768]{1,0:T(8,128)(2,1)S(1)}, bf16[384,768]{1,0:T(8,128)(2,1)S(1)}, u32[]{:S(2)}, u32[]{:S(2)}) collective-permute-start(bf16[384,768]{1,0:T(8,128)(2,1)S(1)} %shard_map.139.refs_6_.refs_3_), channel_id=1, source_target_pairs={{0,8},{4,20},{8,0},{12,28},{16,24},{20,4},{24,16},{28,12},{1,9},{5... | collective-permute-start | bytes 1769480 | tf_op jit(solution)/shard_map/ppermute | solution.py:399
  99.1 11.8 %collective-permute-start.22 = (bf16[384,768]{1,0:T(8,128)(2,1)S(1)}, bf16[384,768]{1,0:T(8,128)(2,1)S(1)}, u32[]{:S(2)}, u32[]{:S(2)}) collective-permute-start(bf16[384,768]{1,0:T(8,128)(2,1)S(1)} %collective-permute-done.21.refs_1_.refs_4_), channel_id=1, source_target_pairs={{0,4},{4,0},{8,12},{12,8},{16,20},{20,16},{24,28},{28,24},{1,5},{5... | collective-permute-start | bytes 1769480 | tf_op jit(solution)/shard_map/ppermute | solution.py:399
  100.9 13.5 %collective-permute-start.20 = (bf16[512,384]{1,0:T(8,128)(2,1)S(1)}, bf16[512,384]{1,0:T(8,128)(2,1)S(1)}, u32[]{:S(2)}, u32[]{:S(2)}) collective-permute-start(bf16[512,384]{1,0:T(8,128)(2,1)S(1)} %get-tuple-element.94), channel_id=1, source_target_pairs={{1,2},{2,1},{5,6},{6,5},{9,10},{10,9},{13,14},{14,13},{17,18},{18,... | collective-permute-start | bytes 1179656 | tf_op jit(solution)/shard_map/ppermute | solution.py:399
  101.5 16.6 %collective-permute-start.26 = (bf16[512,384]{1,0:T(8,128)(2,1)S(1)}, bf16[512,384]{1,0:T(8,128)(2,1)S(1)}, u32[]{:S(2)}, u32[]{:S(2)}) collective-permute-start(bf16[512,384]{1,0:T(8,128)(2,1)S(1)} %shard_map.136.refs_5_.refs_2_), channel_id=1, source_target_pairs={{1,0},{2,3},{5,4},{6,7},{9,8},{10,11},{13,12},{14,15},{17,16},{18,... | collective-permute-start | bytes 1179656 | tf_op jit(solution)/shard_map/ppermute | solution.py:399
  108.1 14.7 %collective-permute-start.30 = (bf16[384,768]{1,0:T(8,128)(2,1)S(1)}, bf16[384,768]{1,0:T(8,128)(2,1)S(1)}, u32[]{:S(2)}, u32[]{:S(2)}) collective-permute-start(bf16[384,768]{1,0:T(8,128)(2,1)S(1)} %collective-permute-done.29.refs_1_.refs_4_), channel_id=1, source_target_pairs={{0,4},{4,0},{8,12},{12,8},{16,20},{20,16},{24,28},{28,24},{1,5},{5... | collective-permute-start | bytes 1769480 | tf_op jit(solution)/shard_map/ppermute | solution.py:399
  108.2 12.2 %collective-permute-start.27 = (bf16[192,768]{1,0:T(8,128)(2,1)S(1)}, bf16[192,768]{1,0:T(8,128)(2,1)S(1)}, u32[]{:S(2)}, u32[]{:S(2)}) collective-permute-start(bf16[192,768]{1,0:T(8,128)(2,1)S(1)} %shard_map.138.refs_3_), channel_id=1, source_target_pairs={{0,16},{4,12},{8,24},{12,4},{16,0},{20,28},{24,8},{28,20},{1,17},{... | collective-permute-start | bytes 884744 | tf_op jit(solution)/shard_map/ppermute | solution.py:399
  119.1 2.5 %collective-permute-start.31 = (bf16[384,384]{1,0:T(8,128)(2,1)S(1)}, bf16[384,384]{1,0:T(8,128)(2,1)S(1)}, u32[]{:S(2)}, u32[]{:S(2)}) collective-permute-start(bf16[384,384]{1,0:T(8,128)(2,1)S(1)} %get-tuple-element.106.refs_2_.refs_1_), channel_id=1, source_target_pairs={{0,4},{4,0},{8,12},{12,8},{16,20},{20,16},{24,28},{28,24},{1,5},{5... | collective-permute-start | bytes 884744 | tf_op jit(solution)/shard_map/ppermute | solution.py:399
  119.2 13.4 %collective-permute-start.25 = (bf16[512,384]{1,0:T(8,128)(2,1)S(1)}, bf16[512,384]{1,0:T(8,128)(2,1)S(1)}, u32[]{:S(2)}, u32[]{:S(2)}) collective-permute-start(bf16[512,384]{1,0:T(8,128)(2,1)S(1)} %shard_map.141.refs_5_.refs_2_), channel_id=1, source_target_pairs={{1,0},{2,3},{5,4},{6,7},{9,8},{10,11},{13,12},{14,15},{17,16},{18,... | collective-permute-start | bytes 1179656 | tf_op jit(solution)/shard_map/ppermute | solution.py:399
  120.5 5.8 %collective-permute-start.28 = (bf16[192,768]{1,0:T(8,128)(2,1)S(1)}, bf16[192,768]{1,0:T(8,128)(2,1)S(1)}, u32[]{:S(2)}, u32[]{:S(2)}) collective-permute-start(bf16[192,768]{1,0:T(8,128)(2,1)S(1)} %collective-permute-done.27.refs_3_), channel_id=1, source_target_pairs={{0,4},{4,0},{8,12},{12,8},{16,20},{20,16},{24,28},{28,24},{1,5},{5... | collective-permute-start | bytes 884744 | tf_op jit(solution)/shard_map/ppermute | solution.py:399
  122.2 11.7 %collective-permute-start.33 = (bf16[384,768]{1,0:T(8,128)(2,1)S(1)}, bf16[384,768]{1,0:T(8,128)(2,1)S(1)}, u32[]{:S(2)}, u32[]{:S(2)}) collective-permute-start(bf16[384,768]{1,0:T(8,128)(2,1)S(1)} %shard_map.144.refs_12_.refs_3_), channel_id=1, source_target_pairs={{0,8},{4,20},{8,0},{12,28},{16,24},{20,4},{24,16},{28,12},{1,9},{5... | collective-permute-start | bytes 1769480 | tf_op jit(solution)/shard_map/ppermute | solution.py:399
  133.8 1.8 %collective-permute-start.39 = (bf16[384,512]{1,0:T(8,128)(2,1)S(1)}, bf16[384,512]{1,0:T(8,128)(2,1)S(1)}, u32[]{:S(2)}, u32[]{:S(2)}) collective-permute-start(bf16[384,512]{1,0:T(8,128)(2,1)S(1)} %get-tuple-element.111.refs_2_.refs_1_), channel_id=1, source_target_pairs={{0,4},{4,0},{8,12},{12,8},{16,20},{20,16},{24,28},{28,24},{1,5},{5... | collective-permute-start | bytes 1179656 | tf_op jit(solution)/shard_map/ppermute | solution.py:399
  136.3 14.2 %collective-permute-start.40 = (bf16[384,896]{1,0:T(8,128)(2,1)S(1)}, bf16[384,896]{1,0:T(8,128)(2,1)S(1)}, u32[]{:S(2)}, u32[]{:S(2)}) collective-permute-start(bf16[384,896]{1,0:T(8,128)(2,1)S(1)} %shard_map.149.refs_12_.refs_3_), channel_id=1, source_target_pairs={{0,8},{4,20},{8,0},{12,28},{16,24},{20,4},{24,16},{28,12},{1,9},{5... | collective-permute-start | bytes 2064392 | tf_op jit(solution)/shard_map/ppermute | solution.py:399
  136.9 13.6 %collective-permute-start.38 = (bf16[384,768]{1,0:T(8,128)(2,1)S(1)}, bf16[384,768]{1,0:T(8,128)(2,1)S(1)}, u32[]{:S(2)}, u32[]{:S(2)}) collective-permute-start(bf16[384,768]{1,0:T(8,128)(2,1)S(1)} %collective-permute-done.33.refs_1_.refs_4_), channel_id=1, source_target_pairs={{0,4},{4,0},{8,12},{12,8},{16,20},{20,16},{24,28},{28,24},{1,5},{5... | collective-permute-start | bytes 1769480 | tf_op jit(solution)/shard_map/ppermute | solution.py:399
  137.4 9.9 %collective-permute-start.36 = (bf16[192,768]{1,0:T(8,128)(2,1)S(1)}, bf16[192,768]{1,0:T(8,128)(2,1)S(1)}, u32[]{:S(2)}, u32[]{:S(2)}) collective-permute-start(bf16[192,768]{1,0:T(8,128)(2,1)S(1)} %shard_map.143.refs_3_), channel_id=1, source_target_pairs={{0,16},{4,12},{8,24},{12,4},{16,0},{20,28},{24,8},{28,20},{1,17},{... | collective-permute-start | bytes 884744 | tf_op jit(solution)/shard_map/ppermute | solution.py:399
  147.4 6.6 %collective-permute-start.37 = (bf16[192,768]{1,0:T(8,128)(2,1)S(1)}, bf16[192,768]{1,0:T(8,128)(2,1)S(1)}, u32[]{:S(2)}, u32[]{:S(2)}) collective-permute-start(bf16[192,768]{1,0:T(8,128)(2,1)S(1)} %collective-permute-done.36.refs_3_), channel_id=1, source_target_pairs={{0,4},{4,0},{8,12},{12,8},{16,20},{20,16},{24,28},{28,24},{1,5},{5... | collective-permute-start | bytes 884744 | tf_op jit(solution)/shard_map/ppermute | solution.py:399
  147.4 10.1 %collective-permute-start.34 = (bf16[192,768]{1,0:T(8,128)(2,1)S(1)}, bf16[192,768]{1,0:T(8,128)(2,1)S(1)}, u32[]{:S(2)}, u32[]{:S(2)}) collective-permute-start(bf16[192,768]{1,0:T(8,128)(2,1)S(1)} %shard_map.148.refs_3_), channel_id=1, source_target_pairs={{0,16},{4,12},{8,24},{12,4},{16,0},{20,28},{24,8},{28,20},{1,17},{... | collective-permute-start | bytes 884744 | tf_op jit(solution)/shard_map/ppermute | solution.py:399
  150.5 16.1 %collective-permute-start.43 = (bf16[384,896]{1,0:T(8,128)(2,1)S(1)}, bf16[384,896]{1,0:T(8,128)(2,1)S(1)}, u32[]{:S(2)}, u32[]{:S(2)}) collective-permute-start(bf16[384,896]{1,0:T(8,128)(2,1)S(1)} %collective-permute-done.40.refs_1_.refs_4_), channel_id=1, source_target_pairs={{0,4},{4,0},{8,12},{12,8},{16,20},{20,16},{24,28},{28,24},{1,5},{5... | collective-permute-start | bytes 2064392 | tf_op jit(solution)/shard_map/ppermute | solution.py:399
  156.3 7.3 %collective-permute-start.41 = (bf16[192,896]{1,0:T(8,128)(2,1)S(1)}, bf16[192,896]{1,0:T(8,128)(2,1)S(1)}, u32[]{:S(2)}, u32[]{:S(2)}) collective-permute-start(bf16[192,896]{1,0:T(8,128)(2,1)S(1)} %shard_map.152.refs_7_.refs_12_), channel_id=1, source_target_pairs={{0,16},{4,12},{8,24},{12,4},{16,0},{20,28},{24,8},{28,20},{1,17},{... | collective-permute-start | bytes 1032200 | tf_op jit(solution)/shard_map/ppermute | solution.py:399
  157.5 6.0 %collective-permute-start.35 = (bf16[192,768]{1,0:T(8,128)(2,1)S(1)}, bf16[192,768]{1,0:T(8,128)(2,1)S(1)}, u32[]{:S(2)}, u32[]{:S(2)}) collective-permute-start(bf16[192,768]{1,0:T(8,128)(2,1)S(1)} %collective-permute-done.34.refs_3_), channel_id=1, source_target_pairs={{0,4},{4,0},{8,12},{12,8},{16,20},{20,16},{24,28},{28,24},{1,5},{5... | collective-permute-start | bytes 884744 | tf_op jit(solution)/shard_map/ppermute | solution.py:399
  157.5 7.7 %collective-permute-start.32 = (bf16[64,1536]{1,0:T(8,128)(2,1)S(1)}, bf16[64,1536]{1,0:T(8,128)(2,1)S(1)}, u32[]{:S(2)}, u32[]{:S(2)}) collective-permute-start(bf16[64,1536]{1,0:T(8,128)(2,1)S(1)} %get-tuple-element.109), channel_id=1, source_target_pairs={{0,4},{4,0},{8,12},{12,8},{16,20},{20,16},{24,28},{28,24},{1,5},{5... | collective-permute-start | bytes 589832 | tf_op jit(solution)/shard_map/ppermute | solution.py:399
  163.6 9.0 %collective-permute-start.42 = (bf16[192,896]{1,0:T(8,128)(2,1)S(1)}, bf16[192,896]{1,0:T(8,128)(2,1)S(1)}, u32[]{:S(2)}, u32[]{:S(2)}) collective-permute-start(bf16[192,896]{1,0:T(8,128)(2,1)S(1)} %collective-permute-done.41.refs_3_), channel_id=1, source_target_pairs={{0,4},{4,0},{8,12},{12,8},{16,20},{20,16},{24,28},{28,24},{1,5},{5... | collective-permute-start | bytes 1032200 | tf_op jit(solution)/shard_map/ppermute | solution.py:399

commit v6 on v5

--- a/solution.py
+++ b/solution.py
@@ -9,6 +9,7 @@
 
 GROUPS = 4
 CORES = 2
+ORDER = (0, 2, 1, 3)
 LANES = 128
 BF16 = jnp.bfloat16
 F32 = jnp.float32
@@ -78,16 +79,15 @@
         for j in range(part):
             head = half * part + j
             cols = tile(head, size)
-            tail = jnp.exp(rate_ref[head][:, :size] * left)
+            tail = jnp.exp(rate_ref[head] * left)
             high, low = halves(k_ref[:, cols].astype(F32) * tail)
             v = v_ref[:, cols]
             out_ref[j] = dot(high, v, TN) + dot(low, v, TN)
 
 
 def local_kernel(rate_ref, q_in, k_ref, v_ref, out_ref, q_ref, sem):
-    heads = rate_ref.shape[0]
-    length = k_ref.shape[0]
-    size = k_ref.shape[1] // heads
+    length, size = k_ref.shape[0], rate_ref.shape[2]
+    heads = k_ref.shape[1] // size
     copy = pltpu.make_async_copy(q_in, q_ref, sem)
     copy.start()
     rows = lax.broadcasted_iota(jnp.int32, (length, length), 0)
@@ -98,17 +98,20 @@
     copy.wait()
     for h in range(heads):
         at = slice(h * size, (h + 1) * size)
-        masked = jnp.where(keep, jnp.exp(rate_ref[h] * offset), 0.0)
+        rate = jnp.concatenate([rate_ref[h]] * (length // LANES), axis=1)
+        masked = jnp.where(keep, jnp.exp(rate * offset), 0.0)
         weighted = (dot(q_ref[:, at], k_ref[:, at], NT) * masked).astype(BF16)
         out_ref[:, at] = dot(weighted, v_ref[:, at], NN)
 
 
 def mix_kernel(recipe, coef_ref, *refs):
     count = 1 + max(i for terms in recipe for i, _ in terms)
-    for j in range(refs[0].shape[0]):
+    part = refs[0].shape[0]
+    first = CORES * part
+    for j in range(part):
         values = [refs[i][j] for i in range(count)]
         for out_ref, terms in zip(refs[count:], recipe):
-            out_ref[j] = sum(values[i] * coef_ref[row, j] for i, row in terms)
+            out_ref[j] = sum(values[i] * coef_ref[first + row * part + j] for i, row in terms)
 
 
 def scan_rows(chip, core, rate, part, length):
@@ -149,7 +152,7 @@
             high, low = halves(state_ref[j])
             q = q_ref[:, at]
             carried = dot(q, high, NN) + dot(q, low, NN)
-            carried = carried * jnp.exp(rate_ref[head][:, :size] * pos)
+            carried = carried * jnp.exp(rate_ref[head] * pos)
             attended = local_ref[:, at] + carried
             scale = lax.rsqrt(jnp.mean(attended * attended, axis=-1, keepdims=True) + 1e-05)
             out_ref[:, at] = (attended * scale).astype(BF16)
@@ -189,16 +192,15 @@
 def project_kernel(t, place_ref, own_ref, got_ref, rest_ref, rest_got_ref, *refs):
     weights, (sum_ref, sent_ref) = refs[:-2], refs[-2:]
     length, tokens, cols = own_ref.shape[0], rest_ref.shape[0], sum_ref.shape[1]
-    first = place_ref[1] == 0
-    weight = weights[0][...]
-    if len(weights) > 1:
-        weight = jnp.where(first, weight, weights[1][...])
+    depth = own_ref.shape[1] // len(weights)
     at = tile((place_ref[0] ^ t) * CORES + place_ref[1], cols)
     for head_ref, row_ref, half in (
         (own_ref, rest_ref, place_ref[1]),
         (got_ref, rest_got_ref, 1 - place_ref[1]),
     ):
-        value = dot(head_ref[...], weight, NN)
+        value = 0.0
+        for n, weight in enumerate(weights):
+            value = value + dot(head_ref[:, n * depth : (n + 1) * depth], weight[...], NN)
         pieces = []
         for z in range(length // tokens):
             piece = value[z * tokens : (z + 1) * tokens, :]
@@ -220,16 +222,13 @@
     return (place_ref[2] == 0) | (place_ref[2] == 3)
 
 
-def outward_kernel(place_ref, part_ref, got_ref, *refs):
-    total = (part_ref[...] + got_ref[...].astype(F32)).astype(BF16)
-    if len(refs) > 1:
-        total = jnp.where(outer(place_ref), refs[0][...], total)
-    refs[-1][...] = total
-
-
-def dispatch_kernel(t, place_ref, got_ref, given_ref, gain_ref, picks_ref, *refs):
+def total_kernel(part_ref, got_ref, out_ref):
+    out_ref[...] = (part_ref[...] + got_ref[...].astype(F32)).astype(BF16)
+
+
+def dispatch_kernel(t, final, place_ref, got_ref, given_ref, gain_ref, picks_ref, *refs):
     earlier, (out_ref, mixed_ref), gives = refs[:-2], refs[-2:], []
-    if t == GROUPS - 1:
+    if final:
         earlier, (out_ref, mixed_ref, give_ref) = refs[:-3], refs[-3:]
         gives = [give_ref]
     cols = mixed_ref.shape[1]
@@ -272,20 +271,17 @@
         out_ref[:, CORES * cols :] = in_three(total)
 
 
-def half_kernel(place_ref, in_ref, out_ref):
+def half_kernel(place_ref, in_ref, out_ref, all_ref):
     out_ref[...] = in_ref[tile(place_ref[1], out_ref.shape[0]), :]
-
-
-def both_kernel(place_ref, own_ref, got_ref, out_ref):
-    rows = own_ref.shape[0]
-    out_ref[tile(place_ref[1], rows), :] = own_ref[...]
-    out_ref[tile(1 - place_ref[1], rows), :] = got_ref[...]
-
-
-def parts_kernel(place_ref, in_ref, keep_ref, give_ref):
-    rows = keep_ref.shape[0]
-    keep_ref[...] = in_ref[tile(place_ref[1], rows), :]
-    give_ref[...] = in_ref[tile(1 - place_ref[1], rows), :]
+    all_ref[...] = in_ref[...]
+
+
+def copy_kernel(in_ref, out_ref):
+    out_ref[...] = in_ref[...]
+
+
+def rows_kernel(start, in_ref, out_ref):
+    out_ref[...] = in_ref[start : start + out_ref.shape[0], :]
 
 
 def mixed_kernel(place_ref, got_ref, *refs):
@@ -293,19 +289,20 @@
     tokens, cols = out_ref.shape[0], mixed[0].shape[1]
     per = mixed[0].shape[0] // CORES // tokens
     own = tile(place_ref[1] * per + place_ref[2], tokens)
-    for t, ref in enumerate(mixed):
+    for t, ref in zip(ORDER, mixed):
         block = (place_ref[0] ^ t) * CORES
+        n = ORDER.index(t)
         out_ref[:, tile(block + place_ref[1], cols)] = ref[own, :]
-        out_ref[:, tile(block + 1 - place_ref[1], cols)] = got_ref[:, t * cols : (t + 1) * cols]
+        out_ref[:, tile(block + 1 - place_ref[1], cols)] = got_ref[:, n * cols : (n + 1) * cols]
 
 
 ROLES = ("own", "mine", "other", "diagonal")
 
 
-def expert_kernel(t, roles, mode, place_ref, gate_ref, up_ref, *refs):
+def expert_kernel(t, roles, mode, has_sums, place_ref, gate_ref, up_ref, *refs):
     refs = list(refs)
     pieces = [[refs.pop(0) for _ in range(2 if r == "diagonal" else 1)] for r in roles]
-    sums = [[refs.pop(0), refs.pop(0)] for _ in roles] if t > 0 else None
+    sums = [[refs.pop(0), refs.pop(0)] for _ in roles] if has_sums else None
     if mode == "next":
         refs.pop(0)
     model = gate_ref.shape[1]
@@ -315,8 +312,9 @@
         outs = refs[: 2 * len(roles)]
         held = refs[2 * len(roles) :]
     else:
-        outs, ready, sems = refs[0], refs[1], refs[2]
-        held = refs[3:]
+        outs, mark_ref, ready, sems = refs[:4]
+        held = refs[4:]
+        mark_ref[...] = jnp.zeros_like(mark_ref)
     copies = []
     for n, role in enumerate(roles):
         source = place_ref[0] ^ away[role]
@@ -344,32 +342,40 @@
         silu = (0.5 * gated) * (1.0 + jnp.tanh(0.5 * gated))
         ready[n] = (silu * lifted).astype(BF16)
         at = tile(source, ready.shape[2])
-        copies.append(pltpu.make_async_copy(ready.at[n], outs.at[:, at], sems.at[n]))
-        copies[-1].start()
+        rows = ready.shape[1] // 4
+        for q in range(4):
+            cut = slice(q * rows, (q + 1) * rows)
+            copies.append(
+                pltpu.make_async_copy(
+                    ready.at[n, cut], outs.at[cut, at], sems.at[4 * n + q]
+                )
+            )
+            copies[-1].start()
     for copy in copies:
         copy.wait()
 
 
-def expert_step(place, t, roles, pieces, gate, up, sums, hidden, deps):
+def expert_step(place, t, final, roles, pieces, gate, up, sums, hidden, deps):
     hid, model = gate.shape
     width = model // GROUPS
     slots = sum(x.shape[0] for x in pieces[0])
     operands = [place, gate, up] + [x for per in pieces for x in per]
-    if t > 0:
+    has_sums = roles[0] in sums
+    if has_sums:
         operands += [x for r in roles for x in sums[r]]
     specs = [SM] + [VM] * (len(operands) - 1)
     kwargs, mode, scratch = {}, None, []
-    if t == GROUPS - 1:
+    if final:
         mode = "first" if hidden is None else "next"
         if hidden is not None:
             kwargs["input_output_aliases"] = {len(operands): 0}
             operands.append(hidden)
             specs.append(ANY)
-        out_shape = like((hid, slots * GROUPS))
-        kwargs["out_specs"] = ANY
+        out_shape = [like((hid, slots * GROUPS)), like((8, LANES), F32)]
+        kwargs["out_specs"] = [ANY, VM]
         scratch += [
             pltpu.VMEM((len(roles), hid, slots), BF16),
-            pltpu.SemaphoreType.DMA((len(roles),)),
+            pltpu.SemaphoreType.DMA((4 * len(roles),)),
         ]
     else:
         out_shape = [like((hid, slots), F32)] * (2 * len(roles))
@@ -377,7 +383,7 @@
         wide = pieces[roles.index("diagonal")][0].shape[1]
         scratch.append(pltpu.VMEM((slots, wide), BF16))
     out = call(
-        functools.partial(expert_kernel, t, roles, mode),
+        functools.partial(expert_kernel, t, roles, mode, has_sums),
         out_shape,
         operands,
         4 * hid * slots * width * len(roles),
@@ -389,7 +395,7 @@
         **kwargs,
     )
     if mode:
-        return out, None
+        return out
     for n, r in enumerate(roles):
         sums[r] = out[2 * n : 2 * n + 2]
     return hidden, out[0]
@@ -443,23 +449,24 @@
         last[:] = [out[0] if isinstance(out, (list, tuple)) else out]
         return out
 
-    rate = jnp.broadcast_to(-decay_rate[:, None, None], (heads, 1, length))
-    rows = jnp.stack(scan_rows(chip, core, decay_rate, part, length))
-    coef = jnp.broadcast_to(rows[:, :, None, None], rows.shape + (1, size))
-    turned = jnp.tile(expert_ids.T, (1, LANES // tokens))
+    rows = jnp.stack(scan_rows(chip, core, decay_rate, part, length)).reshape(-1)
+    rows = jnp.concatenate([-decay_rate, rows])
+    table = jnp.broadcast_to(rows[:, None, None], (rows.shape[0], 1, LANES))
+    ids = jnp.concatenate([expert_ids.T, expert_ids.T], axis=1)
     lane = jnp.arange(LANES, dtype=jnp.int32)[None, :]
-    ids = jnp.where(lane // tokens == exp % (LANES // tokens), turned, -1)
+    ids = jnp.where(lane // tokens == exp % (LANES // tokens), ids, -1)
     ids = jnp.pad(ids, ((0, 6), (0, 0)), constant_values=-1)
-    gain = moe_gain[None, :] * 1.0
+    gain = moe_gain[None, :]
+    weight_y = send(out_weight, "ctx", [(d, d ^ 4) for d in range(8)])
 
     state_like = like((part, size, size), F32)
     mine, theirs, keys, values = run(
         fresh_kernel,
         [state_like] * 2 + [like((length, here))] * 2,
-        [place, rate, key_rows, value_rows],
+        [place, table, key_rows, value_rows],
         4 * heads * length * size * size,
         heads * length * size,
-        deps=[coef, ids],
+        deps=[ids],
         specs=[SM, VM, HBM, HBM],
         scratch_shapes=[pltpu.SemaphoreType.DMA((4,))],
     )
@@ -468,8 +475,16 @@
         return run(
             functools.partial(mix_kernel, recipe),
             [state_like] * len(recipe),
-            [coef] + operands,
+            [table] + operands,
             deps=deps,
+        )
+
+    def copy(x):
+        return run(copy_kernel, like(x.shape, x.dtype), [x])
+
+    def cut(x, start):
+        return run(
+            functools.partial(rows_kernel, start), like((x.shape[0] // 2, x.shape[1])), [x]
         )
 
     got = swap(theirs)
@@ -477,26 +492,25 @@
     got = send(total, "ctx", [(d, d ^ 2) for d in range(8)])
     ids_got = send(ids, "exp", [(d, d ^ 1) for d in range(4)])
     rest_got = swap(residual)
-    weight_got = swap(out_weight)
     local, queries_here = run(
         local_kernel,
         [like((length, here), F32), like((length, here))],
-        [rate, queries, keys, values],
+        [table, queries, keys, values],
         4 * heads * length * length * size,
         heads * length * length,
         specs=[VM, HBM, VM, VM],
         scratch_shapes=[pltpu.SemaphoreType.DMA(())],
     )
     ids = run(larger_kernel, like(ids.shape, ids.dtype), [ids, ids_got])
-    state, total = mix(
-        [[(0, 4)], [(0, 5), (1, 6)]], [got, total], [rest_got, weight_got]
-    )
+    state, total = mix([[(0, 4)], [(0, 5), (1, 6)]], [got, total], [rest_got])
     got = send(total, "ctx", [(d, d + 4) for d in range(4)])
+    weight_x = send(copy(out_weight), "ctx", [(d, d ^ 2) for d in range(8)])
     ids_got = send(ids, "exp", [(d, d ^ 2) for d in range(4)])
     ids = run(
         functools.partial(stack_kernel, 2),
         like((16, LANES), ids.dtype),
         [place, ids, ids_got],
+        deps=[weight_y],
         specs=[SM, VM, VM],
     )
     keep, give = mix(
@@ -504,17 +518,10 @@
     )
     got = swap(give)
     ids_got = swap(ids)
-    whole_weight = run(
-        both_kernel,
-        like((CORES * here, cols)),
-        [place, out_weight, weight_got],
-        specs=[SM, VM, VM],
-    )
-    weight_in = outbound(whole_weight)
     head_out = run(
         head_kernel,
         like((length, here)),
-        [place, rate, queries_here, local, keep, got],
+        [place, table, queries_here, local, keep, got],
         4 * heads * length * size * size,
         heads * length * size,
         specs=[SM] + [VM] * 5,
@@ -528,111 +535,111 @@
     )
 
     chunk_f32, chunk_b16 = like((every, cols), F32), like((every, cols))
-    wide = [cols + LANES * (t == GROUPS - 1) for t in range(GROUPS)]
-    weights = {0: [out_weight]}
-    part_of, sent, mixed, joined, near, far = {}, {}, {}, {}, {}, {}
-    along, across, given = {}, {}, {}
-    sums, hidden, mixed_out = {}, None, None
-
-    def project(t):
-        part_of[t], sent[t] = run(
-            functools.partial(project_kernel, t),
+    end = GROUPS - 1
+    wide = [cols + LANES * (n == end) for n in range(GROUPS)]
+    weights = [[out_weight], [weight_y], [weight_x], None]
+    parts, totals, mixed, joined = [None] * 4, [None] * 4, [None] * 4, [None] * 4
+    moved = {}
+    sums, hidden = {}, None
+
+    def project(n):
+        parts[n], sent = run(
+            functools.partial(project_kernel, ORDER[n]),
             [chunk_f32, chunk_b16],
-            [place, head_out, heads_got, residual, rest_got] + weights[t],
+            [place, head_out, heads_got, residual, rest_got] + weights[n],
             2 * every * here * cols,
-            specs=[SM] + [VM] * (4 + len(weights[t])),
+            specs=[SM] + [VM] * (4 + len(weights[n])),
         )
-
-    def experts(t, roles, pieces):
+        moved["in", n] = send(sent, "exp", [(0, 1), (3, 2)])
+
+    def inward(n):
+        parts[n], sent = run(
+            inward_kernel, [chunk_f32, chunk_b16], [parts[n], moved["in", n]], every * cols
+        )
+        moved["across", n] = send(sent, "exp", [(1, 2), (2, 1)])
+
+    def outward(n):
+        totals[n] = run(total_kernel, chunk_b16, [parts[n], moved["across", n]], every * cols)
+        moved["out", n] = send(totals[n], "exp", [(1, 0), (2, 3)])
+
+    def dispatch(n):
+        outs = [like((slots, wide[n])), chunk_b16]
+        known = []
+        if n == end:
+            outs.append(like((tokens, GROUPS * cols)))
+            known = mixed[:n]
+        x, mixed[n], *gives = run(
+            functools.partial(dispatch_kernel, ORDER[n], n == end),
+            outs,
+            [place, moved["out", n], totals[n], gain, picks] + known,
+            2 * slots * every * wide[n],
+            specs=[SM] + [VM] * (4 + len(known)),
+        )
+        moved["x", n] = (x, swap(x))
+        if gives:
+            moved["mixed"] = swap(gives[0])
+
+    def join(n):
+        joined[n] = run(
+            functools.partial(join_kernel, cols),
+            like((slots, wide[n] + cols)),
+            [place, *moved["x", n]],
+            specs=[SM, VM, VM],
+        )
+        moved["near", n] = outbound(joined[n])
+
+    def half(n):
+        near = moved["near", n]
+        out, copied = run(
+            half_kernel,
+            [like((slots // 2, near.shape[1])), like(near.shape)],
+            [place, near],
+            specs=[SM, VM],
+        )
+        moved["far", n] = onward(out)
+        moved["other", n] = swap(copied)
+
+    def diagonal(n):
+        moved["far", n] = copy(moved["far", n])
+        moved["rest", n] = swap(moved["far", n])
+
+    def experts(n, roles, pieces):
         nonlocal hidden
-        hidden, mark = expert_step(place, t, roles, pieces, gate, up, sums, hidden, last[:])
-        if mark is not None:
-            last[:] = [mark]
+        hidden, mark = expert_step(
+            place, ORDER[n], n == end, roles, pieces, gate, up, sums, hidden, last[:]
+        )
+        last[:] = [mark]
+
+    def nearer(n):
+        experts(n, ROLES[:3], [[joined[n]], [moved["near", n]], [moved["other", n]]])
+
+    def farther(n):
+        experts(n, ROLES[3:], [[moved["far", n], moved["rest", n]]])
 
     project(0)
-    for k in range(GROUPS + 7):
-        if 1 <= k <= GROUPS:
-            t = k - 1
-            part_of[t], out = run(
-                inward_kernel, [chunk_f32, chunk_b16], [part_of[t], along[t]], every * cols
-            )
-            across[t] = send(out, "exp", [(1, 2), (2, 1)])
-        if k == 1:
-            kept, other = run(
-                parts_kernel, [like((here, cols))] * 2, [place, weight_in], specs=[SM, VM]
-            )
-            other = swap(other)
-            weights[3] = [onward(kept)]
-            weights[1], weights[2] = [kept, other], [other, kept]
-            project(1)
-        if k <= GROUPS + 1:
-            pairs = [(0, 1), (3, 2)] if k < GROUPS else []
-            out = sent.get(k)
-            if k >= 2:
-                t = k - 2
-                pairs = pairs + [(1, 0), (2, 3)]
-                operands = [place, part_of[t], across[t]] + ([out] if k < GROUPS else [])
-                out = run(
-                    outward_kernel,
-                    chunk_b16,
-                    operands,
-                    every * cols,
-                    specs=[SM] + [VM] * (len(operands) - 1),
-                )
-            given[k] = out
-            along[k] = send(out, "exp", pairs)
-        if k in (1, 2):
-            project(k + 1)
-        if 3 <= k <= GROUPS + 2:
-            t = k - 3
-            outs = [like((slots, wide[t])), chunk_b16]
-            known = []
-            if t == GROUPS - 1:
-                outs.append(like((tokens, GROUPS * cols)))
-                known = [mixed[n] for n in range(t)]
-            x, mixed[t], *gives = run(
-                functools.partial(dispatch_kernel, t),
-                outs,
-                [place, along[k - 1], given[k - 1], gain, picks] + known,
-                2 * slots * every * wide[t],
-                specs=[SM] + [VM] * (4 + len(known)),
-            )
-            x_got = swap(x)
-            if gives:
-                mixed_got = swap(gives[0])
-        if 4 <= k <= GROUPS + 3:
-            t = k - 4
-            half = run(
-                half_kernel,
-                like((slots // 2, near[t].shape[1])),
-                [place, near[t]],
-                specs=[SM, VM],
-            )
-            far[t] = onward(half)
-            near[t] = [near[t], swap(near[t])]
-        if 3 <= k <= GROUPS + 2:
-            t = k - 3
-            joined[t] = run(
-                functools.partial(join_kernel, cols),
-                like((slots, wide[t] + cols)),
-                [place, x, x_got],
-                specs=[SM, VM, VM],
-            )
-            near[t] = outbound(joined[t])
-        if 4 <= k <= GROUPS + 3:
-            t = k - 4
-            experts(t, ROLES[:3], [[joined[t]], [near[t][0]], [near[t][1]]])
-        if 5 <= k <= GROUPS + 4:
-            t = k - 5
-            if t == GROUPS - 1:
-                mixed_out = call(
-                    mixed_kernel,
-                    like((tokens, model)),
-                    [place, mixed_got] + [mixed[n] for n in range(GROUPS)],
-                    deps=last[:],
-                    specs=[SM] + [VM] * (GROUPS + 1),
-                )
-            experts(t, ROLES[3:], [[far[t], swap(far[t])]])
+    project(1)
+    project(2)
+    weight_top = send(cut(weight_x, 0), "ctx", [(d, d ^ 4) for d in range(8)])
+    weight_bottom = send(cut(weight_y, here // 2), "ctx", [(d, d ^ 2) for d in range(8)])
+    weights[3] = [weight_top, weight_bottom]
+    for work, n in (
+        (inward, 0), (inward, 1), (project, 3), (outward, 0), (inward, 2), (outward, 1),
+        (dispatch, 0), (inward, 3), (join, 0), (outward, 2), (dispatch, 1), (join, 1),
+        (outward, 3), (half, 0), (dispatch, 2), (nearer, 0), (join, 2), (half, 1),
+        (diagonal, 0), (farther, 0), (dispatch, 3), (nearer, 1), (join, 3), (half, 2),
+        (diagonal, 1), (farther, 1), (nearer, 2), (half, 3), (diagonal, 2), (farther, 2),
+        (nearer, 3),
+    ):
+        work(n)
+    mixed_out = call(
+        mixed_kernel,
+        like((tokens, model)),
+        [place, moved["mixed"]] + mixed,
+        deps=last[:],
+        specs=[SM] + [VM] * (GROUPS + 1),
+    )
+    diagonal(3)
+    farther(3)
     return (mixed_out, hidden[None])
 
 

time: 176 us -> 177 us (level)
  starting transfers between devices: 51.2 us -> 55.1 us
  waiting for transfers between devices: 69.2 us -> 66.9 us
  Pallas kernels: 49.3 us -> 47.1 us
    ppermute x44 -> x46, starting transfers between devices: 51.2 us -> 55.1 us  [send(): return lax.ppermute(x, axis, pairs)]
    ppermute x44 -> x46, waiting for transfers between devices: 69.2 us -> 66.9 us  [send(): return lax.ppermute(x, axis, pairs)]
    pallas_call x44 -> x49, Pallas kernels: 49.3 us -> 47.1 us  [call(): pl.pallas_call(body, out_shape=out_shape, in_specs=list(specs or [VM] * c...]
  transfers between devices with their start and end apart: 44 -> 46, of which waited for: 19 -> 19; matrix products, arithmetic and copies ran while one was open for 1% -> 0% of each run, Pallas kernels for 24% -> 22%
where the time goes in v6:
time: 177 us
  waiting for transfers between devices  66.9 us (38%)
  starting transfers between devices  55.1 us (31%)
  Pallas kernels  47.1 us (27%)
  local copies, waits for them, and re-layouts  3.43 us (2%)
  other arithmetic  2.46 us (1%)
    ppermute x46, waiting for transfers between devices, send(): return lax.ppermute(x, axis, pairs)  66.9 us
    ppermute x46, starting transfers between devices, send(): return lax.ppermute(x, axis, pairs)  55.1 us
    pallas_call x49, Pallas kernels, call(): pl.pallas_call(body, out_shape=out_shape, in_specs=list(specs or [VM] * c...  47.1 us
  transfers between devices with their start and end apart: 46, of which 19 were waited for; matrix products, arithmetic and copies ran while one was open for 0% of the time, Pallas kernels for 22%

profile of v6, /device:TPU:0, one launch (start us, length us, event | category | flops | bytes accessed | tf_op | source)
XLA Modules:
  0.0 176.5 jit_solution(2681893319412078772)
XLA Ops:
  1.4 0.7 multiply_bitcast_fusion
  2.4 0.8 add_select_fusion
  3.5 1.0 copy-done.5
  4.5 1.0 copy-done.6
  5.6 1.4 shard_map.113
  7.5 2.6 %collective-permute-start.6 = (bf16[1024,384]{1,0:T(8,128)(2,1)}, bf16[1024,384]{1,0:T(8,128)(2,1)S(1)}, u32[]{:S(2)}, u32[]{:S(2)}) collective-permute-start(bf16[1024,384]{1,0:T(8,128)(2,1)} %refs_5_.1), channel_id=1, source_target_pairs={{0,16},{4,20},{8,24},{12,28},{16,0},{20,4},{24,8},{28,12},{1,17},{... | collective-permute-start | bytes 2359304 | tf_op jit(solution)/shard_map/ppermute | solution.py:405
  10.3 1.6 collective-permute-start.1
  11.9 1.6 collective-permute-start.2
  13.5 1.0 copy-done.4
  14.5 1.1 shard_map.115
  15.7 3.3 %collective-permute-done.1.refs_1_ = f32[4,128,128]{2,1,0:T(8,128)S(1)} collective-permute-done((f32[4,128,128]{2,1,0:T(8,128)S(1)}, f32[4,128,128]{2,1,0:T(8,128)S(1)}, u32[]{:S(2)}, u32[]{:S(2)}) %collective-permute-start.1) | collective-permute-done | bytes 262176 | tf_op jit(solution)/shard_map/ppermute | solution.py:405
  19.0 3.0 %collective-permute-start.4 = (f32[4,128,128]{2,1,0:T(8,128)S(1)}, f32[4,128,128]{2,1,0:T(8,128)S(1)}, u32[]{:S(2)}, u32[]{:S(2)}) collective-permute-start(f32[4,128,128]{2,1,0:T(8,128)S(1)} %get-tuple-element.83), channel_id=1, source_target_pairs={{0,16},{4,20},{8,24},{12,28},{1,17},{5,21},{9,25},{13,29},{2,18},{... | collective-permute-start | bytes 786440 | tf_op jit(solution)/shard_map/ppermute | solution.py:405
  22.0 2.7 %collective-permute-start.5 = (s32[8,128]{1,0:T(8,128)S(1)}, s32[8,128]{1,0:T(8,128)S(1)}, u32[]{:S(2)}, u32[]{:S(2)}) collective-permute-start(s32[8,128]{1,0:T(8,128)S(1)} %shard_map.116.refs_3_.refs_1_), channel_id=1, source_target_pairs={{0,2},{1,3},{2,0},{3,1},{4,6},{5,7},{6,4},{7,5},{8,10},{9,11},{10,... | collective-permute-start | bytes 12296 | tf_op jit(solution)/shard_map/ppermute | solution.py:405
  24.8 1.8 %collective-permute-done.5.refs_2_ = s32[8,128]{1,0:T(8,128)S(1)} collective-permute-done((s32[8,128]{1,0:T(8,128)S(1)}, s32[8,128]{1,0:T(8,128)S(1)}, u32[]{:S(2)}, u32[]{:S(2)}) %collective-permute-start.5) | collective-permute-done | bytes 4128 | tf_op jit(solution)/shard_map/ppermute | solution.py:405
  26.6 1.9 %collective-permute-done.6.refs_4_.refs_5_.refs_0_ = bf16[1024,384]{1,0:T(8,128)(2,1)S(1)} collective-permute-done((bf16[1024,384]{1,0:T(8,128)(2,1)}, bf16[1024,384]{1,0:T(8,128)(2,1)S(1)}, u32[]{:S(2)}, u32[]{:S(2)}) %collective-permute-start.6) | collective-permute-done | bytes 786464 | tf_op jit(solution)/shard_map/ppermute | solution.py:405
  29.0 4.3 %collective-permute-done.4.refs_2_ = f32[4,128,128]{2,1,0:T(8,128)S(1)} collective-permute-done((f32[4,128,128]{2,1,0:T(8,128)S(1)}, f32[4,128,128]{2,1,0:T(8,128)S(1)}, u32[]{:S(2)}, u32[]{:S(2)}) %collective-permute-start.4) | collective-permute-done | bytes 262176 | tf_op jit(solution)/shard_map/ppermute | solution.py:405
  33.5 1.5 collective-permute-done.7.refs_5_
  35.1 1.3 shard_map.121.refs_3_.refs_1_
  36.5 1.5 collective-permute-start.9
  38.1 1.1 collective-permute-done.10.refs_2_
  39.2 0.8 shard_map.122.refs_6_.refs_4_
  40.1 1.3 shard_map.123
  41.3 3.5 %collective-permute-start.14 = (bf16[512,384]{1,0:T(8,128)(2,1)S(1)}, bf16[512,384]{1,0:T(8,128)(2,1)S(1)}, u32[]{:S(2)}, u32[]{:S(2)}) collective-permute-start(bf16[512,384]{1,0:T(8,128)(2,1)S(1)} %get-tuple-element.90), channel_id=1, source_target_pairs={{0,1},{3,2},{4,5},{7,6},{8,9},{11,10},{12,13},{15,14},{16,17},{19,... | collective-permute-start | bytes 1179656 | tf_op jit(solution)/shard_map/ppermute | solution.py:405
  44.9 1.2 shard_map.124
  46.1 1.3 collective-permute-start.13
  47.4 8.9 %collective-permute-done.9.refs_5_.refs_0_ = bf16[1024,384]{1,0:T(8,128)(2,1)S(1)} collective-permute-done((bf16[1024,384]{1,0:T(8,128)(2,1)S(1)}, bf16[1024,384]{1,0:T(8,128)(2,1)S(1)}, u32[]{:S(2)}, u32[]{:S(2)}) %collective-permute-start.9) | collective-permute-done | bytes 786464 | tf_op jit(solution)/shard_map/ppermute | solution.py:405
  56.3 1.3 shard_map.125
  57.7 1.5 collective-permute-start.12
  59.3 2.5 %collective-permute-start.11 = (bf16[512,384]{1,0:T(8,128)(2,1)S(1)}, bf16[512,384]{1,0:T(8,128)(2,1)S(1)}, u32[]{:S(2)}, u32[]{:S(2)}) collective-permute-start(bf16[512,384]{1,0:T(8,128)(2,1)S(1)} %shard_map.126.refs_1_), channel_id=1, source_target_pairs={{0,16},{4,20},{8,24},{12,28},{16,0},{20,4},{24,8},{28,12},{1,17},{... | collective-permute-start | bytes 1179656 | tf_op jit(solution)/shard_map/ppermute | solution.py:405
  62.6 6.3 %collective-permute-start.19 = (bf16[512,384]{1,0:T(8,128)(2,1)S(1)}, bf16[512,384]{1,0:T(8,128)(2,1)S(1)}, u32[]{:S(2)}, u32[]{:S(2)}) collective-permute-start(bf16[512,384]{1,0:T(8,128)(2,1)S(1)} %get-tuple-element.97), channel_id=1, source_target_pairs={{0,1},{3,2},{4,5},{7,6},{8,9},{11,10},{12,13},{15,14},{16,17},{19,... | collective-permute-start | bytes 1179656 | tf_op jit(solution)/shard_map/ppermute | solution.py:405
  70.3 1.3 shard_map.130
  71.7 1.3 collective-permute-start.17
  73.0 7.8 %collective-permute-start.15 = (bf16[512,384]{1,0:T(8,128)(2,1)S(1)}, bf16[512,384]{1,0:T(8,128)(2,1)S(1)}, u32[]{:S(2)}, u32[]{:S(2)}) collective-permute-start(bf16[512,384]{1,0:T(8,128)(2,1)S(1)} %get-tuple-element.94), channel_id=1, source_target_pairs={{0,1},{3,2},{4,5},{7,6},{8,9},{11,10},{12,13},{15,14},{16,17},{19,... | collective-permute-start | bytes 1179656 | tf_op jit(solution)/shard_map/ppermute | solution.py:405
  81.0 3.5 %collective-permute-done.17.refs_1_ = bf16[512,384]{1,0:T(8,128)(2,1)S(1)} collective-permute-done((bf16[512,384]{1,0:T(8,128)(2,1)S(1)}, bf16[512,384]{1,0:T(8,128)(2,1)S(1)}, u32[]{:S(2)}, u32[]{:S(2)}) %collective-permute-start.17) | collective-permute-done | bytes 393248 | tf_op jit(solution)/shard_map/ppermute | solution.py:405
  84.5 0.9 shard_map.134
  86.2 1.3 collective-permute-start.21
  89.7 10.0 %collective-permute-done.21.refs_1_ = bf16[512,384]{1,0:T(8,128)(2,1)S(1)} collective-permute-done((bf16[512,384]{1,0:T(8,128)(2,1)S(1)}, bf16[512,384]{1,0:T(8,128)(2,1)S(1)}, u32[]{:S(2)}, u32[]{:S(2)}) %collective-permute-start.21) | collective-permute-done | bytes 393248 | tf_op jit(solution)/shard_map/ppermute | solution.py:405
  99.6 0.9 shard_map.138
  100.6 1.6 collective-permute-done.24.refs_2_
  103.7 1.3 collective-permute-start.26
  105.6 13.1 %collective-permute-done.26.refs_1_ = bf16[512,384]{1,0:T(8,128)(2,1)S(1)} collective-permute-done((bf16[512,384]{1,0:T(8,128)(2,1)S(1)}, bf16[512,384]{1,0:T(8,128)(2,1)S(1)}, u32[]{:S(2)}, u32[]{:S(2)}) %collective-permute-start.26) | collective-permute-done | bytes 393248 | tf_op jit(solution)/shard_map/ppermute | solution.py:405
  118.7 0.9 shard_map.142
  119.7 1.2 collective-permute-start.28
  120.9 1.5 collective-permute-start.25
  122.4 3.5 %shard_map.143 = (f32[576,384]{1,0:T(8,128)S(1)}, f32[576,384]{1,0:T(8,128)S(1)}, f32[576,384]{1,0:T(8,128)S(1)}, f32[576,384]{1,0:T(8,128)S(1)}, f32[576,384]{1,0:T(8,128)S(1)}, /*index=5*/f32[576,384]{1,0:T(8,128)S(1)}) custom-call(s32[3]{0:T(128)S(1)} %pad_add_fusion.refs_0_, bf16[576,3072]{1,0:T(8,128)(2,1)S(1)} %bitcast.20, ...), custom_call_target="tpu_custom_call" | custom-call | flops 2038431744 | bytes 14155788 | tf_op jit(solution)/shard_map/pallas_call | solution.py:47
  128.4 1.2 collective-permute-done.32.refs_4_
  129.6 1.7 shard_map.147
  131.3 2.1 %collective-permute-done.25.refs_1_ = bf16[512,384]{1,0:T(8,128)(2,1)S(1)} collective-permute-done((bf16[512,384]{1,0:T(8,128)(2,1)S(1)}, bf16[512,384]{1,0:T(8,128)(2,1)S(1)}, u32[]{:S(2)}, u32[]{:S(2)}) %collective-permute-start.25) | collective-permute-done | bytes 393248 | tf_op jit(solution)/shard_map/ppermute | solution.py:405
  133.4 1.3 shard_map.148
  134.7 1.2 collective-permute-start.39
  136.0 3.5 %shard_map.149 = (f32[576,384]{1,0:T(8,128)S(1)}, f32[576,384]{1,0:T(8,128)S(1)}, f32[576,384]{1,0:T(8,128)S(1)}, f32[576,384]{1,0:T(8,128)S(1)}, f32[576,384]{1,0:T(8,128)S(1)}, /*index=5*/f32[576,384]{1,0:T(8,128)S(1)}) custom-call(s32[3]{0:T(128)S(1)} %pad_add_fusion.refs_0_, bf16[576,3072]{1,0:T(8,128)(2,1)S(1)} %bitcast.22, ...), custom_call_target="tpu_custom_call" | custom-call | flops 2038431744 | bytes 19464204 | tf_op jit(solution)/shard_map/pallas_call | solution.py:47
  141.3 1.1 collective-permute-start.36
  142.5 1.6 collective-permute-done.40.refs_4_
  144.1 1.7 shard_map.153
  145.8 3.5 %shard_map.154 = (f32[576,384]{1,0:T(8,128)S(1)}, f32[576,384]{1,0:T(8,128)S(1)}, f32[576,384]{1,0:T(8,128)S(1)}, f32[576,384]{1,0:T(8,128)S(1)}, f32[576,384]{1,0:T(8,128)S(1)}, /*index=5*/f32[576,384]{1,0:T(8,128)S(1)}) custom-call(s32[3]{0:T(128)S(1)} %pad_add_fusion.refs_0_, bf16[576,3072]{1,0:T(8,128)(2,1)S(1)} %bitcast.24, ...), custom_call_target="tpu_custom_call" | custom-call | flops 2038431744 | bytes 19464204 | tf_op jit(solution)/shard_map/pallas_call | solution.py:47
  149.3 3.0 %collective-permute-done.36.refs_1_.refs_4_ = bf16[384,896]{1,0:T(8,128)(2,1)S(1)} collective-permute-done((bf16[384,896]{1,0:T(8,128)(2,1)S(1)}, bf16[384,896]{1,0:T(8,128)(2,1)S(1)}, u32[]{:S(2)}, u32[]{:S(2)}) %collective-permute-start.36) | collective-permute-done | bytes 688160 | tf_op jit(solution)/shard_map/ppermute | solution.py:405
  153.0 1.2 collective-permute-start.42
  154.2 5.6 %collective-permute-done.42.refs_0_ = bf16[192,768]{1,0:T(8,128)(2,1)S(1)} collective-permute-done((bf16[192,768]{1,0:T(8,128)(2,1)S(1)}, bf16[192,768]{1,0:T(8,128)(2,1)S(1)}, u32[]{:S(2)}, u32[]{:S(2)}) %collective-permute-start.42) | collective-permute-done | bytes 294944 | tf_op jit(solution)/shard_map/ppermute | solution.py:405
  159.9 1.2 collective-permute-start.44
  161.4 1.7 shard_map.157
  163.1 6.3 %shard_map.158 = (bf16[576,1536]{1,0:T(8,128)(2,1)}, f32[8,128]{1,0:T(8,128)S(1)}) custom-call(s32[3]{0:T(128)S(1)} %pad_add_fusion.refs_0_, bf16[576,3072]{1,0:T(8,128)(2,1)S(1)} %bitcast.26, bf16[576,3072]{1,0:T(8,128)(2,1)S(1)} %bitcast.34, bf16[384,896]{1,0:T(8,128)(2,1)S(1)} %shard_map.150.refs_2_.refs_3_, ...), custom_call_target="tpu_custom_call" | custom-call | flops 2038431744 | bytes 16224268 | tf_op jit(solution)/shard_map/pallas_call | solution.py:47
  170.0 1.4 collective-permute-done.33.refs_1_
  171.5 1.3 shard_map.159
  172.8 3.5 %shard_map.161 = (bf16[576,1536]{1,0:T(8,128)(2,1)}, f32[8,128]{1,0:T(8,128)}) custom-call(s32[3]{0:T(128)S(1)} %pad_add_fusion.refs_0_, bf16[576,3072]{1,0:T(8,128)(2,1)S(1)} %bitcast.27, bf16[576,3072]{1,0:T(8,128)(2,1)S(1)} %bitcast.35, bf16[192,896]{1,0:T(8,128)(2,1)S(1)} %shard_map.160.refs_3_.refs_8_, ...), custom_call_target="tpu_custom_call", output_to_operand_aliasing={{0}: (7, {})} | custom-call | flops 679477248 | bytes 13078540 | tf_op jit(solution)/shard_map/pallas_call | solution.py:47
  (107 shorter events, 17.0 us)
Async XLA Ops:
  0.6 24.1 %copy-start.3 = (bf16[1024,384]{1,0:T(8,128)(2,1)S(1)}, bf16[1024,384]{1,0:T(8,128)(2,1)}, u32[]{:S(2)}) copy-start(bf16[1024,384]{1,0:T(8,128)(2,1)} %refs_5_.1) | copy-start | bytes 2359300
  3.5 1.0 copy-start.5
  4.5 1.0 copy-start.6
  7.0 3.3 %collective-permute-start = (f32[4,128,128]{2,1,0:T(8,128)S(1)}, f32[4,128,128]{2,1,0:T(8,128)S(1)}, u32[]{:S(2)}, u32[]{:S(2)}) collective-permute-start(f32[4,128,128]{2,1,0:T(8,128)S(1)} %get-tuple-element.77), channel_id=1, source_target_pairs={{0,4},{4,0},{8,12},{12,8},{16,20},{20,16},{24,28},{28,24},{1,5},{5... | collective-permute-start | bytes 786440 | tf_op jit(solution)/shard_map/ppermute | solution.py:405
  7.5 20.9 %collective-permute-start.6 = (bf16[1024,384]{1,0:T(8,128)(2,1)}, bf16[1024,384]{1,0:T(8,128)(2,1)S(1)}, u32[]{:S(2)}, u32[]{:S(2)}) collective-permute-start(bf16[1024,384]{1,0:T(8,128)(2,1)} %refs_5_.1), channel_id=1, source_target_pairs={{0,16},{4,20},{8,24},{12,28},{16,0},{20,4},{24,8},{28,12},{1,17},{... | collective-permute-start | bytes 2359304 | tf_op jit(solution)/shard_map/ppermute | solution.py:405
  10.1 5.5 %collective-permute-start.3 = (bf16[64,3072]{1,0:T(8,128)(2,1)}, bf16[64,3072]{1,0:T(8,128)(2,1)S(1)}, u32[]{:S(2)}, u32[]{:S(2)}) collective-permute-start(bf16[64,3072]{1,0:T(8,128)(2,1)} %refs_3_.9), channel_id=1, source_target_pairs={{0,4},{4,0},{8,12},{12,8},{16,20},{20,16},{24,28},{28,24},{1,5},{5... | collective-permute-start | bytes 1179656 | tf_op jit(solution)/shard_map/ppermute | solution.py:405
  10.3 8.6 %collective-permute-start.1 = (f32[4,128,128]{2,1,0:T(8,128)S(1)}, f32[4,128,128]{2,1,0:T(8,128)S(1)}, u32[]{:S(2)}, u32[]{:S(2)}) collective-permute-start(f32[4,128,128]{2,1,0:T(8,128)S(1)} %get-tuple-element.81.refs_2_), channel_id=1, source_target_pairs={{0,8},{4,12},{8,0},{12,4},{16,24},{20,28},{24,16},{28,20},{1,9},{5... | collective-permute-start | bytes 786440 | tf_op jit(solution)/shard_map/ppermute | solution.py:405
  11.9 3.7 %collective-permute-start.2 = (s32[8,128]{1,0:T(8,128)S(1)}, s32[8,128]{1,0:T(8,128)S(1)}, u32[]{:S(2)}, u32[]{:S(2)}) collective-permute-start(s32[8,128]{1,0:T(8,128)S(1)} %pad.4.refs_4_.refs_0_), channel_id=1, source_target_pairs={{0,1},{1,0},{2,3},{3,2},{4,5},{5,4},{6,7},{7,6},{8,9},{9,8},{10,11... | collective-permute-start | bytes 12296 | tf_op jit(solution)/shard_map/ppermute | solution.py:405
  13.5 1.0 copy-start.4
  19.0 14.3 %collective-permute-start.4 = (f32[4,128,128]{2,1,0:T(8,128)S(1)}, f32[4,128,128]{2,1,0:T(8,128)S(1)}, u32[]{:S(2)}, u32[]{:S(2)}) collective-permute-start(f32[4,128,128]{2,1,0:T(8,128)S(1)} %get-tuple-element.83), channel_id=1, source_target_pairs={{0,16},{4,20},{8,24},{12,28},{1,17},{5,21},{9,25},{13,29},{2,18},{... | collective-permute-start | bytes 786440 | tf_op jit(solution)/shard_map/ppermute | solution.py:405
  22.0 4.6 %collective-permute-start.5 = (s32[8,128]{1,0:T(8,128)S(1)}, s32[8,128]{1,0:T(8,128)S(1)}, u32[]{:S(2)}, u32[]{:S(2)}) collective-permute-start(s32[8,128]{1,0:T(8,128)S(1)} %shard_map.116.refs_3_.refs_1_), channel_id=1, source_target_pairs={{0,2},{1,3},{2,0},{3,1},{4,6},{5,7},{6,4},{7,5},{8,10},{9,11},{10,... | collective-permute-start | bytes 12296 | tf_op jit(solution)/shard_map/ppermute | solution.py:405
  24.8 15.3 %copy-start.2 = (bf16[64,3072]{1,0:T(8,128)(2,1)S(1)}, bf16[64,3072]{1,0:T(8,128)(2,1)}, u32[]{:S(2)}) copy-start(bf16[64,3072]{1,0:T(8,128)(2,1)} %refs_3_.9) | copy-start | bytes 1179652
  33.5 1.6 collective-permute-start.7
  36.3 3.7 %collective-permute-start.8 = (bf16[256,1024]{1,0:T(8,128)(2,1)S(1)}, bf16[256,1024]{1,0:T(8,128)(2,1)S(1)}, u32[]{:S(2)}, u32[]{:S(2)}) collective-permute-start(bf16[256,1024]{1,0:T(8,128)(2,1)S(1)} %shard_map.121.refs_3_.refs_1_), channel_id=1, source_target_pairs={{0,4},{4,0},{8,12},{12,8},{16,20},{20,16},{24,28},{28,24},{1,5},{5... | collective-permute-start | bytes 1572872 | tf_op jit(solution)/shard_map/ppermute | solution.py:405
  36.5 19.8 %collective-permute-start.9 = (bf16[1024,384]{1,0:T(8,128)(2,1)S(1)}, bf16[1024,384]{1,0:T(8,128)(2,1)S(1)}, u32[]{:S(2)}, u32[]{:S(2)}) collective-permute-start(bf16[1024,384]{1,0:T(8,128)(2,1)S(1)} %shard_map.118.refs_3_), channel_id=1, source_target_pairs={{0,8},{4,12},{8,0},{12,4},{16,24},{20,28},{24,16},{28,20},{1,9},{5... | collective-permute-start | bytes 2359304 | tf_op jit(solution)/shard_map/ppermute | solution.py:405
  38.0 1.2 collective-permute-start.10
  41.3 20.4 %collective-permute-start.14 = (bf16[512,384]{1,0:T(8,128)(2,1)S(1)}, bf16[512,384]{1,0:T(8,128)(2,1)S(1)}, u32[]{:S(2)}, u32[]{:S(2)}) collective-permute-start(bf16[512,384]{1,0:T(8,128)(2,1)S(1)} %get-tuple-element.90), channel_id=1, source_target_pairs={{0,1},{3,2},{4,5},{7,6},{8,9},{11,10},{12,13},{15,14},{16,17},{19,... | collective-permute-start | bytes 1179656 | tf_op jit(solution)/shard_map/ppermute | solution.py:405
  46.1 22.8 %collective-permute-start.13 = (bf16[512,384]{1,0:T(8,128)(2,1)S(1)}, bf16[512,384]{1,0:T(8,128)(2,1)S(1)}, u32[]{:S(2)}, u32[]{:S(2)}) collective-permute-start(bf16[512,384]{1,0:T(8,128)(2,1)S(1)} %get-tuple-element.89), channel_id=1, source_target_pairs={{0,1},{3,2},{4,5},{7,6},{8,9},{11,10},{12,13},{15,14},{16,17},{19,... | collective-permute-start | bytes 1179656 | tf_op jit(solution)/shard_map/ppermute | solution.py:405
  57.7 12.0 %collective-permute-start.12 = (bf16[512,384]{1,0:T(8,128)(2,1)S(1)}, bf16[512,384]{1,0:T(8,128)(2,1)S(1)}, u32[]{:S(2)}, u32[]{:S(2)}) collective-permute-start(bf16[512,384]{1,0:T(8,128)(2,1)S(1)} %shard_map.127.refs_2_), channel_id=1, source_target_pairs={{0,8},{4,12},{8,0},{12,4},{16,24},{20,28},{24,16},{28,20},{1,9},{5... | collective-permute-start | bytes 1179656 | tf_op jit(solution)/shard_map/ppermute | solution.py:405
  59.3 11.0 %collective-permute-start.11 = (bf16[512,384]{1,0:T(8,128)(2,1)S(1)}, bf16[512,384]{1,0:T(8,128)(2,1)S(1)}, u32[]{:S(2)}, u32[]{:S(2)}) collective-permute-start(bf16[512,384]{1,0:T(8,128)(2,1)S(1)} %shard_map.126.refs_1_), channel_id=1, source_target_pairs={{0,16},{4,20},{8,24},{12,28},{16,0},{20,4},{24,8},{28,12},{1,17},{... | collective-permute-start | bytes 1179656 | tf_op jit(solution)/shard_map/ppermute | solution.py:405
  61.9 9.7 %collective-permute-start.16 = (bf16[512,384]{1,0:T(8,128)(2,1)S(1)}, bf16[512,384]{1,0:T(8,128)(2,1)S(1)}, u32[]{:S(2)}, u32[]{:S(2)}) collective-permute-start(bf16[512,384]{1,0:T(8,128)(2,1)S(1)} %get-tuple-element.95), channel_id=1, source_target_pairs={{1,2},{2,1},{5,6},{6,5},{9,10},{10,9},{13,14},{14,13},{17,18},{18,... | collective-permute-start | bytes 1179656 | tf_op jit(solution)/shard_map/ppermute | solution.py:405
  62.6 18.2 %collective-permute-start.19 = (bf16[512,384]{1,0:T(8,128)(2,1)S(1)}, bf16[512,384]{1,0:T(8,128)(2,1)S(1)}, u32[]{:S(2)}, u32[]{:S(2)}) collective-permute-start(bf16[512,384]{1,0:T(8,128)(2,1)S(1)} %get-tuple-element.97), channel_id=1, source_target_pairs={{0,1},{3,2},{4,5},{7,6},{8,9},{11,10},{12,13},{15,14},{16,17},{19,... | collective-permute-start | bytes 1179656 | tf_op jit(solution)/shard_map/ppermute | solution.py:405
  69.0 11.9 %collective-permute-start.18 = (bf16[512,384]{1,0:T(8,128)(2,1)S(1)}, bf16[512,384]{1,0:T(8,128)(2,1)S(1)}, u32[]{:S(2)}, u32[]{:S(2)}) collective-permute-start(bf16[512,384]{1,0:T(8,128)(2,1)S(1)} %get-tuple-element.96), channel_id=1, source_target_pairs={{1,2},{2,1},{5,6},{6,5},{9,10},{10,9},{13,14},{14,13},{17,18},{18,... | collective-permute-start | bytes 1179656 | tf_op jit(solution)/shard_map/ppermute | solution.py:405
  71.6 13.0 %copy-start.7 = (f32[3072]{0:T(1024)S(1)}, f32[3072]{0:T(1024)}, u32[]{:S(2)}) copy-start(f32[3072]{0:T(1024)} %param.16) | copy-start | bytes 36868
  71.7 12.9 %collective-permute-start.17 = (bf16[512,384]{1,0:T(8,128)(2,1)S(1)}, bf16[512,384]{1,0:T(8,128)(2,1)S(1)}, u32[]{:S(2)}, u32[]{:S(2)}) collective-permute-start(bf16[512,384]{1,0:T(8,128)(2,1)S(1)} %shard_map.131.refs_2_), channel_id=1, source_target_pairs={{1,0},{2,3},{5,4},{6,7},{9,8},{10,11},{13,12},{14,15},{17,16},{18,... | collective-permute-start | bytes 1179656 | tf_op jit(solution)/shard_map/ppermute | solution.py:405
  73.0 14.6 %collective-permute-start.15 = (bf16[512,384]{1,0:T(8,128)(2,1)S(1)}, bf16[512,384]{1,0:T(8,128)(2,1)S(1)}, u32[]{:S(2)}, u32[]{:S(2)}) collective-permute-start(bf16[512,384]{1,0:T(8,128)(2,1)S(1)} %get-tuple-element.94), channel_id=1, source_target_pairs={{0,1},{3,2},{4,5},{7,6},{8,9},{11,10},{12,13},{15,14},{16,17},{19,... | collective-permute-start | bytes 1179656 | tf_op jit(solution)/shard_map/ppermute | solution.py:405
  85.4 2.2 %collective-permute-start.23 = (bf16[384,384]{1,0:T(8,128)(2,1)S(1)}, bf16[384,384]{1,0:T(8,128)(2,1)S(1)}, u32[]{:S(2)}, u32[]{:S(2)}) collective-permute-start(bf16[384,384]{1,0:T(8,128)(2,1)S(1)} %get-tuple-element.99.refs_2_.refs_1_), channel_id=1, source_target_pairs={{0,4},{4,0},{8,12},{12,8},{16,20},{20,16},{24,28},{28,24},{1,5},{5... | collective-permute-start | bytes 884744 | tf_op jit(solution)/shard_map/ppermute | solution.py:405
  85.5 4.0 %collective-permute-start.22 = (bf16[512,384]{1,0:T(8,128)(2,1)S(1)}, bf16[512,384]{1,0:T(8,128)(2,1)S(1)}, u32[]{:S(2)}, u32[]{:S(2)}) collective-permute-start(bf16[512,384]{1,0:T(8,128)(2,1)S(1)} %get-tuple-element.102), channel_id=1, source_target_pairs={{1,2},{2,1},{5,6},{6,5},{9,10},{10,9},{13,14},{14,13},{17,18},{18,... | collective-permute-start | bytes 1179656 | tf_op jit(solution)/shard_map/ppermute | solution.py:405
  86.2 13.4 %collective-permute-start.21 = (bf16[512,384]{1,0:T(8,128)(2,1)S(1)}, bf16[512,384]{1,0:T(8,128)(2,1)S(1)}, u32[]{:S(2)}, u32[]{:S(2)}) collective-permute-start(bf16[512,384]{1,0:T(8,128)(2,1)S(1)} %shard_map.133.refs_5_.refs_2_), channel_id=1, source_target_pairs={{1,0},{2,3},{5,4},{6,7},{9,8},{10,11},{13,12},{14,15},{17,16},{18,... | collective-permute-start | bytes 1179656 | tf_op jit(solution)/shard_map/ppermute | solution.py:405
  88.3 14.6 %collective-permute-start.27 = (bf16[384,768]{1,0:T(8,128)(2,1)S(1)}, bf16[384,768]{1,0:T(8,128)(2,1)S(1)}, u32[]{:S(2)}, u32[]{:S(2)}) collective-permute-start(bf16[384,768]{1,0:T(8,128)(2,1)S(1)} %shard_map.136.refs_2_.refs_3_), channel_id=1, source_target_pairs={{0,8},{4,20},{8,0},{12,28},{16,24},{20,4},{24,16},{28,12},{1,9},{5... | collective-permute-start | bytes 1769480 | tf_op jit(solution)/shard_map/ppermute | solution.py:405
  88.9 14.0 %collective-permute-start.20 = (bf16[512,384]{1,0:T(8,128)(2,1)S(1)}, bf16[512,384]{1,0:T(8,128)(2,1)S(1)}, u32[]{:S(2)}, u32[]{:S(2)}) collective-permute-start(bf16[512,384]{1,0:T(8,128)(2,1)S(1)} %get-tuple-element.101), channel_id=1, source_target_pairs={{1,2},{2,1},{5,6},{6,5},{9,10},{10,9},{13,14},{14,13},{17,18},{18,... | collective-permute-start | bytes 1179656 | tf_op jit(solution)/shard_map/ppermute | solution.py:405
  89.6 32.8 %copy-start = (bf16[1,576,3072]{2,1,0:T(8,128)(2,1)S(1)}, bf16[1,576,3072]{2,1,0:T(8,128)(2,1)}, u32[]{:S(2)}) copy-start(bf16[1,576,3072]{2,1,0:T(8,128)(2,1)} %param.18) | copy-start | bytes 10616836
  89.6 32.8 %copy-start.1 = (bf16[1,576,3072]{2,1,0:T(8,128)(2,1)S(1)}, bf16[1,576,3072]{2,1,0:T(8,128)(2,1)}, u32[]{:S(2)}) copy-start(bf16[1,576,3072]{2,1,0:T(8,128)(2,1)} %param.19) | copy-start | bytes 10616836
  100.6 1.6 collective-permute-start.24
  103.5 18.9 %collective-permute-start.31 = (bf16[384,768]{1,0:T(8,128)(2,1)S(1)}, bf16[384,768]{1,0:T(8,128)(2,1)S(1)}, u32[]{:S(2)}, u32[]{:S(2)}) collective-permute-start(bf16[384,768]{1,0:T(8,128)(2,1)S(1)} %get-tuple-element.109), channel_id=1, source_target_pairs={{0,4},{4,0},{8,12},{12,8},{16,20},{20,16},{24,28},{28,24},{1,5},{5... | collective-permute-start | bytes 1769480 | tf_op jit(solution)/shard_map/ppermute | solution.py:405
  103.7 15.0 %collective-permute-start.26 = (bf16[512,384]{1,0:T(8,128)(2,1)S(1)}, bf16[512,384]{1,0:T(8,128)(2,1)S(1)}, u32[]{:S(2)}, u32[]{:S(2)}) collective-permute-start(bf16[512,384]{1,0:T(8,128)(2,1)S(1)} %shard_map.137.refs_5_.refs_2_), channel_id=1, source_target_pairs={{1,0},{2,3},{5,4},{6,7},{9,8},{10,11},{13,12},{14,15},{17,16},{18,... | collective-permute-start | bytes 1179656 | tf_op jit(solution)/shard_map/ppermute | solution.py:405
  105.0 21.5 %collective-permute-start.29 = (bf16[384,768]{1,0:T(8,128)(2,1)S(1)}, bf16[384,768]{1,0:T(8,128)(2,1)S(1)}, u32[]{:S(2)}, u32[]{:S(2)}) collective-permute-start(bf16[384,768]{1,0:T(8,128)(2,1)S(1)} %shard_map.139.refs_2_.refs_3_), channel_id=1, source_target_pairs={{0,8},{4,20},{8,0},{12,28},{16,24},{20,4},{24,16},{28,12},{1,9},{5... | collective-permute-start | bytes 1769480 | tf_op jit(solution)/shard_map/ppermute | solution.py:405
  119.7 6.2 %collective-permute-start.30 = (bf16[384,384]{1,0:T(8,128)(2,1)S(1)}, bf16[384,384]{1,0:T(8,128)(2,1)S(1)}, u32[]{:S(2)}, u32[]{:S(2)}) collective-permute-start(bf16[384,384]{1,0:T(8,128)(2,1)S(1)} %get-tuple-element.108.refs_6_.refs_1_), channel_id=1, source_target_pairs={{0,4},{4,0},{8,12},{12,8},{16,20},{20,16},{24,28},{28,24},{1,5},{5... | collective-permute-start | bytes 884744 | tf_op jit(solution)/shard_map/ppermute | solution.py:405
  119.7 7.5 %collective-permute-start.28 = (bf16[192,768]{1,0:T(8,128)(2,1)S(1)}, bf16[192,768]{1,0:T(8,128)(2,1)S(1)}, u32[]{:S(2)}, u32[]{:S(2)}) collective-permute-start(bf16[192,768]{1,0:T(8,128)(2,1)S(1)} %get-tuple-element.106.refs_5_), channel_id=1, source_target_pairs={{0,16},{4,12},{8,24},{12,4},{16,0},{20,28},{24,8},{28,20},{1,17},{... | collective-permute-start | bytes 884744 | tf_op jit(solution)/shard_map/ppermute | solution.py:405
  120.9 12.5 %collective-permute-start.25 = (bf16[512,384]{1,0:T(8,128)(2,1)S(1)}, bf16[512,384]{1,0:T(8,128)(2,1)S(1)}, u32[]{:S(2)}, u32[]{:S(2)}) collective-permute-start(bf16[512,384]{1,0:T(8,128)(2,1)S(1)} %shard_map.140.refs_2_), channel_id=1, source_target_pairs={{1,0},{2,3},{5,4},{6,7},{9,8},{10,11},{13,12},{14,15},{17,16},{18,... | collective-permute-start | bytes 1179656 | tf_op jit(solution)/shard_map/ppermute | solution.py:405
  127.1 8.9 %collective-permute-start.35 = (bf16[384,768]{1,0:T(8,128)(2,1)S(1)}, bf16[384,768]{1,0:T(8,128)(2,1)S(1)}, u32[]{:S(2)}, u32[]{:S(2)}) collective-permute-start(bf16[384,768]{1,0:T(8,128)(2,1)S(1)} %get-tuple-element.116), channel_id=1, source_target_pairs={{0,4},{4,0},{8,12},{12,8},{16,20},{20,16},{24,28},{28,24},{1,5},{5... | collective-permute-start | bytes 1769480 | tf_op jit(solution)/shard_map/ppermute | solution.py:405
  127.2 2.4 %collective-permute-start.32 = (bf16[192,768]{1,0:T(8,128)(2,1)S(1)}, bf16[192,768]{1,0:T(8,128)(2,1)S(1)}, u32[]{:S(2)}, u32[]{:S(2)}) collective-permute-start(bf16[192,768]{1,0:T(8,128)(2,1)S(1)} %shard_map.146.refs_3_.refs_5_), channel_id=1, source_target_pairs={{0,4},{4,0},{8,12},{12,8},{16,20},{20,16},{24,28},{28,24},{1,5},{5... | collective-permute-start | bytes 884744 | tf_op jit(solution)/shard_map/ppermute | solution.py:405
  127.8 12.4 %collective-permute-start.37 = (bf16[384,768]{1,0:T(8,128)(2,1)S(1)}, bf16[384,768]{1,0:T(8,128)(2,1)S(1)}, u32[]{:S(2)}, u32[]{:S(2)}) collective-permute-start(bf16[384,768]{1,0:T(8,128)(2,1)S(1)} %shard_map.144.refs_2_.refs_3_), channel_id=1, source_target_pairs={{0,8},{4,20},{8,0},{12,28},{16,24},{20,4},{24,16},{28,12},{1,9},{5... | collective-permute-start | bytes 1769480 | tf_op jit(solution)/shard_map/ppermute | solution.py:405
  134.7 4.8 %collective-permute-start.34 = (bf16[384,512]{1,0:T(8,128)(2,1)S(1)}, bf16[384,512]{1,0:T(8,128)(2,1)S(1)}, u32[]{:S(2)}, u32[]{:S(2)}) collective-permute-start(bf16[384,512]{1,0:T(8,128)(2,1)S(1)} %get-tuple-element.115.refs_12_.refs_1_), channel_id=1, source_target_pairs={{0,4},{4,0},{8,12},{12,8},{16,20},{20,16},{24,28},{28,24},{1,5},{5... | collective-permute-start | bytes 1179656 | tf_op jit(solution)/shard_map/ppermute | solution.py:405
  134.7 7.7 %collective-permute-start.39 = (bf16[192,768]{1,0:T(8,128)(2,1)S(1)}, bf16[192,768]{1,0:T(8,128)(2,1)S(1)}, u32[]{:S(2)}, u32[]{:S(2)}) collective-permute-start(bf16[192,768]{1,0:T(8,128)(2,1)S(1)} %get-tuple-element.111.refs_1_), channel_id=1, source_target_pairs={{0,16},{4,12},{8,24},{12,4},{16,0},{20,28},{24,8},{28,20},{1,17},{... | collective-permute-start | bytes 884744 | tf_op jit(solution)/shard_map/ppermute | solution.py:405
  140.8 5.0 %collective-permute-start.38 = (bf16[384,768]{1,0:T(8,128)(2,1)S(1)}, bf16[384,768]{1,0:T(8,128)(2,1)S(1)}, u32[]{:S(2)}, u32[]{:S(2)}) collective-permute-start(bf16[384,768]{1,0:T(8,128)(2,1)S(1)} %get-tuple-element.123), channel_id=1, source_target_pairs={{0,4},{4,0},{8,12},{12,8},{16,20},{20,16},{24,28},{28,24},{1,5},{5... | collective-permute-start | bytes 1769480 | tf_op jit(solution)/shard_map/ppermute | solution.py:405
  141.3 10.9 %collective-permute-start.36 = (bf16[384,896]{1,0:T(8,128)(2,1)S(1)}, bf16[384,896]{1,0:T(8,128)(2,1)S(1)}, u32[]{:S(2)}, u32[]{:S(2)}) collective-permute-start(bf16[384,896]{1,0:T(8,128)(2,1)S(1)} %shard_map.150.refs_2_.refs_3_), channel_id=1, source_target_pairs={{0,8},{4,20},{8,0},{12,28},{16,24},{20,4},{24,16},{28,12},{1,9},{5... | collective-permute-start | bytes 2064392 | tf_op jit(solution)/shard_map/ppermute | solution.py:405
  142.4 1.6 collective-permute-start.40
  152.9 10.2 %collective-permute-start.41 = (bf16[384,896]{1,0:T(8,128)(2,1)S(1)}, bf16[384,896]{1,0:T(8,128)(2,1)S(1)}, u32[]{:S(2)}, u32[]{:S(2)}) collective-permute-start(bf16[384,896]{1,0:T(8,128)(2,1)S(1)} %get-tuple-element.133), channel_id=1, source_target_pairs={{0,4},{4,0},{8,12},{12,8},{16,20},{20,16},{24,28},{28,24},{1,5},{5... | collective-permute-start | bytes 2064392 | tf_op jit(solution)/shard_map/ppermute | solution.py:405
  153.0 6.8 %collective-permute-start.42 = (bf16[192,768]{1,0:T(8,128)(2,1)S(1)}, bf16[192,768]{1,0:T(8,128)(2,1)S(1)}, u32[]{:S(2)}, u32[]{:S(2)}) collective-permute-start(bf16[192,768]{1,0:T(8,128)(2,1)S(1)} %get-tuple-element.129.refs_1_), channel_id=1, source_target_pairs={{0,16},{4,12},{8,24},{12,4},{16,0},{20,28},{24,8},{28,20},{1,17},{... | collective-permute-start | bytes 884744 | tf_op jit(solution)/shard_map/ppermute | solution.py:405
  159.8 1.6 collective-permute-start.43
  159.9 9.6 %collective-permute-start.44 = (bf16[192,896]{1,0:T(8,128)(2,1)S(1)}, bf16[192,896]{1,0:T(8,128)(2,1)S(1)}, u32[]{:S(2)}, u32[]{:S(2)}) collective-permute-start(bf16[192,896]{1,0:T(8,128)(2,1)S(1)} %get-tuple-element.139.refs_1_), channel_id=1, source_target_pairs={{0,16},{4,12},{8,24},{12,4},{16,0},{20,28},{24,8},{28,20},{1,17},{... | collective-permute-start | bytes 1032200 | tf_op jit(solution)/shard_map/ppermute | solution.py:405
  169.5 3.3 %collective-permute-start.45 = (bf16[192,896]{1,0:T(8,128)(2,1)S(1)}, bf16[192,896]{1,0:T(8,128)(2,1)S(1)}, u32[]{:S(2)}, u32[]{:S(2)}) collective-permute-start(bf16[192,896]{1,0:T(8,128)(2,1)S(1)} %shard_map.160.refs_3_.refs_8_), channel_id=1, source_target_pairs={{0,4},{4,0},{8,12},{12,8},{16,20},{20,16},{24,28},{28,24},{1,5},{5... | collective-permute-start | bytes 1032200 | tf_op jit(solution)/shard_map/ppermute | solution.py:405
  169.6 1.8 %collective-permute-start.33 = (bf16[64,1536]{1,0:T(8,128)(2,1)S(1)}, bf16[64,1536]{1,0:T(8,128)(2,1)S(1)}, u32[]{:S(2)}, u32[]{:S(2)}) collective-permute-start(bf16[64,1536]{1,0:T(8,128)(2,1)S(1)} %get-tuple-element.113), channel_id=1, source_target_pairs={{0,4},{4,0},{8,12},{12,8},{16,20},{20,16},{24,28},{28,24},{1,5},{5... | collective-permute-start | bytes 589832 | tf_op jit(solution)/shard_map/ppermute | solution.py:405

commit v7 on v6

--- a/solution.py
+++ b/solution.py
@@ -41,17 +41,13 @@
     def body(*refs):
         kernel(*refs[:count], *refs[count + extra :])
 
-    shapes = out_shape if isinstance(out_shape, (list, tuple)) else [out_shape]
-    nbytes = sum(x.size * x.dtype.itemsize for x in list(operands) + list(shapes))
     kwargs.setdefault("out_specs", jax.tree.map(lambda _: VM, out_shape))
     return pl.pallas_call(
         body,
         out_shape=out_shape,
         in_specs=list(specs or [VM] * count) + [ANY] * extra,
         compiler_params=pltpu.CompilerParams(vmem_limit_bytes=limit * 1024 * 1024),
-        cost_estimate=pl.CostEstimate(
-            flops=int(flops), bytes_accessed=int(nbytes), transcendentals=int(exps)
-        ),
+        cost_estimate=pl.CostEstimate(flops=1, bytes_accessed=1, transcendentals=0),
         **kwargs,
     )(*operands, *deps)
 
@@ -502,7 +498,7 @@
         scratch_shapes=[pltpu.SemaphoreType.DMA(())],
     )
     ids = run(larger_kernel, like(ids.shape, ids.dtype), [ids, ids_got])
-    state, total = mix([[(0, 4)], [(0, 5), (1, 6)]], [got, total], [rest_got])
+    state, total = mix([[(0, 4)], [(0, 5), (1, 6)]], [got, total], [rest_got, weight_y])
     got = send(total, "ctx", [(d, d + 4) for d in range(4)])
     weight_x = send(copy(out_weight), "ctx", [(d, d ^ 2) for d in range(8)])
     ids_got = send(ids, "exp", [(d, d ^ 2) for d in range(4)])
@@ -510,7 +506,6 @@
         functools.partial(stack_kernel, 2),
         like((16, LANES), ids.dtype),
         [place, ids, ids_got],
-        deps=[weight_y],
         specs=[SM, VM, VM],
     )
     keep, give = mix(
@@ -616,19 +611,18 @@
     def farther(n):
         experts(n, ROLES[3:], [[moved["far", n], moved["rest", n]]])
 
-    project(0)
-    project(1)
-    project(2)
-    weight_top = send(cut(weight_x, 0), "ctx", [(d, d ^ 4) for d in range(8)])
-    weight_bottom = send(cut(weight_y, here // 2), "ctx", [(d, d ^ 2) for d in range(8)])
-    weights[3] = [weight_top, weight_bottom]
+    def fetch(n):
+        top = send(cut(weight_x, 0), "ctx", [(d, d ^ 4) for d in range(8)])
+        bottom = send(cut(weight_y, here // 2), "ctx", [(d, d ^ 2) for d in range(8)])
+        weights[n] = [top, bottom]
+
     for work, n in (
-        (inward, 0), (inward, 1), (project, 3), (outward, 0), (inward, 2), (outward, 1),
-        (dispatch, 0), (inward, 3), (join, 0), (outward, 2), (dispatch, 1), (join, 1),
-        (outward, 3), (half, 0), (dispatch, 2), (nearer, 0), (join, 2), (half, 1),
-        (diagonal, 0), (farther, 0), (dispatch, 3), (nearer, 1), (join, 3), (half, 2),
-        (diagonal, 1), (farther, 1), (nearer, 2), (half, 3), (diagonal, 2), (farther, 2),
-        (nearer, 3),
+        (project, 0), (project, 1), (inward, 0), (project, 2), (fetch, 3), (inward, 1),
+        (outward, 0), (project, 3), (inward, 2), (outward, 1), (dispatch, 0), (inward, 3),
+        (join, 0), (outward, 2), (dispatch, 1), (join, 1), (outward, 3), (half, 0),
+        (dispatch, 2), (join, 2), (nearer, 0), (half, 1), (diagonal, 0), (farther, 0),
+        (dispatch, 3), (join, 3), (nearer, 1), (half, 2), (diagonal, 1), (farther, 1),
+        (nearer, 2), (half, 3), (diagonal, 2), (farther, 2), (nearer, 3),
     ):
         work(n)
     mixed_out = call(

time: 177 us -> 166 us (0.938)
  waiting for transfers between devices: 66.9 us -> 58.1 us
  starting transfers between devices: 55.1 us -> 53.1 us
    ppermute x46, waiting for transfers between devices: 66.9 us -> 58.1 us  [send(): return lax.ppermute(x, axis, pairs)]
    ppermute x46, starting transfers between devices: 55.1 us -> 53.1 us  [send(): return lax.ppermute(x, axis, pairs)]
  transfers between devices with their start and end apart: 46 -> 46, of which waited for: 19 -> 21; matrix products, arithmetic and copies ran while one was open for 0% -> 2% of each run, Pallas kernels for 22% -> 25%
where the time goes in v7:
time: 166 us
  waiting for transfers between devices  58.1 us (35%)
  starting transfers between devices  53.1 us (32%)
  Pallas kernels  47 us (28%)
  local copies, waits for them, and re-layouts  3.41 us (2%)
  other arithmetic  2.39 us (1%)
    ppermute x46, waiting for transfers between devices, send(): return lax.ppermute(x, axis, pairs)  58.1 us
    ppermute x46, starting transfers between devices, send(): return lax.ppermute(x, axis, pairs)  53.1 us
    pallas_call x49, Pallas kernels, call(): pl.pallas_call(body, out_shape=out_shape, in_specs=list(specs or [VM] * c...  47 us
  transfers between devices with their start and end apart: 46, of which 21 were waited for; matrix products, arithmetic and copies ran while one was open for 2% of the time, Pallas kernels for 25%

profile of v7, /device:TPU:0, one launch (start us, length us, event | category | flops | bytes accessed | tf_op | source)
XLA Modules:
  0.0 165.6 jit_solution(6955353132571396611)
XLA Ops:
  0.6 3.0 %collective-permute-start.4 = (bf16[1024,384]{1,0:T(8,128)(2,1)}, bf16[1024,384]{1,0:T(8,128)(2,1)S(1)}, u32[]{:S(2)}, u32[]{:S(2)}) collective-permute-start(bf16[1024,384]{1,0:T(8,128)(2,1)} %refs_5_.1), channel_id=1, source_target_pairs={{0,16},{4,20},{8,24},{12,28},{16,0},{20,4},{24,8},{28,12},{1,17},{... | collective-permute-start | bytes 2359304 | tf_op jit(solution)/shard_map/ppermute | solution.py:401
  6.4 1.0 copy-done.5
  7.4 1.0 copy-done.6
  8.4 1.4 shard_map.113
  10.5 1.0 collective-permute-done.refs_2_
  11.5 1.6 collective-permute-start.1
  13.1 1.6 collective-permute-start.2
  14.7 1.0 copy-done.4
  15.7 1.1 shard_map.115
  16.9 3.1 %collective-permute-done.1.refs_1_ = f32[4,128,128]{2,1,0:T(8,128)S(1)} collective-permute-done((f32[4,128,128]{2,1,0:T(8,128)S(1)}, f32[4,128,128]{2,1,0:T(8,128)S(1)}, u32[]{:S(2)}, u32[]{:S(2)}) %collective-permute-start.1) | collective-permute-done | bytes 262176 | tf_op jit(solution)/shard_map/ppermute | solution.py:401
  20.0 1.5 collective-permute-done.4.refs_5_.refs_0_
  21.5 3.7 %collective-permute-start.5 = (f32[4,128,128]{2,1,0:T(8,128)S(1)}, f32[4,128,128]{2,1,0:T(8,128)S(1)}, u32[]{:S(2)}, u32[]{:S(2)}) collective-permute-start(f32[4,128,128]{2,1,0:T(8,128)S(1)} %get-tuple-element.83), channel_id=1, source_target_pairs={{0,16},{4,20},{8,24},{12,28},{1,17},{5,21},{9,25},{13,29},{2,18},{... | collective-permute-start | bytes 786440 | tf_op jit(solution)/shard_map/ppermute | solution.py:401
  25.1 2.7 %collective-permute-start.6 = (s32[8,128]{1,0:T(8,128)S(1)}, s32[8,128]{1,0:T(8,128)S(1)}, u32[]{:S(2)}, u32[]{:S(2)}) collective-permute-start(s32[8,128]{1,0:T(8,128)S(1)} %shard_map.116.refs_3_.refs_1_), channel_id=1, source_target_pairs={{0,2},{1,3},{2,0},{3,1},{4,6},{5,7},{6,4},{7,5},{8,10},{9,11},{10,... | collective-permute-start | bytes 12296 | tf_op jit(solution)/shard_map/ppermute | solution.py:401
  27.9 1.8 %collective-permute-done.6.refs_2_ = s32[8,128]{1,0:T(8,128)S(1)} collective-permute-done((s32[8,128]{1,0:T(8,128)S(1)}, s32[8,128]{1,0:T(8,128)S(1)}, u32[]{:S(2)}, u32[]{:S(2)}) %collective-permute-start.6) | collective-permute-done | bytes 4128 | tf_op jit(solution)/shard_map/ppermute | solution.py:401
  30.5 1.5 collective-permute-done.7.refs_5_
  32.0 1.3 shard_map.121.refs_3_.refs_1_
  33.5 1.5 collective-permute-start.9
  35.0 1.1 collective-permute-done.10.refs_2_
  36.1 0.8 shard_map.122.refs_6_.refs_4_
  37.0 1.3 shard_map.123
  38.3 3.5 %collective-permute-start.11 = (bf16[512,384]{1,0:T(8,128)(2,1)S(1)}, bf16[512,384]{1,0:T(8,128)(2,1)S(1)}, u32[]{:S(2)}, u32[]{:S(2)}) collective-permute-start(bf16[512,384]{1,0:T(8,128)(2,1)S(1)} %get-tuple-element.87), channel_id=1, source_target_pairs={{0,1},{3,2},{4,5},{7,6},{8,9},{11,10},{12,13},{15,14},{16,17},{19,... | collective-permute-start | bytes 1179656 | tf_op jit(solution)/shard_map/ppermute | solution.py:401
  41.8 1.3 shard_map.124
  43.1 1.3 collective-permute-start.15
  44.4 6.8 %collective-permute-done.11.refs_1_ = bf16[512,384]{1,0:T(8,128)(2,1)S(1)} collective-permute-done((bf16[512,384]{1,0:T(8,128)(2,1)S(1)}, bf16[512,384]{1,0:T(8,128)(2,1)S(1)}, u32[]{:S(2)}, u32[]{:S(2)}) %collective-permute-start.11) | collective-permute-done | bytes 393248 | tf_op jit(solution)/shard_map/ppermute | solution.py:401
  52.0 1.2 collective-permute-done.9.refs_5_.refs_0_
  53.3 1.3 shard_map.126
  54.6 1.5 collective-permute-start.13
  56.2 2.0 %collective-permute-start.12 = (bf16[512,384]{1,0:T(8,128)(2,1)S(1)}, bf16[512,384]{1,0:T(8,128)(2,1)S(1)}, u32[]{:S(2)}, u32[]{:S(2)}) collective-permute-start(bf16[512,384]{1,0:T(8,128)(2,1)S(1)} %shard_map.127.refs_1_), channel_id=1, source_target_pairs={{0,16},{4,20},{8,24},{12,28},{16,0},{20,4},{24,8},{28,12},{1,17},{... | collective-permute-start | bytes 1179656 | tf_op jit(solution)/shard_map/ppermute | solution.py:401
  58.2 5.1 %collective-permute-start.19 = (bf16[512,384]{1,0:T(8,128)(2,1)S(1)}, bf16[512,384]{1,0:T(8,128)(2,1)S(1)}, u32[]{:S(2)}, u32[]{:S(2)}) collective-permute-start(bf16[512,384]{1,0:T(8,128)(2,1)S(1)} %get-tuple-element.97), channel_id=1, source_target_pairs={{0,1},{3,2},{4,5},{7,6},{8,9},{11,10},{12,13},{15,14},{16,17},{19,... | collective-permute-start | bytes 1179656 | tf_op jit(solution)/shard_map/ppermute | solution.py:401
  64.2 1.3 collective-permute-start.17
  65.5 1.2 collective-permute-done.12.refs_5_
  66.7 1.2 shard_map.131
  68.0 3.8 %collective-permute-start.16 = (bf16[512,384]{1,0:T(8,128)(2,1)S(1)}, bf16[512,384]{1,0:T(8,128)(2,1)S(1)}, u32[]{:S(2)}, u32[]{:S(2)}) collective-permute-start(bf16[512,384]{1,0:T(8,128)(2,1)S(1)} %get-tuple-element.95), channel_id=1, source_target_pairs={{0,1},{3,2},{4,5},{7,6},{8,9},{11,10},{12,13},{15,14},{16,17},{19,... | collective-permute-start | bytes 1179656 | tf_op jit(solution)/shard_map/ppermute | solution.py:401
  72.0 2.7 %collective-permute-done.17.refs_1_ = bf16[512,384]{1,0:T(8,128)(2,1)S(1)} collective-permute-done((bf16[512,384]{1,0:T(8,128)(2,1)S(1)}, bf16[512,384]{1,0:T(8,128)(2,1)S(1)}, u32[]{:S(2)}, u32[]{:S(2)}) %collective-permute-start.17) | collective-permute-done | bytes 393248 | tf_op jit(solution)/shard_map/ppermute | solution.py:401
  74.7 0.9 shard_map.134
  76.4 1.3 collective-permute-start.21
  78.6 1.5 collective-permute-start.27
  80.9 8.9 %collective-permute-done.21.refs_1_ = bf16[512,384]{1,0:T(8,128)(2,1)S(1)} collective-permute-done((bf16[512,384]{1,0:T(8,128)(2,1)S(1)}, bf16[512,384]{1,0:T(8,128)(2,1)S(1)}, u32[]{:S(2)}, u32[]{:S(2)}) %collective-permute-start.21) | collective-permute-done | bytes 393248 | tf_op jit(solution)/shard_map/ppermute | solution.py:401
  89.8 0.9 shard_map.138
  90.9 1.6 collective-permute-start.26
  94.3 1.3 collective-permute-start.29
  95.6 8.9 %collective-permute-done.26.refs_1_ = bf16[512,384]{1,0:T(8,128)(2,1)S(1)} collective-permute-done((bf16[512,384]{1,0:T(8,128)(2,1)S(1)}, bf16[512,384]{1,0:T(8,128)(2,1)S(1)}, u32[]{:S(2)}, u32[]{:S(2)}) %collective-permute-start.26) | collective-permute-done | bytes 393248 | tf_op jit(solution)/shard_map/ppermute | solution.py:401
  104.5 0.9 shard_map.142
  105.5 2.1 %collective-permute-start.28 = (bf16[192,768]{1,0:T(8,128)(2,1)S(1)}, bf16[192,768]{1,0:T(8,128)(2,1)S(1)}, u32[]{:S(2)}, u32[]{:S(2)}) collective-permute-start(bf16[192,768]{1,0:T(8,128)(2,1)S(1)} %get-tuple-element.106.refs_5_), channel_id=1, source_target_pairs={{0,16},{4,12},{8,24},{12,4},{16,0},{20,28},{24,8},{28,20},{1,17},{... | collective-permute-start | bytes 884744 | tf_op jit(solution)/shard_map/ppermute | solution.py:401
  107.6 1.5 collective-permute-start.25
  109.7 3.5 %shard_map.144 = (f32[576,384]{1,0:T(8,128)S(1)}, f32[576,384]{1,0:T(8,128)S(1)}, f32[576,384]{1,0:T(8,128)S(1)}, f32[576,384]{1,0:T(8,128)S(1)}, f32[576,384]{1,0:T(8,128)S(1)}, /*index=5*/f32[576,384]{1,0:T(8,128)S(1)}) custom-call(s32[3]{0:T(128)S(1)} %pad_add_fusion.refs_0_, bf16[576,3072]{1,0:T(8,128)(2,1)S(1)} %bitcast.20, ...), custom_call_target="tpu_custom_call" | custom-call | flops 1 | bytes 1 | tf_op jit(solution)/shard_map/pallas_call | solution.py:45
  115.5 1.7 %shard_map.147 = (f32[576,384]{1,0:T(8,128)S(1)}, f32[576,384]{1,0:T(8,128)S(1)}) custom-call(s32[3]{0:T(128)S(1)} %pad_add_fusion.refs_0_, bf16[576,3072]{1,0:T(8,128)(2,1)S(1)} %bitcast.21, bf16[576,3072]{1,0:T(8,128)(2,1)S(1)} %bitcast.29, bf16[192,768]{1,0:T(8,128)(2,1)S(1)} %shard_map.146.refs_3_.refs_5_, ...), custom_call_target="tpu_custom_call" | custom-call | flops 1 | bytes 1 | tf_op jit(solution)/shard_map/pallas_call | solution.py:45
  117.1 2.8 %collective-permute-done.25.refs_1_ = bf16[512,384]{1,0:T(8,128)(2,1)S(1)} collective-permute-done((bf16[512,384]{1,0:T(8,128)(2,1)S(1)}, bf16[512,384]{1,0:T(8,128)(2,1)S(1)}, u32[]{:S(2)}, u32[]{:S(2)}) %collective-permute-start.25) | collective-permute-done | bytes 393248 | tf_op jit(solution)/shard_map/ppermute | solution.py:401
  119.9 1.3 shard_map.148
  121.3 1.7 %collective-permute-done.34.refs_2_ = bf16[384,512]{1,0:T(8,128)(2,1)S(1)} collective-permute-done((bf16[384,512]{1,0:T(8,128)(2,1)S(1)}, bf16[384,512]{1,0:T(8,128)(2,1)S(1)}, u32[]{:S(2)}, u32[]{:S(2)}) %collective-permute-start.34) | collective-permute-done | bytes 393248 | tf_op jit(solution)/shard_map/ppermute | solution.py:401
  124.5 2.0 %collective-permute-start.39 = (bf16[192,768]{1,0:T(8,128)(2,1)S(1)}, bf16[192,768]{1,0:T(8,128)(2,1)S(1)}, u32[]{:S(2)}, u32[]{:S(2)}) collective-permute-start(bf16[192,768]{1,0:T(8,128)(2,1)S(1)} %get-tuple-element.111.refs_1_), channel_id=1, source_target_pairs={{0,16},{4,12},{8,24},{12,4},{16,0},{20,28},{24,8},{28,20},{1,17},{... | collective-permute-start | bytes 884744 | tf_op jit(solution)/shard_map/ppermute | solution.py:401
  126.5 3.5 %shard_map.150 = (f32[576,384]{1,0:T(8,128)S(1)}, f32[576,384]{1,0:T(8,128)S(1)}, f32[576,384]{1,0:T(8,128)S(1)}, f32[576,384]{1,0:T(8,128)S(1)}, f32[576,384]{1,0:T(8,128)S(1)}, /*index=5*/f32[576,384]{1,0:T(8,128)S(1)}) custom-call(s32[3]{0:T(128)S(1)} %pad_add_fusion.refs_0_, bf16[576,3072]{1,0:T(8,128)(2,1)S(1)} %bitcast.22, ...), custom_call_target="tpu_custom_call" | custom-call | flops 1 | bytes 1 | tf_op jit(solution)/shard_map/pallas_call | solution.py:45
  130.7 3.8 %collective-permute-done.39.refs_0_ = bf16[192,768]{1,0:T(8,128)(2,1)S(1)} collective-permute-done((bf16[192,768]{1,0:T(8,128)(2,1)S(1)}, bf16[192,768]{1,0:T(8,128)(2,1)S(1)}, u32[]{:S(2)}, u32[]{:S(2)}) %collective-permute-start.39) | collective-permute-done | bytes 294944 | tf_op jit(solution)/shard_map/ppermute | solution.py:401
  134.5 1.6 collective-permute-done.40.refs_4_
  136.1 1.7 %shard_map.153 = (f32[576,384]{1,0:T(8,128)S(1)}, f32[576,384]{1,0:T(8,128)S(1)}) custom-call(s32[3]{0:T(128)S(1)} %pad_add_fusion.refs_0_, bf16[576,3072]{1,0:T(8,128)(2,1)S(1)} %bitcast.23, bf16[576,3072]{1,0:T(8,128)(2,1)S(1)} %bitcast.31, bf16[192,768]{1,0:T(8,128)(2,1)S(1)} %shard_map.152.refs_3_.refs_7_, ...), custom_call_target="tpu_custom_call" | custom-call | flops 1 | bytes 1 | tf_op jit(solution)/shard_map/pallas_call | solution.py:45
  137.8 3.5 %shard_map.154 = (f32[576,384]{1,0:T(8,128)S(1)}, f32[576,384]{1,0:T(8,128)S(1)}, f32[576,384]{1,0:T(8,128)S(1)}, f32[576,384]{1,0:T(8,128)S(1)}, f32[576,384]{1,0:T(8,128)S(1)}, /*index=5*/f32[576,384]{1,0:T(8,128)S(1)}) custom-call(s32[3]{0:T(128)S(1)} %pad_add_fusion.refs_0_, bf16[576,3072]{1,0:T(8,128)(2,1)S(1)} %bitcast.24, ...), custom_call_target="tpu_custom_call" | custom-call | flops 1 | bytes 1 | tf_op jit(solution)/shard_map/pallas_call | solution.py:45
  142.1 2.0 %collective-permute-start.42 = (bf16[192,768]{1,0:T(8,128)(2,1)S(1)}, bf16[192,768]{1,0:T(8,128)(2,1)S(1)}, u32[]{:S(2)}, u32[]{:S(2)}) collective-permute-start(bf16[192,768]{1,0:T(8,128)(2,1)S(1)} %get-tuple-element.129.refs_1_), channel_id=1, source_target_pairs={{0,16},{4,12},{8,24},{12,4},{16,0},{20,28},{24,8},{28,20},{1,17},{... | collective-permute-start | bytes 884744 | tf_op jit(solution)/shard_map/ppermute | solution.py:401
  144.2 4.7 %collective-permute-done.42.refs_0_ = bf16[192,768]{1,0:T(8,128)(2,1)S(1)} collective-permute-done((bf16[192,768]{1,0:T(8,128)(2,1)S(1)}, bf16[192,768]{1,0:T(8,128)(2,1)S(1)}, u32[]{:S(2)}, u32[]{:S(2)}) %collective-permute-start.42) | collective-permute-done | bytes 294944 | tf_op jit(solution)/shard_map/ppermute | solution.py:401
  149.0 1.6 collective-permute-done.43.refs_4_
  150.6 1.7 %shard_map.157 = (f32[576,384]{1,0:T(8,128)S(1)}, f32[576,384]{1,0:T(8,128)S(1)}) custom-call(s32[3]{0:T(128)S(1)} %pad_add_fusion.refs_0_, bf16[576,3072]{1,0:T(8,128)(2,1)S(1)} %bitcast.25, bf16[576,3072]{1,0:T(8,128)(2,1)S(1)} %bitcast.33, bf16[192,768]{1,0:T(8,128)(2,1)S(1)} %shard_map.156.refs_3_.refs_7_, ...), custom_call_target="tpu_custom_call" | custom-call | flops 1 | bytes 1 | tf_op jit(solution)/shard_map/pallas_call | solution.py:45
  152.2 6.3 %shard_map.158 = (bf16[576,1536]{1,0:T(8,128)(2,1)}, f32[8,128]{1,0:T(8,128)S(1)}) custom-call(s32[3]{0:T(128)S(1)} %pad_add_fusion.refs_0_, bf16[576,3072]{1,0:T(8,128)(2,1)S(1)} %bitcast.26, bf16[576,3072]{1,0:T(8,128)(2,1)S(1)} %bitcast.34, bf16[384,896]{1,0:T(8,128)(2,1)S(1)} %shard_map.149.refs_12_.refs_3_, ...), custom_call_target="tpu_custom_call" | custom-call | flops 1 | bytes 1 | tf_op jit(solution)/shard_map/pallas_call | solution.py:45
  159.1 1.4 collective-permute-done.33.refs_1_
  160.6 1.3 shard_map.159
  161.9 3.6 %shard_map.161 = (bf16[576,1536]{1,0:T(8,128)(2,1)}, f32[8,128]{1,0:T(8,128)}) custom-call(s32[3]{0:T(128)S(1)} %pad_add_fusion.refs_0_, bf16[576,3072]{1,0:T(8,128)(2,1)S(1)} %bitcast.27, bf16[576,3072]{1,0:T(8,128)(2,1)S(1)} %bitcast.35, bf16[192,896]{1,0:T(8,128)(2,1)S(1)} %shard_map.160.refs_3_.refs_8_, ...), custom_call_target="tpu_custom_call", output_to_operand_aliasing={{0}: (7, {})} | custom-call | flops 1 | bytes 1 | tf_op jit(solution)/shard_map/pallas_call | solution.py:45
  (107 shorter events, 17.5 us)
Async XLA Ops:
  0.6 27.2 %copy-start.3 = (bf16[1024,384]{1,0:T(8,128)(2,1)S(1)}, bf16[1024,384]{1,0:T(8,128)(2,1)}, u32[]{:S(2)}) copy-start(bf16[1024,384]{1,0:T(8,128)(2,1)} %refs_5_.1) | copy-start | bytes 2359300
  0.6 20.8 %collective-permute-start.4 = (bf16[1024,384]{1,0:T(8,128)(2,1)}, bf16[1024,384]{1,0:T(8,128)(2,1)S(1)}, u32[]{:S(2)}, u32[]{:S(2)}) collective-permute-start(bf16[1024,384]{1,0:T(8,128)(2,1)} %refs_5_.1), channel_id=1, source_target_pairs={{0,16},{4,20},{8,24},{12,28},{16,0},{20,4},{24,8},{28,12},{1,17},{... | collective-permute-start | bytes 2359304 | tf_op jit(solution)/shard_map/ppermute | solution.py:401
  6.4 1.0 copy-start.5
  7.4 1.0 copy-start.6
  9.9 1.6 collective-permute-start
  10.0 6.9 %collective-permute-start.3 = (bf16[64,3072]{1,0:T(8,128)(2,1)}, bf16[64,3072]{1,0:T(8,128)(2,1)S(1)}, u32[]{:S(2)}, u32[]{:S(2)}) collective-permute-start(bf16[64,3072]{1,0:T(8,128)(2,1)} %refs_3_.9), channel_id=1, source_target_pairs={{0,4},{4,0},{8,12},{12,8},{16,20},{20,16},{24,28},{28,24},{1,5},{5... | collective-permute-start | bytes 1179656 | tf_op jit(solution)/shard_map/ppermute | solution.py:401
  11.5 8.4 %collective-permute-start.1 = (f32[4,128,128]{2,1,0:T(8,128)S(1)}, f32[4,128,128]{2,1,0:T(8,128)S(1)}, u32[]{:S(2)}, u32[]{:S(2)}) collective-permute-start(f32[4,128,128]{2,1,0:T(8,128)S(1)} %get-tuple-element.81.refs_2_), channel_id=1, source_target_pairs={{0,8},{4,12},{8,0},{12,4},{16,24},{20,28},{24,16},{28,20},{1,9},{5... | collective-permute-start | bytes 786440 | tf_op jit(solution)/shard_map/ppermute | solution.py:401
  13.1 3.7 %collective-permute-start.2 = (s32[8,128]{1,0:T(8,128)S(1)}, s32[8,128]{1,0:T(8,128)S(1)}, u32[]{:S(2)}, u32[]{:S(2)}) collective-permute-start(s32[8,128]{1,0:T(8,128)S(1)} %pad.4.refs_4_.refs_0_), channel_id=1, source_target_pairs={{0,1},{1,0},{2,3},{3,2},{4,5},{5,4},{6,7},{7,6},{8,9},{9,8},{10,11... | collective-permute-start | bytes 12296 | tf_op jit(solution)/shard_map/ppermute | solution.py:401
  14.7 1.0 copy-start.4
  21.5 8.8 %collective-permute-start.5 = (f32[4,128,128]{2,1,0:T(8,128)S(1)}, f32[4,128,128]{2,1,0:T(8,128)S(1)}, u32[]{:S(2)}, u32[]{:S(2)}) collective-permute-start(f32[4,128,128]{2,1,0:T(8,128)S(1)} %get-tuple-element.83), channel_id=1, source_target_pairs={{0,16},{4,20},{8,24},{12,28},{1,17},{5,21},{9,25},{13,29},{2,18},{... | collective-permute-start | bytes 786440 | tf_op jit(solution)/shard_map/ppermute | solution.py:401
  25.1 4.6 %collective-permute-start.6 = (s32[8,128]{1,0:T(8,128)S(1)}, s32[8,128]{1,0:T(8,128)S(1)}, u32[]{:S(2)}, u32[]{:S(2)}) collective-permute-start(s32[8,128]{1,0:T(8,128)S(1)} %shard_map.116.refs_3_.refs_1_), channel_id=1, source_target_pairs={{0,2},{1,3},{2,0},{3,1},{4,6},{5,7},{6,4},{7,5},{8,10},{9,11},{10,... | collective-permute-start | bytes 12296 | tf_op jit(solution)/shard_map/ppermute | solution.py:401
  27.8 9.2 %copy-start.2 = (bf16[64,3072]{1,0:T(8,128)(2,1)S(1)}, bf16[64,3072]{1,0:T(8,128)(2,1)}, u32[]{:S(2)}) copy-start(bf16[64,3072]{1,0:T(8,128)(2,1)} %refs_3_.9) | copy-start | bytes 1179652
  30.4 1.6 collective-permute-start.7
  33.3 3.7 %collective-permute-start.8 = (bf16[256,1024]{1,0:T(8,128)(2,1)S(1)}, bf16[256,1024]{1,0:T(8,128)(2,1)S(1)}, u32[]{:S(2)}, u32[]{:S(2)}) collective-permute-start(bf16[256,1024]{1,0:T(8,128)(2,1)S(1)} %shard_map.121.refs_3_.refs_1_), channel_id=1, source_target_pairs={{0,4},{4,0},{8,12},{12,8},{16,20},{20,16},{24,28},{28,24},{1,5},{5... | collective-permute-start | bytes 1572872 | tf_op jit(solution)/shard_map/ppermute | solution.py:401
  33.5 19.8 %collective-permute-start.9 = (bf16[1024,384]{1,0:T(8,128)(2,1)S(1)}, bf16[1024,384]{1,0:T(8,128)(2,1)S(1)}, u32[]{:S(2)}, u32[]{:S(2)}) collective-permute-start(bf16[1024,384]{1,0:T(8,128)(2,1)S(1)} %shard_map.118.refs_3_), channel_id=1, source_target_pairs={{0,8},{4,12},{8,0},{12,4},{16,24},{20,28},{24,16},{28,20},{1,9},{5... | collective-permute-start | bytes 2359304 | tf_op jit(solution)/shard_map/ppermute | solution.py:401
  35.0 1.2 collective-permute-start.10
  38.3 12.9 %collective-permute-start.11 = (bf16[512,384]{1,0:T(8,128)(2,1)S(1)}, bf16[512,384]{1,0:T(8,128)(2,1)S(1)}, u32[]{:S(2)}, u32[]{:S(2)}) collective-permute-start(bf16[512,384]{1,0:T(8,128)(2,1)S(1)} %get-tuple-element.87), channel_id=1, source_target_pairs={{0,1},{3,2},{4,5},{7,6},{8,9},{11,10},{12,13},{15,14},{16,17},{19,... | collective-permute-start | bytes 1179656 | tf_op jit(solution)/shard_map/ppermute | solution.py:401
  43.1 20.2 %collective-permute-start.15 = (bf16[512,384]{1,0:T(8,128)(2,1)S(1)}, bf16[512,384]{1,0:T(8,128)(2,1)S(1)}, u32[]{:S(2)}, u32[]{:S(2)}) collective-permute-start(bf16[512,384]{1,0:T(8,128)(2,1)S(1)} %get-tuple-element.92), channel_id=1, source_target_pairs={{0,1},{3,2},{4,5},{7,6},{8,9},{11,10},{12,13},{15,14},{16,17},{19,... | collective-permute-start | bytes 1179656 | tf_op jit(solution)/shard_map/ppermute | solution.py:401
  51.3 12.8 %collective-permute-start.14 = (bf16[512,384]{1,0:T(8,128)(2,1)S(1)}, bf16[512,384]{1,0:T(8,128)(2,1)S(1)}, u32[]{:S(2)}, u32[]{:S(2)}) collective-permute-start(bf16[512,384]{1,0:T(8,128)(2,1)S(1)} %get-tuple-element.91), channel_id=1, source_target_pairs={{1,2},{2,1},{5,6},{6,5},{9,10},{10,9},{13,14},{14,13},{17,18},{18,... | collective-permute-start | bytes 1179656 | tf_op jit(solution)/shard_map/ppermute | solution.py:401
  54.6 10.9 %collective-permute-start.13 = (bf16[512,384]{1,0:T(8,128)(2,1)S(1)}, bf16[512,384]{1,0:T(8,128)(2,1)S(1)}, u32[]{:S(2)}, u32[]{:S(2)}) collective-permute-start(bf16[512,384]{1,0:T(8,128)(2,1)S(1)} %shard_map.128.refs_2_), channel_id=1, source_target_pairs={{0,8},{4,12},{8,0},{12,4},{16,24},{20,28},{24,16},{28,20},{1,9},{5... | collective-permute-start | bytes 1179656 | tf_op jit(solution)/shard_map/ppermute | solution.py:401
  56.2 10.5 %collective-permute-start.12 = (bf16[512,384]{1,0:T(8,128)(2,1)S(1)}, bf16[512,384]{1,0:T(8,128)(2,1)S(1)}, u32[]{:S(2)}, u32[]{:S(2)}) collective-permute-start(bf16[512,384]{1,0:T(8,128)(2,1)S(1)} %shard_map.127.refs_1_), channel_id=1, source_target_pairs={{0,16},{4,20},{8,24},{12,28},{16,0},{20,4},{24,8},{28,12},{1,17},{... | collective-permute-start | bytes 1179656 | tf_op jit(solution)/shard_map/ppermute | solution.py:401
  58.2 13.6 %collective-permute-start.19 = (bf16[512,384]{1,0:T(8,128)(2,1)S(1)}, bf16[512,384]{1,0:T(8,128)(2,1)S(1)}, u32[]{:S(2)}, u32[]{:S(2)}) collective-permute-start(bf16[512,384]{1,0:T(8,128)(2,1)S(1)} %get-tuple-element.97), channel_id=1, source_target_pairs={{0,1},{3,2},{4,5},{7,6},{8,9},{11,10},{12,13},{15,14},{16,17},{19,... | collective-permute-start | bytes 1179656 | tf_op jit(solution)/shard_map/ppermute | solution.py:401
  63.4 8.5 %collective-permute-start.18 = (bf16[512,384]{1,0:T(8,128)(2,1)S(1)}, bf16[512,384]{1,0:T(8,128)(2,1)S(1)}, u32[]{:S(2)}, u32[]{:S(2)}) collective-permute-start(bf16[512,384]{1,0:T(8,128)(2,1)S(1)} %get-tuple-element.96), channel_id=1, source_target_pairs={{1,2},{2,1},{5,6},{6,5},{9,10},{10,9},{13,14},{14,13},{17,18},{18,... | collective-permute-start | bytes 1179656 | tf_op jit(solution)/shard_map/ppermute | solution.py:401
  64.2 10.5 %copy-start.7 = (f32[3072]{0:T(1024)S(1)}, f32[3072]{0:T(1024)}, u32[]{:S(2)}) copy-start(f32[3072]{0:T(1024)} %param.16) | copy-start | bytes 36868
  64.2 10.5 %collective-permute-start.17 = (bf16[512,384]{1,0:T(8,128)(2,1)S(1)}, bf16[512,384]{1,0:T(8,128)(2,1)S(1)}, u32[]{:S(2)}, u32[]{:S(2)}) collective-permute-start(bf16[512,384]{1,0:T(8,128)(2,1)S(1)} %shard_map.130.refs_7_.refs_2_), channel_id=1, source_target_pairs={{1,0},{2,3},{5,4},{6,7},{9,8},{10,11},{13,12},{14,15},{17,16},{18,... | collective-permute-start | bytes 1179656 | tf_op jit(solution)/shard_map/ppermute | solution.py:401
  68.0 9.9 %collective-permute-start.16 = (bf16[512,384]{1,0:T(8,128)(2,1)S(1)}, bf16[512,384]{1,0:T(8,128)(2,1)S(1)}, u32[]{:S(2)}, u32[]{:S(2)}) collective-permute-start(bf16[512,384]{1,0:T(8,128)(2,1)S(1)} %get-tuple-element.95), channel_id=1, source_target_pairs={{0,1},{3,2},{4,5},{7,6},{8,9},{11,10},{12,13},{15,14},{16,17},{19,... | collective-permute-start | bytes 1179656 | tf_op jit(solution)/shard_map/ppermute | solution.py:401
  75.6 2.3 %collective-permute-start.23 = (bf16[384,384]{1,0:T(8,128)(2,1)S(1)}, bf16[384,384]{1,0:T(8,128)(2,1)S(1)}, u32[]{:S(2)}, u32[]{:S(2)}) collective-permute-start(bf16[384,384]{1,0:T(8,128)(2,1)S(1)} %get-tuple-element.99.refs_2_.refs_1_), channel_id=1, source_target_pairs={{0,4},{4,0},{8,12},{12,8},{16,20},{20,16},{24,28},{28,24},{1,5},{5... | collective-permute-start | bytes 884744 | tf_op jit(solution)/shard_map/ppermute | solution.py:401
  75.7 5.1 %collective-permute-start.22 = (bf16[512,384]{1,0:T(8,128)(2,1)S(1)}, bf16[512,384]{1,0:T(8,128)(2,1)S(1)}, u32[]{:S(2)}, u32[]{:S(2)}) collective-permute-start(bf16[512,384]{1,0:T(8,128)(2,1)S(1)} %get-tuple-element.102), channel_id=1, source_target_pairs={{1,2},{2,1},{5,6},{6,5},{9,10},{10,9},{13,14},{14,13},{17,18},{18,... | collective-permute-start | bytes 1179656 | tf_op jit(solution)/shard_map/ppermute | solution.py:401
  76.4 13.4 %collective-permute-start.21 = (bf16[512,384]{1,0:T(8,128)(2,1)S(1)}, bf16[512,384]{1,0:T(8,128)(2,1)S(1)}, u32[]{:S(2)}, u32[]{:S(2)}) collective-permute-start(bf16[512,384]{1,0:T(8,128)(2,1)S(1)} %shard_map.133.refs_5_.refs_2_), channel_id=1, source_target_pairs={{1,0},{2,3},{5,4},{6,7},{9,8},{10,11},{13,12},{14,15},{17,16},{18,... | collective-permute-start | bytes 1179656 | tf_op jit(solution)/shard_map/ppermute | solution.py:401
  78.6 14.5 %collective-permute-start.27 = (bf16[384,768]{1,0:T(8,128)(2,1)S(1)}, bf16[384,768]{1,0:T(8,128)(2,1)S(1)}, u32[]{:S(2)}, u32[]{:S(2)}) collective-permute-start(bf16[384,768]{1,0:T(8,128)(2,1)S(1)} %shard_map.136.refs_2_.refs_3_), channel_id=1, source_target_pairs={{0,8},{4,20},{8,0},{12,28},{16,24},{20,4},{24,16},{28,12},{1,9},{5... | collective-permute-start | bytes 1769480 | tf_op jit(solution)/shard_map/ppermute | solution.py:401
  80.2 12.9 %collective-permute-start.20 = (bf16[512,384]{1,0:T(8,128)(2,1)S(1)}, bf16[512,384]{1,0:T(8,128)(2,1)S(1)}, u32[]{:S(2)}, u32[]{:S(2)}) collective-permute-start(bf16[512,384]{1,0:T(8,128)(2,1)S(1)} %get-tuple-element.101), channel_id=1, source_target_pairs={{1,2},{2,1},{5,6},{6,5},{9,10},{10,9},{13,14},{14,13},{17,18},{18,... | collective-permute-start | bytes 1179656 | tf_op jit(solution)/shard_map/ppermute | solution.py:401
  90.8 18.9 %copy-start = (bf16[1,576,3072]{2,1,0:T(8,128)(2,1)S(1)}, bf16[1,576,3072]{2,1,0:T(8,128)(2,1)}, u32[]{:S(2)}) copy-start(bf16[1,576,3072]{2,1,0:T(8,128)(2,1)} %param.18) | copy-start | bytes 10616836
  90.8 18.9 %copy-start.1 = (bf16[1,576,3072]{2,1,0:T(8,128)(2,1)S(1)}, bf16[1,576,3072]{2,1,0:T(8,128)(2,1)}, u32[]{:S(2)}) copy-start(bf16[1,576,3072]{2,1,0:T(8,128)(2,1)} %param.19) | copy-start | bytes 10616836
  90.8 1.6 collective-permute-start.24
  90.9 13.7 %collective-permute-start.26 = (bf16[512,384]{1,0:T(8,128)(2,1)S(1)}, bf16[512,384]{1,0:T(8,128)(2,1)S(1)}, u32[]{:S(2)}, u32[]{:S(2)}) collective-permute-start(bf16[512,384]{1,0:T(8,128)(2,1)S(1)} %shard_map.137.refs_5_.refs_2_), channel_id=1, source_target_pairs={{1,0},{2,3},{5,4},{6,7},{9,8},{10,11},{13,12},{14,15},{17,16},{18,... | collective-permute-start | bytes 1179656 | tf_op jit(solution)/shard_map/ppermute | solution.py:401
  93.7 15.9 %collective-permute-start.30 = (bf16[384,768]{1,0:T(8,128)(2,1)S(1)}, bf16[384,768]{1,0:T(8,128)(2,1)S(1)}, u32[]{:S(2)}, u32[]{:S(2)}) collective-permute-start(bf16[384,768]{1,0:T(8,128)(2,1)S(1)} %get-tuple-element.108), channel_id=1, source_target_pairs={{0,4},{4,0},{8,12},{12,8},{16,20},{20,16},{24,28},{28,24},{1,5},{5... | collective-permute-start | bytes 1769480 | tf_op jit(solution)/shard_map/ppermute | solution.py:401
  94.3 18.9 %collective-permute-start.29 = (bf16[384,768]{1,0:T(8,128)(2,1)S(1)}, bf16[384,768]{1,0:T(8,128)(2,1)S(1)}, u32[]{:S(2)}, u32[]{:S(2)}) collective-permute-start(bf16[384,768]{1,0:T(8,128)(2,1)S(1)} %shard_map.139.refs_2_.refs_3_), channel_id=1, source_target_pairs={{0,8},{4,20},{8,0},{12,28},{16,24},{20,4},{24,16},{28,12},{1,9},{5... | collective-permute-start | bytes 1769480 | tf_op jit(solution)/shard_map/ppermute | solution.py:401
  105.4 3.6 %collective-permute-start.31 = (bf16[384,384]{1,0:T(8,128)(2,1)S(1)}, bf16[384,384]{1,0:T(8,128)(2,1)S(1)}, u32[]{:S(2)}, u32[]{:S(2)}) collective-permute-start(bf16[384,384]{1,0:T(8,128)(2,1)S(1)} %get-tuple-element.109.refs_1_.refs_3_), channel_id=1, source_target_pairs={{0,4},{4,0},{8,12},{12,8},{16,20},{20,16},{24,28},{28,24},{1,5},{5... | collective-permute-start | bytes 884744 | tf_op jit(solution)/shard_map/ppermute | solution.py:401
  105.5 8.3 %collective-permute-start.28 = (bf16[192,768]{1,0:T(8,128)(2,1)S(1)}, bf16[192,768]{1,0:T(8,128)(2,1)S(1)}, u32[]{:S(2)}, u32[]{:S(2)}) collective-permute-start(bf16[192,768]{1,0:T(8,128)(2,1)S(1)} %get-tuple-element.106.refs_5_), channel_id=1, source_target_pairs={{0,16},{4,12},{8,24},{12,4},{16,0},{20,28},{24,8},{28,20},{1,17},{... | collective-permute-start | bytes 884744 | tf_op jit(solution)/shard_map/ppermute | solution.py:401
  107.6 12.4 %collective-permute-start.25 = (bf16[512,384]{1,0:T(8,128)(2,1)S(1)}, bf16[512,384]{1,0:T(8,128)(2,1)S(1)}, u32[]{:S(2)}, u32[]{:S(2)}) collective-permute-start(bf16[512,384]{1,0:T(8,128)(2,1)S(1)} %shard_map.140.refs_2_), channel_id=1, source_target_pairs={{1,0},{2,3},{5,4},{6,7},{9,8},{10,11},{13,12},{14,15},{17,16},{18,... | collective-permute-start | bytes 1179656 | tf_op jit(solution)/shard_map/ppermute | solution.py:401
  113.8 1.6 collective-permute-start.32
  113.9 12.6 %collective-permute-start.37 = (bf16[384,768]{1,0:T(8,128)(2,1)S(1)}, bf16[384,768]{1,0:T(8,128)(2,1)S(1)}, u32[]{:S(2)}, u32[]{:S(2)}) collective-permute-start(bf16[384,768]{1,0:T(8,128)(2,1)S(1)} %get-tuple-element.116), channel_id=1, source_target_pairs={{0,4},{4,0},{8,12},{12,8},{16,20},{20,16},{24,28},{28,24},{1,5},{5... | collective-permute-start | bytes 1769480 | tf_op jit(solution)/shard_map/ppermute | solution.py:401
  114.4 15.6 %collective-permute-start.36 = (bf16[384,768]{1,0:T(8,128)(2,1)S(1)}, bf16[384,768]{1,0:T(8,128)(2,1)S(1)}, u32[]{:S(2)}, u32[]{:S(2)}) collective-permute-start(bf16[384,768]{1,0:T(8,128)(2,1)S(1)} %shard_map.143.refs_6_.refs_3_), channel_id=1, source_target_pairs={{0,8},{4,20},{8,0},{12,28},{16,24},{20,4},{24,16},{28,12},{1,9},{5... | collective-permute-start | bytes 1769480 | tf_op jit(solution)/shard_map/ppermute | solution.py:401
  121.2 1.8 %collective-permute-start.34 = (bf16[384,512]{1,0:T(8,128)(2,1)S(1)}, bf16[384,512]{1,0:T(8,128)(2,1)S(1)}, u32[]{:S(2)}, u32[]{:S(2)}) collective-permute-start(bf16[384,512]{1,0:T(8,128)(2,1)S(1)} %get-tuple-element.115.refs_1_.refs_3_), channel_id=1, source_target_pairs={{0,4},{4,0},{8,12},{12,8},{16,20},{20,16},{24,28},{28,24},{1,5},{5... | collective-permute-start | bytes 1179656 | tf_op jit(solution)/shard_map/ppermute | solution.py:401
  123.7 17.6 %collective-permute-start.35 = (bf16[384,896]{1,0:T(8,128)(2,1)S(1)}, bf16[384,896]{1,0:T(8,128)(2,1)S(1)}, u32[]{:S(2)}, u32[]{:S(2)}) collective-permute-start(bf16[384,896]{1,0:T(8,128)(2,1)S(1)} %shard_map.149.refs_12_.refs_3_), channel_id=1, source_target_pairs={{0,8},{4,20},{8,0},{12,28},{16,24},{20,4},{24,16},{28,12},{1,9},{5... | collective-permute-start | bytes 2064392 | tf_op jit(solution)/shard_map/ppermute | solution.py:401
  124.5 9.9 %collective-permute-start.39 = (bf16[192,768]{1,0:T(8,128)(2,1)S(1)}, bf16[192,768]{1,0:T(8,128)(2,1)S(1)}, u32[]{:S(2)}, u32[]{:S(2)}) collective-permute-start(bf16[192,768]{1,0:T(8,128)(2,1)S(1)} %get-tuple-element.111.refs_1_), channel_id=1, source_target_pairs={{0,16},{4,12},{8,24},{12,4},{16,0},{20,28},{24,8},{28,20},{1,17},{... | collective-permute-start | bytes 884744 | tf_op jit(solution)/shard_map/ppermute | solution.py:401
  130.6 7.2 %collective-permute-start.38 = (bf16[384,768]{1,0:T(8,128)(2,1)S(1)}, bf16[384,768]{1,0:T(8,128)(2,1)S(1)}, u32[]{:S(2)}, u32[]{:S(2)}) collective-permute-start(bf16[384,768]{1,0:T(8,128)(2,1)S(1)} %get-tuple-element.123), channel_id=1, source_target_pairs={{0,4},{4,0},{8,12},{12,8},{16,20},{20,16},{24,28},{28,24},{1,5},{5... | collective-permute-start | bytes 1769480 | tf_op jit(solution)/shard_map/ppermute | solution.py:401
  134.5 1.6 collective-permute-start.40
  141.9 10.3 %collective-permute-start.41 = (bf16[384,896]{1,0:T(8,128)(2,1)S(1)}, bf16[384,896]{1,0:T(8,128)(2,1)S(1)}, u32[]{:S(2)}, u32[]{:S(2)}) collective-permute-start(bf16[384,896]{1,0:T(8,128)(2,1)S(1)} %get-tuple-element.133), channel_id=1, source_target_pairs={{0,4},{4,0},{8,12},{12,8},{16,20},{20,16},{24,28},{28,24},{1,5},{5... | collective-permute-start | bytes 2064392 | tf_op jit(solution)/shard_map/ppermute | solution.py:401
  142.1 6.7 %collective-permute-start.42 = (bf16[192,768]{1,0:T(8,128)(2,1)S(1)}, bf16[192,768]{1,0:T(8,128)(2,1)S(1)}, u32[]{:S(2)}, u32[]{:S(2)}) collective-permute-start(bf16[192,768]{1,0:T(8,128)(2,1)S(1)} %get-tuple-element.129.refs_1_), channel_id=1, source_target_pairs={{0,16},{4,12},{8,24},{12,4},{16,0},{20,28},{24,8},{28,20},{1,17},{... | collective-permute-start | bytes 884744 | tf_op jit(solution)/shard_map/ppermute | solution.py:401
  144.2 14.3 %collective-permute-start.44 = (bf16[192,896]{1,0:T(8,128)(2,1)S(1)}, bf16[192,896]{1,0:T(8,128)(2,1)S(1)}, u32[]{:S(2)}, u32[]{:S(2)}) collective-permute-start(bf16[192,896]{1,0:T(8,128)(2,1)S(1)} %get-tuple-element.139.refs_1_), channel_id=1, source_target_pairs={{0,16},{4,12},{8,24},{12,4},{16,0},{20,28},{24,8},{28,20},{1,17},{... | collective-permute-start | bytes 1032200 | tf_op jit(solution)/shard_map/ppermute | solution.py:401
  148.9 1.6 collective-permute-start.43
  158.6 3.3 %collective-permute-start.45 = (bf16[192,896]{1,0:T(8,128)(2,1)S(1)}, bf16[192,896]{1,0:T(8,128)(2,1)S(1)}, u32[]{:S(2)}, u32[]{:S(2)}) collective-permute-start(bf16[192,896]{1,0:T(8,128)(2,1)S(1)} %shard_map.160.refs_3_.refs_8_), channel_id=1, source_target_pairs={{0,4},{4,0},{8,12},{12,8},{16,20},{20,16},{24,28},{28,24},{1,5},{5... | collective-permute-start | bytes 1032200 | tf_op jit(solution)/shard_map/ppermute | solution.py:401
  158.8 1.8 %collective-permute-start.33 = (bf16[64,1536]{1,0:T(8,128)(2,1)S(1)}, bf16[64,1536]{1,0:T(8,128)(2,1)S(1)}, u32[]{:S(2)}, u32[]{:S(2)}) collective-permute-start(bf16[64,1536]{1,0:T(8,128)(2,1)S(1)} %get-tuple-element.113), channel_id=1, source_target_pairs={{0,4},{4,0},{8,12},{12,8},{16,20},{20,16},{24,28},{28,24},{1,5},{5... | collective-permute-start | bytes 589832 | tf_op jit(solution)/shard_map/ppermute | solution.py:401

commit v8 on v7

--- a/solution.py
+++ b/solution.py
@@ -35,7 +35,7 @@
     return jax.ShapeDtypeStruct(tuple(shape), dtype)
 
 
-def call(kernel, out_shape, operands, flops=0, exps=0, deps=(), specs=None, limit=12, **kwargs):
+def call(kernel, out_shape, operands, deps=(), specs=None, limit=12, **kwargs):
     count, extra = len(operands), len(deps)
 
     def body(*refs):
@@ -258,18 +258,11 @@
     return out.astype(BF16)
 
 
-def join_kernel(cols, place_ref, own_ref, got_ref, out_ref):
-    out_ref[:, tile(place_ref[1], cols)] = own_ref[:, :cols]
-    out_ref[:, tile(1 - place_ref[1], cols)] = got_ref[:, :cols]
-    if own_ref.shape[1] > cols:
-        extra = own_ref[:, cols:].astype(F32) + got_ref[:, cols:].astype(F32)
-        total = jnp.sum(extra, axis=1, keepdims=True)
-        out_ref[:, CORES * cols :] = in_three(total)
-
-
-def half_kernel(place_ref, in_ref, out_ref, all_ref):
-    out_ref[...] = in_ref[tile(place_ref[1], out_ref.shape[0]), :]
-    all_ref[...] = in_ref[...]
+def pack_kernel(place_ref, own_ref, near_ref, far_ref, onward_ref, pack_ref):
+    wide = own_ref.shape[1]
+    onward_ref[...] = jnp.where(place_ref[1] == 0, near_ref[...], far_ref[...])
+    for n, ref in enumerate((own_ref, near_ref, far_ref)):
+        pack_ref[:, n * wide : (n + 1) * wide] = ref[...]
 
 
 def copy_kernel(in_ref, out_ref):
@@ -292,38 +285,31 @@
         out_ref[:, tile(block + 1 - place_ref[1], cols)] = got_ref[:, n * cols : (n + 1) * cols]
 
 
-ROLES = ("own", "mine", "other", "diagonal")
-
-
-def expert_kernel(t, roles, mode, has_sums, place_ref, gate_ref, up_ref, *refs):
+def expert_kernel(t, away, mode, has_sums, place_ref, gate_ref, up_ref, *refs):
     refs = list(refs)
-    pieces = [[refs.pop(0) for _ in range(2 if r == "diagonal" else 1)] for r in roles]
-    sums = [[refs.pop(0), refs.pop(0)] for _ in roles] if has_sums else None
+    pieces, others = refs[: len(away)], refs[len(away)]
+    refs = refs[len(away) + 1 :]
+    sums = [[refs.pop(0), refs.pop(0)] for _ in away] if has_sums else None
     if mode == "next":
         refs.pop(0)
     model = gate_ref.shape[1]
     width = model // GROUPS
-    away = {"own": 0, "mine": 1 + place_ref[1], "other": 2 - place_ref[1], "diagonal": 3}
+    cols, wide = width // CORES, pieces[0].shape[1]
     if mode is None:
-        outs = refs[: 2 * len(roles)]
-        held = refs[2 * len(roles) :]
+        outs = refs[: 2 * len(away)]
+        held = refs[2 * len(away)]
     else:
-        outs, mark_ref, ready, sems = refs[:4]
-        held = refs[4:]
+        outs, mark_ref, held, ready, sems = refs
         mark_ref[...] = jnp.zeros_like(mark_ref)
     copies = []
-    for n, role in enumerate(roles):
-        source = place_ref[0] ^ away[role]
-        ref = pieces[n][0]
-        if role == "diagonal":
-            rows = ref.shape[0]
-            held[0][tile(place_ref[1], rows), :] = ref[...]
-            held[0][tile(1 - place_ref[1], rows), :] = pieces[n][1][...]
-            ref = held[0]
-        x = ref[:, :width]
-        cols = tile(source ^ t, width)
-        gated = dot(gate_ref[:, cols], x, NT)
-        lifted = dot(up_ref[:, cols], x, NT)
+    for n, s in enumerate(away):
+        source = place_ref[0] ^ s
+        held[n, :, tile(place_ref[1], cols)] = pieces[n][:, :cols]
+        held[n, :, tile(1 - place_ref[1], cols)] = others[:, n * wide : n * wide + cols]
+        x = held[n]
+        at = tile(source ^ t, width)
+        gated = dot(gate_ref[:, at], x, NT)
+        lifted = dot(up_ref[:, at], x, NT)
         if sums is not None:
             gated = gated + sums[n][0][...]
             lifted = lifted + sums[n][1][...]
@@ -332,35 +318,36 @@
             outs[2 * n + 1][...] = lifted
             continue
         lane = lax.broadcasted_iota(jnp.int32, (8, LANES), 1)
-        squares = dot((lane < 3).astype(BF16), ref[:, width:], NT)[0:1, :]
-        scale = lax.rsqrt(squares / model + 1e-05)
+        pick = (lane < 3).astype(BF16)
+        squares = dot(pick, pieces[n][:, cols:], NT)
+        squares = squares + dot(pick, others[:, n * wide + cols : (n + 1) * wide], NT)
+        scale = lax.rsqrt(squares[0:1, :] / model + 1e-05)
         gated, lifted = gated * scale, lifted * scale
         silu = (0.5 * gated) * (1.0 + jnp.tanh(0.5 * gated))
         ready[n] = (silu * lifted).astype(BF16)
         at = tile(source, ready.shape[2])
         rows = ready.shape[1] // 4
         for q in range(4):
-            cut = slice(q * rows, (q + 1) * rows)
+            part = slice(q * rows, (q + 1) * rows)
             copies.append(
-                pltpu.make_async_copy(
-                    ready.at[n, cut], outs.at[cut, at], sems.at[4 * n + q]
-                )
+                pltpu.make_async_copy(ready.at[n, part], outs.at[part, at], sems.at[4 * n + q])
             )
             copies[-1].start()
     for copy in copies:
         copy.wait()
 
 
-def expert_step(place, t, final, roles, pieces, gate, up, sums, hidden, deps):
+def expert_step(place, t, final, away, pieces, others, gate, up, sums, hidden, deps):
     hid, model = gate.shape
     width = model // GROUPS
-    slots = sum(x.shape[0] for x in pieces[0])
-    operands = [place, gate, up] + [x for per in pieces for x in per]
-    has_sums = roles[0] in sums
+    slots = pieces[0].shape[0]
+    operands = [place, gate, up] + pieces + [others]
+    has_sums = away[0] in sums
     if has_sums:
-        operands += [x for r in roles for x in sums[r]]
+        operands += [x for s in away for x in sums[s]]
     specs = [SM] + [VM] * (len(operands) - 1)
-    kwargs, mode, scratch = {}, None, []
+    kwargs, mode = {}, None
+    scratch = [pltpu.VMEM((len(away), slots, width), BF16)]
     if final:
         mode = "first" if hidden is None else "next"
         if hidden is not None:
@@ -370,30 +357,25 @@
         out_shape = [like((hid, slots * GROUPS)), like((8, LANES), F32)]
         kwargs["out_specs"] = [ANY, VM]
         scratch += [
-            pltpu.VMEM((len(roles), hid, slots), BF16),
-            pltpu.SemaphoreType.DMA((4 * len(roles),)),
+            pltpu.VMEM((len(away), hid, slots), BF16),
+            pltpu.SemaphoreType.DMA((4 * len(away),)),
         ]
     else:
-        out_shape = [like((hid, slots), F32)] * (2 * len(roles))
-    if "diagonal" in roles:
-        wide = pieces[roles.index("diagonal")][0].shape[1]
-        scratch.append(pltpu.VMEM((slots, wide), BF16))
+        out_shape = [like((hid, slots), F32)] * (2 * len(away))
     out = call(
-        functools.partial(expert_kernel, t, roles, mode, has_sums),
+        functools.partial(expert_kernel, t, away, mode, has_sums),
         out_shape,
         operands,
-        4 * hid * slots * width * len(roles),
-        hid * slots * len(roles) if mode else 0,
-        deps,
-        specs,
-        20,
+        deps=deps,
+        specs=specs,
+        limit=20,
         scratch_shapes=scratch,
         **kwargs,
     )
     if mode:
         return out
-    for n, r in enumerate(roles):
-        sums[r] = out[2 * n : 2 * n + 2]
+    for n, s in enumerate(away):
+        sums[s] = out[2 * n : 2 * n + 2]
     return hidden, out[0]
 
 
@@ -403,10 +385,6 @@
 
 def swap(x):
     return send(x, "ctx", [(d, d ^ 1) for d in range(lax.axis_size("ctx"))])
-
-
-def outbound(x):
-    return send(x, "ctx", [(d, d ^ (4 if d % 2 else 2)) for d in range(lax.axis_size("ctx"))])
 
 
 def onward(x):
@@ -440,8 +418,8 @@
     gate, up = gate_weight[0], up_weight[0]
     last = []
 
-    def run(kernel, out_shape, operands, *more, deps=(), **kwargs):
-        out = call(kernel, out_shape, operands, *more, deps=list(last) + list(deps), **kwargs)
+    def run(kernel, out_shape, operands, deps=(), **kwargs):
+        out = call(kernel, out_shape, operands, list(last) + list(deps), **kwargs)
         last[:] = [out[0] if isinstance(out, (list, tuple)) else out]
         return out
 
@@ -460,8 +438,6 @@
         fresh_kernel,
         [state_like] * 2 + [like((length, here))] * 2,
         [place, table, key_rows, value_rows],
-        4 * heads * length * size * size,
-        heads * length * size,
         deps=[ids],
         specs=[SM, VM, HBM, HBM],
         scratch_shapes=[pltpu.SemaphoreType.DMA((4,))],
@@ -492,8 +468,6 @@
         local_kernel,
         [like((length, here), F32), like((length, here))],
         [table, queries, keys, values],
-        4 * heads * length * length * size,
-        heads * length * length,
         specs=[VM, HBM, VM, VM],
         scratch_shapes=[pltpu.SemaphoreType.DMA(())],
     )
@@ -517,44 +491,43 @@
         head_kernel,
         like((length, here)),
         [place, table, queries_here, local, keep, got],
-        4 * heads * length * size * size,
-        heads * length * size,
         specs=[SM] + [VM] * 5,
     )
     heads_got = swap(head_out)
-    picks = run(
-        functools.partial(picks_kernel, tokens, capacity),
-        like((slots, every)),
-        [place, ids, ids_got],
-        specs=[SM, VM, VM],
-    )
 
     chunk_f32, chunk_b16 = like((every, cols), F32), like((every, cols))
     end = GROUPS - 1
     wide = [cols + LANES * (n == end) for n in range(GROUPS)]
     weights = [[out_weight], [weight_y], [weight_x], None]
-    parts, totals, mixed, joined = [None] * 4, [None] * 4, [None] * 4, [None] * 4
+    parts, totals, mixed = [None] * 4, [None] * 4, [None] * 4
     moved = {}
     sums, hidden = {}, None
+
+    def routes(n):
+        moved["picks", n] = run(
+            functools.partial(picks_kernel, tokens, capacity),
+            like((slots, every)),
+            [place, ids, ids_got],
+            specs=[SM, VM, VM],
+        )
 
     def project(n):
         parts[n], sent = run(
             functools.partial(project_kernel, ORDER[n]),
             [chunk_f32, chunk_b16],
             [place, head_out, heads_got, residual, rest_got] + weights[n],
-            2 * every * here * cols,
             specs=[SM] + [VM] * (4 + len(weights[n])),
         )
         moved["in", n] = send(sent, "exp", [(0, 1), (3, 2)])
 
     def inward(n):
         parts[n], sent = run(
-            inward_kernel, [chunk_f32, chunk_b16], [parts[n], moved["in", n]], every * cols
+            inward_kernel, [chunk_f32, chunk_b16], [parts[n], moved["in", n]]
         )
         moved["across", n] = send(sent, "exp", [(1, 2), (2, 1)])
 
     def outward(n):
-        totals[n] = run(total_kernel, chunk_b16, [parts[n], moved["across", n]], every * cols)
+        totals[n] = run(total_kernel, chunk_b16, [parts[n], moved["across", n]])
         moved["out", n] = send(totals[n], "exp", [(1, 0), (2, 3)])
 
     def dispatch(n):
@@ -566,50 +539,43 @@
         x, mixed[n], *gives = run(
             functools.partial(dispatch_kernel, ORDER[n], n == end),
             outs,
-            [place, moved["out", n], totals[n], gain, picks] + known,
-            2 * slots * every * wide[n],
+            [place, moved["out", n], totals[n], gain, moved["picks", 0]] + known,
             specs=[SM] + [VM] * (4 + len(known)),
         )
-        moved["x", n] = (x, swap(x))
+        moved["own", n] = x
+        moved["near", n] = send(x, "ctx", [(d, d ^ 2) for d in range(8)])
+        moved["far", n] = send(x, "ctx", [(d, d ^ 4) for d in range(8)])
         if gives:
             moved["mixed"] = swap(gives[0])
 
-    def join(n):
-        joined[n] = run(
-            functools.partial(join_kernel, cols),
-            like((slots, wide[n] + cols)),
-            [place, *moved["x", n]],
-            specs=[SM, VM, VM],
+    def forward(n):
+        x = moved["own", n]
+        out, pack = run(
+            pack_kernel,
+            [like(x.shape), like((slots, 3 * wide[n]))],
+            [place, x, moved["near", n], moved["far", n]],
+            specs=[SM] + [VM] * 3,
         )
-        moved["near", n] = outbound(joined[n])
-
-    def half(n):
-        near = moved["near", n]
-        out, copied = run(
-            half_kernel,
-            [like((slots // 2, near.shape[1])), like(near.shape)],
-            [place, near],
-            specs=[SM, VM],
-        )
-        moved["far", n] = onward(out)
-        moved["other", n] = swap(copied)
+        moved["diagonal", n] = onward(out)
+        moved["others", n] = swap(pack)
 
     def diagonal(n):
-        moved["far", n] = copy(moved["far", n])
-        moved["rest", n] = swap(moved["far", n])
-
-    def experts(n, roles, pieces):
+        moved["diagonal", n] = copy(moved["diagonal", n])
+        moved["rest", n] = swap(moved["diagonal", n])
+
+    def experts(n, away, pieces, others):
         nonlocal hidden
         hidden, mark = expert_step(
-            place, ORDER[n], n == end, roles, pieces, gate, up, sums, hidden, last[:]
+            place, ORDER[n], n == end, away, pieces, others, gate, up, sums, hidden, last[:]
         )
         last[:] = [mark]
 
     def nearer(n):
-        experts(n, ROLES[:3], [[joined[n]], [moved["near", n]], [moved["other", n]]])
+        pieces = [moved["own", n], moved["near", n], moved["far", n]]
+        experts(n, (0, 1, 2), pieces, moved["others", n])
 
     def farther(n):
-        experts(n, ROLES[3:], [[moved["far", n], moved["rest", n]]])
+        experts(n, (3,), [moved["diagonal", n]], moved["rest", n])
 
     def fetch(n):
         top = send(cut(weight_x, 0), "ctx", [(d, d ^ 4) for d in range(8)])
@@ -617,12 +583,12 @@
         weights[n] = [top, bottom]
 
     for work, n in (
-        (project, 0), (project, 1), (inward, 0), (project, 2), (fetch, 3), (inward, 1),
-        (outward, 0), (project, 3), (inward, 2), (outward, 1), (dispatch, 0), (inward, 3),
-        (join, 0), (outward, 2), (dispatch, 1), (join, 1), (outward, 3), (half, 0),
-        (dispatch, 2), (join, 2), (nearer, 0), (half, 1), (diagonal, 0), (farther, 0),
-        (dispatch, 3), (join, 3), (nearer, 1), (half, 2), (diagonal, 1), (farther, 1),
-        (nearer, 2), (half, 3), (diagonal, 2), (farther, 2), (nearer, 3),
+        (project, 0), (project, 1), (routes, 0), (inward, 0), (fetch, 3), (project, 2),
+        (inward, 1), (outward, 0), (project, 3), (inward, 2), (outward, 1), (dispatch, 0),
+        (inward, 3), (outward, 2), (dispatch, 1), (forward, 0), (outward, 3), (dispatch, 2),
+        (forward, 1), (dispatch, 3), (forward, 2), (nearer, 0), (diagonal, 0), (nearer, 1),
+        (farther, 0), (diagonal, 1), (forward, 3), (farther, 1), (nearer, 2), (diagonal, 2),
+        (farther, 2), (nearer, 3),
     ):
         work(n)
     mixed_out = call(

time: 166 us -> 146 us (0.88)
  waiting for transfers between devices: 58.1 us -> 42 us
  Pallas kernels: 47 us -> 45.2 us
    ppermute x46, waiting for transfers between devices: 58.1 us -> 42 us  [send(): return lax.ppermute(x, axis, pairs)]
    pallas_call x49 -> x45, Pallas kernels: 47 us -> 45.2 us  [call(): pl.pallas_call(body, out_shape=out_shape, in_specs=list(specs or [VM] * c...]
  transfers between devices with their start and end apart: 46 -> 46, of which waited for: 21 -> 22; matrix products, arithmetic and copies ran while one was open for 2% -> 2% of each run, Pallas kernels for 25% -> 28%
where the time goes in v8:
time: 146 us; the launch traced here: 145 us
  starting transfers between devices  51.8 us (35%)
  Pallas kernels  45.2 us (31%)
  waiting for transfers between devices  42 us (29%)
  local copies, waits for them, and re-layouts  2.39 us (2%)
  other arithmetic  2.39 us (2%)
  between operations  1.5 us (1%)
    ppermute x46, starting transfers between devices, send(): return lax.ppermute(x, axis, pairs)  51.8 us
    pallas_call x45, Pallas kernels, call(): pl.pallas_call(body, out_shape=out_shape, in_specs=list(specs or [VM] * c...  45.2 us
    ppermute x46, waiting for transfers between devices, send(): return lax.ppermute(x, axis, pairs)  42 us
  transfers between devices with their start and end apart: 46, of which 22 were waited for; matrix products, arithmetic and copies ran while one was open for 2% of the time, Pallas kernels for 28%

profile of v8, /device:TPU:0, one launch (start us, length us, event | category | flops | bytes accessed | tf_op | source)
XLA Modules:
  0.0 145.3 jit_solution(13090049822525545664)
XLA Ops:
  0.6 3.0 %collective-permute-start.4 = (bf16[1024,384]{1,0:T(8,128)(2,1)}, bf16[1024,384]{1,0:T(8,128)(2,1)S(1)}, u32[]{:S(2)}, u32[]{:S(2)}) collective-permute-start(bf16[1024,384]{1,0:T(8,128)(2,1)} %refs_5_.1), channel_id=1, source_target_pairs={{0,16},{4,20},{8,24},{12,28},{16,0},{20,4},{24,8},{28,12},{1,17},{... | collective-permute-start | bytes 2359304 | tf_op jit(solution)/shard_map/ppermute | solution.py:383
  3.7 0.7 multiply_bitcast_fusion
  4.4 0.8 add_select_fusion
  6.4 1.0 copy-done.5
  7.4 1.0 copy-done.6
  8.5 1.4 shard_map.113
  10.5 1.0 collective-permute-done.refs_2_
  11.6 1.6 %collective-permute-start.1 = (f32[4,128,128]{2,1,0:T(8,128)S(1)}, f32[4,128,128]{2,1,0:T(8,128)S(1)}, u32[]{:S(2)}, u32[]{:S(2)}) collective-permute-start(f32[4,128,128]{2,1,0:T(8,128)S(1)} %get-tuple-element.81.refs_2_), channel_id=1, source_target_pairs={{0,8},{4,12},{8,0},{12,4},{16,24},{20,28},{24,16},{28,20},{1,9},{5... | collective-permute-start | bytes 786440 | tf_op jit(solution)/shard_map/ppermute | solution.py:383
  13.1 1.6 %collective-permute-start.2 = (s32[8,128]{1,0:T(8,128)S(1)}, s32[8,128]{1,0:T(8,128)S(1)}, u32[]{:S(2)}, u32[]{:S(2)}) collective-permute-start(s32[8,128]{1,0:T(8,128)S(1)} %pad.4.refs_4_.refs_0_), channel_id=1, source_target_pairs={{0,1},{1,0},{2,3},{3,2},{4,5},{5,4},{6,7},{7,6},{8,9},{9,8},{10,11... | collective-permute-start | bytes 12296 | tf_op jit(solution)/shard_map/ppermute | solution.py:383
  14.7 1.1 shard_map.115
  15.8 0.9 collective-permute-done.2.refs_1_
  16.7 3.2 %collective-permute-done.1.refs_1_ = f32[4,128,128]{2,1,0:T(8,128)S(1)} collective-permute-done((f32[4,128,128]{2,1,0:T(8,128)S(1)}, f32[4,128,128]{2,1,0:T(8,128)S(1)}, u32[]{:S(2)}, u32[]{:S(2)}) %collective-permute-start.1) | collective-permute-done | bytes 262176 | tf_op jit(solution)/shard_map/ppermute | solution.py:383
  20.0 1.5 %collective-permute-done.4.refs_5_.refs_0_ = bf16[1024,384]{1,0:T(8,128)(2,1)S(1)} collective-permute-done((bf16[1024,384]{1,0:T(8,128)(2,1)}, bf16[1024,384]{1,0:T(8,128)(2,1)S(1)}, u32[]{:S(2)}, u32[]{:S(2)}) %collective-permute-start.4) | collective-permute-done | bytes 786464 | tf_op jit(solution)/shard_map/ppermute | solution.py:383
  21.5 3.7 %collective-permute-start.5 = (f32[4,128,128]{2,1,0:T(8,128)S(1)}, f32[4,128,128]{2,1,0:T(8,128)S(1)}, u32[]{:S(2)}, u32[]{:S(2)}) collective-permute-start(f32[4,128,128]{2,1,0:T(8,128)S(1)} %get-tuple-element.83), channel_id=1, source_target_pairs={{0,16},{4,20},{8,24},{12,28},{1,17},{5,21},{9,25},{13,29},{2,18},{... | collective-permute-start | bytes 786440 | tf_op jit(solution)/shard_map/ppermute | solution.py:383
  25.1 2.7 %collective-permute-start.6 = (s32[8,128]{1,0:T(8,128)S(1)}, s32[8,128]{1,0:T(8,128)S(1)}, u32[]{:S(2)}, u32[]{:S(2)}) collective-permute-start(s32[8,128]{1,0:T(8,128)S(1)} %shard_map.116.refs_3_.refs_1_), channel_id=1, source_target_pairs={{0,2},{1,3},{2,0},{3,1},{4,6},{5,7},{6,4},{7,5},{8,10},{9,11},{10,... | collective-permute-start | bytes 12296 | tf_op jit(solution)/shard_map/ppermute | solution.py:383
  27.9 1.8 %collective-permute-done.6.refs_2_ = s32[8,128]{1,0:T(8,128)S(1)} collective-permute-done((s32[8,128]{1,0:T(8,128)S(1)}, s32[8,128]{1,0:T(8,128)S(1)}, u32[]{:S(2)}, u32[]{:S(2)}) %collective-permute-start.6) | collective-permute-done | bytes 4128 | tf_op jit(solution)/shard_map/ppermute | solution.py:383
  30.5 1.5 %collective-permute-done.7.refs_5_ = f32[4,128,128]{2,1,0:T(8,128)S(1)} collective-permute-done((f32[4,128,128]{2,1,0:T(8,128)S(1)}, f32[4,128,128]{2,1,0:T(8,128)S(1)}, u32[]{:S(2)}, u32[]{:S(2)}) %collective-permute-start.7) | collective-permute-done | bytes 262176 | tf_op jit(solution)/shard_map/ppermute | solution.py:383
  32.0 1.2 shard_map.121.refs_1_.refs_6_
  33.5 1.5 %collective-permute-start.9 = (bf16[1024,384]{1,0:T(8,128)(2,1)S(1)}, bf16[1024,384]{1,0:T(8,128)(2,1)S(1)}, u32[]{:S(2)}, u32[]{:S(2)}) collective-permute-start(bf16[1024,384]{1,0:T(8,128)(2,1)S(1)} %shard_map.118.refs_3_), channel_id=1, source_target_pairs={{0,8},{4,12},{8,0},{12,4},{16,24},{20,28},{24,16},{28,20},{1,9},{5... | collective-permute-start | bytes 2359304 | tf_op jit(solution)/shard_map/ppermute | solution.py:383
  35.2 1.2 shard_map.122
  36.5 3.5 %collective-permute-start.10 = (bf16[512,384]{1,0:T(8,128)(2,1)S(1)}, bf16[512,384]{1,0:T(8,128)(2,1)S(1)}, u32[]{:S(2)}, u32[]{:S(2)}) collective-permute-start(bf16[512,384]{1,0:T(8,128)(2,1)S(1)} %get-tuple-element.87), channel_id=1, source_target_pairs={{0,1},{3,2},{4,5},{7,6},{8,9},{11,10},{12,13},{15,14},{16,17},{19,... | collective-permute-start | bytes 1179656 | tf_op jit(solution)/shard_map/ppermute | solution.py:383
  40.0 1.3 shard_map.123
  41.3 1.3 collective-permute-start.15
  42.7 1.2 collective-permute-done.11.refs_2_
  43.8 0.8 shard_map.124.refs_2_.refs_4_
  44.7 4.8 %collective-permute-done.10.refs_1_ = bf16[512,384]{1,0:T(8,128)(2,1)S(1)} collective-permute-done((bf16[512,384]{1,0:T(8,128)(2,1)S(1)}, bf16[512,384]{1,0:T(8,128)(2,1)S(1)}, u32[]{:S(2)}, u32[]{:S(2)}) %collective-permute-start.10) | collective-permute-done | bytes 393248 | tf_op jit(solution)/shard_map/ppermute | solution.py:383
  50.3 3.0 %collective-permute-done.9.refs_0_.refs_5_ = bf16[1024,384]{1,0:T(8,128)(2,1)S(1)} collective-permute-done((bf16[1024,384]{1,0:T(8,128)(2,1)S(1)}, bf16[1024,384]{1,0:T(8,128)(2,1)S(1)}, u32[]{:S(2)}, u32[]{:S(2)}) %collective-permute-start.9) | collective-permute-done | bytes 786464 | tf_op jit(solution)/shard_map/ppermute | solution.py:383
  53.4 1.6 %collective-permute-start.13 = (bf16[512,384]{1,0:T(8,128)(2,1)S(1)}, bf16[512,384]{1,0:T(8,128)(2,1)S(1)}, u32[]{:S(2)}, u32[]{:S(2)}) collective-permute-start(bf16[512,384]{1,0:T(8,128)(2,1)S(1)} %shard_map.127.refs_6_), channel_id=1, source_target_pairs={{0,8},{4,12},{8,0},{12,4},{16,24},{20,28},{24,16},{28,20},{1,9},{5... | collective-permute-start | bytes 1179656 | tf_op jit(solution)/shard_map/ppermute | solution.py:383
  54.9 2.0 %collective-permute-start.12 = (bf16[512,384]{1,0:T(8,128)(2,1)S(1)}, bf16[512,384]{1,0:T(8,128)(2,1)S(1)}, u32[]{:S(2)}, u32[]{:S(2)}) collective-permute-start(bf16[512,384]{1,0:T(8,128)(2,1)S(1)} %shard_map.126.refs_1_), channel_id=1, source_target_pairs={{0,16},{4,20},{8,24},{12,28},{16,0},{20,4},{24,8},{28,12},{1,17},{... | collective-permute-start | bytes 1179656 | tf_op jit(solution)/shard_map/ppermute | solution.py:383
  56.9 1.2 shard_map.128
  58.2 4.2 %collective-permute-start.19 = (bf16[512,384]{1,0:T(8,128)(2,1)S(1)}, bf16[512,384]{1,0:T(8,128)(2,1)S(1)}, u32[]{:S(2)}, u32[]{:S(2)}) collective-permute-start(bf16[512,384]{1,0:T(8,128)(2,1)S(1)} %get-tuple-element.97), channel_id=1, source_target_pairs={{0,1},{3,2},{4,5},{7,6},{8,9},{11,10},{12,13},{15,14},{16,17},{19,... | collective-permute-start | bytes 1179656 | tf_op jit(solution)/shard_map/ppermute | solution.py:383
  63.3 1.3 collective-permute-start.17
  64.6 0.8 collective-permute-done.12.refs_5_
  65.5 1.2 shard_map.131
  66.7 3.8 %collective-permute-start.16 = (bf16[512,384]{1,0:T(8,128)(2,1)S(1)}, bf16[512,384]{1,0:T(8,128)(2,1)S(1)}, u32[]{:S(2)}, u32[]{:S(2)}) collective-permute-start(bf16[512,384]{1,0:T(8,128)(2,1)S(1)} %get-tuple-element.95), channel_id=1, source_target_pairs={{0,1},{3,2},{4,5},{7,6},{8,9},{11,10},{12,13},{15,14},{16,17},{19,... | collective-permute-start | bytes 1179656 | tf_op jit(solution)/shard_map/ppermute | solution.py:383
  71.5 1.3 collective-permute-start.23
  72.8 1.5 %collective-permute-done.17.refs_1_ = bf16[512,384]{1,0:T(8,128)(2,1)S(1)} collective-permute-done((bf16[512,384]{1,0:T(8,128)(2,1)S(1)}, bf16[512,384]{1,0:T(8,128)(2,1)S(1)}, u32[]{:S(2)}, u32[]{:S(2)}) %collective-permute-start.17) | collective-permute-done | bytes 393248 | tf_op jit(solution)/shard_map/ppermute | solution.py:383
  74.2 0.9 shard_map.134
  75.9 1.5 %collective-permute-start.21 = (bf16[384,384]{1,0:T(8,128)(2,1)S(1)}, bf16[384,384]{1,0:T(8,128)(2,1)S(1)}, u32[]{:S(2)}, u32[]{:S(2)}) collective-permute-start(bf16[384,384]{1,0:T(8,128)(2,1)S(1)} %get-tuple-element.99.refs_2_.refs_1_.refs_3_), channel_id=1, source_target_pairs={{0,8},{4,12},{8,0},{12,4},{16,24},{20,28},{24,16},{28,20},{1,9},{5... | collective-permute-start | bytes 884744 | tf_op jit(solution)/shard_map/ppermute | solution.py:383
  78.5 1.3 collective-permute-start.26
  79.8 4.0 %collective-permute-done.23.refs_1_ = bf16[512,384]{1,0:T(8,128)(2,1)S(1)} collective-permute-done((bf16[512,384]{1,0:T(8,128)(2,1)S(1)}, bf16[512,384]{1,0:T(8,128)(2,1)S(1)}, u32[]{:S(2)}, u32[]{:S(2)}) %collective-permute-start.23) | collective-permute-done | bytes 393248 | tf_op jit(solution)/shard_map/ppermute | solution.py:383
  83.8 0.9 shard_map.137
  86.6 1.7 %collective-permute-start.25 = (bf16[512,384]{1,0:T(8,128)(2,1)S(1)}, bf16[512,384]{1,0:T(8,128)(2,1)S(1)}, u32[]{:S(2)}, u32[]{:S(2)}) collective-permute-start(bf16[512,384]{1,0:T(8,128)(2,1)S(1)} %shard_map.139.refs_5_.refs_2_), channel_id=1, source_target_pairs={{1,0},{2,3},{5,4},{6,7},{9,8},{10,11},{13,12},{14,15},{17,16},{18,... | collective-permute-start | bytes 1179656 | tf_op jit(solution)/shard_map/ppermute | solution.py:383
  88.4 4.0 %collective-permute-done.26.refs_1_ = bf16[512,384]{1,0:T(8,128)(2,1)S(1)} collective-permute-done((bf16[512,384]{1,0:T(8,128)(2,1)S(1)}, bf16[512,384]{1,0:T(8,128)(2,1)S(1)}, u32[]{:S(2)}, u32[]{:S(2)}) %collective-permute-start.26) | collective-permute-done | bytes 393248 | tf_op jit(solution)/shard_map/ppermute | solution.py:383
  92.4 0.9 shard_map.140
  95.1 5.4 %collective-permute-done.25.refs_1_ = bf16[512,384]{1,0:T(8,128)(2,1)S(1)} collective-permute-done((bf16[512,384]{1,0:T(8,128)(2,1)S(1)}, bf16[512,384]{1,0:T(8,128)(2,1)S(1)}, u32[]{:S(2)}, u32[]{:S(2)}) %collective-permute-start.25) | collective-permute-done | bytes 393248 | tf_op jit(solution)/shard_map/ppermute | solution.py:383
  100.6 1.2 collective-permute-start.33
  101.8 1.3 shard_map.142
  104.4 0.8 collective-permute-start.30
  105.9 3.5 %shard_map.144 = (f32[576,384]{1,0:T(8,128)S(1)}, f32[576,384]{1,0:T(8,128)S(1)}, f32[576,384]{1,0:T(8,128)S(1)}, f32[576,384]{1,0:T(8,128)S(1)}, f32[576,384]{1,0:T(8,128)S(1)}, /*index=5*/f32[576,384]{1,0:T(8,128)S(1)}) custom-call(s32[3]{0:T(128)S(1)} %pad_add_fusion.refs_0_, bf16[576,3072]{1,0:T(8,128)(2,1)S(1)} %bitcast.20, ...), custom_call_target="tpu_custom_call" | custom-call | flops 1 | bytes 1 | tf_op jit(solution)/shard_map/pallas_call | solution.py:45
  109.5 1.6 %collective-permute-start.32 = (bf16[384,384]{1,0:T(8,128)(2,1)S(1)}, bf16[384,384]{1,0:T(8,128)(2,1)S(1)}, u32[]{:S(2)}, u32[]{:S(2)}) collective-permute-start(bf16[384,384]{1,0:T(8,128)(2,1)S(1)} %get-tuple-element.109.refs_8_), channel_id=1, source_target_pairs={{0,16},{4,12},{8,24},{12,4},{16,0},{20,28},{24,8},{28,20},{1,17},{... | collective-permute-start | bytes 884744 | tf_op jit(solution)/shard_map/ppermute | solution.py:383
  111.3 3.6 %shard_map.146 = (f32[576,384]{1,0:T(8,128)S(1)}, f32[576,384]{1,0:T(8,128)S(1)}, f32[576,384]{1,0:T(8,128)S(1)}, f32[576,384]{1,0:T(8,128)S(1)}, f32[576,384]{1,0:T(8,128)S(1)}, /*index=5*/f32[576,384]{1,0:T(8,128)S(1)}) custom-call(s32[3]{0:T(128)S(1)} %pad_add_fusion.refs_0_, bf16[576,3072]{1,0:T(8,128)(2,1)S(1)} %bitcast.21, ...), custom_call_target="tpu_custom_call" | custom-call | flops 1 | bytes 1 | tf_op jit(solution)/shard_map/pallas_call | solution.py:45
  114.9 1.7 %shard_map.147 = (f32[576,384]{1,0:T(8,128)S(1)}, f32[576,384]{1,0:T(8,128)S(1)}) custom-call(s32[3]{0:T(128)S(1)} %pad_add_fusion.refs_0_, bf16[576,3072]{1,0:T(8,128)(2,1)S(1)} %bitcast.22, bf16[576,3072]{1,0:T(8,128)(2,1)S(1)} %bitcast.30, bf16[384,384]{1,0:T(8,128)(2,1)S(1)} %shard_map.145.refs_13_.refs_3_, ...), custom_call_target="tpu_custom_call" | custom-call | flops 1 | bytes 1 | tf_op jit(solution)/shard_map/pallas_call | solution.py:45
  116.6 2.3 %collective-permute-done.32.refs_0_ = bf16[384,384]{1,0:T(8,128)(2,1)S(1)} collective-permute-done((bf16[384,384]{1,0:T(8,128)(2,1)S(1)}, bf16[384,384]{1,0:T(8,128)(2,1)S(1)}, u32[]{:S(2)}, u32[]{:S(2)}) %collective-permute-start.32) | collective-permute-done | bytes 294944 | tf_op jit(solution)/shard_map/ppermute | solution.py:383
  120.2 1.2 collective-permute-start.42
  121.4 0.8 collective-permute-start.44
  122.9 1.7 %shard_map.150 = (f32[576,384]{1,0:T(8,128)S(1)}, f32[576,384]{1,0:T(8,128)S(1)}) custom-call(s32[3]{0:T(128)S(1)} %pad_add_fusion.refs_0_, bf16[576,3072]{1,0:T(8,128)(2,1)S(1)} %bitcast.23, bf16[576,3072]{1,0:T(8,128)(2,1)S(1)} %bitcast.31, bf16[384,384]{1,0:T(8,128)(2,1)S(1)} %shard_map.148.refs_4_.refs_3_, ...), custom_call_target="tpu_custom_call" | custom-call | flops 1 | bytes 1 | tf_op jit(solution)/shard_map/pallas_call | solution.py:45
  124.6 3.6 %shard_map.151 = (f32[576,384]{1,0:T(8,128)S(1)}, f32[576,384]{1,0:T(8,128)S(1)}, f32[576,384]{1,0:T(8,128)S(1)}, f32[576,384]{1,0:T(8,128)S(1)}, f32[576,384]{1,0:T(8,128)S(1)}, /*index=5*/f32[576,384]{1,0:T(8,128)S(1)}) custom-call(s32[3]{0:T(128)S(1)} %pad_add_fusion.refs_0_, bf16[576,3072]{1,0:T(8,128)(2,1)S(1)} %bitcast.24, ...), custom_call_target="tpu_custom_call" | custom-call | flops 1 | bytes 1 | tf_op jit(solution)/shard_map/pallas_call | solution.py:45
  128.5 1.4 collective-permute-done.43.refs_4_
  129.9 1.7 %shard_map.153 = (f32[576,384]{1,0:T(8,128)S(1)}, f32[576,384]{1,0:T(8,128)S(1)}) custom-call(s32[3]{0:T(128)S(1)} %pad_add_fusion.refs_0_, bf16[576,3072]{1,0:T(8,128)(2,1)S(1)} %bitcast.25, bf16[576,3072]{1,0:T(8,128)(2,1)S(1)} %bitcast.33, bf16[384,384]{1,0:T(8,128)(2,1)S(1)} %shard_map.152.refs_3_.refs_7_, ...), custom_call_target="tpu_custom_call" | custom-call | flops 1 | bytes 1 | tf_op jit(solution)/shard_map/pallas_call | solution.py:45
  131.6 6.4 %shard_map.154 = (bf16[576,1536]{1,0:T(8,128)(2,1)}, f32[8,128]{1,0:T(8,128)S(1)}) custom-call(s32[3]{0:T(128)S(1)} %pad_add_fusion.refs_0_, bf16[576,3072]{1,0:T(8,128)(2,1)S(1)} %bitcast.26, bf16[576,3072]{1,0:T(8,128)(2,1)S(1)} %bitcast.34, bf16[384,512]{1,0:T(8,128)(2,1)S(1)} %get-tuple-element.112.refs_4_.refs_1_.refs_3_, ...), custom_call_target="tpu_custom_call" | custom-call | flops 1 | bytes 1 | tf_op jit(solution)/shard_map/pallas_call | solution.py:45
  138.7 1.5 %collective-permute-done.29.refs_1_ = bf16[64,1536]{1,0:T(8,128)(2,1)S(1)} collective-permute-done((bf16[64,1536]{1,0:T(8,128)(2,1)S(1)}, bf16[64,1536]{1,0:T(8,128)(2,1)S(1)}, u32[]{:S(2)}, u32[]{:S(2)}) %collective-permute-start.29) | collective-permute-done | bytes 196640 | tf_op jit(solution)/shard_map/ppermute | solution.py:383
  140.2 1.3 shard_map.155
  141.5 3.6 %shard_map.157 = (bf16[576,1536]{1,0:T(8,128)(2,1)}, f32[8,128]{1,0:T(8,128)}) custom-call(s32[3]{0:T(128)S(1)} %pad_add_fusion.refs_0_, bf16[576,3072]{1,0:T(8,128)(2,1)S(1)} %bitcast.27, bf16[576,3072]{1,0:T(8,128)(2,1)S(1)} %bitcast.35, bf16[384,512]{1,0:T(8,128)(2,1)S(1)} %shard_map.156.refs_3_.refs_8_, ...), custom_call_target="tpu_custom_call", output_to_operand_aliasing={{0}: (7, {})} | custom-call | flops 1 | bytes 1 | tf_op jit(solution)/shard_map/pallas_call | solution.py:45
  (103 shorter events, 16.3 us)
Async XLA Ops:
  0.6 14.1 %copy-start.4 = (bf16[256,1024]{1,0:T(8,128)(2,1)S(1)}, bf16[256,1024]{1,0:T(8,128)(2,1)}, u32[]{:S(2)}) copy-start(bf16[256,1024]{1,0:T(8,128)(2,1)} %refs_1_.1) | copy-start | bytes 1572868
  0.6 20.8 %collective-permute-start.4 = (bf16[1024,384]{1,0:T(8,128)(2,1)}, bf16[1024,384]{1,0:T(8,128)(2,1)S(1)}, u32[]{:S(2)}, u32[]{:S(2)}) collective-permute-start(bf16[1024,384]{1,0:T(8,128)(2,1)} %refs_5_.1), channel_id=1, source_target_pairs={{0,16},{4,20},{8,24},{12,28},{16,0},{20,4},{24,8},{28,12},{1,17},{... | collective-permute-start | bytes 2359304 | tf_op jit(solution)/shard_map/ppermute | solution.py:383
  6.4 1.0 copy-start.5
  7.4 1.0 copy-start.6
  9.9 1.6 %collective-permute-start = (f32[4,128,128]{2,1,0:T(8,128)S(1)}, f32[4,128,128]{2,1,0:T(8,128)S(1)}, u32[]{:S(2)}, u32[]{:S(2)}) collective-permute-start(f32[4,128,128]{2,1,0:T(8,128)S(1)} %get-tuple-element.77), channel_id=1, source_target_pairs={{0,4},{4,0},{8,12},{12,8},{16,20},{20,16},{24,28},{28,24},{1,5},{5... | collective-permute-start | bytes 786440 | tf_op jit(solution)/shard_map/ppermute | solution.py:383
  10.0 6.8 %collective-permute-start.3 = (bf16[64,3072]{1,0:T(8,128)(2,1)}, bf16[64,3072]{1,0:T(8,128)(2,1)S(1)}, u32[]{:S(2)}, u32[]{:S(2)}) collective-permute-start(bf16[64,3072]{1,0:T(8,128)(2,1)} %refs_3_.9), channel_id=1, source_target_pairs={{0,4},{4,0},{8,12},{12,8},{16,20},{20,16},{24,28},{28,24},{1,5},{5... | collective-permute-start | bytes 1179656 | tf_op jit(solution)/shard_map/ppermute | solution.py:383
  11.6 8.4 %collective-permute-start.1 = (f32[4,128,128]{2,1,0:T(8,128)S(1)}, f32[4,128,128]{2,1,0:T(8,128)S(1)}, u32[]{:S(2)}, u32[]{:S(2)}) collective-permute-start(f32[4,128,128]{2,1,0:T(8,128)S(1)} %get-tuple-element.81.refs_2_), channel_id=1, source_target_pairs={{0,8},{4,12},{8,0},{12,4},{16,24},{20,28},{24,16},{28,20},{1,9},{5... | collective-permute-start | bytes 786440 | tf_op jit(solution)/shard_map/ppermute | solution.py:383
  13.1 3.6 %collective-permute-start.2 = (s32[8,128]{1,0:T(8,128)S(1)}, s32[8,128]{1,0:T(8,128)S(1)}, u32[]{:S(2)}, u32[]{:S(2)}) collective-permute-start(s32[8,128]{1,0:T(8,128)S(1)} %pad.4.refs_4_.refs_0_), channel_id=1, source_target_pairs={{0,1},{1,0},{2,3},{3,2},{4,5},{5,4},{6,7},{7,6},{8,9},{9,8},{10,11... | collective-permute-start | bytes 12296 | tf_op jit(solution)/shard_map/ppermute | solution.py:383
  15.8 12.0 %copy-start.3 = (bf16[1024,384]{1,0:T(8,128)(2,1)S(1)}, bf16[1024,384]{1,0:T(8,128)(2,1)}, u32[]{:S(2)}) copy-start(bf16[1024,384]{1,0:T(8,128)(2,1)} %refs_5_.1) | copy-start | bytes 2359300
  21.5 8.8 %collective-permute-start.5 = (f32[4,128,128]{2,1,0:T(8,128)S(1)}, f32[4,128,128]{2,1,0:T(8,128)S(1)}, u32[]{:S(2)}, u32[]{:S(2)}) collective-permute-start(f32[4,128,128]{2,1,0:T(8,128)S(1)} %get-tuple-element.83), channel_id=1, source_target_pairs={{0,16},{4,20},{8,24},{12,28},{1,17},{5,21},{9,25},{13,29},{2,18},{... | collective-permute-start | bytes 786440 | tf_op jit(solution)/shard_map/ppermute | solution.py:383
  25.1 4.6 %collective-permute-start.6 = (s32[8,128]{1,0:T(8,128)S(1)}, s32[8,128]{1,0:T(8,128)S(1)}, u32[]{:S(2)}, u32[]{:S(2)}) collective-permute-start(s32[8,128]{1,0:T(8,128)S(1)} %shard_map.116.refs_3_.refs_1_), channel_id=1, source_target_pairs={{0,2},{1,3},{2,0},{3,1},{4,6},{5,7},{6,4},{7,5},{8,10},{9,11},{10,... | collective-permute-start | bytes 12296 | tf_op jit(solution)/shard_map/ppermute | solution.py:383
  30.3 5.0 %copy-start.2 = (bf16[64,3072]{1,0:T(8,128)(2,1)S(1)}, bf16[64,3072]{1,0:T(8,128)(2,1)}, u32[]{:S(2)}) copy-start(bf16[64,3072]{1,0:T(8,128)(2,1)} %refs_3_.9) | copy-start | bytes 1179652
  30.4 1.6 %collective-permute-start.7 = (f32[4,128,128]{2,1,0:T(8,128)S(1)}, f32[4,128,128]{2,1,0:T(8,128)S(1)}, u32[]{:S(2)}, u32[]{:S(2)}) collective-permute-start(f32[4,128,128]{2,1,0:T(8,128)S(1)} %get-tuple-element.85), channel_id=1, source_target_pairs={{0,4},{4,0},{8,12},{12,8},{16,20},{20,16},{24,28},{28,24},{1,5},{5... | collective-permute-start | bytes 786440 | tf_op jit(solution)/shard_map/ppermute | solution.py:383
  33.3 2.0 %collective-permute-start.8 = (bf16[256,1024]{1,0:T(8,128)(2,1)S(1)}, bf16[256,1024]{1,0:T(8,128)(2,1)S(1)}, u32[]{:S(2)}, u32[]{:S(2)}) collective-permute-start(bf16[256,1024]{1,0:T(8,128)(2,1)S(1)} %shard_map.121.refs_1_.refs_6_), channel_id=1, source_target_pairs={{0,4},{4,0},{8,12},{12,8},{16,20},{20,16},{24,28},{28,24},{1,5},{5... | collective-permute-start | bytes 1572872 | tf_op jit(solution)/shard_map/ppermute | solution.py:383
  33.5 19.8 %collective-permute-start.9 = (bf16[1024,384]{1,0:T(8,128)(2,1)S(1)}, bf16[1024,384]{1,0:T(8,128)(2,1)S(1)}, u32[]{:S(2)}, u32[]{:S(2)}) collective-permute-start(bf16[1024,384]{1,0:T(8,128)(2,1)S(1)} %shard_map.118.refs_3_), channel_id=1, source_target_pairs={{0,8},{4,12},{8,0},{12,4},{16,24},{20,28},{24,16},{28,20},{1,9},{5... | collective-permute-start | bytes 2359304 | tf_op jit(solution)/shard_map/ppermute | solution.py:383
  36.5 13.0 %collective-permute-start.10 = (bf16[512,384]{1,0:T(8,128)(2,1)S(1)}, bf16[512,384]{1,0:T(8,128)(2,1)S(1)}, u32[]{:S(2)}, u32[]{:S(2)}) collective-permute-start(bf16[512,384]{1,0:T(8,128)(2,1)S(1)} %get-tuple-element.87), channel_id=1, source_target_pairs={{0,1},{3,2},{4,5},{7,6},{8,9},{11,10},{12,13},{15,14},{16,17},{19,... | collective-permute-start | bytes 1179656 | tf_op jit(solution)/shard_map/ppermute | solution.py:383
  41.3 21.1 %collective-permute-start.15 = (bf16[512,384]{1,0:T(8,128)(2,1)S(1)}, bf16[512,384]{1,0:T(8,128)(2,1)S(1)}, u32[]{:S(2)}, u32[]{:S(2)}) collective-permute-start(bf16[512,384]{1,0:T(8,128)(2,1)S(1)} %get-tuple-element.91), channel_id=1, source_target_pairs={{0,1},{3,2},{4,5},{7,6},{8,9},{11,10},{12,13},{15,14},{16,17},{19,... | collective-permute-start | bytes 1179656 | tf_op jit(solution)/shard_map/ppermute | solution.py:383
  42.6 1.2 collective-permute-start.11
  49.6 13.7 %collective-permute-start.14 = (bf16[512,384]{1,0:T(8,128)(2,1)S(1)}, bf16[512,384]{1,0:T(8,128)(2,1)S(1)}, u32[]{:S(2)}, u32[]{:S(2)}) collective-permute-start(bf16[512,384]{1,0:T(8,128)(2,1)S(1)} %get-tuple-element.90), channel_id=1, source_target_pairs={{1,2},{2,1},{5,6},{6,5},{9,10},{10,9},{13,14},{14,13},{17,18},{18,... | collective-permute-start | bytes 1179656 | tf_op jit(solution)/shard_map/ppermute | solution.py:383
  53.4 11.3 %collective-permute-start.13 = (bf16[512,384]{1,0:T(8,128)(2,1)S(1)}, bf16[512,384]{1,0:T(8,128)(2,1)S(1)}, u32[]{:S(2)}, u32[]{:S(2)}) collective-permute-start(bf16[512,384]{1,0:T(8,128)(2,1)S(1)} %shard_map.127.refs_6_), channel_id=1, source_target_pairs={{0,8},{4,12},{8,0},{12,4},{16,24},{20,28},{24,16},{28,20},{1,9},{5... | collective-permute-start | bytes 1179656 | tf_op jit(solution)/shard_map/ppermute | solution.py:383
  54.9 10.5 %collective-permute-start.12 = (bf16[512,384]{1,0:T(8,128)(2,1)S(1)}, bf16[512,384]{1,0:T(8,128)(2,1)S(1)}, u32[]{:S(2)}, u32[]{:S(2)}) collective-permute-start(bf16[512,384]{1,0:T(8,128)(2,1)S(1)} %shard_map.126.refs_1_), channel_id=1, source_target_pairs={{0,16},{4,20},{8,24},{12,28},{16,0},{20,4},{24,8},{28,12},{1,17},{... | collective-permute-start | bytes 1179656 | tf_op jit(solution)/shard_map/ppermute | solution.py:383
  58.2 12.4 %collective-permute-start.19 = (bf16[512,384]{1,0:T(8,128)(2,1)S(1)}, bf16[512,384]{1,0:T(8,128)(2,1)S(1)}, u32[]{:S(2)}, u32[]{:S(2)}) collective-permute-start(bf16[512,384]{1,0:T(8,128)(2,1)S(1)} %get-tuple-element.97), channel_id=1, source_target_pairs={{0,1},{3,2},{4,5},{7,6},{8,9},{11,10},{12,13},{15,14},{16,17},{19,... | collective-permute-start | bytes 1179656 | tf_op jit(solution)/shard_map/ppermute | solution.py:383
  62.6 8.8 %collective-permute-start.18 = (bf16[512,384]{1,0:T(8,128)(2,1)S(1)}, bf16[512,384]{1,0:T(8,128)(2,1)S(1)}, u32[]{:S(2)}, u32[]{:S(2)}) collective-permute-start(bf16[512,384]{1,0:T(8,128)(2,1)S(1)} %get-tuple-element.96), channel_id=1, source_target_pairs={{1,2},{2,1},{5,6},{6,5},{9,10},{10,9},{13,14},{14,13},{17,18},{18,... | collective-permute-start | bytes 1179656 | tf_op jit(solution)/shard_map/ppermute | solution.py:383
  63.3 10.9 %collective-permute-start.17 = (bf16[512,384]{1,0:T(8,128)(2,1)S(1)}, bf16[512,384]{1,0:T(8,128)(2,1)S(1)}, u32[]{:S(2)}, u32[]{:S(2)}) collective-permute-start(bf16[512,384]{1,0:T(8,128)(2,1)S(1)} %shard_map.130.refs_7_.refs_2_), channel_id=1, source_target_pairs={{1,0},{2,3},{5,4},{6,7},{9,8},{10,11},{13,12},{14,15},{17,16},{18,... | collective-permute-start | bytes 1179656 | tf_op jit(solution)/shard_map/ppermute | solution.py:383
  66.7 10.9 %collective-permute-start.16 = (bf16[512,384]{1,0:T(8,128)(2,1)S(1)}, bf16[512,384]{1,0:T(8,128)(2,1)S(1)}, u32[]{:S(2)}, u32[]{:S(2)}) collective-permute-start(bf16[512,384]{1,0:T(8,128)(2,1)S(1)} %get-tuple-element.95), channel_id=1, source_target_pairs={{0,1},{3,2},{4,5},{7,6},{8,9},{11,10},{12,13},{15,14},{16,17},{19,... | collective-permute-start | bytes 1179656 | tf_op jit(solution)/shard_map/ppermute | solution.py:383
  70.5 3.7 %copy-start.7 = (f32[3072]{0:T(1024)S(1)}, f32[3072]{0:T(1024)}, u32[]{:S(2)}) copy-start(f32[3072]{0:T(1024)} %param.16) | copy-start | bytes 36868
  70.7 7.8 %collective-permute-start.24 = (bf16[512,384]{1,0:T(8,128)(2,1)S(1)}, bf16[512,384]{1,0:T(8,128)(2,1)S(1)}, u32[]{:S(2)}, u32[]{:S(2)}) collective-permute-start(bf16[512,384]{1,0:T(8,128)(2,1)S(1)} %get-tuple-element.102), channel_id=1, source_target_pairs={{1,2},{2,1},{5,6},{6,5},{9,10},{10,9},{13,14},{14,13},{17,18},{18,... | collective-permute-start | bytes 1179656 | tf_op jit(solution)/shard_map/ppermute | solution.py:383
  71.5 12.3 %collective-permute-start.23 = (bf16[512,384]{1,0:T(8,128)(2,1)S(1)}, bf16[512,384]{1,0:T(8,128)(2,1)S(1)}, u32[]{:S(2)}, u32[]{:S(2)}) collective-permute-start(bf16[512,384]{1,0:T(8,128)(2,1)S(1)} %shard_map.133.refs_5_.refs_2_), channel_id=1, source_target_pairs={{1,0},{2,3},{5,4},{6,7},{9,8},{10,11},{13,12},{14,15},{17,16},{18,... | collective-permute-start | bytes 1179656 | tf_op jit(solution)/shard_map/ppermute | solution.py:383
  75.2 10.1 %collective-permute-start.22 = (bf16[384,384]{1,0:T(8,128)(2,1)S(1)}, bf16[384,384]{1,0:T(8,128)(2,1)S(1)}, u32[]{:S(2)}, u32[]{:S(2)}) collective-permute-start(bf16[384,384]{1,0:T(8,128)(2,1)S(1)} %get-tuple-element.99.refs_2_.refs_1_.refs_3_), channel_id=1, source_target_pairs={{0,16},{4,20},{8,24},{12,28},{16,0},{20,4},{24,8},{28,12},{1,17},{... | collective-permute-start | bytes 884744 | tf_op jit(solution)/shard_map/ppermute | solution.py:383
  75.9 9.9 %collective-permute-start.21 = (bf16[384,384]{1,0:T(8,128)(2,1)S(1)}, bf16[384,384]{1,0:T(8,128)(2,1)S(1)}, u32[]{:S(2)}, u32[]{:S(2)}) collective-permute-start(bf16[384,384]{1,0:T(8,128)(2,1)S(1)} %get-tuple-element.99.refs_2_.refs_1_.refs_3_), channel_id=1, source_target_pairs={{0,8},{4,12},{8,0},{12,4},{16,24},{20,28},{24,16},{28,20},{1,9},{5... | collective-permute-start | bytes 884744 | tf_op jit(solution)/shard_map/ppermute | solution.py:383
  77.7 8.8 %collective-permute-start.20 = (bf16[512,384]{1,0:T(8,128)(2,1)S(1)}, bf16[512,384]{1,0:T(8,128)(2,1)S(1)}, u32[]{:S(2)}, u32[]{:S(2)}) collective-permute-start(bf16[512,384]{1,0:T(8,128)(2,1)S(1)} %get-tuple-element.101), channel_id=1, source_target_pairs={{1,2},{2,1},{5,6},{6,5},{9,10},{10,9},{13,14},{14,13},{17,18},{18,... | collective-permute-start | bytes 1179656 | tf_op jit(solution)/shard_map/ppermute | solution.py:383
  78.5 13.9 %collective-permute-start.26 = (bf16[512,384]{1,0:T(8,128)(2,1)S(1)}, bf16[512,384]{1,0:T(8,128)(2,1)S(1)}, u32[]{:S(2)}, u32[]{:S(2)}) collective-permute-start(bf16[512,384]{1,0:T(8,128)(2,1)S(1)} %shard_map.136.refs_5_.refs_2_), channel_id=1, source_target_pairs={{1,0},{2,3},{5,4},{6,7},{9,8},{10,11},{13,12},{14,15},{17,16},{18,... | collective-permute-start | bytes 1179656 | tf_op jit(solution)/shard_map/ppermute | solution.py:383
  84.7 8.6 %collective-permute-start.28 = (bf16[384,384]{1,0:T(8,128)(2,1)S(1)}, bf16[384,384]{1,0:T(8,128)(2,1)S(1)}, u32[]{:S(2)}, u32[]{:S(2)}) collective-permute-start(bf16[384,384]{1,0:T(8,128)(2,1)S(1)} %get-tuple-element.103.refs_4_.refs_1_.refs_3_), channel_id=1, source_target_pairs={{0,16},{4,20},{8,24},{12,28},{16,0},{20,4},{24,8},{28,12},{1,17},{... | collective-permute-start | bytes 884744 | tf_op jit(solution)/shard_map/ppermute | solution.py:383
  85.3 8.1 %collective-permute-start.27 = (bf16[384,384]{1,0:T(8,128)(2,1)S(1)}, bf16[384,384]{1,0:T(8,128)(2,1)S(1)}, u32[]{:S(2)}, u32[]{:S(2)}) collective-permute-start(bf16[384,384]{1,0:T(8,128)(2,1)S(1)} %get-tuple-element.103.refs_4_.refs_1_.refs_3_), channel_id=1, source_target_pairs={{0,8},{4,12},{8,0},{12,4},{16,24},{20,28},{24,16},{28,20},{1,9},{5... | collective-permute-start | bytes 884744 | tf_op jit(solution)/shard_map/ppermute | solution.py:383
  86.4 19.4 %collective-permute-start.34 = (bf16[384,1152]{1,0:T(8,128)(2,1)S(1)}, bf16[384,1152]{1,0:T(8,128)(2,1)S(1)}, u32[]{:S(2)}, u32[]{:S(2)}) collective-permute-start(bf16[384,1152]{1,0:T(8,128)(2,1)S(1)} %get-tuple-element.113), channel_id=1, source_target_pairs={{0,4},{4,0},{8,12},{12,8},{16,20},{20,16},{24,28},{28,24},{1,5},{5... | collective-permute-start | bytes 2654216 | tf_op jit(solution)/shard_map/ppermute | solution.py:383
  86.5 19.3 %copy-start.1 = (bf16[1,576,3072]{2,1,0:T(8,128)(2,1)S(1)}, bf16[1,576,3072]{2,1,0:T(8,128)(2,1)}, u32[]{:S(2)}) copy-start(bf16[1,576,3072]{2,1,0:T(8,128)(2,1)} %param.19) | copy-start | bytes 10616836
  86.6 14.0 %collective-permute-start.25 = (bf16[512,384]{1,0:T(8,128)(2,1)S(1)}, bf16[512,384]{1,0:T(8,128)(2,1)S(1)}, u32[]{:S(2)}, u32[]{:S(2)}) collective-permute-start(bf16[512,384]{1,0:T(8,128)(2,1)S(1)} %shard_map.139.refs_5_.refs_2_), channel_id=1, source_target_pairs={{1,0},{2,3},{5,4},{6,7},{9,8},{10,11},{13,12},{14,15},{17,16},{18,... | collective-permute-start | bytes 1179656 | tf_op jit(solution)/shard_map/ppermute | solution.py:383
  94.0 17.1 %collective-permute-start.38 = (bf16[384,1152]{1,0:T(8,128)(2,1)S(1)}, bf16[384,1152]{1,0:T(8,128)(2,1)S(1)}, u32[]{:S(2)}, u32[]{:S(2)}) collective-permute-start(bf16[384,1152]{1,0:T(8,128)(2,1)S(1)} %get-tuple-element.116), channel_id=1, source_target_pairs={{0,4},{4,0},{8,12},{12,8},{16,20},{20,16},{24,28},{28,24},{1,5},{5... | collective-permute-start | bytes 2654216 | tf_op jit(solution)/shard_map/ppermute | solution.py:383
  94.1 9.4 %collective-permute-start.36 = (bf16[384,384]{1,0:T(8,128)(2,1)S(1)}, bf16[384,384]{1,0:T(8,128)(2,1)S(1)}, u32[]{:S(2)}, u32[]{:S(2)}) collective-permute-start(bf16[384,384]{1,0:T(8,128)(2,1)S(1)} %get-tuple-element.108.refs_4_.refs_1_.refs_3_), channel_id=1, source_target_pairs={{0,16},{4,20},{8,24},{12,28},{16,0},{20,4},{24,8},{28,12},{1,17},{... | collective-permute-start | bytes 884744 | tf_op jit(solution)/shard_map/ppermute | solution.py:383
  94.5 9.9 %collective-permute-start.35 = (bf16[384,384]{1,0:T(8,128)(2,1)S(1)}, bf16[384,384]{1,0:T(8,128)(2,1)S(1)}, u32[]{:S(2)}, u32[]{:S(2)}) collective-permute-start(bf16[384,384]{1,0:T(8,128)(2,1)S(1)} %get-tuple-element.108.refs_4_.refs_1_.refs_3_), channel_id=1, source_target_pairs={{0,8},{4,12},{8,0},{12,4},{16,24},{20,28},{24,16},{28,20},{1,9},{5... | collective-permute-start | bytes 884744 | tf_op jit(solution)/shard_map/ppermute | solution.py:383
  100.6 8.8 %collective-permute-start.33 = (bf16[384,384]{1,0:T(8,128)(2,1)S(1)}, bf16[384,384]{1,0:T(8,128)(2,1)S(1)}, u32[]{:S(2)}, u32[]{:S(2)}) collective-permute-start(bf16[384,384]{1,0:T(8,128)(2,1)S(1)} %get-tuple-element.104.refs_2_), channel_id=1, source_target_pairs={{0,16},{4,12},{8,24},{12,4},{16,0},{20,28},{24,8},{28,20},{1,17},{... | collective-permute-start | bytes 884744 | tf_op jit(solution)/shard_map/ppermute | solution.py:383
  101.8 4.0 %copy-start = (bf16[1,576,3072]{2,1,0:T(8,128)(2,1)S(1)}, bf16[1,576,3072]{2,1,0:T(8,128)(2,1)}, u32[]{:S(2)}) copy-start(bf16[1,576,3072]{2,1,0:T(8,128)(2,1)} %param.18) | copy-start | bytes 10616836
  103.5 15.4 %collective-permute-start.31 = (bf16[384,512]{1,0:T(8,128)(2,1)S(1)}, bf16[384,512]{1,0:T(8,128)(2,1)S(1)}, u32[]{:S(2)}, u32[]{:S(2)}) collective-permute-start(bf16[384,512]{1,0:T(8,128)(2,1)S(1)} %get-tuple-element.112.refs_4_.refs_1_.refs_3_), channel_id=1, source_target_pairs={{0,16},{4,20},{8,24},{12,28},{16,0},{20,4},{24,8},{28,12},{1,17},{... | collective-permute-start | bytes 1179656 | tf_op jit(solution)/shard_map/ppermute | solution.py:383
  104.4 14.6 %collective-permute-start.30 = (bf16[384,512]{1,0:T(8,128)(2,1)S(1)}, bf16[384,512]{1,0:T(8,128)(2,1)S(1)}, u32[]{:S(2)}, u32[]{:S(2)}) collective-permute-start(bf16[384,512]{1,0:T(8,128)(2,1)S(1)} %get-tuple-element.112.refs_4_.refs_1_.refs_3_), channel_id=1, source_target_pairs={{0,8},{4,12},{8,0},{12,4},{16,24},{20,28},{24,16},{28,20},{1,9},{5... | collective-permute-start | bytes 1179656 | tf_op jit(solution)/shard_map/ppermute | solution.py:383
  109.4 5.5 %collective-permute-start.37 = (bf16[384,384]{1,0:T(8,128)(2,1)S(1)}, bf16[384,384]{1,0:T(8,128)(2,1)S(1)}, u32[]{:S(2)}, u32[]{:S(2)}) collective-permute-start(bf16[384,384]{1,0:T(8,128)(2,1)S(1)} %shard_map.145.refs_13_.refs_3_), channel_id=1, source_target_pairs={{0,4},{4,0},{8,12},{12,8},{16,20},{20,16},{24,28},{28,24},{1,5},{5... | collective-permute-start | bytes 884744 | tf_op jit(solution)/shard_map/ppermute | solution.py:383
  109.5 9.4 %collective-permute-start.32 = (bf16[384,384]{1,0:T(8,128)(2,1)S(1)}, bf16[384,384]{1,0:T(8,128)(2,1)S(1)}, u32[]{:S(2)}, u32[]{:S(2)}) collective-permute-start(bf16[384,384]{1,0:T(8,128)(2,1)S(1)} %get-tuple-element.109.refs_8_), channel_id=1, source_target_pairs={{0,16},{4,12},{8,24},{12,4},{16,0},{20,28},{24,8},{28,20},{1,17},{... | collective-permute-start | bytes 884744 | tf_op jit(solution)/shard_map/ppermute | solution.py:383
  111.1 13.5 %collective-permute-start.40 = (bf16[384,1152]{1,0:T(8,128)(2,1)S(1)}, bf16[384,1152]{1,0:T(8,128)(2,1)S(1)}, u32[]{:S(2)}, u32[]{:S(2)}) collective-permute-start(bf16[384,1152]{1,0:T(8,128)(2,1)S(1)} %get-tuple-element.125), channel_id=1, source_target_pairs={{0,4},{4,0},{8,12},{12,8},{16,20},{20,16},{24,28},{28,24},{1,5},{5... | collective-permute-start | bytes 2654216 | tf_op jit(solution)/shard_map/ppermute | solution.py:383
  119.6 12.0 %collective-permute-start.39 = (bf16[384,1536]{1,0:T(8,128)(2,1)S(1)}, bf16[384,1536]{1,0:T(8,128)(2,1)S(1)}, u32[]{:S(2)}, u32[]{:S(2)}) collective-permute-start(bf16[384,1536]{1,0:T(8,128)(2,1)S(1)} %get-tuple-element.124), channel_id=1, source_target_pairs={{0,4},{4,0},{8,12},{12,8},{16,20},{20,16},{24,28},{28,24},{1,5},{5... | collective-permute-start | bytes 3538952 | tf_op jit(solution)/shard_map/ppermute | solution.py:383
  119.7 3.3 %collective-permute-start.41 = (bf16[384,384]{1,0:T(8,128)(2,1)S(1)}, bf16[384,384]{1,0:T(8,128)(2,1)S(1)}, u32[]{:S(2)}, u32[]{:S(2)}) collective-permute-start(bf16[384,384]{1,0:T(8,128)(2,1)S(1)} %shard_map.148.refs_4_.refs_3_), channel_id=1, source_target_pairs={{0,4},{4,0},{8,12},{12,8},{16,20},{20,16},{24,28},{28,24},{1,5},{5... | collective-permute-start | bytes 884744 | tf_op jit(solution)/shard_map/ppermute | solution.py:383
  120.2 8.1 %collective-permute-start.42 = (bf16[384,384]{1,0:T(8,128)(2,1)S(1)}, bf16[384,384]{1,0:T(8,128)(2,1)S(1)}, u32[]{:S(2)}, u32[]{:S(2)}) collective-permute-start(bf16[384,384]{1,0:T(8,128)(2,1)S(1)} %get-tuple-element.114.refs_7_), channel_id=1, source_target_pairs={{0,16},{4,12},{8,24},{12,4},{16,0},{20,28},{24,8},{28,20},{1,17},{... | collective-permute-start | bytes 884744 | tf_op jit(solution)/shard_map/ppermute | solution.py:383
  121.4 16.7 %collective-permute-start.44 = (bf16[384,512]{1,0:T(8,128)(2,1)S(1)}, bf16[384,512]{1,0:T(8,128)(2,1)S(1)}, u32[]{:S(2)}, u32[]{:S(2)}) collective-permute-start(bf16[384,512]{1,0:T(8,128)(2,1)S(1)} %get-tuple-element.132.refs_7_), channel_id=1, source_target_pairs={{0,16},{4,12},{8,24},{12,4},{16,0},{20,28},{24,8},{28,20},{1,17},{... | collective-permute-start | bytes 1179656 | tf_op jit(solution)/shard_map/ppermute | solution.py:383
  128.3 1.6 %collective-permute-start.43 = (bf16[384,384]{1,0:T(8,128)(2,1)S(1)}, bf16[384,384]{1,0:T(8,128)(2,1)S(1)}, u32[]{:S(2)}, u32[]{:S(2)}) collective-permute-start(bf16[384,384]{1,0:T(8,128)(2,1)S(1)} %shard_map.152.refs_3_.refs_7_), channel_id=1, source_target_pairs={{0,4},{4,0},{8,12},{12,8},{16,20},{20,16},{24,28},{28,24},{1,5},{5... | collective-permute-start | bytes 884744 | tf_op jit(solution)/shard_map/ppermute | solution.py:383
  138.1 3.4 %collective-permute-start.45 = (bf16[384,512]{1,0:T(8,128)(2,1)S(1)}, bf16[384,512]{1,0:T(8,128)(2,1)S(1)}, u32[]{:S(2)}, u32[]{:S(2)}) collective-permute-start(bf16[384,512]{1,0:T(8,128)(2,1)S(1)} %shard_map.156.refs_3_.refs_8_), channel_id=1, source_target_pairs={{0,4},{4,0},{8,12},{12,8},{16,20},{20,16},{24,28},{28,24},{1,5},{5... | collective-permute-start | bytes 1179656 | tf_op jit(solution)/shard_map/ppermute | solution.py:383
  138.3 1.9 %collective-permute-start.29 = (bf16[64,1536]{1,0:T(8,128)(2,1)S(1)}, bf16[64,1536]{1,0:T(8,128)(2,1)S(1)}, u32[]{:S(2)}, u32[]{:S(2)}) collective-permute-start(bf16[64,1536]{1,0:T(8,128)(2,1)S(1)} %get-tuple-element.110), channel_id=1, source_target_pairs={{0,4},{4,0},{8,12},{12,8},{16,20},{20,16},{24,28},{28,24},{1,5},{5... | collective-permute-start | bytes 589832 | tf_op jit(solution)/shard_map/ppermute | solution.py:383

commit v9 on v8

--- a/solution.py
+++ b/solution.py
@@ -274,7 +274,8 @@
 
 
 def mixed_kernel(place_ref, got_ref, *refs):
-    mixed, out_ref = refs[:-1], refs[-1]
+    mixed, (mark_ref, out_ref) = refs[:-2], refs[-2:]
+    mark_ref[...] = jnp.zeros_like(mark_ref)
     tokens, cols = out_ref.shape[0], mixed[0].shape[1]
     per = mixed[0].shape[0] // CORES // tokens
     own = tile(place_ref[1] * per + place_ref[2], tokens)
@@ -285,42 +286,46 @@
         out_ref[:, tile(block + 1 - place_ref[1], cols)] = got_ref[:, n * cols : (n + 1) * cols]
 
 
-def expert_kernel(t, away, mode, has_sums, place_ref, gate_ref, up_ref, *refs):
-    refs = list(refs)
-    pieces, others = refs[: len(away)], refs[len(away)]
-    refs = refs[len(away) + 1 :]
-    sums = [[refs.pop(0), refs.pop(0)] for _ in away] if has_sums else None
+def expert_kernel(jobs, mode, held_sums, place_ref, gate_ref, up_ref, *refs):
+    count = 1 + max(max(own, other) for _, terms in jobs for _, own, other, _ in terms)
+    inputs, refs = refs[:count], list(refs[count:])
+    sums = {s: (refs.pop(0), refs.pop(0)) for s, _ in jobs if s in held_sums}
     if mode == "next":
         refs.pop(0)
     model = gate_ref.shape[1]
     width = model // GROUPS
-    cols, wide = width // CORES, pieces[0].shape[1]
+    cols = width // CORES
     if mode is None:
-        outs = refs[: 2 * len(away)]
-        held = refs[2 * len(away)]
+        outs, held = refs[:-1], refs[-1]
     else:
-        outs, mark_ref, held, ready, sems = refs
+        outs, mark_ref, ready, sems, held = refs
         mark_ref[...] = jnp.zeros_like(mark_ref)
-    copies = []
-    for n, s in enumerate(away):
+    copies, slot = [], 0
+    for n, (s, terms) in enumerate(jobs):
         source = place_ref[0] ^ s
-        held[n, :, tile(place_ref[1], cols)] = pieces[n][:, :cols]
-        held[n, :, tile(1 - place_ref[1], cols)] = others[:, n * wide : n * wide + cols]
-        x = held[n]
-        at = tile(source ^ t, width)
-        gated = dot(gate_ref[:, at], x, NT)
-        lifted = dot(up_ref[:, at], x, NT)
-        if sums is not None:
-            gated = gated + sums[n][0][...]
-            lifted = lifted + sums[n][1][...]
+        gated, lifted = 0.0, 0.0
+        if s in sums:
+            gated, lifted = sums[s][0][...], sums[s][1][...]
+        for t, own, other, part in terms:
+            own_ref, other_ref = inputs[own], inputs[other]
+            wide = own_ref.shape[1]
+            held[slot, :, tile(place_ref[1], cols)] = own_ref[:, :cols]
+            held[slot, :, tile(1 - place_ref[1], cols)] = other_ref[
+                :, part * wide : part * wide + cols
+            ]
+            x = held[slot]
+            slot += 1
+            at = tile(source ^ t, width)
+            gated = gated + dot(gate_ref[:, at], x, NT)
+            lifted = lifted + dot(up_ref[:, at], x, NT)
         if mode is None:
             outs[2 * n][...] = gated
             outs[2 * n + 1][...] = lifted
             continue
         lane = lax.broadcasted_iota(jnp.int32, (8, LANES), 1)
         pick = (lane < 3).astype(BF16)
-        squares = dot(pick, pieces[n][:, cols:], NT)
-        squares = squares + dot(pick, others[:, n * wide + cols : (n + 1) * wide], NT)
+        squares = dot(pick, own_ref[:, cols:], NT)
+        squares = squares + dot(pick, other_ref[:, part * wide + cols : (part + 1) * wide], NT)
         scale = lax.rsqrt(squares[0:1, :] / model + 1e-05)
         gated, lifted = gated * scale, lifted * scale
         silu = (0.5 * gated) * (1.0 + jnp.tanh(0.5 * gated))
@@ -328,26 +333,32 @@
         at = tile(source, ready.shape[2])
         rows = ready.shape[1] // 4
         for q in range(4):
-            part = slice(q * rows, (q + 1) * rows)
+            piece = slice(q * rows, (q + 1) * rows)
             copies.append(
-                pltpu.make_async_copy(ready.at[n, part], outs.at[part, at], sems.at[4 * n + q])
+                pltpu.make_async_copy(ready.at[n, piece], outs.at[piece, at], sems.at[4 * n + q])
             )
             copies[-1].start()
     for copy in copies:
         copy.wait()
 
 
-def expert_step(place, t, final, away, pieces, others, gate, up, sums, hidden, deps):
+def expert_step(place, final, work, gate, up, sums, hidden, deps):
     hid, model = gate.shape
     width = model // GROUPS
-    slots = pieces[0].shape[0]
-    operands = [place, gate, up] + pieces + [others]
-    has_sums = away[0] in sums
-    if has_sums:
-        operands += [x for s in away for x in sums[s]]
+    arrays = []
+
+    def index(x):
+        if not any(x is y for y in arrays):
+            arrays.append(x)
+        return [x is y for y in arrays].index(True)
+
+    jobs = [(s, [(t, index(a), index(b), n) for t, a, b, n in terms]) for s, terms in work]
+    slots = arrays[0].shape[0]
+    operands = [place, gate, up] + arrays
+    held_sums = [s for s, _ in jobs if s in sums]
+    operands += [x for s in held_sums for x in sums[s]]
     specs = [SM] + [VM] * (len(operands) - 1)
-    kwargs, mode = {}, None
-    scratch = [pltpu.VMEM((len(away), slots, width), BF16)]
+    kwargs, mode, scratch = {}, None, []
     if final:
         mode = "first" if hidden is None else "next"
         if hidden is not None:
@@ -357,24 +368,25 @@
         out_shape = [like((hid, slots * GROUPS)), like((8, LANES), F32)]
         kwargs["out_specs"] = [ANY, VM]
         scratch += [
-            pltpu.VMEM((len(away), hid, slots), BF16),
-            pltpu.SemaphoreType.DMA((4 * len(away),)),
+            pltpu.VMEM((len(jobs), hid, slots), BF16),
+            pltpu.SemaphoreType.DMA((4 * len(jobs),)),
         ]
     else:
-        out_shape = [like((hid, slots), F32)] * (2 * len(away))
+        out_shape = [like((hid, slots), F32)] * (2 * len(jobs))
+    scratch.append(pltpu.VMEM((sum(len(terms) for _, terms in jobs), slots, width), BF16))
     out = call(
-        functools.partial(expert_kernel, t, away, mode, has_sums),
+        functools.partial(expert_kernel, jobs, mode, held_sums),
         out_shape,
         operands,
         deps=deps,
         specs=specs,
-        limit=20,
+        limit=24,
         scratch_shapes=scratch,
         **kwargs,
     )
     if mode:
         return out
-    for n, s in enumerate(away):
+    for n, (s, _) in enumerate(jobs):
         sums[s] = out[2 * n : 2 * n + 2]
     return hidden, out[0]
 
@@ -563,19 +575,34 @@
         moved["diagonal", n] = copy(moved["diagonal", n])
         moved["rest", n] = swap(moved["diagonal", n])
 
-    def experts(n, away, pieces, others):
+    def near_terms(n):
+        held = ("own", "near", "far")
+        return [
+            (s, [(ORDER[n], moved[name, n], moved["others", n], s)])
+            for s, name in enumerate(held)
+        ]
+
+    def far_terms(*ns):
+        return [(3, [(ORDER[n], moved["diagonal", n], moved["rest", n], 0) for n in ns])]
+
+    def experts(n):
         nonlocal hidden
-        hidden, mark = expert_step(
-            place, ORDER[n], n == end, away, pieces, others, gate, up, sums, hidden, last[:]
+        work = near_terms(n) + (far_terms(n - 1) if 0 < n < end else [])
+        hidden, mark = expert_step(place, n == end, work, gate, up, sums, hidden, last[:])
+        last[:] = [mark]
+
+    def finish(n):
+        nonlocal hidden
+        work = far_terms(n - 1, n)
+        hidden, _ = expert_step(place, True, work, gate, up, sums, hidden, last[:])
+
+    def finish_rows(n):
+        mark, moved["rows"] = run(
+            mixed_kernel,
+            [like((8, LANES), F32), like((tokens, model))],
+            [place, moved["mixed"]] + mixed,
+            specs=[SM] + [VM] * (GROUPS + 1),
         )
-        last[:] = [mark]
-
-    def nearer(n):
-        pieces = [moved["own", n], moved["near", n], moved["far", n]]
-        experts(n, (0, 1, 2), pieces, moved["others", n])
-
-    def farther(n):
-        experts(n, (3,), [moved["diagonal", n]], moved["rest", n])
 
     def fetch(n):
         top = send(cut(weight_x, 0), "ctx", [(d, d ^ 4) for d in range(8)])
@@ -586,21 +613,12 @@
         (project, 0), (project, 1), (routes, 0), (inward, 0), (fetch, 3), (project, 2),
         (inward, 1), (outward, 0), (project, 3), (inward, 2), (outward, 1), (dispatch, 0),
         (inward, 3), (outward, 2), (dispatch, 1), (forward, 0), (outward, 3), (dispatch, 2),
-        (forward, 1), (dispatch, 3), (forward, 2), (nearer, 0), (diagonal, 0), (nearer, 1),
-        (farther, 0), (diagonal, 1), (forward, 3), (farther, 1), (nearer, 2), (diagonal, 2),
-        (farther, 2), (nearer, 3),
+        (forward, 1), (dispatch, 3), (forward, 2), (experts, 0), (diagonal, 0), (experts, 1),
+        (diagonal, 1), (forward, 3), (experts, 2), (diagonal, 2), (experts, 3), (diagonal, 3),
+        (finish_rows, 0), (finish, 3),
     ):
         work(n)
-    mixed_out = call(
-        mixed_kernel,
-        like((tokens, model)),
-        [place, moved["mixed"]] + mixed,
-        deps=last[:],
-        specs=[SM] + [VM] * (GROUPS + 1),
-    )
-    diagonal(3)
-    farther(3)
-    return (mixed_out, hidden[None])
+    return (moved["rows"], hidden[None])
 
 
 def entering(value, axis, combine, identity):

time: 146 us -> 148 us (1.014)
  waiting for transfers between devices: 42 us -> 46.1 us
  Pallas kernels: 45.2 us -> 43.1 us
    ppermute x46, waiting for transfers between devices: 42 us -> 46.1 us  [send(): return lax.ppermute(x, axis, pairs)]
    pallas_call x45 -> x42, Pallas kernels: 45.2 us -> 43.1 us  [call(): pl.pallas_call(body, out_shape=out_shape, in_specs=list(specs or [VM] * c...]
  transfers between devices with their start and end apart: 46 -> 46, of which waited for: 22 -> 26; matrix products, arithmetic and copies ran while one was open for 2% -> 2% of each run, Pallas kernels for 28% -> 25%
where the time goes in v9:
time: 148 us
  starting transfers between devices  52.3 us (35%)
  waiting for transfers between devices  46.1 us (31%)
  Pallas kernels  43.1 us (29%)
  other arithmetic  2.39 us (2%)
  local copies, waits for them, and re-layouts  2.38 us (2%)
    ppermute x46, starting transfers between devices, send(): return lax.ppermute(x, axis, pairs)  52.3 us
    ppermute x46, waiting for transfers between devices, send(): return lax.ppermute(x, axis, pairs)  46.1 us
    pallas_call x42, Pallas kernels, call(): pl.pallas_call(body, out_shape=out_shape, in_specs=list(specs or [VM] * c...  43.1 us
  transfers between devices with their start and end apart: 46, of which 26 were waited for; matrix products, arithmetic and copies ran while one was open for 2% of the time, Pallas kernels for 25%

profile of v9, /device:TPU:0, one launch (start us, length us, event | category | flops | bytes accessed | tf_op | source)
XLA Modules:
  0.0 147.8 jit_solution(15954969243394924115)
XLA Ops:
  0.6 3.0 %collective-permute-start.4 = (bf16[1024,384]{1,0:T(8,128)(2,1)}, bf16[1024,384]{1,0:T(8,128)(2,1)S(1)}, u32[]{:S(2)}, u32[]{:S(2)}) collective-permute-start(bf16[1024,384]{1,0:T(8,128)(2,1)} %refs_5_.1), channel_id=1, source_target_pairs={{0,16},{4,20},{8,24},{12,28},{16,0},{20,4},{24,8},{28,12},{1,17},{... | collective-permute-start | bytes 2359304 | tf_op jit(solution)/shard_map/ppermute | solution.py:395
  4.4 0.8 add_select_fusion
  6.4 1.0 copy-done.5
  7.4 1.0 copy-done.6
  8.5 1.4 shard_map.113
  10.5 1.0 collective-permute-done.refs_2_
  11.6 1.6 %collective-permute-start.1 = (f32[4,128,128]{2,1,0:T(8,128)S(1)}, f32[4,128,128]{2,1,0:T(8,128)S(1)}, u32[]{:S(2)}, u32[]{:S(2)}) collective-permute-start(f32[4,128,128]{2,1,0:T(8,128)S(1)} %get-tuple-element.81.refs_2_), channel_id=1, source_target_pairs={{0,8},{4,12},{8,0},{12,4},{16,24},{20,28},{24,16},{28,20},{1,9},{5... | collective-permute-start | bytes 786440 | tf_op jit(solution)/shard_map/ppermute | solution.py:395
  13.1 1.6 %collective-permute-start.2 = (s32[8,128]{1,0:T(8,128)S(1)}, s32[8,128]{1,0:T(8,128)S(1)}, u32[]{:S(2)}, u32[]{:S(2)}) collective-permute-start(s32[8,128]{1,0:T(8,128)S(1)} %pad.4.refs_4_.refs_0_), channel_id=1, source_target_pairs={{0,1},{1,0},{2,3},{3,2},{4,5},{5,4},{6,7},{7,6},{8,9},{9,8},{10,11... | collective-permute-start | bytes 12296 | tf_op jit(solution)/shard_map/ppermute | solution.py:395
  14.7 1.1 shard_map.115
  15.8 0.9 collective-permute-done.2.refs_1_
  16.7 3.2 %collective-permute-done.1.refs_1_ = f32[4,128,128]{2,1,0:T(8,128)S(1)} collective-permute-done((f32[4,128,128]{2,1,0:T(8,128)S(1)}, f32[4,128,128]{2,1,0:T(8,128)S(1)}, u32[]{:S(2)}, u32[]{:S(2)}) %collective-permute-start.1) | collective-permute-done | bytes 262176 | tf_op jit(solution)/shard_map/ppermute | solution.py:395
  20.0 1.5 collective-permute-done.4.refs_5_.refs_0_
  21.5 3.7 %collective-permute-start.5 = (f32[4,128,128]{2,1,0:T(8,128)S(1)}, f32[4,128,128]{2,1,0:T(8,128)S(1)}, u32[]{:S(2)}, u32[]{:S(2)}) collective-permute-start(f32[4,128,128]{2,1,0:T(8,128)S(1)} %get-tuple-element.83), channel_id=1, source_target_pairs={{0,16},{4,20},{8,24},{12,28},{1,17},{5,21},{9,25},{13,29},{2,18},{... | collective-permute-start | bytes 786440 | tf_op jit(solution)/shard_map/ppermute | solution.py:395
  25.1 2.7 %collective-permute-start.6 = (s32[8,128]{1,0:T(8,128)S(1)}, s32[8,128]{1,0:T(8,128)S(1)}, u32[]{:S(2)}, u32[]{:S(2)}) collective-permute-start(s32[8,128]{1,0:T(8,128)S(1)} %shard_map.116.refs_3_.refs_1_), channel_id=1, source_target_pairs={{0,2},{1,3},{2,0},{3,1},{4,6},{5,7},{6,4},{7,5},{8,10},{9,11},{10,... | collective-permute-start | bytes 12296 | tf_op jit(solution)/shard_map/ppermute | solution.py:395
  27.9 1.8 %collective-permute-done.6.refs_2_ = s32[8,128]{1,0:T(8,128)S(1)} collective-permute-done((s32[8,128]{1,0:T(8,128)S(1)}, s32[8,128]{1,0:T(8,128)S(1)}, u32[]{:S(2)}, u32[]{:S(2)}) %collective-permute-start.6) | collective-permute-done | bytes 4128 | tf_op jit(solution)/shard_map/ppermute | solution.py:395
  30.5 1.5 %collective-permute-done.7.refs_5_ = f32[4,128,128]{2,1,0:T(8,128)S(1)} collective-permute-done((f32[4,128,128]{2,1,0:T(8,128)S(1)}, f32[4,128,128]{2,1,0:T(8,128)S(1)}, u32[]{:S(2)}, u32[]{:S(2)}) %collective-permute-start.7) | collective-permute-done | bytes 262176 | tf_op jit(solution)/shard_map/ppermute | solution.py:395
  32.0 1.2 shard_map.121.refs_1_.refs_6_
  33.5 1.5 %collective-permute-start.9 = (bf16[1024,384]{1,0:T(8,128)(2,1)S(1)}, bf16[1024,384]{1,0:T(8,128)(2,1)S(1)}, u32[]{:S(2)}, u32[]{:S(2)}) collective-permute-start(bf16[1024,384]{1,0:T(8,128)(2,1)S(1)} %shard_map.118.refs_3_), channel_id=1, source_target_pairs={{0,8},{4,12},{8,0},{12,4},{16,24},{20,28},{24,16},{28,20},{1,9},{5... | collective-permute-start | bytes 2359304 | tf_op jit(solution)/shard_map/ppermute | solution.py:395
  35.2 1.2 shard_map.122
  36.5 3.5 %collective-permute-start.10 = (bf16[512,384]{1,0:T(8,128)(2,1)S(1)}, bf16[512,384]{1,0:T(8,128)(2,1)S(1)}, u32[]{:S(2)}, u32[]{:S(2)}) collective-permute-start(bf16[512,384]{1,0:T(8,128)(2,1)S(1)} %get-tuple-element.87), channel_id=1, source_target_pairs={{0,1},{3,2},{4,5},{7,6},{8,9},{11,10},{12,13},{15,14},{16,17},{19,... | collective-permute-start | bytes 1179656 | tf_op jit(solution)/shard_map/ppermute | solution.py:395
  40.0 1.3 shard_map.123
  41.3 1.3 collective-permute-start.15
  42.7 1.2 collective-permute-done.11.refs_2_
  43.8 0.8 shard_map.124.refs_2_.refs_4_
  44.7 4.8 %collective-permute-done.10.refs_1_ = bf16[512,384]{1,0:T(8,128)(2,1)S(1)} collective-permute-done((bf16[512,384]{1,0:T(8,128)(2,1)S(1)}, bf16[512,384]{1,0:T(8,128)(2,1)S(1)}, u32[]{:S(2)}, u32[]{:S(2)}) %collective-permute-start.10) | collective-permute-done | bytes 393248 | tf_op jit(solution)/shard_map/ppermute | solution.py:395
  50.3 3.0 %collective-permute-done.9.refs_0_.refs_5_ = bf16[1024,384]{1,0:T(8,128)(2,1)S(1)} collective-permute-done((bf16[1024,384]{1,0:T(8,128)(2,1)S(1)}, bf16[1024,384]{1,0:T(8,128)(2,1)S(1)}, u32[]{:S(2)}, u32[]{:S(2)}) %collective-permute-start.9) | collective-permute-done | bytes 786464 | tf_op jit(solution)/shard_map/ppermute | solution.py:395
  53.4 1.6 %collective-permute-start.13 = (bf16[512,384]{1,0:T(8,128)(2,1)S(1)}, bf16[512,384]{1,0:T(8,128)(2,1)S(1)}, u32[]{:S(2)}, u32[]{:S(2)}) collective-permute-start(bf16[512,384]{1,0:T(8,128)(2,1)S(1)} %shard_map.127.refs_6_), channel_id=1, source_target_pairs={{0,8},{4,12},{8,0},{12,4},{16,24},{20,28},{24,16},{28,20},{1,9},{5... | collective-permute-start | bytes 1179656 | tf_op jit(solution)/shard_map/ppermute | solution.py:395
  54.9 2.0 %collective-permute-start.12 = (bf16[512,384]{1,0:T(8,128)(2,1)S(1)}, bf16[512,384]{1,0:T(8,128)(2,1)S(1)}, u32[]{:S(2)}, u32[]{:S(2)}) collective-permute-start(bf16[512,384]{1,0:T(8,128)(2,1)S(1)} %shard_map.126.refs_1_), channel_id=1, source_target_pairs={{0,16},{4,20},{8,24},{12,28},{16,0},{20,4},{24,8},{28,12},{1,17},{... | collective-permute-start | bytes 1179656 | tf_op jit(solution)/shard_map/ppermute | solution.py:395
  56.9 1.2 shard_map.128
  58.2 4.2 %collective-permute-start.19 = (bf16[512,384]{1,0:T(8,128)(2,1)S(1)}, bf16[512,384]{1,0:T(8,128)(2,1)S(1)}, u32[]{:S(2)}, u32[]{:S(2)}) collective-permute-start(bf16[512,384]{1,0:T(8,128)(2,1)S(1)} %get-tuple-element.97), channel_id=1, source_target_pairs={{0,1},{3,2},{4,5},{7,6},{8,9},{11,10},{12,13},{15,14},{16,17},{19,... | collective-permute-start | bytes 1179656 | tf_op jit(solution)/shard_map/ppermute | solution.py:395
  63.3 1.3 collective-permute-start.17
  64.6 0.8 collective-permute-done.12.refs_5_
  65.5 1.2 shard_map.131
  66.7 3.8 %collective-permute-start.16 = (bf16[512,384]{1,0:T(8,128)(2,1)S(1)}, bf16[512,384]{1,0:T(8,128)(2,1)S(1)}, u32[]{:S(2)}, u32[]{:S(2)}) collective-permute-start(bf16[512,384]{1,0:T(8,128)(2,1)S(1)} %get-tuple-element.95), channel_id=1, source_target_pairs={{0,1},{3,2},{4,5},{7,6},{8,9},{11,10},{12,13},{15,14},{16,17},{19,... | collective-permute-start | bytes 1179656 | tf_op jit(solution)/shard_map/ppermute | solution.py:395
  71.5 1.3 collective-permute-start.23
  72.8 1.5 %collective-permute-done.17.refs_1_ = bf16[512,384]{1,0:T(8,128)(2,1)S(1)} collective-permute-done((bf16[512,384]{1,0:T(8,128)(2,1)S(1)}, bf16[512,384]{1,0:T(8,128)(2,1)S(1)}, u32[]{:S(2)}, u32[]{:S(2)}) %collective-permute-start.17) | collective-permute-done | bytes 393248 | tf_op jit(solution)/shard_map/ppermute | solution.py:395
  74.2 0.9 shard_map.134
  75.9 1.5 collective-permute-start.21
  78.5 1.3 collective-permute-start.26
  79.8 4.0 %collective-permute-done.23.refs_1_ = bf16[512,384]{1,0:T(8,128)(2,1)S(1)} collective-permute-done((bf16[512,384]{1,0:T(8,128)(2,1)S(1)}, bf16[512,384]{1,0:T(8,128)(2,1)S(1)}, u32[]{:S(2)}, u32[]{:S(2)}) %collective-permute-start.23) | collective-permute-done | bytes 393248 | tf_op jit(solution)/shard_map/ppermute | solution.py:395
  83.8 0.9 shard_map.137
  86.6 1.7 %collective-permute-start.25 = (bf16[512,384]{1,0:T(8,128)(2,1)S(1)}, bf16[512,384]{1,0:T(8,128)(2,1)S(1)}, u32[]{:S(2)}, u32[]{:S(2)}) collective-permute-start(bf16[512,384]{1,0:T(8,128)(2,1)S(1)} %shard_map.139.refs_5_.refs_2_), channel_id=1, source_target_pairs={{1,0},{2,3},{5,4},{6,7},{9,8},{10,11},{13,12},{14,15},{17,16},{18,... | collective-permute-start | bytes 1179656 | tf_op jit(solution)/shard_map/ppermute | solution.py:395
  88.4 4.6 %collective-permute-done.26.refs_1_ = bf16[512,384]{1,0:T(8,128)(2,1)S(1)} collective-permute-done((bf16[512,384]{1,0:T(8,128)(2,1)S(1)}, bf16[512,384]{1,0:T(8,128)(2,1)S(1)}, u32[]{:S(2)}, u32[]{:S(2)}) %collective-permute-start.26) | collective-permute-done | bytes 393248 | tf_op jit(solution)/shard_map/ppermute | solution.py:395
  93.0 0.9 shard_map.140
  93.9 1.0 collective-permute-done.28.refs_3_.refs_6_
  95.8 1.6 %collective-permute-start.37 = (bf16[384,384]{1,0:T(8,128)(2,1)S(1)}, bf16[384,384]{1,0:T(8,128)(2,1)S(1)}, u32[]{:S(2)}, u32[]{:S(2)}) collective-permute-start(bf16[384,384]{1,0:T(8,128)(2,1)S(1)} %get-tuple-element.108.refs_4_.refs_1_.refs_3_), channel_id=1, source_target_pairs={{0,16},{4,20},{8,24},{12,28},{16,0},{20,4},{24,8},{28,12},{1,17},{... | collective-permute-start | bytes 884744 | tf_op jit(solution)/shard_map/ppermute | solution.py:395
  98.0 2.6 %collective-permute-done.25.refs_1_ = bf16[512,384]{1,0:T(8,128)(2,1)S(1)} collective-permute-done((bf16[512,384]{1,0:T(8,128)(2,1)S(1)}, bf16[512,384]{1,0:T(8,128)(2,1)S(1)}, u32[]{:S(2)}, u32[]{:S(2)}) %collective-permute-start.25) | collective-permute-done | bytes 393248 | tf_op jit(solution)/shard_map/ppermute | solution.py:395
  101.2 1.3 shard_map.142
  102.5 2.7 %collective-permute-done.37.refs_3_.refs_6_ = bf16[384,384]{1,0:T(8,128)(2,1)S(1)} collective-permute-done((bf16[384,384]{1,0:T(8,128)(2,1)S(1)}, bf16[384,384]{1,0:T(8,128)(2,1)S(1)}, u32[]{:S(2)}, u32[]{:S(2)}) %collective-permute-start.37) | collective-permute-done | bytes 294944 | tf_op jit(solution)/shard_map/ppermute | solution.py:395
  105.3 1.6 %collective-permute-start.31 = (bf16[384,512]{1,0:T(8,128)(2,1)S(1)}, bf16[384,512]{1,0:T(8,128)(2,1)S(1)}, u32[]{:S(2)}, u32[]{:S(2)}) collective-permute-start(bf16[384,512]{1,0:T(8,128)(2,1)S(1)} %get-tuple-element.112.refs_4_.refs_1_.refs_3_), channel_id=1, source_target_pairs={{0,16},{4,20},{8,24},{12,28},{16,0},{20,4},{24,8},{28,12},{1,17},{... | collective-permute-start | bytes 1179656 | tf_op jit(solution)/shard_map/ppermute | solution.py:395
  108.5 3.5 %shard_map.144 = (f32[576,384]{1,0:T(8,128)S(1)}, f32[576,384]{1,0:T(8,128)S(1)}, f32[576,384]{1,0:T(8,128)S(1)}, f32[576,384]{1,0:T(8,128)S(1)}, f32[576,384]{1,0:T(8,128)S(1)}, /*index=5*/f32[576,384]{1,0:T(8,128)S(1)}) custom-call(s32[3]{0:T(128)S(1)} %pad_add_fusion.refs_0_, bf16[576,3072]{1,0:T(8,128)(2,1)S(1)} %bitcast.20, ...), custom_call_target="tpu_custom_call" | custom-call | flops 1 | bytes 1 | tf_op jit(solution)/shard_map/pallas_call | solution.py:45
  112.7 1.0 collective-permute-done.38.refs_8_
  113.7 4.6 %shard_map.146 = (f32[576,384]{1,0:T(8,128)S(1)}, f32[576,384]{1,0:T(8,128)S(1)}, f32[576,384]{1,0:T(8,128)S(1)}, f32[576,384]{1,0:T(8,128)S(1)}, f32[576,384]{1...) custom-call(s32[3]{0:T(128)S(1)} %pad_add_fusion.refs_0_, ...), custom_call_target="tpu_custom_call" | custom-call | flops 1 | bytes 1 | tf_op jit(solution)/shard_map/pallas_call | solution.py:45
  118.3 1.7 %collective-permute-done.32.refs_0_ = bf16[384,384]{1,0:T(8,128)(2,1)S(1)} collective-permute-done((bf16[384,384]{1,0:T(8,128)(2,1)S(1)}, bf16[384,384]{1,0:T(8,128)(2,1)S(1)}, u32[]{:S(2)}, u32[]{:S(2)}) %collective-permute-start.32) | collective-permute-done | bytes 294944 | tf_op jit(solution)/shard_map/ppermute | solution.py:395
  120.7 1.2 collective-permute-start.40
  121.9 0.9 collective-permute-start.39
  122.8 1.1 collective-permute-start.43
  124.0 1.6 %collective-permute-done.41.refs_4_ = bf16[384,1152]{1,0:T(8,128)(2,1)S(1)} collective-permute-done((bf16[384,1152]{1,0:T(8,128)(2,1)S(1)}, bf16[384,1152]{1,0:T(8,128)(2,1)S(1)}, u32[]{:S(2)}, u32[]{:S(2)}) %collective-permute-start.41) | collective-permute-done | bytes 884768 | tf_op jit(solution)/shard_map/ppermute | solution.py:395
  126.0 4.8 %shard_map.149 = (f32[576,384]{1,0:T(8,128)S(1)}, f32[576,384]{1,0:T(8,128)S(1)}, f32[576,384]{1,0:T(8,128)S(1)}, f32[576,384]{1,0:T(8,128)S(1)}, f32[576,384]{1...) custom-call(s32[3]{0:T(128)S(1)} %pad_add_fusion.refs_0_, ...), custom_call_target="tpu_custom_call" | custom-call | flops 1 | bytes 1 | tf_op jit(solution)/shard_map/pallas_call | solution.py:45
  130.8 2.1 %collective-permute-done.43.refs_0_ = bf16[384,384]{1,0:T(8,128)(2,1)S(1)} collective-permute-done((bf16[384,384]{1,0:T(8,128)(2,1)S(1)}, bf16[384,384]{1,0:T(8,128)(2,1)S(1)}, u32[]{:S(2)}, u32[]{:S(2)}) %collective-permute-start.43) | collective-permute-done | bytes 294944 | tf_op jit(solution)/shard_map/ppermute | solution.py:395
  132.9 6.3 %shard_map.151 = (bf16[576,1536]{1,0:T(8,128)(2,1)}, f32[8,128]{1,0:T(8,128)S(1)}) custom-call(s32[3]{0:T(128)S(1)} %pad_add_fusion.refs_0_, bf16[576,3072]{1,0:T(8,128)(2,1)S(1)} %bitcast.23, bf16[576,3072]{1,0:T(8,128)(2,1)S(1)} %bitcast.28, bf16[384,512]{1,0:T(8,128)(2,1)S(1)} %get-tuple-element.112.refs_4_.refs_1_.refs_3_, ...), custom_call_target="tpu_custom_call" | custom-call | flops 1 | bytes 1 | tf_op jit(solution)/shard_map/pallas_call | solution.py:45
  139.9 1.8 %collective-permute-done.29.refs_1_ = bf16[64,1536]{1,0:T(8,128)(2,1)S(1)} collective-permute-done((bf16[64,1536]{1,0:T(8,128)(2,1)S(1)}, bf16[64,1536]{1,0:T(8,128)(2,1)S(1)}, u32[]{:S(2)}, u32[]{:S(2)}) %collective-permute-start.29) | collective-permute-done | bytes 196640 | tf_op jit(solution)/shard_map/ppermute | solution.py:395
  141.8 1.3 shard_map.153
  143.1 4.5 %shard_map.154 = (bf16[576,1536]{1,0:T(8,128)(2,1)}, f32[8,128]{1,0:T(8,128)}) custom-call(s32[3]{0:T(128)S(1)} %pad_add_fusion.refs_0_, bf16[576,3072]{1,0:T(8,128)(2,1)S(1)} %bitcast.24, bf16[576,3072]{1,0:T(8,128)(2,1)S(1)} %bitcast.29, bf16[384,384]{1,0:T(8,128)(2,1)S(1)} %shard_map.150.refs_13_.refs_3_, ...), custom_call_target="tpu_custom_call", output_to_operand_aliasing={{0}: (9, {})} | custom-call | flops 1 | bytes 1 | tf_op jit(solution)/shard_map/pallas_call | solution.py:45
  (100 shorter events, 16.6 us)
Async XLA Ops:
  0.6 14.1 %copy-start.4 = (bf16[256,1024]{1,0:T(8,128)(2,1)S(1)}, bf16[256,1024]{1,0:T(8,128)(2,1)}, u32[]{:S(2)}) copy-start(bf16[256,1024]{1,0:T(8,128)(2,1)} %refs_1_.1) | copy-start | bytes 1572868
  0.6 20.8 %collective-permute-start.4 = (bf16[1024,384]{1,0:T(8,128)(2,1)}, bf16[1024,384]{1,0:T(8,128)(2,1)S(1)}, u32[]{:S(2)}, u32[]{:S(2)}) collective-permute-start(bf16[1024,384]{1,0:T(8,128)(2,1)} %refs_5_.1), channel_id=1, source_target_pairs={{0,16},{4,20},{8,24},{12,28},{16,0},{20,4},{24,8},{28,12},{1,17},{... | collective-permute-start | bytes 2359304 | tf_op jit(solution)/shard_map/ppermute | solution.py:395
  6.4 1.0 copy-start.5
  7.4 1.0 copy-start.6
  9.9 1.6 %collective-permute-start = (f32[4,128,128]{2,1,0:T(8,128)S(1)}, f32[4,128,128]{2,1,0:T(8,128)S(1)}, u32[]{:S(2)}, u32[]{:S(2)}) collective-permute-start(f32[4,128,128]{2,1,0:T(8,128)S(1)} %get-tuple-element.77), channel_id=1, source_target_pairs={{0,4},{4,0},{8,12},{12,8},{16,20},{20,16},{24,28},{28,24},{1,5},{5... | collective-permute-start | bytes 786440 | tf_op jit(solution)/shard_map/ppermute | solution.py:395
  10.0 6.8 %collective-permute-start.3 = (bf16[64,3072]{1,0:T(8,128)(2,1)}, bf16[64,3072]{1,0:T(8,128)(2,1)S(1)}, u32[]{:S(2)}, u32[]{:S(2)}) collective-permute-start(bf16[64,3072]{1,0:T(8,128)(2,1)} %refs_3_.9), channel_id=1, source_target_pairs={{0,4},{4,0},{8,12},{12,8},{16,20},{20,16},{24,28},{28,24},{1,5},{5... | collective-permute-start | bytes 1179656 | tf_op jit(solution)/shard_map/ppermute | solution.py:395
  11.6 8.4 %collective-permute-start.1 = (f32[4,128,128]{2,1,0:T(8,128)S(1)}, f32[4,128,128]{2,1,0:T(8,128)S(1)}, u32[]{:S(2)}, u32[]{:S(2)}) collective-permute-start(f32[4,128,128]{2,1,0:T(8,128)S(1)} %get-tuple-element.81.refs_2_), channel_id=1, source_target_pairs={{0,8},{4,12},{8,0},{12,4},{16,24},{20,28},{24,16},{28,20},{1,9},{5... | collective-permute-start | bytes 786440 | tf_op jit(solution)/shard_map/ppermute | solution.py:395
  13.1 3.6 %collective-permute-start.2 = (s32[8,128]{1,0:T(8,128)S(1)}, s32[8,128]{1,0:T(8,128)S(1)}, u32[]{:S(2)}, u32[]{:S(2)}) collective-permute-start(s32[8,128]{1,0:T(8,128)S(1)} %pad.4.refs_4_.refs_0_), channel_id=1, source_target_pairs={{0,1},{1,0},{2,3},{3,2},{4,5},{5,4},{6,7},{7,6},{8,9},{9,8},{10,11... | collective-permute-start | bytes 12296 | tf_op jit(solution)/shard_map/ppermute | solution.py:395
  15.8 12.0 %copy-start.3 = (bf16[1024,384]{1,0:T(8,128)(2,1)S(1)}, bf16[1024,384]{1,0:T(8,128)(2,1)}, u32[]{:S(2)}) copy-start(bf16[1024,384]{1,0:T(8,128)(2,1)} %refs_5_.1) | copy-start | bytes 2359300
  21.5 8.8 %collective-permute-start.5 = (f32[4,128,128]{2,1,0:T(8,128)S(1)}, f32[4,128,128]{2,1,0:T(8,128)S(1)}, u32[]{:S(2)}, u32[]{:S(2)}) collective-permute-start(f32[4,128,128]{2,1,0:T(8,128)S(1)} %get-tuple-element.83), channel_id=1, source_target_pairs={{0,16},{4,20},{8,24},{12,28},{1,17},{5,21},{9,25},{13,29},{2,18},{... | collective-permute-start | bytes 786440 | tf_op jit(solution)/shard_map/ppermute | solution.py:395
  25.1 4.6 %collective-permute-start.6 = (s32[8,128]{1,0:T(8,128)S(1)}, s32[8,128]{1,0:T(8,128)S(1)}, u32[]{:S(2)}, u32[]{:S(2)}) collective-permute-start(s32[8,128]{1,0:T(8,128)S(1)} %shard_map.116.refs_3_.refs_1_), channel_id=1, source_target_pairs={{0,2},{1,3},{2,0},{3,1},{4,6},{5,7},{6,4},{7,5},{8,10},{9,11},{10,... | collective-permute-start | bytes 12296 | tf_op jit(solution)/shard_map/ppermute | solution.py:395
  30.3 5.0 %copy-start.2 = (bf16[64,3072]{1,0:T(8,128)(2,1)S(1)}, bf16[64,3072]{1,0:T(8,128)(2,1)}, u32[]{:S(2)}) copy-start(bf16[64,3072]{1,0:T(8,128)(2,1)} %refs_3_.9) | copy-start | bytes 1179652
  30.4 1.6 %collective-permute-start.7 = (f32[4,128,128]{2,1,0:T(8,128)S(1)}, f32[4,128,128]{2,1,0:T(8,128)S(1)}, u32[]{:S(2)}, u32[]{:S(2)}) collective-permute-start(f32[4,128,128]{2,1,0:T(8,128)S(1)} %get-tuple-element.85), channel_id=1, source_target_pairs={{0,4},{4,0},{8,12},{12,8},{16,20},{20,16},{24,28},{28,24},{1,5},{5... | collective-permute-start | bytes 786440 | tf_op jit(solution)/shard_map/ppermute | solution.py:395
  33.3 2.0 %collective-permute-start.8 = (bf16[256,1024]{1,0:T(8,128)(2,1)S(1)}, bf16[256,1024]{1,0:T(8,128)(2,1)S(1)}, u32[]{:S(2)}, u32[]{:S(2)}) collective-permute-start(bf16[256,1024]{1,0:T(8,128)(2,1)S(1)} %shard_map.121.refs_1_.refs_6_), channel_id=1, source_target_pairs={{0,4},{4,0},{8,12},{12,8},{16,20},{20,16},{24,28},{28,24},{1,5},{5... | collective-permute-start | bytes 1572872 | tf_op jit(solution)/shard_map/ppermute | solution.py:395
  33.5 19.8 %collective-permute-start.9 = (bf16[1024,384]{1,0:T(8,128)(2,1)S(1)}, bf16[1024,384]{1,0:T(8,128)(2,1)S(1)}, u32[]{:S(2)}, u32[]{:S(2)}) collective-permute-start(bf16[1024,384]{1,0:T(8,128)(2,1)S(1)} %shard_map.118.refs_3_), channel_id=1, source_target_pairs={{0,8},{4,12},{8,0},{12,4},{16,24},{20,28},{24,16},{28,20},{1,9},{5... | collective-permute-start | bytes 2359304 | tf_op jit(solution)/shard_map/ppermute | solution.py:395
  36.5 13.0 %collective-permute-start.10 = (bf16[512,384]{1,0:T(8,128)(2,1)S(1)}, bf16[512,384]{1,0:T(8,128)(2,1)S(1)}, u32[]{:S(2)}, u32[]{:S(2)}) collective-permute-start(bf16[512,384]{1,0:T(8,128)(2,1)S(1)} %get-tuple-element.87), channel_id=1, source_target_pairs={{0,1},{3,2},{4,5},{7,6},{8,9},{11,10},{12,13},{15,14},{16,17},{19,... | collective-permute-start | bytes 1179656 | tf_op jit(solution)/shard_map/ppermute | solution.py:395
  41.3 21.1 %collective-permute-start.15 = (bf16[512,384]{1,0:T(8,128)(2,1)S(1)}, bf16[512,384]{1,0:T(8,128)(2,1)S(1)}, u32[]{:S(2)}, u32[]{:S(2)}) collective-permute-start(bf16[512,384]{1,0:T(8,128)(2,1)S(1)} %get-tuple-element.91), channel_id=1, source_target_pairs={{0,1},{3,2},{4,5},{7,6},{8,9},{11,10},{12,13},{15,14},{16,17},{19,... | collective-permute-start | bytes 1179656 | tf_op jit(solution)/shard_map/ppermute | solution.py:395
  42.6 1.2 collective-permute-start.11
  49.6 13.7 %collective-permute-start.14 = (bf16[512,384]{1,0:T(8,128)(2,1)S(1)}, bf16[512,384]{1,0:T(8,128)(2,1)S(1)}, u32[]{:S(2)}, u32[]{:S(2)}) collective-permute-start(bf16[512,384]{1,0:T(8,128)(2,1)S(1)} %get-tuple-element.90), channel_id=1, source_target_pairs={{1,2},{2,1},{5,6},{6,5},{9,10},{10,9},{13,14},{14,13},{17,18},{18,... | collective-permute-start | bytes 1179656 | tf_op jit(solution)/shard_map/ppermute | solution.py:395
  53.4 11.3 %collective-permute-start.13 = (bf16[512,384]{1,0:T(8,128)(2,1)S(1)}, bf16[512,384]{1,0:T(8,128)(2,1)S(1)}, u32[]{:S(2)}, u32[]{:S(2)}) collective-permute-start(bf16[512,384]{1,0:T(8,128)(2,1)S(1)} %shard_map.127.refs_6_), channel_id=1, source_target_pairs={{0,8},{4,12},{8,0},{12,4},{16,24},{20,28},{24,16},{28,20},{1,9},{5... | collective-permute-start | bytes 1179656 | tf_op jit(solution)/shard_map/ppermute | solution.py:395
  54.9 10.5 %collective-permute-start.12 = (bf16[512,384]{1,0:T(8,128)(2,1)S(1)}, bf16[512,384]{1,0:T(8,128)(2,1)S(1)}, u32[]{:S(2)}, u32[]{:S(2)}) collective-permute-start(bf16[512,384]{1,0:T(8,128)(2,1)S(1)} %shard_map.126.refs_1_), channel_id=1, source_target_pairs={{0,16},{4,20},{8,24},{12,28},{16,0},{20,4},{24,8},{28,12},{1,17},{... | collective-permute-start | bytes 1179656 | tf_op jit(solution)/shard_map/ppermute | solution.py:395
  58.2 12.4 %collective-permute-start.19 = (bf16[512,384]{1,0:T(8,128)(2,1)S(1)}, bf16[512,384]{1,0:T(8,128)(2,1)S(1)}, u32[]{:S(2)}, u32[]{:S(2)}) collective-permute-start(bf16[512,384]{1,0:T(8,128)(2,1)S(1)} %get-tuple-element.97), channel_id=1, source_target_pairs={{0,1},{3,2},{4,5},{7,6},{8,9},{11,10},{12,13},{15,14},{16,17},{19,... | collective-permute-start | bytes 1179656 | tf_op jit(solution)/shard_map/ppermute | solution.py:395
  62.6 8.8 %collective-permute-start.18 = (bf16[512,384]{1,0:T(8,128)(2,1)S(1)}, bf16[512,384]{1,0:T(8,128)(2,1)S(1)}, u32[]{:S(2)}, u32[]{:S(2)}) collective-permute-start(bf16[512,384]{1,0:T(8,128)(2,1)S(1)} %get-tuple-element.96), channel_id=1, source_target_pairs={{1,2},{2,1},{5,6},{6,5},{9,10},{10,9},{13,14},{14,13},{17,18},{18,... | collective-permute-start | bytes 1179656 | tf_op jit(solution)/shard_map/ppermute | solution.py:395
  63.3 10.9 %collective-permute-start.17 = (bf16[512,384]{1,0:T(8,128)(2,1)S(1)}, bf16[512,384]{1,0:T(8,128)(2,1)S(1)}, u32[]{:S(2)}, u32[]{:S(2)}) collective-permute-start(bf16[512,384]{1,0:T(8,128)(2,1)S(1)} %shard_map.130.refs_7_.refs_2_), channel_id=1, source_target_pairs={{1,0},{2,3},{5,4},{6,7},{9,8},{10,11},{13,12},{14,15},{17,16},{18,... | collective-permute-start | bytes 1179656 | tf_op jit(solution)/shard_map/ppermute | solution.py:395
  66.7 10.9 %collective-permute-start.16 = (bf16[512,384]{1,0:T(8,128)(2,1)S(1)}, bf16[512,384]{1,0:T(8,128)(2,1)S(1)}, u32[]{:S(2)}, u32[]{:S(2)}) collective-permute-start(bf16[512,384]{1,0:T(8,128)(2,1)S(1)} %get-tuple-element.95), channel_id=1, source_target_pairs={{0,1},{3,2},{4,5},{7,6},{8,9},{11,10},{12,13},{15,14},{16,17},{19,... | collective-permute-start | bytes 1179656 | tf_op jit(solution)/shard_map/ppermute | solution.py:395
  70.5 3.7 %copy-start.7 = (f32[3072]{0:T(1024)S(1)}, f32[3072]{0:T(1024)}, u32[]{:S(2)}) copy-start(f32[3072]{0:T(1024)} %param.16) | copy-start | bytes 36868
  70.7 7.8 %collective-permute-start.24 = (bf16[512,384]{1,0:T(8,128)(2,1)S(1)}, bf16[512,384]{1,0:T(8,128)(2,1)S(1)}, u32[]{:S(2)}, u32[]{:S(2)}) collective-permute-start(bf16[512,384]{1,0:T(8,128)(2,1)S(1)} %get-tuple-element.102), channel_id=1, source_target_pairs={{1,2},{2,1},{5,6},{6,5},{9,10},{10,9},{13,14},{14,13},{17,18},{18,... | collective-permute-start | bytes 1179656 | tf_op jit(solution)/shard_map/ppermute | solution.py:395
  71.5 12.3 %collective-permute-start.23 = (bf16[512,384]{1,0:T(8,128)(2,1)S(1)}, bf16[512,384]{1,0:T(8,128)(2,1)S(1)}, u32[]{:S(2)}, u32[]{:S(2)}) collective-permute-start(bf16[512,384]{1,0:T(8,128)(2,1)S(1)} %shard_map.133.refs_5_.refs_2_), channel_id=1, source_target_pairs={{1,0},{2,3},{5,4},{6,7},{9,8},{10,11},{13,12},{14,15},{17,16},{18,... | collective-permute-start | bytes 1179656 | tf_op jit(solution)/shard_map/ppermute | solution.py:395
  75.2 9.5 %collective-permute-start.22 = (bf16[384,384]{1,0:T(8,128)(2,1)S(1)}, bf16[384,384]{1,0:T(8,128)(2,1)S(1)}, u32[]{:S(2)}, u32[]{:S(2)}) collective-permute-start(bf16[384,384]{1,0:T(8,128)(2,1)S(1)} %get-tuple-element.99.refs_2_.refs_1_.refs_3_), channel_id=1, source_target_pairs={{0,16},{4,20},{8,24},{12,28},{16,0},{20,4},{24,8},{28,12},{1,17},{... | collective-permute-start | bytes 884744 | tf_op jit(solution)/shard_map/ppermute | solution.py:395
  75.9 8.9 %collective-permute-start.21 = (bf16[384,384]{1,0:T(8,128)(2,1)S(1)}, bf16[384,384]{1,0:T(8,128)(2,1)S(1)}, u32[]{:S(2)}, u32[]{:S(2)}) collective-permute-start(bf16[384,384]{1,0:T(8,128)(2,1)S(1)} %get-tuple-element.99.refs_2_.refs_1_.refs_3_), channel_id=1, source_target_pairs={{0,8},{4,12},{8,0},{12,4},{16,24},{20,28},{24,16},{28,20},{1,9},{5... | collective-permute-start | bytes 884744 | tf_op jit(solution)/shard_map/ppermute | solution.py:395
  77.7 8.8 %collective-permute-start.20 = (bf16[512,384]{1,0:T(8,128)(2,1)S(1)}, bf16[512,384]{1,0:T(8,128)(2,1)S(1)}, u32[]{:S(2)}, u32[]{:S(2)}) collective-permute-start(bf16[512,384]{1,0:T(8,128)(2,1)S(1)} %get-tuple-element.101), channel_id=1, source_target_pairs={{1,2},{2,1},{5,6},{6,5},{9,10},{10,9},{13,14},{14,13},{17,18},{18,... | collective-permute-start | bytes 1179656 | tf_op jit(solution)/shard_map/ppermute | solution.py:395
  78.5 14.5 %collective-permute-start.26 = (bf16[512,384]{1,0:T(8,128)(2,1)S(1)}, bf16[512,384]{1,0:T(8,128)(2,1)S(1)}, u32[]{:S(2)}, u32[]{:S(2)}) collective-permute-start(bf16[512,384]{1,0:T(8,128)(2,1)S(1)} %shard_map.136.refs_5_.refs_2_), channel_id=1, source_target_pairs={{1,0},{2,3},{5,4},{6,7},{9,8},{10,11},{13,12},{14,15},{17,16},{18,... | collective-permute-start | bytes 1179656 | tf_op jit(solution)/shard_map/ppermute | solution.py:395
  85.4 23.1 %collective-permute-start.35 = (bf16[384,1152]{1,0:T(8,128)(2,1)S(1)}, bf16[384,1152]{1,0:T(8,128)(2,1)S(1)}, u32[]{:S(2)}, u32[]{:S(2)}) collective-permute-start(bf16[384,1152]{1,0:T(8,128)(2,1)S(1)} %get-tuple-element.114), channel_id=1, source_target_pairs={{0,4},{4,0},{8,12},{12,8},{16,20},{20,16},{24,28},{28,24},{1,5},{5... | collective-permute-start | bytes 2654216 | tf_op jit(solution)/shard_map/ppermute | solution.py:395
  85.5 9.4 %collective-permute-start.28 = (bf16[384,384]{1,0:T(8,128)(2,1)S(1)}, bf16[384,384]{1,0:T(8,128)(2,1)S(1)}, u32[]{:S(2)}, u32[]{:S(2)}) collective-permute-start(bf16[384,384]{1,0:T(8,128)(2,1)S(1)} %get-tuple-element.103.refs_4_.refs_1_.refs_3_), channel_id=1, source_target_pairs={{0,16},{4,20},{8,24},{12,28},{16,0},{20,4},{24,8},{28,12},{1,17},{... | collective-permute-start | bytes 884744 | tf_op jit(solution)/shard_map/ppermute | solution.py:395
  86.0 9.1 %collective-permute-start.27 = (bf16[384,384]{1,0:T(8,128)(2,1)S(1)}, bf16[384,384]{1,0:T(8,128)(2,1)S(1)}, u32[]{:S(2)}, u32[]{:S(2)}) collective-permute-start(bf16[384,384]{1,0:T(8,128)(2,1)S(1)} %get-tuple-element.103.refs_4_.refs_1_.refs_3_), channel_id=1, source_target_pairs={{0,8},{4,12},{8,0},{12,4},{16,24},{20,28},{24,16},{28,20},{1,9},{5... | collective-permute-start | bytes 884744 | tf_op jit(solution)/shard_map/ppermute | solution.py:395
  86.5 22.0 %copy-start.1 = (bf16[1,576,3072]{2,1,0:T(8,128)(2,1)S(1)}, bf16[1,576,3072]{2,1,0:T(8,128)(2,1)}, u32[]{:S(2)}) copy-start(bf16[1,576,3072]{2,1,0:T(8,128)(2,1)} %param.19) | copy-start | bytes 10616836
  86.6 14.0 %collective-permute-start.25 = (bf16[512,384]{1,0:T(8,128)(2,1)S(1)}, bf16[512,384]{1,0:T(8,128)(2,1)S(1)}, u32[]{:S(2)}, u32[]{:S(2)}) collective-permute-start(bf16[512,384]{1,0:T(8,128)(2,1)S(1)} %shard_map.139.refs_5_.refs_2_), channel_id=1, source_target_pairs={{1,0},{2,3},{5,4},{6,7},{9,8},{10,11},{13,12},{14,15},{17,16},{18,... | collective-permute-start | bytes 1179656 | tf_op jit(solution)/shard_map/ppermute | solution.py:395
  95.8 17.0 %collective-permute-start.33 = (bf16[384,1152]{1,0:T(8,128)(2,1)S(1)}, bf16[384,1152]{1,0:T(8,128)(2,1)S(1)}, u32[]{:S(2)}, u32[]{:S(2)}) collective-permute-start(bf16[384,1152]{1,0:T(8,128)(2,1)S(1)} %get-tuple-element.113), channel_id=1, source_target_pairs={{0,4},{4,0},{8,12},{12,8},{16,20},{20,16},{24,28},{28,24},{1,5},{5... | collective-permute-start | bytes 2654216 | tf_op jit(solution)/shard_map/ppermute | solution.py:395
  95.8 9.4 %collective-permute-start.37 = (bf16[384,384]{1,0:T(8,128)(2,1)S(1)}, bf16[384,384]{1,0:T(8,128)(2,1)S(1)}, u32[]{:S(2)}, u32[]{:S(2)}) collective-permute-start(bf16[384,384]{1,0:T(8,128)(2,1)S(1)} %get-tuple-element.108.refs_4_.refs_1_.refs_3_), channel_id=1, source_target_pairs={{0,16},{4,20},{8,24},{12,28},{16,0},{20,4},{24,8},{28,12},{1,17},{... | collective-permute-start | bytes 884744 | tf_op jit(solution)/shard_map/ppermute | solution.py:395
  97.4 9.9 %collective-permute-start.36 = (bf16[384,384]{1,0:T(8,128)(2,1)S(1)}, bf16[384,384]{1,0:T(8,128)(2,1)S(1)}, u32[]{:S(2)}, u32[]{:S(2)}) collective-permute-start(bf16[384,384]{1,0:T(8,128)(2,1)S(1)} %get-tuple-element.108.refs_4_.refs_1_.refs_3_), channel_id=1, source_target_pairs={{0,8},{4,12},{8,0},{12,4},{16,24},{20,28},{24,16},{28,20},{1,9},{5... | collective-permute-start | bytes 884744 | tf_op jit(solution)/shard_map/ppermute | solution.py:395
  100.6 11.4 %collective-permute-start.34 = (bf16[384,384]{1,0:T(8,128)(2,1)S(1)}, bf16[384,384]{1,0:T(8,128)(2,1)S(1)}, u32[]{:S(2)}, u32[]{:S(2)}) collective-permute-start(bf16[384,384]{1,0:T(8,128)(2,1)S(1)} %get-tuple-element.104.refs_2_), channel_id=1, source_target_pairs={{0,16},{4,12},{8,24},{12,4},{16,0},{20,28},{24,8},{28,20},{1,17},{... | collective-permute-start | bytes 884744 | tf_op jit(solution)/shard_map/ppermute | solution.py:395
  101.2 7.3 %copy-start = (bf16[1,576,3072]{2,1,0:T(8,128)(2,1)S(1)}, bf16[1,576,3072]{2,1,0:T(8,128)(2,1)}, u32[]{:S(2)}) copy-start(bf16[1,576,3072]{2,1,0:T(8,128)(2,1)} %param.18) | copy-start | bytes 10616836
  105.3 14.8 %collective-permute-start.31 = (bf16[384,512]{1,0:T(8,128)(2,1)S(1)}, bf16[384,512]{1,0:T(8,128)(2,1)S(1)}, u32[]{:S(2)}, u32[]{:S(2)}) collective-permute-start(bf16[384,512]{1,0:T(8,128)(2,1)S(1)} %get-tuple-element.112.refs_4_.refs_1_.refs_3_), channel_id=1, source_target_pairs={{0,16},{4,20},{8,24},{12,28},{16,0},{20,4},{24,8},{28,12},{1,17},{... | collective-permute-start | bytes 1179656 | tf_op jit(solution)/shard_map/ppermute | solution.py:395
  107.3 12.7 %collective-permute-start.30 = (bf16[384,512]{1,0:T(8,128)(2,1)S(1)}, bf16[384,512]{1,0:T(8,128)(2,1)S(1)}, u32[]{:S(2)}, u32[]{:S(2)}) collective-permute-start(bf16[384,512]{1,0:T(8,128)(2,1)S(1)} %get-tuple-element.112.refs_4_.refs_1_.refs_3_), channel_id=1, source_target_pairs={{0,8},{4,12},{8,0},{12,4},{16,24},{20,28},{24,16},{28,20},{1,9},{5... | collective-permute-start | bytes 1179656 | tf_op jit(solution)/shard_map/ppermute | solution.py:395
  112.1 1.6 %collective-permute-start.38 = (bf16[384,384]{1,0:T(8,128)(2,1)S(1)}, bf16[384,384]{1,0:T(8,128)(2,1)S(1)}, u32[]{:S(2)}, u32[]{:S(2)}) collective-permute-start(bf16[384,384]{1,0:T(8,128)(2,1)S(1)} %shard_map.145.refs_7_.refs_15_), channel_id=1, source_target_pairs={{0,4},{4,0},{8,12},{12,8},{16,20},{20,16},{24,28},{28,24},{1,5},{5... | collective-permute-start | bytes 884744 | tf_op jit(solution)/shard_map/ppermute | solution.py:395
  112.2 7.8 %collective-permute-start.32 = (bf16[384,384]{1,0:T(8,128)(2,1)S(1)}, bf16[384,384]{1,0:T(8,128)(2,1)S(1)}, u32[]{:S(2)}, u32[]{:S(2)}) collective-permute-start(bf16[384,384]{1,0:T(8,128)(2,1)S(1)} %get-tuple-element.109.refs_8_), channel_id=1, source_target_pairs={{0,16},{4,12},{8,24},{12,4},{16,0},{20,28},{24,8},{28,20},{1,17},{... | collective-permute-start | bytes 884744 | tf_op jit(solution)/shard_map/ppermute | solution.py:395
  120.7 12.2 %collective-permute-start.40 = (bf16[384,1536]{1,0:T(8,128)(2,1)S(1)}, bf16[384,1536]{1,0:T(8,128)(2,1)S(1)}, u32[]{:S(2)}, u32[]{:S(2)}) collective-permute-start(bf16[384,1536]{1,0:T(8,128)(2,1)S(1)} %get-tuple-element.124), channel_id=1, source_target_pairs={{0,4},{4,0},{8,12},{12,8},{16,20},{20,16},{24,28},{28,24},{1,5},{5... | collective-permute-start | bytes 3538952 | tf_op jit(solution)/shard_map/ppermute | solution.py:395
  121.9 3.7 %collective-permute-start.41 = (bf16[384,1152]{1,0:T(8,128)(2,1)S(1)}, bf16[384,1152]{1,0:T(8,128)(2,1)S(1)}, u32[]{:S(2)}, u32[]{:S(2)}) collective-permute-start(bf16[384,1152]{1,0:T(8,128)(2,1)S(1)} %get-tuple-element.125), channel_id=1, source_target_pairs={{0,4},{4,0},{8,12},{12,8},{16,20},{20,16},{24,28},{28,24},{1,5},{5... | collective-permute-start | bytes 2654216 | tf_op jit(solution)/shard_map/ppermute | solution.py:395
  121.9 17.3 %collective-permute-start.39 = (bf16[384,512]{1,0:T(8,128)(2,1)S(1)}, bf16[384,512]{1,0:T(8,128)(2,1)S(1)}, u32[]{:S(2)}, u32[]{:S(2)}) collective-permute-start(bf16[384,512]{1,0:T(8,128)(2,1)S(1)} %get-tuple-element.123.refs_17_), channel_id=1, source_target_pairs={{0,16},{4,12},{8,24},{12,4},{16,0},{20,28},{24,8},{28,20},{1,17},{... | collective-permute-start | bytes 1179656 | tf_op jit(solution)/shard_map/ppermute | solution.py:395
  122.8 3.2 %collective-permute-start.42 = (bf16[384,384]{1,0:T(8,128)(2,1)S(1)}, bf16[384,384]{1,0:T(8,128)(2,1)S(1)}, u32[]{:S(2)}, u32[]{:S(2)}) collective-permute-start(bf16[384,384]{1,0:T(8,128)(2,1)S(1)} %shard_map.147.refs_4_.refs_7_), channel_id=1, source_target_pairs={{0,4},{4,0},{8,12},{12,8},{16,20},{20,16},{24,28},{28,24},{1,5},{5... | collective-permute-start | bytes 884744 | tf_op jit(solution)/shard_map/ppermute | solution.py:395
  122.8 10.0 %collective-permute-start.43 = (bf16[384,384]{1,0:T(8,128)(2,1)S(1)}, bf16[384,384]{1,0:T(8,128)(2,1)S(1)}, u32[]{:S(2)}, u32[]{:S(2)}) collective-permute-start(bf16[384,384]{1,0:T(8,128)(2,1)S(1)} %get-tuple-element.115.refs_7_), channel_id=1, source_target_pairs={{0,16},{4,12},{8,24},{12,4},{16,0},{20,28},{24,8},{28,20},{1,17},{... | collective-permute-start | bytes 884744 | tf_op jit(solution)/shard_map/ppermute | solution.py:395
  139.3 3.8 %collective-permute-start.45 = (bf16[384,512]{1,0:T(8,128)(2,1)S(1)}, bf16[384,512]{1,0:T(8,128)(2,1)S(1)}, u32[]{:S(2)}, u32[]{:S(2)}) collective-permute-start(bf16[384,512]{1,0:T(8,128)(2,1)S(1)} %shard_map.152.refs_6_.refs_5_), channel_id=1, source_target_pairs={{0,4},{4,0},{8,12},{12,8},{16,20},{20,16},{24,28},{28,24},{1,5},{5... | collective-permute-start | bytes 1179656 | tf_op jit(solution)/shard_map/ppermute | solution.py:395
  139.3 3.8 %collective-permute-start.44 = (bf16[384,384]{1,0:T(8,128)(2,1)S(1)}, bf16[384,384]{1,0:T(8,128)(2,1)S(1)}, u32[]{:S(2)}, u32[]{:S(2)}) collective-permute-start(bf16[384,384]{1,0:T(8,128)(2,1)S(1)} %shard_map.150.refs_13_.refs_3_), channel_id=1, source_target_pairs={{0,4},{4,0},{8,12},{12,8},{16,20},{20,16},{24,28},{28,24},{1,5},{5... | collective-permute-start | bytes 884744 | tf_op jit(solution)/shard_map/ppermute | solution.py:395
  139.8 1.9 %collective-permute-start.29 = (bf16[64,1536]{1,0:T(8,128)(2,1)S(1)}, bf16[64,1536]{1,0:T(8,128)(2,1)S(1)}, u32[]{:S(2)}, u32[]{:S(2)}) collective-permute-start(bf16[64,1536]{1,0:T(8,128)(2,1)S(1)} %get-tuple-element.110), channel_id=1, source_target_pairs={{0,4},{4,0},{8,12},{12,8},{16,20},{20,16},{24,28},{28,24},{1,5},{5... | collective-permute-start | bytes 589832 | tf_op jit(solution)/shard_map/ppermute | solution.py:395

commit v10 on v8

--- a/solution.py
+++ b/solution.py
@@ -258,11 +258,14 @@
     return out.astype(BF16)
 
 
-def pack_kernel(place_ref, own_ref, near_ref, far_ref, onward_ref, pack_ref):
-    wide = own_ref.shape[1]
+def pack_kernel(place_ref, own_ref, near_ref, far_ref, *refs):
+    rows, (onward_ref, pack_ref) = refs[:-2], refs[-2:]
+    slots, wide = own_ref.shape
+    for ref in rows:
+        pack_ref[slots:, : ref.shape[1]] = ref[...]
     onward_ref[...] = jnp.where(place_ref[1] == 0, near_ref[...], far_ref[...])
     for n, ref in enumerate((own_ref, near_ref, far_ref)):
-        pack_ref[:, n * wide : (n + 1) * wide] = ref[...]
+        pack_ref[:slots, n * wide : (n + 1) * wide] = ref[...]
 
 
 def copy_kernel(in_ref, out_ref):
@@ -274,15 +277,16 @@
 
 
 def mixed_kernel(place_ref, got_ref, *refs):
-    mixed, out_ref = refs[:-1], refs[-1]
+    mixed, (mark_ref, out_ref) = refs[:-2], refs[-2:]
+    mark_ref[...] = jnp.zeros_like(mark_ref)
     tokens, cols = out_ref.shape[0], mixed[0].shape[1]
-    per = mixed[0].shape[0] // CORES // tokens
+    per, first = mixed[0].shape[0] // CORES // tokens, got_ref.shape[0] - tokens
     own = tile(place_ref[1] * per + place_ref[2], tokens)
     for t, ref in zip(ORDER, mixed):
         block = (place_ref[0] ^ t) * CORES
         n = ORDER.index(t)
         out_ref[:, tile(block + place_ref[1], cols)] = ref[own, :]
-        out_ref[:, tile(block + 1 - place_ref[1], cols)] = got_ref[:, n * cols : (n + 1) * cols]
+        out_ref[:, tile(block + 1 - place_ref[1], cols)] = got_ref[first:, n * cols : (n + 1) * cols]
 
 
 def expert_kernel(t, away, mode, has_sums, place_ref, gate_ref, up_ref, *refs):
@@ -305,7 +309,8 @@
     for n, s in enumerate(away):
         source = place_ref[0] ^ s
         held[n, :, tile(place_ref[1], cols)] = pieces[n][:, :cols]
-        held[n, :, tile(1 - place_ref[1], cols)] = others[:, n * wide : n * wide + cols]
+        slots = held.shape[1]
+        held[n, :, tile(1 - place_ref[1], cols)] = others[:slots, n * wide : n * wide + cols]
         x = held[n]
         at = tile(source ^ t, width)
         gated = dot(gate_ref[:, at], x, NT)
@@ -320,7 +325,8 @@
         lane = lax.broadcasted_iota(jnp.int32, (8, LANES), 1)
         pick = (lane < 3).astype(BF16)
         squares = dot(pick, pieces[n][:, cols:], NT)
-        squares = squares + dot(pick, others[:, n * wide + cols : (n + 1) * wide], NT)
+        extra = others[:slots, n * wide + cols : (n + 1) * wide]
+        squares = squares + dot(pick, extra, NT)
         scale = lax.rsqrt(squares[0:1, :] / model + 1e-05)
         gated, lifted = gated * scale, lifted * scale
         silu = (0.5 * gated) * (1.0 + jnp.tanh(0.5 * gated))
@@ -546,15 +552,16 @@
         moved["near", n] = send(x, "ctx", [(d, d ^ 2) for d in range(8)])
         moved["far", n] = send(x, "ctx", [(d, d ^ 4) for d in range(8)])
         if gives:
-            moved["mixed"] = swap(gives[0])
+            moved["rows"] = gives[0]
 
     def forward(n):
         x = moved["own", n]
+        rows = [moved["rows"]] if n == end else []
         out, pack = run(
             pack_kernel,
-            [like(x.shape), like((slots, 3 * wide[n]))],
-            [place, x, moved["near", n], moved["far", n]],
-            specs=[SM] + [VM] * 3,
+            [like(x.shape), like((slots + tokens * len(rows), 3 * wide[n]))],
+            [place, x, moved["near", n], moved["far", n]] + rows,
+            specs=[SM] + [VM] * (3 + len(rows)),
         )
         moved["diagonal", n] = onward(out)
         moved["others", n] = swap(pack)
@@ -576,6 +583,14 @@
 
     def farther(n):
         experts(n, (3,), [moved["diagonal", n]], moved["rest", n])
+
+    def finish_rows(n):
+        mark, moved["out"] = run(
+            mixed_kernel,
+            [like((8, LANES), F32), like((tokens, model))],
+            [place, moved["others", end]] + mixed,
+            specs=[SM] + [VM] * (GROUPS + 1),
+        )
 
     def fetch(n):
         top = send(cut(weight_x, 0), "ctx", [(d, d ^ 4) for d in range(8)])
@@ -589,18 +604,10 @@
         (forward, 1), (dispatch, 3), (forward, 2), (nearer, 0), (diagonal, 0), (nearer, 1),
         (farther, 0), (diagonal, 1), (forward, 3), (farther, 1), (nearer, 2), (diagonal, 2),
         (farther, 2), (nearer, 3),
+        (diagonal, 3), (finish_rows, 0), (farther, 3),
     ):
         work(n)
-    mixed_out = call(
-        mixed_kernel,
-        like((tokens, model)),
-        [place, moved["mixed"]] + mixed,
-        deps=last[:],
-        specs=[SM] + [VM] * (GROUPS + 1),
-    )
-    diagonal(3)
-    farther(3)
-    return (mixed_out, hidden[None])
+    return (moved["out"], hidden[None])
 
 
 def entering(value, axis, combine, identity):

time: 146 us -> 146 us (level)
    ppermute x46 -> x45, starting transfers between devices: 51.8 us -> 51.3 us  [send(): return lax.ppermute(x, axis, pairs)]
    ppermute x46 -> x45, waiting for transfers between devices: 42 us -> 42.4 us  [send(): return lax.ppermute(x, axis, pairs)]
  transfers between devices with their start and end apart: 46 -> 45, of which waited for: 22 -> 22; matrix products, arithmetic and copies ran while one was open for 2% -> 2% of each run, Pallas kernels for 28% -> 27%
where the time goes in v10:
time: 146 us; the launch traced here: 145 us
  starting transfers between devices  51.3 us (35%)
  Pallas kernels  45.3 us (31%)
  waiting for transfers between devices  42.4 us (29%)
  local copies, waits for them, and re-layouts  2.39 us (2%)
  other arithmetic  2.39 us (2%)
  between operations  1.5 us (1%)
    ppermute x45, starting transfers between devices, send(): return lax.ppermute(x, axis, pairs)  51.3 us
    pallas_call x45, Pallas kernels, call(): pl.pallas_call(body, out_shape=out_shape, in_specs=list(specs or [VM] * c...  45.3 us
    ppermute x45, waiting for transfers between devices, send(): return lax.ppermute(x, axis, pairs)  42.4 us
  transfers between devices with their start and end apart: 45, of which 22 were waited for; matrix products, arithmetic and copies ran while one was open for 2% of the time, Pallas kernels for 27%

profile of v10, /device:TPU:0, one launch (start us, length us, event | category | flops | bytes accessed | tf_op | source)
XLA Modules:
  0.0 145.2 jit_solution(15325391035057048568)
XLA Ops:
  0.6 3.0 %collective-permute-start.4 = (bf16[1024,384]{1,0:T(8,128)(2,1)}, bf16[1024,384]{1,0:T(8,128)(2,1)S(1)}, u32[]{:S(2)}, u32[]{:S(2)}) collective-permute-start(bf16[1024,384]{1,0:T(8,128)(2,1)} %refs_5_.1), channel_id=1, source_target_pairs={{0,16},{4,20},{8,24},{12,28},{16,0},{20,4},{24,8},{28,12},{1,17},{... | collective-permute-start | bytes 2359304 | tf_op jit(solution)/shard_map/ppermute | solution.py:389
  3.7 0.7 multiply_bitcast_fusion
  4.4 0.8 add_select_fusion
  6.4 1.0 copy-done.5
  7.4 1.0 copy-done.6
  8.5 1.4 shard_map.113
  10.5 1.0 collective-permute-done.refs_2_
  11.6 1.6 %collective-permute-start.1 = (f32[4,128,128]{2,1,0:T(8,128)S(1)}, f32[4,128,128]{2,1,0:T(8,128)S(1)}, u32[]{:S(2)}, u32[]{:S(2)}) collective-permute-start(f32[4,128,128]{2,1,0:T(8,128)S(1)} %get-tuple-element.83.refs_2_), channel_id=1, source_target_pairs={{0,8},{4,12},{8,0},{12,4},{16,24},{20,28},{24,16},{28,20},{1,9},{5... | collective-permute-start | bytes 786440 | tf_op jit(solution)/shard_map/ppermute | solution.py:389
  13.1 1.6 %collective-permute-start.2 = (s32[8,128]{1,0:T(8,128)S(1)}, s32[8,128]{1,0:T(8,128)S(1)}, u32[]{:S(2)}, u32[]{:S(2)}) collective-permute-start(s32[8,128]{1,0:T(8,128)S(1)} %pad.4.refs_4_.refs_0_), channel_id=1, source_target_pairs={{0,1},{1,0},{2,3},{3,2},{4,5},{5,4},{6,7},{7,6},{8,9},{9,8},{10,11... | collective-permute-start | bytes 12296 | tf_op jit(solution)/shard_map/ppermute | solution.py:389
  14.7 1.1 shard_map.115
  15.8 0.9 collective-permute-done.2.refs_1_
  16.7 3.2 %collective-permute-done.1.refs_1_ = f32[4,128,128]{2,1,0:T(8,128)S(1)} collective-permute-done((f32[4,128,128]{2,1,0:T(8,128)S(1)}, f32[4,128,128]{2,1,0:T(8,128)S(1)}, u32[]{:S(2)}, u32[]{:S(2)}) %collective-permute-start.1) | collective-permute-done | bytes 262176 | tf_op jit(solution)/shard_map/ppermute | solution.py:389
  20.0 1.5 %collective-permute-done.4.refs_5_.refs_0_ = bf16[1024,384]{1,0:T(8,128)(2,1)S(1)} collective-permute-done((bf16[1024,384]{1,0:T(8,128)(2,1)}, bf16[1024,384]{1,0:T(8,128)(2,1)S(1)}, u32[]{:S(2)}, u32[]{:S(2)}) %collective-permute-start.4) | collective-permute-done | bytes 786464 | tf_op jit(solution)/shard_map/ppermute | solution.py:389
  21.5 3.7 %collective-permute-start.5 = (f32[4,128,128]{2,1,0:T(8,128)S(1)}, f32[4,128,128]{2,1,0:T(8,128)S(1)}, u32[]{:S(2)}, u32[]{:S(2)}) collective-permute-start(f32[4,128,128]{2,1,0:T(8,128)S(1)} %get-tuple-element.85), channel_id=1, source_target_pairs={{0,16},{4,20},{8,24},{12,28},{1,17},{5,21},{9,25},{13,29},{2,18},{... | collective-permute-start | bytes 786440 | tf_op jit(solution)/shard_map/ppermute | solution.py:389
  25.1 2.7 %collective-permute-start.6 = (s32[8,128]{1,0:T(8,128)S(1)}, s32[8,128]{1,0:T(8,128)S(1)}, u32[]{:S(2)}, u32[]{:S(2)}) collective-permute-start(s32[8,128]{1,0:T(8,128)S(1)} %shard_map.116.refs_3_.refs_1_), channel_id=1, source_target_pairs={{0,2},{1,3},{2,0},{3,1},{4,6},{5,7},{6,4},{7,5},{8,10},{9,11},{10,... | collective-permute-start | bytes 12296 | tf_op jit(solution)/shard_map/ppermute | solution.py:389
  27.9 1.8 %collective-permute-done.6.refs_2_ = s32[8,128]{1,0:T(8,128)S(1)} collective-permute-done((s32[8,128]{1,0:T(8,128)S(1)}, s32[8,128]{1,0:T(8,128)S(1)}, u32[]{:S(2)}, u32[]{:S(2)}) %collective-permute-start.6) | collective-permute-done | bytes 4128 | tf_op jit(solution)/shard_map/ppermute | solution.py:389
  30.5 1.5 %collective-permute-done.7.refs_5_ = f32[4,128,128]{2,1,0:T(8,128)S(1)} collective-permute-done((f32[4,128,128]{2,1,0:T(8,128)S(1)}, f32[4,128,128]{2,1,0:T(8,128)S(1)}, u32[]{:S(2)}, u32[]{:S(2)}) %collective-permute-start.7) | collective-permute-done | bytes 262176 | tf_op jit(solution)/shard_map/ppermute | solution.py:389
  32.0 1.2 shard_map.121.refs_1_.refs_6_
  33.5 1.5 %collective-permute-start.9 = (bf16[1024,384]{1,0:T(8,128)(2,1)S(1)}, bf16[1024,384]{1,0:T(8,128)(2,1)S(1)}, u32[]{:S(2)}, u32[]{:S(2)}) collective-permute-start(bf16[1024,384]{1,0:T(8,128)(2,1)S(1)} %shard_map.118.refs_3_), channel_id=1, source_target_pairs={{0,8},{4,12},{8,0},{12,4},{16,24},{20,28},{24,16},{28,20},{1,9},{5... | collective-permute-start | bytes 2359304 | tf_op jit(solution)/shard_map/ppermute | solution.py:389
  35.2 1.2 shard_map.122
  36.5 3.5 %collective-permute-start.10 = (bf16[512,384]{1,0:T(8,128)(2,1)S(1)}, bf16[512,384]{1,0:T(8,128)(2,1)S(1)}, u32[]{:S(2)}, u32[]{:S(2)}) collective-permute-start(bf16[512,384]{1,0:T(8,128)(2,1)S(1)} %get-tuple-element.89), channel_id=1, source_target_pairs={{0,1},{3,2},{4,5},{7,6},{8,9},{11,10},{12,13},{15,14},{16,17},{19,... | collective-permute-start | bytes 1179656 | tf_op jit(solution)/shard_map/ppermute | solution.py:389
  40.0 1.3 shard_map.123
  41.3 1.3 collective-permute-start.15
  42.7 1.2 collective-permute-done.11.refs_2_
  43.8 0.8 shard_map.124.refs_2_.refs_4_
  44.7 4.8 %collective-permute-done.10.refs_1_ = bf16[512,384]{1,0:T(8,128)(2,1)S(1)} collective-permute-done((bf16[512,384]{1,0:T(8,128)(2,1)S(1)}, bf16[512,384]{1,0:T(8,128)(2,1)S(1)}, u32[]{:S(2)}, u32[]{:S(2)}) %collective-permute-start.10) | collective-permute-done | bytes 393248 | tf_op jit(solution)/shard_map/ppermute | solution.py:389
  50.3 3.0 %collective-permute-done.9.refs_0_.refs_5_ = bf16[1024,384]{1,0:T(8,128)(2,1)S(1)} collective-permute-done((bf16[1024,384]{1,0:T(8,128)(2,1)S(1)}, bf16[1024,384]{1,0:T(8,128)(2,1)S(1)}, u32[]{:S(2)}, u32[]{:S(2)}) %collective-permute-start.9) | collective-permute-done | bytes 786464 | tf_op jit(solution)/shard_map/ppermute | solution.py:389
  53.4 1.6 %collective-permute-start.13 = (bf16[512,384]{1,0:T(8,128)(2,1)S(1)}, bf16[512,384]{1,0:T(8,128)(2,1)S(1)}, u32[]{:S(2)}, u32[]{:S(2)}) collective-permute-start(bf16[512,384]{1,0:T(8,128)(2,1)S(1)} %shard_map.127.refs_6_), channel_id=1, source_target_pairs={{0,8},{4,12},{8,0},{12,4},{16,24},{20,28},{24,16},{28,20},{1,9},{5... | collective-permute-start | bytes 1179656 | tf_op jit(solution)/shard_map/ppermute | solution.py:389
  54.9 2.0 %collective-permute-start.12 = (bf16[512,384]{1,0:T(8,128)(2,1)S(1)}, bf16[512,384]{1,0:T(8,128)(2,1)S(1)}, u32[]{:S(2)}, u32[]{:S(2)}) collective-permute-start(bf16[512,384]{1,0:T(8,128)(2,1)S(1)} %shard_map.126.refs_1_), channel_id=1, source_target_pairs={{0,16},{4,20},{8,24},{12,28},{16,0},{20,4},{24,8},{28,12},{1,17},{... | collective-permute-start | bytes 1179656 | tf_op jit(solution)/shard_map/ppermute | solution.py:389
  56.9 1.2 shard_map.128
  58.2 4.2 %collective-permute-start.19 = (bf16[512,384]{1,0:T(8,128)(2,1)S(1)}, bf16[512,384]{1,0:T(8,128)(2,1)S(1)}, u32[]{:S(2)}, u32[]{:S(2)}) collective-permute-start(bf16[512,384]{1,0:T(8,128)(2,1)S(1)} %get-tuple-element.99), channel_id=1, source_target_pairs={{0,1},{3,2},{4,5},{7,6},{8,9},{11,10},{12,13},{15,14},{16,17},{19,... | collective-permute-start | bytes 1179656 | tf_op jit(solution)/shard_map/ppermute | solution.py:389
  63.3 1.3 collective-permute-start.17
  64.6 0.8 collective-permute-done.12.refs_5_
  65.5 1.2 shard_map.131
  66.7 3.8 %collective-permute-start.16 = (bf16[512,384]{1,0:T(8,128)(2,1)S(1)}, bf16[512,384]{1,0:T(8,128)(2,1)S(1)}, u32[]{:S(2)}, u32[]{:S(2)}) collective-permute-start(bf16[512,384]{1,0:T(8,128)(2,1)S(1)} %get-tuple-element.97), channel_id=1, source_target_pairs={{0,1},{3,2},{4,5},{7,6},{8,9},{11,10},{12,13},{15,14},{16,17},{19,... | collective-permute-start | bytes 1179656 | tf_op jit(solution)/shard_map/ppermute | solution.py:389
  71.5 1.3 collective-permute-start.23
  72.8 1.5 %collective-permute-done.17.refs_1_ = bf16[512,384]{1,0:T(8,128)(2,1)S(1)} collective-permute-done((bf16[512,384]{1,0:T(8,128)(2,1)S(1)}, bf16[512,384]{1,0:T(8,128)(2,1)S(1)}, u32[]{:S(2)}, u32[]{:S(2)}) %collective-permute-start.17) | collective-permute-done | bytes 393248 | tf_op jit(solution)/shard_map/ppermute | solution.py:389
  74.2 0.9 shard_map.134
  75.9 1.5 %collective-permute-start.21 = (bf16[384,384]{1,0:T(8,128)(2,1)S(1)}, bf16[384,384]{1,0:T(8,128)(2,1)S(1)}, u32[]{:S(2)}, u32[]{:S(2)}) collective-permute-start(bf16[384,384]{1,0:T(8,128)(2,1)S(1)} %get-tuple-element.101.refs_2_.refs_1_.refs_3_), channel_id=1, source_target_pairs={{0,8},{4,12},{8,0},{12,4},{16,24},{20,28},{24,16},{28,20},{1,9},{5... | collective-permute-start | bytes 884744 | tf_op jit(solution)/shard_map/ppermute | solution.py:389
  78.5 1.3 collective-permute-start.26
  79.8 4.0 %collective-permute-done.23.refs_1_ = bf16[512,384]{1,0:T(8,128)(2,1)S(1)} collective-permute-done((bf16[512,384]{1,0:T(8,128)(2,1)S(1)}, bf16[512,384]{1,0:T(8,128)(2,1)S(1)}, u32[]{:S(2)}, u32[]{:S(2)}) %collective-permute-start.23) | collective-permute-done | bytes 393248 | tf_op jit(solution)/shard_map/ppermute | solution.py:389
  83.8 0.9 shard_map.137
  86.6 1.7 %collective-permute-start.25 = (bf16[512,384]{1,0:T(8,128)(2,1)S(1)}, bf16[512,384]{1,0:T(8,128)(2,1)S(1)}, u32[]{:S(2)}, u32[]{:S(2)}) collective-permute-start(bf16[512,384]{1,0:T(8,128)(2,1)S(1)} %shard_map.139.refs_5_.refs_2_), channel_id=1, source_target_pairs={{1,0},{2,3},{5,4},{6,7},{9,8},{10,11},{13,12},{14,15},{17,16},{18,... | collective-permute-start | bytes 1179656 | tf_op jit(solution)/shard_map/ppermute | solution.py:389
  88.4 4.0 %collective-permute-done.26.refs_1_ = bf16[512,384]{1,0:T(8,128)(2,1)S(1)} collective-permute-done((bf16[512,384]{1,0:T(8,128)(2,1)S(1)}, bf16[512,384]{1,0:T(8,128)(2,1)S(1)}, u32[]{:S(2)}, u32[]{:S(2)}) %collective-permute-start.26) | collective-permute-done | bytes 393248 | tf_op jit(solution)/shard_map/ppermute | solution.py:389
  92.4 0.9 shard_map.140
  95.1 5.4 %collective-permute-done.25.refs_1_ = bf16[512,384]{1,0:T(8,128)(2,1)S(1)} collective-permute-done((bf16[512,384]{1,0:T(8,128)(2,1)S(1)}, bf16[512,384]{1,0:T(8,128)(2,1)S(1)}, u32[]{:S(2)}, u32[]{:S(2)}) %collective-permute-start.25) | collective-permute-done | bytes 393248 | tf_op jit(solution)/shard_map/ppermute | solution.py:389
  100.6 1.2 collective-permute-start.32
  101.8 1.3 shard_map.142
  104.4 0.8 collective-permute-start.29
  105.9 3.5 %shard_map.144 = (f32[576,384]{1,0:T(8,128)S(1)}, f32[576,384]{1,0:T(8,128)S(1)}, f32[576,384]{1,0:T(8,128)S(1)}, f32[576,384]{1,0:T(8,128)S(1)}, f32[576,384]{1,0:T(8,128)S(1)}, /*index=5*/f32[576,384]{1,0:T(8,128)S(1)}) custom-call(s32[3]{0:T(128)S(1)} %pad_add_fusion.refs_0_, bf16[576,3072]{1,0:T(8,128)(2,1)S(1)} %bitcast.20, ...), custom_call_target="tpu_custom_call" | custom-call | flops 1 | bytes 1 | tf_op jit(solution)/shard_map/pallas_call | solution.py:45
  109.5 1.6 %collective-permute-start.31 = (bf16[384,384]{1,0:T(8,128)(2,1)S(1)}, bf16[384,384]{1,0:T(8,128)(2,1)S(1)}, u32[]{:S(2)}, u32[]{:S(2)}) collective-permute-start(bf16[384,384]{1,0:T(8,128)(2,1)S(1)} %get-tuple-element.111.refs_8_), channel_id=1, source_target_pairs={{0,16},{4,12},{8,24},{12,4},{16,0},{20,28},{24,8},{28,20},{1,17},{... | collective-permute-start | bytes 884744 | tf_op jit(solution)/shard_map/ppermute | solution.py:389
  111.1 3.6 %shard_map.146 = (f32[576,384]{1,0:T(8,128)S(1)}, f32[576,384]{1,0:T(8,128)S(1)}, f32[576,384]{1,0:T(8,128)S(1)}, f32[576,384]{1,0:T(8,128)S(1)}, f32[576,384]{1,0:T(8,128)S(1)}, /*index=5*/f32[576,384]{1,0:T(8,128)S(1)}) custom-call(s32[3]{0:T(128)S(1)} %pad_add_fusion.refs_0_, bf16[576,3072]{1,0:T(8,128)(2,1)S(1)} %bitcast.21, ...), custom_call_target="tpu_custom_call" | custom-call | flops 1 | bytes 1 | tf_op jit(solution)/shard_map/pallas_call | solution.py:45
  114.7 1.7 %shard_map.147 = (f32[576,384]{1,0:T(8,128)S(1)}, f32[576,384]{1,0:T(8,128)S(1)}) custom-call(s32[3]{0:T(128)S(1)} %pad_add_fusion.refs_0_, bf16[576,3072]{1,0:T(8,128)(2,1)S(1)} %bitcast.22, bf16[576,3072]{1,0:T(8,128)(2,1)S(1)} %bitcast.30, bf16[384,384]{1,0:T(8,128)(2,1)S(1)} %shard_map.145.refs_13_.refs_3_, ...), custom_call_target="tpu_custom_call" | custom-call | flops 1 | bytes 1 | tf_op jit(solution)/shard_map/pallas_call | solution.py:45
  116.4 2.5 %collective-permute-done.31.refs_0_ = bf16[384,384]{1,0:T(8,128)(2,1)S(1)} collective-permute-done((bf16[384,384]{1,0:T(8,128)(2,1)S(1)}, bf16[384,384]{1,0:T(8,128)(2,1)S(1)}, u32[]{:S(2)}, u32[]{:S(2)}) %collective-permute-start.31) | collective-permute-done | bytes 294944 | tf_op jit(solution)/shard_map/ppermute | solution.py:389
  120.3 1.2 collective-permute-start.42
  121.5 0.8 collective-permute-start.39
  122.3 2.2 %collective-permute-done.41.refs_4_ = bf16[384,384]{1,0:T(8,128)(2,1)S(1)} collective-permute-done((bf16[384,384]{1,0:T(8,128)(2,1)S(1)}, bf16[384,384]{1,0:T(8,128)(2,1)S(1)}, u32[]{:S(2)}, u32[]{:S(2)}) %collective-permute-start.41) | collective-permute-done | bytes 294944 | tf_op jit(solution)/shard_map/ppermute | solution.py:389
  124.5 1.7 %shard_map.150 = (f32[576,384]{1,0:T(8,128)S(1)}, f32[576,384]{1,0:T(8,128)S(1)}) custom-call(s32[3]{0:T(128)S(1)} %pad_add_fusion.refs_0_, bf16[576,3072]{1,0:T(8,128)(2,1)S(1)} %bitcast.23, bf16[576,3072]{1,0:T(8,128)(2,1)S(1)} %bitcast.31, bf16[384,384]{1,0:T(8,128)(2,1)S(1)} %shard_map.148.refs_5_.refs_3_, ...), custom_call_target="tpu_custom_call" | custom-call | flops 1 | bytes 1 | tf_op jit(solution)/shard_map/pallas_call | solution.py:45
  126.2 3.6 %shard_map.151 = (f32[576,384]{1,0:T(8,128)S(1)}, f32[576,384]{1,0:T(8,128)S(1)}, f32[576,384]{1,0:T(8,128)S(1)}, f32[576,384]{1,0:T(8,128)S(1)}, f32[576,384]{1,0:T(8,128)S(1)}, /*index=5*/f32[576,384]{1,0:T(8,128)S(1)}) custom-call(s32[3]{0:T(128)S(1)} %pad_add_fusion.refs_0_, bf16[576,3072]{1,0:T(8,128)(2,1)S(1)} %bitcast.24, ...), custom_call_target="tpu_custom_call" | custom-call | flops 1 | bytes 1 | tf_op jit(solution)/shard_map/pallas_call | solution.py:45
  130.0 1.4 collective-permute-done.43.refs_4_
  131.5 1.7 %shard_map.153 = (f32[576,384]{1,0:T(8,128)S(1)}, f32[576,384]{1,0:T(8,128)S(1)}) custom-call(s32[3]{0:T(128)S(1)} %pad_add_fusion.refs_0_, bf16[576,3072]{1,0:T(8,128)(2,1)S(1)} %bitcast.25, bf16[576,3072]{1,0:T(8,128)(2,1)S(1)} %bitcast.33, bf16[384,384]{1,0:T(8,128)(2,1)S(1)} %shard_map.152.refs_3_.refs_7_, ...), custom_call_target="tpu_custom_call" | custom-call | flops 1 | bytes 1 | tf_op jit(solution)/shard_map/pallas_call | solution.py:45
  133.2 6.4 %shard_map.154 = (bf16[576,1536]{1,0:T(8,128)(2,1)}, f32[8,128]{1,0:T(8,128)S(1)}) custom-call(s32[3]{0:T(128)S(1)} %pad_add_fusion.refs_0_, bf16[576,3072]{1,0:T(8,128)(2,1)S(1)} %bitcast.26, bf16[576,3072]{1,0:T(8,128)(2,1)S(1)} %bitcast.34, bf16[384,512]{1,0:T(8,128)(2,1)S(1)} %get-tuple-element.112.refs_4_.refs_1_.refs_3_, ...), custom_call_target="tpu_custom_call" | custom-call | flops 1 | bytes 1 | tf_op jit(solution)/shard_map/pallas_call | solution.py:45
  139.9 1.3 shard_map.156
  141.5 3.6 %shard_map.157 = (bf16[576,1536]{1,0:T(8,128)(2,1)}, f32[8,128]{1,0:T(8,128)}) custom-call(s32[3]{0:T(128)S(1)} %pad_add_fusion.refs_0_, bf16[576,3072]{1,0:T(8,128)(2,1)S(1)} %bitcast.27, bf16[576,3072]{1,0:T(8,128)(2,1)S(1)} %bitcast.35, bf16[384,512]{1,0:T(8,128)(2,1)S(1)} %shard_map.155.refs_6_.refs_3_, ...), custom_call_target="tpu_custom_call", output_to_operand_aliasing={{0}: (7, {})} | custom-call | flops 1 | bytes 1 | tf_op jit(solution)/shard_map/pallas_call | solution.py:45
  (101 shorter events, 15.4 us)
Async XLA Ops:
  0.6 14.1 %copy-start.4 = (bf16[256,1024]{1,0:T(8,128)(2,1)S(1)}, bf16[256,1024]{1,0:T(8,128)(2,1)}, u32[]{:S(2)}) copy-start(bf16[256,1024]{1,0:T(8,128)(2,1)} %refs_1_.1) | copy-start | bytes 1572868
  0.6 20.8 %collective-permute-start.4 = (bf16[1024,384]{1,0:T(8,128)(2,1)}, bf16[1024,384]{1,0:T(8,128)(2,1)S(1)}, u32[]{:S(2)}, u32[]{:S(2)}) collective-permute-start(bf16[1024,384]{1,0:T(8,128)(2,1)} %refs_5_.1), channel_id=1, source_target_pairs={{0,16},{4,20},{8,24},{12,28},{16,0},{20,4},{24,8},{28,12},{1,17},{... | collective-permute-start | bytes 2359304 | tf_op jit(solution)/shard_map/ppermute | solution.py:389
  6.4 1.0 copy-start.5
  7.4 1.0 copy-start.6
  9.9 1.6 %collective-permute-start = (f32[4,128,128]{2,1,0:T(8,128)S(1)}, f32[4,128,128]{2,1,0:T(8,128)S(1)}, u32[]{:S(2)}, u32[]{:S(2)}) collective-permute-start(f32[4,128,128]{2,1,0:T(8,128)S(1)} %get-tuple-element.79), channel_id=1, source_target_pairs={{0,4},{4,0},{8,12},{12,8},{16,20},{20,16},{24,28},{28,24},{1,5},{5... | collective-permute-start | bytes 786440 | tf_op jit(solution)/shard_map/ppermute | solution.py:389
  10.0 6.8 %collective-permute-start.3 = (bf16[64,3072]{1,0:T(8,128)(2,1)}, bf16[64,3072]{1,0:T(8,128)(2,1)S(1)}, u32[]{:S(2)}, u32[]{:S(2)}) collective-permute-start(bf16[64,3072]{1,0:T(8,128)(2,1)} %refs_3_.9), channel_id=1, source_target_pairs={{0,4},{4,0},{8,12},{12,8},{16,20},{20,16},{24,28},{28,24},{1,5},{5... | collective-permute-start | bytes 1179656 | tf_op jit(solution)/shard_map/ppermute | solution.py:389
  11.6 8.4 %collective-permute-start.1 = (f32[4,128,128]{2,1,0:T(8,128)S(1)}, f32[4,128,128]{2,1,0:T(8,128)S(1)}, u32[]{:S(2)}, u32[]{:S(2)}) collective-permute-start(f32[4,128,128]{2,1,0:T(8,128)S(1)} %get-tuple-element.83.refs_2_), channel_id=1, source_target_pairs={{0,8},{4,12},{8,0},{12,4},{16,24},{20,28},{24,16},{28,20},{1,9},{5... | collective-permute-start | bytes 786440 | tf_op jit(solution)/shard_map/ppermute | solution.py:389
  13.1 3.6 %collective-permute-start.2 = (s32[8,128]{1,0:T(8,128)S(1)}, s32[8,128]{1,0:T(8,128)S(1)}, u32[]{:S(2)}, u32[]{:S(2)}) collective-permute-start(s32[8,128]{1,0:T(8,128)S(1)} %pad.4.refs_4_.refs_0_), channel_id=1, source_target_pairs={{0,1},{1,0},{2,3},{3,2},{4,5},{5,4},{6,7},{7,6},{8,9},{9,8},{10,11... | collective-permute-start | bytes 12296 | tf_op jit(solution)/shard_map/ppermute | solution.py:389
  15.8 12.0 %copy-start.3 = (bf16[1024,384]{1,0:T(8,128)(2,1)S(1)}, bf16[1024,384]{1,0:T(8,128)(2,1)}, u32[]{:S(2)}) copy-start(bf16[1024,384]{1,0:T(8,128)(2,1)} %refs_5_.1) | copy-start | bytes 2359300
  21.5 8.8 %collective-permute-start.5 = (f32[4,128,128]{2,1,0:T(8,128)S(1)}, f32[4,128,128]{2,1,0:T(8,128)S(1)}, u32[]{:S(2)}, u32[]{:S(2)}) collective-permute-start(f32[4,128,128]{2,1,0:T(8,128)S(1)} %get-tuple-element.85), channel_id=1, source_target_pairs={{0,16},{4,20},{8,24},{12,28},{1,17},{5,21},{9,25},{13,29},{2,18},{... | collective-permute-start | bytes 786440 | tf_op jit(solution)/shard_map/ppermute | solution.py:389
  25.1 4.6 %collective-permute-start.6 = (s32[8,128]{1,0:T(8,128)S(1)}, s32[8,128]{1,0:T(8,128)S(1)}, u32[]{:S(2)}, u32[]{:S(2)}) collective-permute-start(s32[8,128]{1,0:T(8,128)S(1)} %shard_map.116.refs_3_.refs_1_), channel_id=1, source_target_pairs={{0,2},{1,3},{2,0},{3,1},{4,6},{5,7},{6,4},{7,5},{8,10},{9,11},{10,... | collective-permute-start | bytes 12296 | tf_op jit(solution)/shard_map/ppermute | solution.py:389
  30.3 5.0 %copy-start.2 = (bf16[64,3072]{1,0:T(8,128)(2,1)S(1)}, bf16[64,3072]{1,0:T(8,128)(2,1)}, u32[]{:S(2)}) copy-start(bf16[64,3072]{1,0:T(8,128)(2,1)} %refs_3_.9) | copy-start | bytes 1179652
  30.4 1.6 %collective-permute-start.7 = (f32[4,128,128]{2,1,0:T(8,128)S(1)}, f32[4,128,128]{2,1,0:T(8,128)S(1)}, u32[]{:S(2)}, u32[]{:S(2)}) collective-permute-start(f32[4,128,128]{2,1,0:T(8,128)S(1)} %get-tuple-element.87), channel_id=1, source_target_pairs={{0,4},{4,0},{8,12},{12,8},{16,20},{20,16},{24,28},{28,24},{1,5},{5... | collective-permute-start | bytes 786440 | tf_op jit(solution)/shard_map/ppermute | solution.py:389
  33.3 2.0 %collective-permute-start.8 = (bf16[256,1024]{1,0:T(8,128)(2,1)S(1)}, bf16[256,1024]{1,0:T(8,128)(2,1)S(1)}, u32[]{:S(2)}, u32[]{:S(2)}) collective-permute-start(bf16[256,1024]{1,0:T(8,128)(2,1)S(1)} %shard_map.121.refs_1_.refs_6_), channel_id=1, source_target_pairs={{0,4},{4,0},{8,12},{12,8},{16,20},{20,16},{24,28},{28,24},{1,5},{5... | collective-permute-start | bytes 1572872 | tf_op jit(solution)/shard_map/ppermute | solution.py:389
  33.5 19.8 %collective-permute-start.9 = (bf16[1024,384]{1,0:T(8,128)(2,1)S(1)}, bf16[1024,384]{1,0:T(8,128)(2,1)S(1)}, u32[]{:S(2)}, u32[]{:S(2)}) collective-permute-start(bf16[1024,384]{1,0:T(8,128)(2,1)S(1)} %shard_map.118.refs_3_), channel_id=1, source_target_pairs={{0,8},{4,12},{8,0},{12,4},{16,24},{20,28},{24,16},{28,20},{1,9},{5... | collective-permute-start | bytes 2359304 | tf_op jit(solution)/shard_map/ppermute | solution.py:389
  36.5 13.0 %collective-permute-start.10 = (bf16[512,384]{1,0:T(8,128)(2,1)S(1)}, bf16[512,384]{1,0:T(8,128)(2,1)S(1)}, u32[]{:S(2)}, u32[]{:S(2)}) collective-permute-start(bf16[512,384]{1,0:T(8,128)(2,1)S(1)} %get-tuple-element.89), channel_id=1, source_target_pairs={{0,1},{3,2},{4,5},{7,6},{8,9},{11,10},{12,13},{15,14},{16,17},{19,... | collective-permute-start | bytes 1179656 | tf_op jit(solution)/shard_map/ppermute | solution.py:389
  41.3 21.1 %collective-permute-start.15 = (bf16[512,384]{1,0:T(8,128)(2,1)S(1)}, bf16[512,384]{1,0:T(8,128)(2,1)S(1)}, u32[]{:S(2)}, u32[]{:S(2)}) collective-permute-start(bf16[512,384]{1,0:T(8,128)(2,1)S(1)} %get-tuple-element.93), channel_id=1, source_target_pairs={{0,1},{3,2},{4,5},{7,6},{8,9},{11,10},{12,13},{15,14},{16,17},{19,... | collective-permute-start | bytes 1179656 | tf_op jit(solution)/shard_map/ppermute | solution.py:389
  42.6 1.2 collective-permute-start.11
  49.6 13.7 %collective-permute-start.14 = (bf16[512,384]{1,0:T(8,128)(2,1)S(1)}, bf16[512,384]{1,0:T(8,128)(2,1)S(1)}, u32[]{:S(2)}, u32[]{:S(2)}) collective-permute-start(bf16[512,384]{1,0:T(8,128)(2,1)S(1)} %get-tuple-element.92), channel_id=1, source_target_pairs={{1,2},{2,1},{5,6},{6,5},{9,10},{10,9},{13,14},{14,13},{17,18},{18,... | collective-permute-start | bytes 1179656 | tf_op jit(solution)/shard_map/ppermute | solution.py:389
  53.4 11.3 %collective-permute-start.13 = (bf16[512,384]{1,0:T(8,128)(2,1)S(1)}, bf16[512,384]{1,0:T(8,128)(2,1)S(1)}, u32[]{:S(2)}, u32[]{:S(2)}) collective-permute-start(bf16[512,384]{1,0:T(8,128)(2,1)S(1)} %shard_map.127.refs_6_), channel_id=1, source_target_pairs={{0,8},{4,12},{8,0},{12,4},{16,24},{20,28},{24,16},{28,20},{1,9},{5... | collective-permute-start | bytes 1179656 | tf_op jit(solution)/shard_map/ppermute | solution.py:389
  54.9 10.5 %collective-permute-start.12 = (bf16[512,384]{1,0:T(8,128)(2,1)S(1)}, bf16[512,384]{1,0:T(8,128)(2,1)S(1)}, u32[]{:S(2)}, u32[]{:S(2)}) collective-permute-start(bf16[512,384]{1,0:T(8,128)(2,1)S(1)} %shard_map.126.refs_1_), channel_id=1, source_target_pairs={{0,16},{4,20},{8,24},{12,28},{16,0},{20,4},{24,8},{28,12},{1,17},{... | collective-permute-start | bytes 1179656 | tf_op jit(solution)/shard_map/ppermute | solution.py:389
  58.2 12.4 %collective-permute-start.19 = (bf16[512,384]{1,0:T(8,128)(2,1)S(1)}, bf16[512,384]{1,0:T(8,128)(2,1)S(1)}, u32[]{:S(2)}, u32[]{:S(2)}) collective-permute-start(bf16[512,384]{1,0:T(8,128)(2,1)S(1)} %get-tuple-element.99), channel_id=1, source_target_pairs={{0,1},{3,2},{4,5},{7,6},{8,9},{11,10},{12,13},{15,14},{16,17},{19,... | collective-permute-start | bytes 1179656 | tf_op jit(solution)/shard_map/ppermute | solution.py:389
  62.6 8.8 %collective-permute-start.18 = (bf16[512,384]{1,0:T(8,128)(2,1)S(1)}, bf16[512,384]{1,0:T(8,128)(2,1)S(1)}, u32[]{:S(2)}, u32[]{:S(2)}) collective-permute-start(bf16[512,384]{1,0:T(8,128)(2,1)S(1)} %get-tuple-element.98), channel_id=1, source_target_pairs={{1,2},{2,1},{5,6},{6,5},{9,10},{10,9},{13,14},{14,13},{17,18},{18,... | collective-permute-start | bytes 1179656 | tf_op jit(solution)/shard_map/ppermute | solution.py:389
  63.3 10.9 %collective-permute-start.17 = (bf16[512,384]{1,0:T(8,128)(2,1)S(1)}, bf16[512,384]{1,0:T(8,128)(2,1)S(1)}, u32[]{:S(2)}, u32[]{:S(2)}) collective-permute-start(bf16[512,384]{1,0:T(8,128)(2,1)S(1)} %shard_map.130.refs_7_.refs_2_), channel_id=1, source_target_pairs={{1,0},{2,3},{5,4},{6,7},{9,8},{10,11},{13,12},{14,15},{17,16},{18,... | collective-permute-start | bytes 1179656 | tf_op jit(solution)/shard_map/ppermute | solution.py:389
  66.7 10.9 %collective-permute-start.16 = (bf16[512,384]{1,0:T(8,128)(2,1)S(1)}, bf16[512,384]{1,0:T(8,128)(2,1)S(1)}, u32[]{:S(2)}, u32[]{:S(2)}) collective-permute-start(bf16[512,384]{1,0:T(8,128)(2,1)S(1)} %get-tuple-element.97), channel_id=1, source_target_pairs={{0,1},{3,2},{4,5},{7,6},{8,9},{11,10},{12,13},{15,14},{16,17},{19,... | collective-permute-start | bytes 1179656 | tf_op jit(solution)/shard_map/ppermute | solution.py:389
  70.5 3.7 %copy-start.7 = (f32[3072]{0:T(1024)S(1)}, f32[3072]{0:T(1024)}, u32[]{:S(2)}) copy-start(f32[3072]{0:T(1024)} %param.16) | copy-start | bytes 36868
  70.7 7.8 %collective-permute-start.24 = (bf16[512,384]{1,0:T(8,128)(2,1)S(1)}, bf16[512,384]{1,0:T(8,128)(2,1)S(1)}, u32[]{:S(2)}, u32[]{:S(2)}) collective-permute-start(bf16[512,384]{1,0:T(8,128)(2,1)S(1)} %get-tuple-element.104), channel_id=1, source_target_pairs={{1,2},{2,1},{5,6},{6,5},{9,10},{10,9},{13,14},{14,13},{17,18},{18,... | collective-permute-start | bytes 1179656 | tf_op jit(solution)/shard_map/ppermute | solution.py:389
  71.5 12.3 %collective-permute-start.23 = (bf16[512,384]{1,0:T(8,128)(2,1)S(1)}, bf16[512,384]{1,0:T(8,128)(2,1)S(1)}, u32[]{:S(2)}, u32[]{:S(2)}) collective-permute-start(bf16[512,384]{1,0:T(8,128)(2,1)S(1)} %shard_map.133.refs_5_.refs_2_), channel_id=1, source_target_pairs={{1,0},{2,3},{5,4},{6,7},{9,8},{10,11},{13,12},{14,15},{17,16},{18,... | collective-permute-start | bytes 1179656 | tf_op jit(solution)/shard_map/ppermute | solution.py:389
  75.2 10.1 %collective-permute-start.22 = (bf16[384,384]{1,0:T(8,128)(2,1)S(1)}, bf16[384,384]{1,0:T(8,128)(2,1)S(1)}, u32[]{:S(2)}, u32[]{:S(2)}) collective-permute-start(bf16[384,384]{1,0:T(8,128)(2,1)S(1)} %get-tuple-element.101.refs_2_.refs_1_.refs_3_), channel_id=1, source_target_pairs={{0,16},{4,20},{8,24},{12,28},{16,0},{20,4},{24,8},{28,12},{1,17},{... | collective-permute-start | bytes 884744 | tf_op jit(solution)/shard_map/ppermute | solution.py:389
  75.9 9.9 %collective-permute-start.21 = (bf16[384,384]{1,0:T(8,128)(2,1)S(1)}, bf16[384,384]{1,0:T(8,128)(2,1)S(1)}, u32[]{:S(2)}, u32[]{:S(2)}) collective-permute-start(bf16[384,384]{1,0:T(8,128)(2,1)S(1)} %get-tuple-element.101.refs_2_.refs_1_.refs_3_), channel_id=1, source_target_pairs={{0,8},{4,12},{8,0},{12,4},{16,24},{20,28},{24,16},{28,20},{1,9},{5... | collective-permute-start | bytes 884744 | tf_op jit(solution)/shard_map/ppermute | solution.py:389
  77.7 8.8 %collective-permute-start.20 = (bf16[512,384]{1,0:T(8,128)(2,1)S(1)}, bf16[512,384]{1,0:T(8,128)(2,1)S(1)}, u32[]{:S(2)}, u32[]{:S(2)}) collective-permute-start(bf16[512,384]{1,0:T(8,128)(2,1)S(1)} %get-tuple-element.103), channel_id=1, source_target_pairs={{1,2},{2,1},{5,6},{6,5},{9,10},{10,9},{13,14},{14,13},{17,18},{18,... | collective-permute-start | bytes 1179656 | tf_op jit(solution)/shard_map/ppermute | solution.py:389
  78.5 13.9 %collective-permute-start.26 = (bf16[512,384]{1,0:T(8,128)(2,1)S(1)}, bf16[512,384]{1,0:T(8,128)(2,1)S(1)}, u32[]{:S(2)}, u32[]{:S(2)}) collective-permute-start(bf16[512,384]{1,0:T(8,128)(2,1)S(1)} %shard_map.136.refs_5_.refs_2_), channel_id=1, source_target_pairs={{1,0},{2,3},{5,4},{6,7},{9,8},{10,11},{13,12},{14,15},{17,16},{18,... | collective-permute-start | bytes 1179656 | tf_op jit(solution)/shard_map/ppermute | solution.py:389
  84.7 8.6 %collective-permute-start.28 = (bf16[384,384]{1,0:T(8,128)(2,1)S(1)}, bf16[384,384]{1,0:T(8,128)(2,1)S(1)}, u32[]{:S(2)}, u32[]{:S(2)}) collective-permute-start(bf16[384,384]{1,0:T(8,128)(2,1)S(1)} %get-tuple-element.105.refs_4_.refs_1_.refs_3_), channel_id=1, source_target_pairs={{0,16},{4,20},{8,24},{12,28},{16,0},{20,4},{24,8},{28,12},{1,17},{... | collective-permute-start | bytes 884744 | tf_op jit(solution)/shard_map/ppermute | solution.py:389
  85.3 8.1 %collective-permute-start.27 = (bf16[384,384]{1,0:T(8,128)(2,1)S(1)}, bf16[384,384]{1,0:T(8,128)(2,1)S(1)}, u32[]{:S(2)}, u32[]{:S(2)}) collective-permute-start(bf16[384,384]{1,0:T(8,128)(2,1)S(1)} %get-tuple-element.105.refs_4_.refs_1_.refs_3_), channel_id=1, source_target_pairs={{0,8},{4,12},{8,0},{12,4},{16,24},{20,28},{24,16},{28,20},{1,9},{5... | collective-permute-start | bytes 884744 | tf_op jit(solution)/shard_map/ppermute | solution.py:389
  86.4 19.4 %collective-permute-start.33 = (bf16[384,1152]{1,0:T(8,128)(2,1)S(1)}, bf16[384,1152]{1,0:T(8,128)(2,1)S(1)}, u32[]{:S(2)}, u32[]{:S(2)}) collective-permute-start(bf16[384,1152]{1,0:T(8,128)(2,1)S(1)} %get-tuple-element.114), channel_id=1, source_target_pairs={{0,4},{4,0},{8,12},{12,8},{16,20},{20,16},{24,28},{28,24},{1,5},{5... | collective-permute-start | bytes 2654216 | tf_op jit(solution)/shard_map/ppermute | solution.py:389
  86.5 19.3 %copy-start.1 = (bf16[1,576,3072]{2,1,0:T(8,128)(2,1)S(1)}, bf16[1,576,3072]{2,1,0:T(8,128)(2,1)}, u32[]{:S(2)}) copy-start(bf16[1,576,3072]{2,1,0:T(8,128)(2,1)} %param.19) | copy-start | bytes 10616836
  86.6 14.0 %collective-permute-start.25 = (bf16[512,384]{1,0:T(8,128)(2,1)S(1)}, bf16[512,384]{1,0:T(8,128)(2,1)S(1)}, u32[]{:S(2)}, u32[]{:S(2)}) collective-permute-start(bf16[512,384]{1,0:T(8,128)(2,1)S(1)} %shard_map.139.refs_5_.refs_2_), channel_id=1, source_target_pairs={{1,0},{2,3},{5,4},{6,7},{9,8},{10,11},{13,12},{14,15},{17,16},{18,... | collective-permute-start | bytes 1179656 | tf_op jit(solution)/shard_map/ppermute | solution.py:389
  94.0 17.1 %collective-permute-start.37 = (bf16[384,1152]{1,0:T(8,128)(2,1)S(1)}, bf16[384,1152]{1,0:T(8,128)(2,1)S(1)}, u32[]{:S(2)}, u32[]{:S(2)}) collective-permute-start(bf16[384,1152]{1,0:T(8,128)(2,1)S(1)} %get-tuple-element.117), channel_id=1, source_target_pairs={{0,4},{4,0},{8,12},{12,8},{16,20},{20,16},{24,28},{28,24},{1,5},{5... | collective-permute-start | bytes 2654216 | tf_op jit(solution)/shard_map/ppermute | solution.py:389
  94.1 9.4 %collective-permute-start.35 = (bf16[384,384]{1,0:T(8,128)(2,1)S(1)}, bf16[384,384]{1,0:T(8,128)(2,1)S(1)}, u32[]{:S(2)}, u32[]{:S(2)}) collective-permute-start(bf16[384,384]{1,0:T(8,128)(2,1)S(1)} %get-tuple-element.110.refs_4_.refs_1_.refs_3_), channel_id=1, source_target_pairs={{0,16},{4,20},{8,24},{12,28},{16,0},{20,4},{24,8},{28,12},{1,17},{... | collective-permute-start | bytes 884744 | tf_op jit(solution)/shard_map/ppermute | solution.py:389
  94.5 9.9 %collective-permute-start.34 = (bf16[384,384]{1,0:T(8,128)(2,1)S(1)}, bf16[384,384]{1,0:T(8,128)(2,1)S(1)}, u32[]{:S(2)}, u32[]{:S(2)}) collective-permute-start(bf16[384,384]{1,0:T(8,128)(2,1)S(1)} %get-tuple-element.110.refs_4_.refs_1_.refs_3_), channel_id=1, source_target_pairs={{0,8},{4,12},{8,0},{12,4},{16,24},{20,28},{24,16},{28,20},{1,9},{5... | collective-permute-start | bytes 884744 | tf_op jit(solution)/shard_map/ppermute | solution.py:389
  100.6 8.8 %collective-permute-start.32 = (bf16[384,384]{1,0:T(8,128)(2,1)S(1)}, bf16[384,384]{1,0:T(8,128)(2,1)S(1)}, u32[]{:S(2)}, u32[]{:S(2)}) collective-permute-start(bf16[384,384]{1,0:T(8,128)(2,1)S(1)} %get-tuple-element.106.refs_2_), channel_id=1, source_target_pairs={{0,16},{4,12},{8,24},{12,4},{16,0},{20,28},{24,8},{28,20},{1,17},{... | collective-permute-start | bytes 884744 | tf_op jit(solution)/shard_map/ppermute | solution.py:389
  101.8 4.0 %copy-start = (bf16[1,576,3072]{2,1,0:T(8,128)(2,1)S(1)}, bf16[1,576,3072]{2,1,0:T(8,128)(2,1)}, u32[]{:S(2)}) copy-start(bf16[1,576,3072]{2,1,0:T(8,128)(2,1)} %param.18) | copy-start | bytes 10616836
  103.5 15.4 %collective-permute-start.30 = (bf16[384,512]{1,0:T(8,128)(2,1)S(1)}, bf16[384,512]{1,0:T(8,128)(2,1)S(1)}, u32[]{:S(2)}, u32[]{:S(2)}) collective-permute-start(bf16[384,512]{1,0:T(8,128)(2,1)S(1)} %get-tuple-element.112.refs_4_.refs_1_.refs_3_), channel_id=1, source_target_pairs={{0,16},{4,20},{8,24},{12,28},{16,0},{20,4},{24,8},{28,12},{1,17},{... | collective-permute-start | bytes 1179656 | tf_op jit(solution)/shard_map/ppermute | solution.py:389
  104.4 14.6 %collective-permute-start.29 = (bf16[384,512]{1,0:T(8,128)(2,1)S(1)}, bf16[384,512]{1,0:T(8,128)(2,1)S(1)}, u32[]{:S(2)}, u32[]{:S(2)}) collective-permute-start(bf16[384,512]{1,0:T(8,128)(2,1)S(1)} %get-tuple-element.112.refs_4_.refs_1_.refs_3_), channel_id=1, source_target_pairs={{0,8},{4,12},{8,0},{12,4},{16,24},{20,28},{24,16},{28,20},{1,9},{5... | collective-permute-start | bytes 1179656 | tf_op jit(solution)/shard_map/ppermute | solution.py:389
  109.4 5.3 %collective-permute-start.36 = (bf16[384,384]{1,0:T(8,128)(2,1)S(1)}, bf16[384,384]{1,0:T(8,128)(2,1)S(1)}, u32[]{:S(2)}, u32[]{:S(2)}) collective-permute-start(bf16[384,384]{1,0:T(8,128)(2,1)S(1)} %shard_map.145.refs_13_.refs_3_), channel_id=1, source_target_pairs={{0,4},{4,0},{8,12},{12,8},{16,20},{20,16},{24,28},{28,24},{1,5},{5... | collective-permute-start | bytes 884744 | tf_op jit(solution)/shard_map/ppermute | solution.py:389
  109.5 9.4 %collective-permute-start.31 = (bf16[384,384]{1,0:T(8,128)(2,1)S(1)}, bf16[384,384]{1,0:T(8,128)(2,1)S(1)}, u32[]{:S(2)}, u32[]{:S(2)}) collective-permute-start(bf16[384,384]{1,0:T(8,128)(2,1)S(1)} %get-tuple-element.111.refs_8_), channel_id=1, source_target_pairs={{0,16},{4,12},{8,24},{12,4},{16,0},{20,28},{24,8},{28,20},{1,17},{... | collective-permute-start | bytes 884744 | tf_op jit(solution)/shard_map/ppermute | solution.py:389
  119.6 13.6 %collective-permute-start.38 = (bf16[448,1536]{1,0:T(8,128)(2,1)S(1)}, bf16[448,1536]{1,0:T(8,128)(2,1)S(1)}, u32[]{:S(2)}, u32[]{:S(2)}) collective-permute-start(bf16[448,1536]{1,0:T(8,128)(2,1)S(1)} %get-tuple-element.125), channel_id=1, source_target_pairs={{0,4},{4,0},{8,12},{12,8},{16,20},{20,16},{24,28},{28,24},{1,5},{5... | collective-permute-start | bytes 4128776 | tf_op jit(solution)/shard_map/ppermute | solution.py:389
  119.7 6.5 %collective-permute-start.40 = (bf16[384,1152]{1,0:T(8,128)(2,1)S(1)}, bf16[384,1152]{1,0:T(8,128)(2,1)S(1)}, u32[]{:S(2)}, u32[]{:S(2)}) collective-permute-start(bf16[384,1152]{1,0:T(8,128)(2,1)S(1)} %get-tuple-element.128), channel_id=1, source_target_pairs={{0,4},{4,0},{8,12},{12,8},{16,20},{20,16},{24,28},{28,24},{1,5},{5... | collective-permute-start | bytes 2654216 | tf_op jit(solution)/shard_map/ppermute | solution.py:389
  120.2 4.3 %collective-permute-start.41 = (bf16[384,384]{1,0:T(8,128)(2,1)S(1)}, bf16[384,384]{1,0:T(8,128)(2,1)S(1)}, u32[]{:S(2)}, u32[]{:S(2)}) collective-permute-start(bf16[384,384]{1,0:T(8,128)(2,1)S(1)} %shard_map.148.refs_5_.refs_3_), channel_id=1, source_target_pairs={{0,4},{4,0},{8,12},{12,8},{16,20},{20,16},{24,28},{28,24},{1,5},{5... | collective-permute-start | bytes 884744 | tf_op jit(solution)/shard_map/ppermute | solution.py:389
  120.3 9.5 %collective-permute-start.42 = (bf16[384,384]{1,0:T(8,128)(2,1)S(1)}, bf16[384,384]{1,0:T(8,128)(2,1)S(1)}, u32[]{:S(2)}, u32[]{:S(2)}) collective-permute-start(bf16[384,384]{1,0:T(8,128)(2,1)S(1)} %get-tuple-element.115.refs_7_), channel_id=1, source_target_pairs={{0,16},{4,12},{8,24},{12,4},{16,0},{20,28},{24,8},{28,20},{1,17},{... | collective-permute-start | bytes 884744 | tf_op jit(solution)/shard_map/ppermute | solution.py:389
  121.5 18.1 %collective-permute-start.39 = (bf16[384,512]{1,0:T(8,128)(2,1)S(1)}, bf16[384,512]{1,0:T(8,128)(2,1)S(1)}, u32[]{:S(2)}, u32[]{:S(2)}) collective-permute-start(bf16[384,512]{1,0:T(8,128)(2,1)S(1)} %get-tuple-element.127.refs_7_), channel_id=1, source_target_pairs={{0,16},{4,12},{8,24},{12,4},{16,0},{20,28},{24,8},{28,20},{1,17},{... | collective-permute-start | bytes 1179656 | tf_op jit(solution)/shard_map/ppermute | solution.py:389
  129.8 1.6 %collective-permute-start.43 = (bf16[384,384]{1,0:T(8,128)(2,1)S(1)}, bf16[384,384]{1,0:T(8,128)(2,1)S(1)}, u32[]{:S(2)}, u32[]{:S(2)}) collective-permute-start(bf16[384,384]{1,0:T(8,128)(2,1)S(1)} %shard_map.152.refs_3_.refs_7_), channel_id=1, source_target_pairs={{0,4},{4,0},{8,12},{12,8},{16,20},{20,16},{24,28},{28,24},{1,5},{5... | collective-permute-start | bytes 884744 | tf_op jit(solution)/shard_map/ppermute | solution.py:389
  139.7 1.8 %collective-permute-start.44 = (bf16[384,512]{1,0:T(8,128)(2,1)S(1)}, bf16[384,512]{1,0:T(8,128)(2,1)S(1)}, u32[]{:S(2)}, u32[]{:S(2)}) collective-permute-start(bf16[384,512]{1,0:T(8,128)(2,1)S(1)} %shard_map.155.refs_6_.refs_3_), channel_id=1, source_target_pairs={{0,4},{4,0},{8,12},{12,8},{16,20},{20,16},{24,28},{28,24},{1,5},{5... | collective-permute-start | bytes 1179656 | tf_op jit(solution)/shard_map/ppermute | solution.py:389
